TPU v7x, 32 devices: a whole 2x2x4 slice. The times are simulated.
32 devices in a mesh: dp: 8 (over y, x, core), fsdp: 4 (over z).
Axes of the slice: x: 2, y: 2, z: 4, core: 2. Of those that a mesh axis runs over, the one named last changes fastest.
Arguments:
- tokens: bfloat16 [8, 1024, 2048], P('dp', 'fsdp'), may hold values from -6 to 6
- doc_lengths: int32 [8, 8], P('dp'), may hold values from 1 to 512, as said below
- norm_gain: bfloat16 [2048], P(('dp', 'fsdp')), may hold values from 0.099609375 to 1.8984375
- w_query: bfloat16 [2048, 1024], P(('dp', 'fsdp')), may hold values from -0.125 to 0.125
- w_key: bfloat16 [2048, 1024], P(('dp', 'fsdp')), may hold values from -0.125 to 0.125
- w_value: bfloat16 [2048, 2048], P(('dp', 'fsdp')), may hold values from -0.125 to 0.125
- w_outgate: bfloat16 [2048, 2048], P(('dp', 'fsdp')), may hold values from -0.125 to 0.125
- w_lowrank: bfloat16 [2048, 16], P(('dp', 'fsdp')), may hold values from -0.125 to 0.125
- w_gaterank: bfloat16 [16, 1024], P(None, ('dp', 'fsdp')), may hold values from -1.5 to 1.5
- gate_bias: bfloat16 [1024], P(('dp', 'fsdp')), may hold values from -1 to 7
- head_gain: bfloat16 [512], P(('dp', 'fsdp')), may hold values from 0.099609375 to 1.8984375
- w_output: bfloat16 [2048, 2048], P(('dp', 'fsdp')), may hold values from -0.25 to 0.25
- ffn_gain: bfloat16 [2048], P(('dp', 'fsdp')), may hold values from 0.099609375 to 1.8984375
- w_gate: bfloat16 [2048, 5632], P(('dp', 'fsdp')), may hold values from -0.125 to 0.125
- w_up: bfloat16 [2048, 5632], P(('dp', 'fsdp')), may hold values from -0.125 to 0.125
- w_down: bfloat16 [5632, 2048], P(('dp', 'fsdp')), may hold values from -0.15625 to 0.15625
- cotangent: bfloat16 [8, 1024, 2048], P('dp', 'fsdp'), may hold values from -6 to 6
Outputs:
- output: bfloat16 [8, 1024, 2048], P('dp', 'fsdp')
- tokens_grad: bfloat16 [8, 1024, 2048], P('dp', 'fsdp')
- norm_gain_grad: float32 [2048], P(('dp', 'fsdp'))
- w_query_grad: float32 [2048, 1024], P(('dp', 'fsdp'))
- w_key_grad: float32 [2048, 1024], P(('dp', 'fsdp'))
- w_value_grad: float32 [2048, 2048], P(('dp', 'fsdp'))
- w_outgate_grad: float32 [2048, 2048], P(('dp', 'fsdp'))
- w_lowrank_grad: float32 [2048, 16], P(('dp', 'fsdp'))
- w_gaterank_grad: float32 [16, 1024], P(None, ('dp', 'fsdp'))
- gate_bias_grad: float32 [1024], P(('dp', 'fsdp'))
- head_gain_grad: float32 [512], P(('dp', 'fsdp'))
- w_output_grad: float32 [2048, 2048], P(('dp', 'fsdp'))
- ffn_gain_grad: float32 [2048], P(('dp', 'fsdp'))
- w_gate_grad: float32 [2048, 5632], P(('dp', 'fsdp'))
- w_up_grad: float32 [2048, 5632], P(('dp', 'fsdp'))
- w_down_grad: float32 [5632, 2048], P(('dp', 'fsdp'))
Inputs may be any that keep to these rules, and one draw needn't show every extreme that they name: `doc_lengths`: each row lists, in order, the lengths of the 7 documents packed into one sequence, each of 60 to 512 tokens with one of exactly 512, then the padding at the sequence's end, 1 to 59 tokens; a row sums to 1024.
All inputs are finite; a program needn't handle non-finite values.
Results may differ from a plain program's by a relative error of at most 0.018.
Values may be sent and summed in bfloat16 or wider, within the bound.
A program may use at most 328 MiB of HBM per device.

v0:
```python
import jax
import jax.numpy as jnp
from jax import lax
from jax.sharding import PartitionSpec as P

H = 4
DK = 256
DV = 512
C = 64
DOCS = 8


EPS = 1e-05
HEAD_EPS = 1.0
PRECISION_FULL = lax.Precision.HIGHEST


def prefix(value, axis, join, neutral, backward):
    count = lax.axis_size(axis)
    place = lax.axis_index(axis)
    ahead = count - 1 - place if backward else place
    gathered = jax.tree.map(
        lambda a, kind: lax.all_gather(a.astype(kind), axis), value, (jnp.bfloat16, jnp.bfloat16)
    )
    state = jax.tree.map(lambda a, e: jnp.zeros_like(a) + jnp.asarray(e, a.dtype), value, neutral)

    def one(step, state):
        source = count - 1 - step if backward else step
        return join(
            state,
            jax.tree.map(
                lambda a, own: lax.dynamic_index_in_dim(a, source, 0, False).astype(own.dtype),
                gathered,
                value,
            ),
        )

    return lax.fori_loop(0, ahead, one, state)


def matmul(left_op, right_op):
    return jnp.dot(left_op, right_op, preferred_element_type=jnp.float32)


def matmul_high(left_op, right_op):
    return jnp.dot(left_op, right_op, precision=PRECISION_FULL, preferred_element_type=jnp.float32)


def rows_product(left_op, right_op):
    return lax.dot_general(
        left_op, right_op, (((0,), (0,)), ((), ())), preferred_element_type=jnp.float32
    )


def rows_product_high(left_op, right_op):
    return lax.dot_general(
        left_op,
        right_op,
        (((0,), (0,)), ((), ())),
        precision=PRECISION_FULL,
        preferred_element_type=jnp.float32,
    )


def back_product(left_op, right_op):
    return lax.dot_general(
        left_op, right_op, (((1,), (1,)), ((), ())), preferred_element_type=jnp.float32
    )


def back_product_high(left_op, right_op):
    return lax.dot_general(
        left_op,
        right_op,
        (((1,), (1,)), ((), ())),
        precision=PRECISION_FULL,
        preferred_element_type=jnp.float32,
    )


def rms_scale(values, epsilon):
    return lax.rsqrt(jnp.mean(values * values, axis=-1, keepdims=True) + epsilon)


def rms_back(upstream, values, scale_vec):
    return scale_vec * upstream - values * scale_vec**3 * jnp.mean(
        upstream * values, axis=-1, keepdims=True
    )


def to_blocks(matrix, seqs_here, block_count, block_len, head_count):
    inner = matrix.shape[-1] // head_count
    shaped = matrix.reshape(seqs_here, block_count, block_len, head_count, inner)
    return shaped.transpose(0, 1, 3, 2, 4).reshape(
        seqs_here * block_count, head_count, block_len, inner
    )


def from_blocks(blocked, seqs_here, block_count):
    head_count, block_len, inner = (blocked.shape[1], blocked.shape[2], blocked.shape[3])
    shaped = blocked.reshape(seqs_here, block_count, head_count, block_len, inner)
    return shaped.transpose(0, 1, 3, 2, 4).reshape(
        seqs_here * block_count * block_len, head_count * inner
    )


def run_states(initial, decays, updates, backward):

    def advance(carry_state, pair):
        return (pair[0][..., None] * carry_state + pair[1], carry_state)

    final, entering = lax.scan(
        advance,
        initial,
        (jnp.moveaxis(decays, 1, 0), jnp.moveaxis(updates, 1, 0)),
        reverse=backward,
    )
    return (final, jnp.moveaxis(entering, 0, 1))


def chain_combine(earlier, later):
    return (earlier[0] * later[0], later[0][..., None] * earlier[1] + later[1])


def block_weights(cum_logs, segment):
    block_len = cum_logs.shape[1]
    places = jnp.arange(block_len, dtype=jnp.int32)
    same_doc = ((segment[:, None] == segment[None, :]) & (places[:, None] >= places[None, :]))[
        None, :, :, None
    ]
    return jnp.where(
        same_doc,
        jnp.exp(jnp.where(same_doc, cum_logs[:, :, None, :] - cum_logs[:, None, :, :], 0.0)),
        0.0,
    )


def block_output(pieces):
    query_rows, key_rows, value_matrix_rows, cum_logs, segment, carried, initial_recurrent_state = (
        pieces
    )
    weights = block_weights(cum_logs, segment)
    scores = jnp.sum(query_rows[:, :, None, :] * key_rows[:, None, :, :] * weights, axis=-1)
    scaled_query_rows = query_rows * jnp.exp(cum_logs) * carried[None, :, None]
    layer_result = jnp.einsum("hij,hjv->hiv", scores, value_matrix_rows, precision=PRECISION_FULL)
    return layer_result + jnp.einsum(
        "tjp,tpu->tju", scaled_query_rows, initial_recurrent_state, precision=PRECISION_FULL
    )


def block_grads(pieces):
    (
        query_rows,
        key_rows,
        value_matrix_rows,
        cum_logs,
        segment,
        carried,
        tail_mask,
        link_flag,
        initial_recurrent_state,
        output_cotangent,
        final_state_gradient,
    ) = pieces
    block_len = cum_logs.shape[1]
    weights = block_weights(cum_logs, segment)
    pair_grads = jnp.einsum(
        "hiv,hjv->hij", output_cotangent, value_matrix_rows, precision=PRECISION_FULL
    )
    terms = query_rows[:, :, None, :] * key_rows[:, None, :, :] * weights
    scores = jnp.sum(terms, axis=-1)
    value_row_gradient = jnp.einsum(
        "hij,hiv->hjv", scores, output_cotangent, precision=PRECISION_FULL
    )
    spread_pairs = pair_grads[:, :, :, None] * weights
    grad_queries = jnp.sum(spread_pairs * key_rows[:, None, :, :], axis=2)
    grad_keys = jnp.sum(spread_pairs * query_rows[:, :, None, :], axis=1)
    flow = pair_grads[:, :, :, None] * terms
    grad_cums = jnp.sum(flow, axis=2) - jnp.sum(flow, axis=1)
    decay_growth_factor = jnp.exp(cum_logs) * carried[None, :, None]
    scaled_query_gradient = (
        jnp.einsum(
            "bot,but->buo", initial_recurrent_state, output_cotangent, precision=PRECISION_FULL
        )
        * decay_growth_factor
    )
    grad_queries = grad_queries + scaled_query_gradient
    grad_cums = grad_cums + scaled_query_gradient * query_rows
    last_cum = cum_logs[:, -1, :]
    spread = jnp.exp(last_cum[:, None, :] - cum_logs) * tail_mask[None, :, None]
    scaled_key_rows = key_rows * spread
    scaled_key_gradient = jnp.einsum(
        "pfx,prx->prf", final_state_gradient, value_matrix_rows, precision=PRECISION_FULL
    )
    value_row_gradient = value_row_gradient + jnp.einsum(
        "xli,xel->xei", final_state_gradient, scaled_key_rows, precision=PRECISION_FULL
    )
    grad_keys = grad_keys + scaled_key_gradient * spread
    through = scaled_key_gradient * scaled_key_rows
    grad_last = jnp.sum(through, axis=1) + link_flag * jnp.exp(last_cum) * jnp.sum(
        final_state_gradient * initial_recurrent_state, axis=-1
    )
    ending = (jnp.arange(block_len, dtype=jnp.int32) == block_len - 1).astype(jnp.float32)
    grad_cums = grad_cums - through + ending[None, :, None] * grad_last[:, None, :]
    grad_logs = lax.cumsum(grad_cums, axis=1, reverse=True)
    return (grad_queries, grad_keys, value_row_gradient, grad_logs)


def per_device(
    tokens,
    doc_lengths,
    norm_gain,
    w_query,
    w_key,
    w_value,
    w_outgate,
    w_lowrank,
    w_gaterank,
    gate_bias,
    head_gain,
    w_output,
    ffn_gain,
    w_gate,
    w_up,
    w_down,
    cotangent,
):
    seqs_here, local_len, width = tokens.shape
    block_len = C
    block_count = local_len // block_len
    all_blocks = seqs_here * block_count
    head_count = H
    key_dim = DK
    value_dim = DV
    offset = lax.axis_index("fsdp") * local_len
    doc_ends = jnp.cumsum(doc_lengths, axis=-1)
    places = offset + jnp.arange(local_len, dtype=jnp.int32)
    segment = jnp.sum(
        (places[None, :, None] >= doc_ends[:, None, :]).astype(jnp.int32), axis=-1, dtype=jnp.int32
    )
    previous = jnp.sum(
        (places[None, :, None] - 1 >= doc_ends[:, None, :]).astype(jnp.int32),
        axis=-1,
        dtype=jnp.int32,
    )
    live = (segment != DOCS - 1).astype(jnp.float32).reshape(-1, 1, 1)
    seg_blocks = segment.reshape(all_blocks, block_len)
    before = previous.reshape(all_blocks, block_len)[:, 0]
    (
        gain_one,
        query_w,
        key_w,
        value_w,
        outgate_w,
        lowrank_w,
        gaterank_w,
        bias_vec,
        headgain_w,
        output_w,
    ) = (
        lax.all_gather(norm_gain, ("dp", "fsdp"), axis=0, tiled=True),
        lax.all_gather(w_query, ("dp", "fsdp"), axis=0, tiled=True),
        lax.all_gather(w_key, ("dp", "fsdp"), axis=0, tiled=True),
        lax.all_gather(w_value, ("dp", "fsdp"), axis=0, tiled=True),
        lax.all_gather(w_outgate, ("dp", "fsdp"), axis=0, tiled=True),
        lax.all_gather(w_lowrank, ("dp", "fsdp"), axis=0, tiled=True),
        lax.all_gather(w_gaterank, ("dp", "fsdp"), axis=1, tiled=True),
        lax.all_gather(gate_bias, ("dp", "fsdp"), axis=0, tiled=True),
        lax.all_gather(head_gain, ("dp", "fsdp"), axis=0, tiled=True),
        lax.all_gather(w_output, ("dp", "fsdp"), axis=0, tiled=True),
    )
    gain_two, gate_w, up_w, down_w = (
        lax.all_gather(ffn_gain, ("dp", "fsdp"), axis=0, tiled=True),
        lax.all_gather(w_gate, ("dp", "fsdp"), axis=0, tiled=True),
        lax.all_gather(w_up, ("dp", "fsdp"), axis=0, tiled=True),
        lax.all_gather(w_down, ("dp", "fsdp"), axis=0, tiled=True),
    )
    inputs = tokens.reshape(-1, width).astype(jnp.float32)
    scale_one = rms_scale(inputs, EPS)
    normed = (inputs * scale_one * gain_one.astype(jnp.float32)).astype(jnp.bfloat16)
    query_scale = key_dim ** (-0.5)
    query_rows = matmul(normed, query_w) * query_scale
    key_rows = matmul(normed, key_w)
    value_matrix_rows = matmul(normed, value_w)
    outgate = matmul(normed, outgate_w)
    lowrank = matmul(normed, lowrank_w)
    gaterank_f = gaterank_w.astype(jnp.float32)
    logits = matmul_high(lowrank, gaterank_f) + bias_vec.astype(jnp.float32)
    log_rates = jax.nn.log_sigmoid(logits) / 16.0
    query_blocks = to_blocks(query_rows, seqs_here, block_count, block_len, head_count)
    key_blocks = to_blocks(key_rows, seqs_here, block_count, block_len, head_count)
    value_blocks = to_blocks(value_matrix_rows, seqs_here, block_count, block_len, head_count)
    cum_logs = jnp.cumsum(
        to_blocks(log_rates, seqs_here, block_count, block_len, head_count), axis=2
    )
    last_cum = cum_logs[:, :, -1, :]
    tail_mask = (seg_blocks == seg_blocks[:, -1:]).astype(jnp.float32)
    carried = (seg_blocks == before[:, None]).astype(jnp.float32)
    link_flag = (seg_blocks[:, -1] == before).astype(jnp.float32)
    spread = jnp.exp(last_cum[:, :, None, :] - cum_logs) * tail_mask[:, None, :, None]
    updates = jnp.einsum(
        "bhjk,bhjv->bhkv", key_blocks * spread, value_blocks, precision=PRECISION_FULL
    )
    decays = (jnp.exp(last_cum) * link_flag[:, None, None]).reshape(
        seqs_here, block_count, head_count, key_dim
    )
    updates = updates.reshape(seqs_here, block_count, head_count, key_dim, value_dim)
    zero_state = jnp.zeros((seqs_here, head_count, key_dim, value_dim), jnp.float32)
    total_decay = jnp.prod(decays, axis=1)
    local_end, _ = run_states(zero_state, decays, updates, False)
    _, incoming = prefix(
        (total_decay, local_end),
        "fsdp",
        chain_combine,
        (jnp.ones_like(total_decay), zero_state),
        False,
    )
    _, start_states = run_states(incoming, decays, updates, False)
    start_states = start_states.reshape(all_blocks, head_count, key_dim, value_dim)
    mixed_blocks = lax.map(
        block_output,
        (query_blocks, key_blocks, value_blocks, cum_logs, seg_blocks, carried, start_states),
    )
    attended = (
        from_blocks(mixed_blocks, seqs_here, block_count).reshape(-1, head_count, value_dim) * live
    )
    scale_head = rms_scale(attended, HEAD_EPS)
    headgain_f = headgain_w.astype(jnp.float32)
    headed = (attended * scale_head * headgain_f).reshape(-1, head_count * value_dim)
    swish_gate = jax.nn.silu(outgate)
    gated = (headed * swish_gate).astype(jnp.bfloat16)
    hidden = inputs + matmul(gated, output_w)
    scale_two = rms_scale(hidden, EPS)
    gain_two_f = gain_two.astype(jnp.float32)
    normed_two = (hidden * scale_two * gain_two_f).astype(jnp.bfloat16)
    gate_pre = matmul(normed_two, gate_w)
    up_pre = matmul(normed_two, up_w)
    activated = (jax.nn.silu(gate_pre) * up_pre).astype(jnp.bfloat16)
    layer_result = hidden + matmul(activated, down_w)
    output = layer_result.astype(jnp.bfloat16).reshape(tokens.shape)
    gain_two, gate_w, up_w, down_w = (
        lax.all_gather(ffn_gain, ("dp", "fsdp"), axis=0, tiled=True),
        lax.all_gather(w_gate, ("dp", "fsdp"), axis=0, tiled=True),
        lax.all_gather(w_up, ("dp", "fsdp"), axis=0, tiled=True),
        lax.all_gather(w_down, ("dp", "fsdp"), axis=0, tiled=True),
    )
    gain_two_f = gain_two.astype(jnp.float32)
    cot_rows = cotangent.reshape(-1, width)
    upstream = cot_rows.astype(jnp.float32)
    grad_down = rows_product(activated, cot_rows)
    grad_act = back_product(cot_rows, down_w)
    sig_gate = jax.nn.sigmoid(gate_pre)
    grad_up_pre = (grad_act * gate_pre * sig_gate).astype(jnp.bfloat16)
    grad_gate_pre = (grad_act * up_pre * sig_gate * (1.0 + gate_pre * (1.0 - sig_gate))).astype(
        jnp.bfloat16
    )
    grad_gate_w = rows_product(normed_two, grad_gate_pre)
    grad_up_w = rows_product(normed_two, grad_up_pre)
    grad_normed_two = back_product(grad_gate_pre, gate_w) + back_product(grad_up_pre, up_w)
    grad_gain_two = jnp.sum(grad_normed_two * hidden * scale_two, axis=0)
    grad_hidden = upstream + rms_back(grad_normed_two * gain_two_f, hidden, scale_two)
    ffn_gain_grad, w_gate_grad, w_up_grad, w_down_grad = (
        lax.psum_scatter(grad_gain_two, ("dp", "fsdp"), scatter_dimension=0, tiled=True),
        lax.psum_scatter(grad_gate_w, ("dp", "fsdp"), scatter_dimension=0, tiled=True),
        lax.psum_scatter(grad_up_w, ("dp", "fsdp"), scatter_dimension=0, tiled=True),
        lax.psum_scatter(grad_down, ("dp", "fsdp"), scatter_dimension=0, tiled=True),
    )
    (
        gain_one,
        query_w,
        key_w,
        value_w,
        outgate_w,
        lowrank_w,
        gaterank_w,
        bias_vec,
        headgain_w,
        output_w,
    ) = (
        lax.all_gather(norm_gain, ("dp", "fsdp"), axis=0, tiled=True),
        lax.all_gather(w_query, ("dp", "fsdp"), axis=0, tiled=True),
        lax.all_gather(w_key, ("dp", "fsdp"), axis=0, tiled=True),
        lax.all_gather(w_value, ("dp", "fsdp"), axis=0, tiled=True),
        lax.all_gather(w_outgate, ("dp", "fsdp"), axis=0, tiled=True),
        lax.all_gather(w_lowrank, ("dp", "fsdp"), axis=0, tiled=True),
        lax.all_gather(w_gaterank, ("dp", "fsdp"), axis=1, tiled=True),
        lax.all_gather(gate_bias, ("dp", "fsdp"), axis=0, tiled=True),
        lax.all_gather(head_gain, ("dp", "fsdp"), axis=0, tiled=True),
        lax.all_gather(w_output, ("dp", "fsdp"), axis=0, tiled=True),
    )
    gaterank_f = gaterank_w.astype(jnp.float32)
    headgain_f = headgain_w.astype(jnp.float32)
    grad_branch = grad_hidden.astype(jnp.bfloat16)
    grad_output_w = rows_product(gated, grad_branch)
    grad_gated = back_product(grad_branch, output_w)
    sig_out = jax.nn.sigmoid(outgate)
    grad_outgate = (grad_gated * headed * sig_out * (1.0 + outgate * (1.0 - sig_out))).astype(
        jnp.bfloat16
    )
    grad_headed = (grad_gated * swish_gate).reshape(-1, head_count, value_dim)
    grad_headgain = jnp.sum(grad_headed * attended * scale_head, axis=(0, 1))
    grad_attended = rms_back(grad_headed * headgain_f, attended, scale_head) * live
    grad_blocks = to_blocks(
        grad_attended.reshape(-1, head_count * value_dim),
        seqs_here,
        block_count,
        block_len,
        head_count,
    )
    scaled_query_rows = query_blocks * jnp.exp(cum_logs) * carried[:, None, :, None]
    back_updates = jnp.einsum(
        "bhik,bhiv->bhkv", scaled_query_rows, grad_blocks, precision=PRECISION_FULL
    )
    back_updates = back_updates.reshape(seqs_here, block_count, head_count, key_dim, value_dim)
    local_first, _ = run_states(zero_state, decays, back_updates, True)
    _, outgoing = prefix(
        (total_decay, local_first),
        "fsdp",
        chain_combine,
        (jnp.ones_like(total_decay), zero_state),
        True,
    )
    _, end_grads = run_states(outgoing, decays, back_updates, True)
    end_grads = end_grads.reshape(all_blocks, head_count, key_dim, value_dim)
    grad_query_b, grad_key_b, grad_value_b, grad_log_b = lax.map(
        block_grads,
        (
            query_blocks,
            key_blocks,
            value_blocks,
            cum_logs,
            seg_blocks,
            carried,
            tail_mask,
            link_flag,
            start_states,
            grad_blocks,
            end_grads,
        ),
    )
    grad_query = (from_blocks(grad_query_b, seqs_here, block_count) * query_scale).astype(
        jnp.bfloat16
    )
    grad_key = from_blocks(grad_key_b, seqs_here, block_count).astype(jnp.bfloat16)
    grad_value = from_blocks(grad_value_b, seqs_here, block_count).astype(jnp.bfloat16)
    grad_logits = from_blocks(grad_log_b, seqs_here, block_count) / 16.0 * jax.nn.sigmoid(-logits)
    grad_bias = jnp.sum(grad_logits, axis=0)
    grad_gaterank = rows_product_high(lowrank, grad_logits)
    grad_lowrank = back_product_high(grad_logits, gaterank_f).astype(jnp.bfloat16)
    grad_query_w = rows_product(normed, grad_query)
    grad_key_w = rows_product(normed, grad_key)
    grad_value_w = rows_product(normed, grad_value)
    grad_outgate_w = rows_product(normed, grad_outgate)
    grad_lowrank_w = rows_product(normed, grad_lowrank)
    grad_normed = (
        back_product(grad_query, query_w)
        + back_product(grad_key, key_w)
        + back_product(grad_value, value_w)
    )
    grad_normed = (
        grad_normed + back_product(grad_outgate, outgate_w) + back_product(grad_lowrank, lowrank_w)
    )
    gain_one_f = gain_one.astype(jnp.float32)
    grad_gain_one = jnp.sum(grad_normed * inputs * scale_one, axis=0)
    grad_inputs = grad_hidden + rms_back(grad_normed * gain_one_f, inputs, scale_one)
    (
        norm_gain_grad,
        w_query_grad,
        w_key_grad,
        w_value_grad,
        w_outgate_grad,
        w_lowrank_grad,
        w_gaterank_grad,
        gate_bias_grad,
        head_gain_grad,
        w_output_grad,
    ) = (
        lax.psum_scatter(grad_gain_one, ("dp", "fsdp"), scatter_dimension=0, tiled=True),
        lax.psum_scatter(grad_query_w, ("dp", "fsdp"), scatter_dimension=0, tiled=True),
        lax.psum_scatter(grad_key_w, ("dp", "fsdp"), scatter_dimension=0, tiled=True),
        lax.psum_scatter(grad_value_w, ("dp", "fsdp"), scatter_dimension=0, tiled=True),
        lax.psum_scatter(grad_outgate_w, ("dp", "fsdp"), scatter_dimension=0, tiled=True),
        lax.psum_scatter(grad_lowrank_w, ("dp", "fsdp"), scatter_dimension=0, tiled=True),
        lax.psum_scatter(grad_gaterank, ("dp", "fsdp"), scatter_dimension=1, tiled=True),
        lax.psum_scatter(grad_bias, ("dp", "fsdp"), scatter_dimension=0, tiled=True),
        lax.psum_scatter(grad_headgain, ("dp", "fsdp"), scatter_dimension=0, tiled=True),
        lax.psum_scatter(grad_output_w, ("dp", "fsdp"), scatter_dimension=0, tiled=True),
    )
    tokens_grad = grad_inputs.astype(jnp.bfloat16).reshape(tokens.shape)
    return (
        output,
        tokens_grad,
        norm_gain_grad,
        w_query_grad,
        w_key_grad,
        w_value_grad,
        w_outgate_grad,
        w_lowrank_grad,
        w_gaterank_grad,
        gate_bias_grad,
        head_gain_grad,
        w_output_grad,
        ffn_gain_grad,
        w_gate_grad,
        w_up_grad,
        w_down_grad,
    )


def solution(mesh):
    placed = (
        P("dp", "fsdp", None),
        P("dp", None),
        P(("dp", "fsdp")),
        P(("dp", "fsdp"), None),
        P(("dp", "fsdp"), None),
        P(("dp", "fsdp"), None),
        P(("dp", "fsdp"), None),
        P(("dp", "fsdp"), None),
        P(None, ("dp", "fsdp")),
        P(("dp", "fsdp")),
        P(("dp", "fsdp")),
        P(("dp", "fsdp"), None),
        P(("dp", "fsdp")),
        P(("dp", "fsdp"), None),
        P(("dp", "fsdp"), None),
        P(("dp", "fsdp"), None),
        P("dp", "fsdp", None),
    )
    return jax.shard_map(
        per_device,
        mesh=mesh,
        in_specs=placed,
        out_specs=(
            P("dp", "fsdp", None),
            P("dp", "fsdp", None),
            P(("dp", "fsdp")),
            P(("dp", "fsdp"), None),
            P(("dp", "fsdp"), None),
            P(("dp", "fsdp"), None),
            P(("dp", "fsdp"), None),
            P(("dp", "fsdp"), None),
            P(None, ("dp", "fsdp")),
            P(("dp", "fsdp")),
            P(("dp", "fsdp")),
            P(("dp", "fsdp"), None),
            P(("dp", "fsdp")),
            P(("dp", "fsdp"), None),
            P(("dp", "fsdp"), None),
            P(("dp", "fsdp"), None),
        ),
        check_vma=False,
    )
```

profile of v0, /device:TPU:0, one launch (start us, length us, event | category | flops | bytes accessed | tf_op | source)
XLA Modules:
  0.0 5957.4 jit_solution(9806235078119057526)
XLA Ops:
  13.9 42.2 all-reduce.9
  56.2 68.1 %all-gather.3 = bf16[32,64,16]{1,2,0:T(8,128)(2,1)S(1)} all-gather(bf16[1,64,16]{1,2,0:T(8,128)(2,1)} %bitcast.549), channel_id=1, replica_groups=mesh['dp'=8,'fsdp'=4] {'dp','fsdp'}, dimensions={0}, use_global_device_ids=true | all-gather | bytes 67584 | tf_op jit(solution)/shard_map/all_gather | solution.py:266
  124.5 66.1 %all-gather.4 = bf16[32,32,16]{1,2,0:T(8,128)(2,1)S(1)} all-gather(bf16[1,32,16]{1,2,0:T(8,128)(2,1)} %bitcast.550), channel_id=1, replica_groups=mesh['dp'=8,'fsdp'=4] {'dp','fsdp'}, dimensions={0}, use_global_device_ids=true | all-gather | bytes 33792 | tf_op jit(solution)/shard_map/all_gather | solution.py:267
  275.6 57.5 all-gather.33.cloned.1.call-done
  352.0 54.8 while.108
  423.9 66.7 %all-gather.25.cloned.1.call-done = bf16[2048,2048]{1,0:T(8,128)(2,1)} async-done(((bf16[64,2048]{1,0:T(8,128)(2,1)}), bf16[2048,2048]{1,0:T(8,128)(2,1)}) %all-gather.25.cloned.1.call-update) | async-done | bytes 8388624 | tf_op jit(solution)/shard_map/all_gather | solution.py:270
  498.0 138.6 %all-gather.27.cloned.1.call-done = bf16[2048,5632]{1,0:T(8,128)(2,1)} async-done(((bf16[64,5632]{1,0:T(8,128)(2,1)}), bf16[2048,5632]{1,0:T(8,128)(2,1)}) %all-gather.27.cloned.1.call-update) | async-done | bytes 23068688 | tf_op jit(solution)/shard_map/all_gather | solution.py:274
  649.8 132.5 %all-gather.29.cloned.1.call-done = bf16[2048,5632]{1,0:T(8,128)(2,1)} async-done(((bf16[64,5632]{1,0:T(8,128)(2,1)}), bf16[2048,5632]{1,0:T(8,128)(2,1)}) %all-gather.29.cloned.1.call-update) | async-done | bytes 23068688 | tf_op jit(solution)/shard_map/all_gather | solution.py:275
  795.6 132.4 %all-gather.31.cloned.1.call-done = bf16[5632,2048]{1,0:T(8,128)(2,1)} async-done(((bf16[176,2048]{1,0:T(8,128)(2,1)}), bf16[5632,2048]{1,0:T(8,128)(2,1)}) %all-gather.31.cloned.1.call-update) | async-done | bytes 23068688 | tf_op jit(solution)/shard_map/all_gather | solution.py:276
  928.0 25.8 multiply_convert_fusion
  1024.8 75.8 %all-gather.35.cloned.1.call-done = bf16[4,4,256,512]{3,2,1,0:T(8,128)(2,1)} async-done(((bf16[1,4,256,512]{3,2,1,0:T(8,128)(2,1)}), bf16[4,4,256,512]{3,2,1,0:T(8,128)(2,1)}) %all-gather.35.cloned.1.call-update) | async-done | bytes 4194320 | tf_op jit(solution)/shard_map/all_gather | solution.py:23
  1127.2 158.1 %while.111 = (s32[]{:T(128)}, f32[4,4,64,256]{3,2,1,0:T(8,128)}, bf16[4,4,64,256]{3,2,1,0:T(8,128)(2,1)}, bf16[4,4,64,512]{3,2,1,0:T(8,128)(2,1)}, f32[4,4,64,25...) while((s32[]{:T(128)}, f32[4,4,64,256]{3,2,1,0:T(8,128)}, ...), condition=%wide.region_34.35_spmd, body=%wide.region_25.34_spmd.sunk | while | flops 1474294912 | bytes 75051088 | solution.py:425
  1359.7 19.7 fusion.148
  1380.6 19.8 fusion.109
  1428.9 38.4 all-reduce.8
  1474.2 86.2 %reduce-scatter.31.cloned.1.call-done = f32[64,16]{1,0:T(8,128)} async-done(((f32[2048,16]{1,0:T(8,128)}), f32[64,16]{1,0:T(8,128)}) %reduce-scatter.31.cloned.1.call-update) | async-done | bytes 4112
  1561.8 183.6 %reduce-scatter.15.cloned.1.call-done = f32[64,1024]{1,0:T(8,128)} async-done(((f32[2048,1024]{1,0:T(8,128)}), f32[64,1024]{1,0:T(8,128)}) %reduce-scatter.15.cloned.1.call-update) | async-done | bytes 262160 | tf_op jit(solution)/shard_map/reduce_scatter | solution.py:479
  1745.4 186.2 %reduce-scatter.17.cloned.1.call-done = f32[64,1024]{1,0:T(8,128)} async-done(((f32[2048,1024]{1,0:T(8,128)}), f32[64,1024]{1,0:T(8,128)}) %reduce-scatter.17.cloned.1.call-update) | async-done | bytes 262160 | tf_op jit(solution)/shard_map/reduce_scatter | solution.py:480
  1931.7 364.6 %reduce-scatter.21.cloned.1.call-done = f32[64,2048]{1,0:T(8,128)} async-done(((f32[2048,2048]{1,0:T(8,128)}), f32[64,2048]{1,0:T(8,128)}) %reduce-scatter.21.cloned.1.call-update) | async-done | bytes 524304 | tf_op jit(solution)/shard_map/reduce_scatter | solution.py:482
  2296.3 364.9 %reduce-scatter.23.cloned.1.call-done = f32[64,2048]{1,0:T(8,128)} async-done(((f32[2048,2048]{1,0:T(8,128)}), f32[64,2048]{1,0:T(8,128)}) %reduce-scatter.23.cloned.1.call-update) | async-done | bytes 524304 | tf_op jit(solution)/shard_map/reduce_scatter | solution.py:487
  2661.2 364.9 %reduce-scatter.19.cloned.1.call-done = f32[64,2048]{1,0:T(8,128)} async-done(((f32[2048,2048]{1,0:T(8,128)}), f32[64,2048]{1,0:T(8,128)}) %reduce-scatter.19.cloned.1.call-update) | async-done | bytes 524304 | tf_op jit(solution)/shard_map/reduce_scatter | solution.py:481
  3026.1 973.1 %reduce-scatter.25.cloned.1.call-done = f32[64,5632]{1,0:T(8,128)} async-done(((f32[2048,5632]{1,0:T(8,128)}), f32[64,5632]{1,0:T(8,128)}) %reduce-scatter.25.cloned.1.call-update) | async-done | bytes 1441808 | tf_op jit(solution)/shard_map/reduce_scatter | solution.py:364
  3999.2 975.7 %reduce-scatter.27.cloned.1.call-done = f32[64,5632]{1,0:T(8,128)} async-done(((f32[2048,5632]{1,0:T(8,128)}), f32[64,5632]{1,0:T(8,128)}) %reduce-scatter.27.cloned.1.call-update) | async-done | bytes 1441808 | tf_op jit(solution)/shard_map/reduce_scatter | solution.py:365
  4974.8 975.5 %reduce-scatter.29.cloned.1.call-done = f32[176,2048]{1,0:T(8,128)} async-done(((f32[5632,2048]{1,0:T(8,128)}), f32[176,2048]{1,0:T(8,128)}) %reduce-scatter.29.cloned.1.call-update) | async-done | bytes 1441808 | tf_op jit(solution)/shard_map/reduce_scatter | solution.py:366
  (510 shorter events, 635.4 us)
Async XLA Ops:
  7.2 197.9 %all-gather.19.cloned.1.call-start = ((), (), s32[]{:S(2)}) async-start(), calls=%async_computation.11 | async-start | bytes 4325376 | tf_op jit(solution)/shard_map/all_gather | solution.py:263
  7.9 208.5 %all-gather.21.cloned.1.call-start = ((), (), s32[]{:S(2)}) async-start(), calls=%async_computation.12 | async-start | bytes 8650752 | tf_op jit(solution)/shard_map/all_gather | solution.py:264
  8.7 261.6 %all-gather.17.cloned.1.call-start = ((), (), s32[]{:S(2)}) async-start(), calls=%async_computation.10 | async-start | bytes 4325376 | tf_op jit(solution)/shard_map/all_gather | solution.py:262
  9.4 323.7 %all-gather.33.cloned.1.call-start = ((), (), s32[]{:S(2)}) async-start(), calls=%async_computation.26 | async-start | bytes 5242880 | tf_op jit(solution)/shard_map/all_gather | solution.py:23
  56.2 359.1 %copy-start.43 = (f32[2048]{0:T(1024)}, f32[2048]{0:T(1024)S(1)}, u32[]{:S(2)}) copy-start(f32[2048]{0:T(1024)S(1)} %convert_element_type.284) | copy-start | bytes 24580
  191.6 223.6 %copy-start.52 = (f32[256]{0:T(256)}, f32[256]{0:T(256)S(1)}, u32[]{:S(2)}) copy-start(f32[256]{0:T(256)S(1)} %get-tuple-element.905) | copy-start | bytes 3076
  254.0 161.2 %all-gather.23.cloned.1.call-start = ((), (), s32[]{:S(2)}) async-start(), calls=%async_computation.13 | async-start | bytes 8650752 | tf_op jit(solution)/shard_map/all_gather | solution.py:265
  254.6 236.0 %all-gather.25.cloned.1.call-start = ((), (), s32[]{:S(2)}) async-start(), calls=%async_computation.14 | async-start | bytes 8650752 | tf_op jit(solution)/shard_map/all_gather | solution.py:270
  255.2 381.5 %all-gather.27.cloned.1.call-start = ((), (), s32[]{:S(2)}) async-start(), calls=%async_computation.15 | async-start | bytes 23789568 | tf_op jit(solution)/shard_map/all_gather | solution.py:274
  255.9 526.4 %all-gather.29.cloned.1.call-start = ((), (), s32[]{:S(2)}) async-start(), calls=%async_computation.16 | async-start | bytes 23789568 | tf_op jit(solution)/shard_map/all_gather | solution.py:275
  256.7 671.3 %all-gather.31.cloned.1.call-start = ((), (), s32[]{:S(2)}) async-start(), calls=%async_computation.17 | async-start | bytes 23789568 | tf_op jit(solution)/shard_map/all_gather | solution.py:276
  257.4 843.1 %all-gather.35.cloned.1.call-start = ((), (), s32[]{:S(2)}) async-start(), calls=%async_computation.27 | async-start | bytes 5242880 | tf_op jit(solution)/shard_map/all_gather | solution.py:23
  498.0 284.3 %copy-start.18 = (bf16[256,2048]{1,0:T(8,128)(2,1)}, bf16[256,2048]{1,0:T(8,128)(2,1)S(1)}, u32[]{:S(2)}) copy-start(bf16[256,2048]{1,0:T(8,128)(2,1)S(1)} %multiply_convert_fusion.4) | copy-start | bytes 3145732
  649.8 278.2 %copy-start.27 = (bf16[1,256,2048]{2,1,0:T(8,128)(2,1)S(1)}, bf16[1,256,2048]{2,1,0:T(8,128)(2,1)}, u32[]{:S(2)}) copy-start(bf16[1,256,2048]{2,1,0:T(8,128)(2,1)} %param.49) | copy-start | bytes 3145732
  1021.4 451.4 %reduce-scatter.33.cloned.1.call-start = ((), (), s32[]{:S(2)}) async-start(), calls=%async_computation.29 | async-start | bytes 540672
  1293.7 266.7 %reduce-scatter.31.cloned.1.call-start = ((), (), s32[]{:S(2)}) async-start(), calls=%async_computation.28 | async-start | bytes 1081344
  1294.5 451.0 %reduce-scatter.15.cloned.1.call-start = ((), (), s32[]{:S(2)}) async-start(), calls=%async_computation.18 | async-start | bytes 8650752 | tf_op jit(solution)/shard_map/reduce_scatter | solution.py:479
  1299.7 632.0 %reduce-scatter.17.cloned.1.call-start = ((), (), s32[]{:S(2)}) async-start(), calls=%async_computation.19 | async-start | bytes 8650752 | tf_op jit(solution)/shard_map/reduce_scatter | solution.py:480
  1306.7 989.6 %reduce-scatter.21.cloned.1.call-start = ((), (), s32[]{:S(2)}) async-start(), calls=%async_computation.21 | async-start | bytes 17301504 | tf_op jit(solution)/shard_map/reduce_scatter | solution.py:482
  1316.2 1345.0 %reduce-scatter.23.cloned.1.call-start = ((), (), s32[]{:S(2)}) async-start(), calls=%async_computation.22 | async-start | bytes 17301504 | tf_op jit(solution)/shard_map/reduce_scatter | solution.py:487
  1327.2 1698.9 %reduce-scatter.19.cloned.1.call-start = ((), (), s32[]{:S(2)}) async-start(), calls=%async_computation.20 | async-start | bytes 17301504 | tf_op jit(solution)/shard_map/reduce_scatter | solution.py:481
  1338.7 2660.4 %reduce-scatter.25.cloned.1.call-start = ((), (), s32[]{:S(2)}) async-start(), calls=%async_computation.23 | async-start | bytes 47579136 | tf_op jit(solution)/shard_map/reduce_scatter | solution.py:364
  1359.6 3615.2 %reduce-scatter.27.cloned.1.call-start = ((), (), s32[]{:S(2)}) async-start(), calls=%async_computation.24 | async-start | bytes 47579136 | tf_op jit(solution)/shard_map/reduce_scatter | solution.py:365
  1379.4 4571.0 %reduce-scatter.29.cloned.1.call-start = ((), (), s32[]{:S(2)}) async-start(), calls=%async_computation.25 | async-start | bytes 47579136 | tf_op jit(solution)/shard_map/reduce_scatter | solution.py:366
  (78 other events, 900.4 us)
Sparse Core Ops, SparseCore 0:
  11.0 65.0 all-gather.18
  79.0 76.4 all-gather.20
  158.6 60.9 all-gather.16
  254.1 78.8 all-gather.32
  335.8 75.8 all-gather.22
  414.5 76.0 all-gather.24
  493.4 143.1 all-gather.26
  639.5 142.7 all-gather.28
  785.1 142.7 all-gather.30
  1021.6 78.9 all-gather.34
  1293.8 132.2 reduce-scatter.32
  1428.3 131.9 reduce-scatter.30
  1563.3 182.1 reduce-scatter.14
  1748.2 183.4 reduce-scatter.16
  1934.4 361.8 reduce-scatter.20
  2299.0 362.1 reduce-scatter.22
  2663.9 362.1 reduce-scatter.18
  3028.8 970.2 reduce-scatter.24
  4002.0 972.7 reduce-scatter.26
  4977.6 972.7 reduce-scatter.28
where the time goes:
time: 5970 us; the launch traced here: 5960 us
  waiting for transfers between devices  5080 us (85%)
  matrix products  339 us (6%)
  blocking collectives  227 us (4%)
  other arithmetic  177 us (3%)
  local copies, waits for them, and re-layouts  111 us (2%)
    reduce_scatter x1, waiting for transfers between devices, per_device(): lax.psum_scatter(grad_up_w, ('dp', 'fsdp'), scatter_dimension=0, tiled=True)  976 us
    reduce_scatter x1, waiting for transfers between devices, per_device(): lax.psum_scatter(grad_down, ('dp', 'fsdp'), scatter_dimension=0, tiled=True)  976 us
    reduce_scatter x1, waiting for transfers between devices, per_device(): lax.psum_scatter(grad_gate_w, ('dp', 'fsdp'), scatter_dimension=0, tiled=...  973 us
    reduce_scatter x1, waiting for transfers between devices, per_device(): lax.psum_scatter(grad_output_w, ('dp', 'fsdp'), scatter_dimension=0, tile...  365 us
    reduce_scatter x1, waiting for transfers between devices, per_device(): lax.psum_scatter(grad_value_w, ('dp', 'fsdp'), scatter_dimension=0, tiled...  365 us
    reduce_scatter x1, waiting for transfers between devices, per_device(): lax.psum_scatter(grad_outgate_w, ('dp', 'fsdp'), scatter_dimension=0, til...  365 us
    reduce_scatter x1, waiting for transfers between devices, per_device(): lax.psum_scatter(grad_key_w, ('dp', 'fsdp'), scatter_dimension=0, tiled=T...  186 us
    reduce_scatter x1, waiting for transfers between devices, per_device(): lax.psum_scatter(grad_query_w, ('dp', 'fsdp'), scatter_dimension=0, tiled...  184 us
  transfers between devices with their start and end apart: 20, of which 15 were waited for; matrix products, arithmetic and copies ran while one was open for 6% of the time, Pallas kernels for 0%

commit v1 on v0

v1 whole, which is shorter than its diff:
```python
import jax
import jax.numpy as jnp
from jax import lax
from jax.sharding import Mesh
from jax.sharding import PartitionSpec as P

H = 4
DK = 256
DV = 512
CORES = 2
DOCS = 8

EPS = 1e-05
HEAD_EPS = 1.0
HIGHEST = lax.Precision.HIGHEST
F32 = jnp.float32
BF16 = jnp.bfloat16

SHARE = ("rep", "core", "fsdp")
EVERY = ("rep", "head", "core", "fsdp")


def dot(a, b, dims, precision=None):
    return lax.dot_general(a, b, (dims, ((), ())), precision=precision, preferred_element_type=F32)


def matmul(a, b):
    return dot(a, b, ((1,), (0,)))


def rows_product(a, b):
    return dot(a, b, ((0,), (0,)))


def back_product(a, b):
    return dot(a, b, ((1,), (1,)))


def batched(form, a, b):
    return jnp.einsum(form, a, b, preferred_element_type=F32)


def rms_scale(values, epsilon):
    return lax.rsqrt(jnp.mean(values * values, axis=-1, keepdims=True) + epsilon)


def rms_back(upstream, values, scale):
    return scale * upstream - values * scale**3 * jnp.mean(upstream * values, axis=-1, keepdims=True)


def share_rows(part):
    spread = jnp.broadcast_to(part[None], (H,) + part.shape)
    whole = lax.all_to_all(spread, "head", split_axis=0, concat_axis=0, tiled=True)
    return whole.reshape(-1, part.shape[-1])


def sum_rows(partial):
    pieces = partial.astype(BF16).reshape(H, -1, partial.shape[-1])
    pieces = lax.all_to_all(pieces, "head", split_axis=0, concat_axis=0, tiled=True)
    return jnp.sum(pieces.astype(F32), axis=0)


def level_sums(length):
    rows = jnp.arange(length)[:, None]
    cols = jnp.arange(length)[None, :]
    sums, pairs = [], []
    step = 1
    while step < length:
        bound = rows // (2 * step) * (2 * step) + step - 1
        upper = rows > bound
        sums.append(jnp.where(upper, (cols > bound) & (cols <= rows), (cols > rows) & (cols <= bound)))
        pairs.append(upper & (cols // (2 * step) == rows // (2 * step)) & (cols <= bound))
        step *= 2
    sums.append(cols <= rows)
    sums.append(cols > rows)
    return jnp.stack(sums), jnp.stack(pairs)


def chain_before(decay, state, backward):
    count = lax.axis_size("fsdp")
    place = lax.axis_index("fsdp")
    decays = lax.all_gather(decay.astype(BF16), "fsdp")
    states = lax.all_gather(state.astype(BF16), "fsdp")
    total = jnp.zeros_like(state)
    for step in range(count - 1):
        source = count - 1 - step if backward else step
        ahead = source > place if backward else source < place
        joined = decays[source].astype(F32)[..., None] * total + states[source].astype(F32)
        total = jnp.where(ahead, joined, total)
    return total


def per_device(
    tokens,
    doc_lengths,
    norm_gain,
    w_query,
    w_key,
    w_value,
    w_outgate,
    w_lowrank,
    w_gaterank,
    gate_bias,
    head_gain,
    w_output,
    ffn_gain,
    w_gate,
    w_up,
    w_down,
    cotangent,
):
    seqs_here, length, width = tokens.shape
    reps = lax.axis_size("rep")
    parts = lax.axis_size("fsdp")
    devices = reps * H * CORES * parts
    here = lax.axis_index("head")
    key_dim, value_dim = DK, DV
    rank = w_lowrank.shape[1]
    rows = width // devices
    count = H * seqs_here

    def to_shared(a):
        shaped = a.reshape(a.shape[0], reps, H, CORES * parts, rows)
        return shaped.transpose(0, 1, 3, 2, 4).reshape(a.shape)

    def from_shared(a):
        shaped = a.reshape(a.shape[0], reps, CORES * parts, H, rows)
        return shaped.transpose(0, 1, 3, 2, 4).reshape(a.shape)

    def gather_columns(w):
        moved = lax.all_to_all(w.transpose(1, 0, 2), "head", split_axis=0, concat_axis=0, tiled=True)
        return lax.all_gather(moved.reshape(-1, w.shape[2]), SHARE, axis=0, tiled=True)

    def scatter_columns(g):
        g = g.astype(BF16)
        for axis in SHARE:
            g = lax.psum_scatter(g, axis, scatter_dimension=0, tiled=True)
        moved = lax.all_to_all(g.reshape(H, rows, -1), "head", split_axis=0, concat_axis=0, tiled=True)
        return moved.transpose(1, 0, 2).astype(F32)

    def gather_part(w):
        if reps == 1:
            return lax.all_gather(w, SHARE, axis=0, tiled=True)
        whole = lax.all_gather(w, EVERY, axis=0, tiled=True)
        size = whole.shape[0] // H
        return lax.dynamic_slice_in_dim(whole, here * size, size, 0)

    def scatter_part(g):
        g = g.astype(BF16)
        if reps == 1:
            for axis in SHARE:
                g = lax.psum_scatter(g, axis, scatter_dimension=0, tiled=True)
            return g.astype(F32)
        whole = jnp.zeros((H * g.shape[0], g.shape[1]), BF16)
        whole = lax.dynamic_update_slice_in_dim(whole, g, here * g.shape[0], 0)
        return lax.psum_scatter(whole, EVERY, scatter_dimension=0, tiled=True).astype(F32)

    small = (
        norm_gain,
        ffn_gain,
        gate_bias,
        head_gain,
        w_gaterank.reshape(-1),
    )
    sizes = [a.shape[0] for a in small]
    packed = jnp.concatenate(small).reshape(1, -1)
    packed = lax.all_gather(packed, EVERY, axis=0, tiled=True).astype(F32)
    gain_one, gain_two, bias, gain_head, gaterank = jnp.split(
        packed, [sum(sizes[:i]) for i in range(1, len(sizes))], axis=1
    )
    gain_one, gain_two, bias, gain_head = (
        gain_one.reshape(-1),
        gain_two.reshape(-1),
        bias.reshape(-1),
        gain_head.reshape(-1),
    )
    gaterank = gaterank.reshape(devices, rank, -1).transpose(1, 0, 2).reshape(rank, -1)
    bias = lax.dynamic_slice_in_dim(bias, here * key_dim, key_dim, 0)
    gaterank = lax.dynamic_slice_in_dim(gaterank, here * key_dim, key_dim, 1)
    lengths = lax.all_gather(doc_lengths, "head", axis=0, tiled=True)

    mix_w = gather_columns(
        jnp.concatenate(
            [
                w_query.reshape(rows, H, key_dim),
                w_key.reshape(rows, H, key_dim),
                w_value.reshape(rows, H, value_dim),
                w_outgate.reshape(rows, H, value_dim),
                jnp.broadcast_to(w_lowrank[:, None, :], (rows, H, rank)),
            ],
            axis=2,
        )
    )
    output_w = gather_part(w_output)
    gate_w = gather_columns(w_gate.reshape(rows, H, -1))
    up_w = gather_columns(w_up.reshape(rows, H, -1))
    down_w = gather_part(w_down)

    offset = lax.axis_index("fsdp") * length
    doc_ends = jnp.cumsum(lengths, axis=-1)
    places = offset + jnp.arange(length, dtype=jnp.int32)
    segment = jnp.sum((places[None, :, None] >= doc_ends[:, None, :]).astype(jnp.int32), axis=-1)
    before = jnp.sum((offset - 1 >= doc_ends).astype(jnp.int32), axis=-1)
    live = (segment != DOCS - 1).astype(F32)[:, :, None]
    same = segment[:, :, None] == segment[:, None, :]
    tail = (segment == segment[:, -1:]).astype(F32)[:, :, None]
    carried = (segment == before[:, None]).astype(F32)[:, :, None]
    link = (segment[:, -1] == before).astype(F32)[:, None]

    inputs = tokens.reshape(-1, width).astype(F32)
    scale_one = rms_scale(inputs, EPS)
    normed = share_rows(to_shared((inputs * scale_one * gain_one).astype(BF16)))
    mixed = matmul(normed, mix_w)
    edges = [key_dim, 2 * key_dim, 2 * key_dim + value_dim, 2 * key_dim + 2 * value_dim]
    query, key, value, outgate, lowrank = jnp.split(mixed, edges, axis=1)
    query_scale = key_dim ** (-0.5)
    query = (query * query_scale).reshape(count, length, key_dim)
    key = key.reshape(count, length, key_dim)
    value = value.astype(BF16).reshape(count, length, value_dim)
    logits = dot(lowrank, gaterank, ((1,), (0,)), HIGHEST) + bias
    rates = (jax.nn.log_sigmoid(logits) / 16.0).reshape(count, length, key_dim)

    sums, pairs = level_sums(length)
    sums = sums.astype(BF16)
    levels = pairs.shape[0]
    high = rates.astype(BF16)
    low = (rates - high.astype(F32)).astype(BF16)
    decayed = jnp.exp(batched("sim,bmk->bsik", sums, high) + batched("sim,bmk->bsik", sums, low))
    level_decay = decayed[:, :levels]
    from_start = decayed[:, levels] * carried
    to_end = decayed[:, levels + 1] * tail
    decay = decayed[:, levels, -1] * link

    mask = pairs[None] & same[:, None]
    level_query = (query[:, None] * level_decay).astype(BF16)
    level_key = (key[:, None] * level_decay).astype(BF16)
    own = (jnp.arange(length)[:, None] == jnp.arange(length)[None, :])[None]
    scores = jnp.sum(
        jnp.where(mask, batched("bsik,bsjk->bsij", level_query, level_key), 0.0), axis=1
    ) + jnp.where(own, jnp.sum(query * key, axis=-1)[:, :, None], 0.0)
    scores = scores.astype(BF16)
    start_query = (query * from_start).astype(BF16)
    end_key = (key * to_end).astype(BF16)
    local_end = batched("bjk,bjv->bkv", end_key, value)
    entering = chain_before(decay, local_end, False).astype(BF16)
    attended = (
        batched("bij,bjv->biv", scores, value) + batched("bik,bkv->biv", start_query, entering)
    ) * live
    attended = attended.reshape(-1, value_dim)
    scale_head = rms_scale(attended, HEAD_EPS)
    headed = attended * scale_head * gain_head
    sig_out = jax.nn.sigmoid(outgate)
    swish = outgate * sig_out
    gated = (headed * swish).astype(BF16)
    hidden = inputs + sum_rows(matmul(gated, output_w))

    scale_two = rms_scale(hidden, EPS)
    normed_two = share_rows(to_shared((hidden * scale_two * gain_two).astype(BF16)))
    gate_pre = matmul(normed_two, gate_w)
    up_pre = matmul(normed_two, up_w)
    sig_gate = jax.nn.sigmoid(gate_pre)
    activated = (gate_pre * sig_gate * up_pre).astype(BF16)
    output = (hidden + sum_rows(matmul(activated, down_w))).astype(BF16).reshape(tokens.shape)

    cot_rows = cotangent.reshape(-1, width)
    cot_shared = share_rows(cot_rows)
    grad_act = back_product(cot_shared, down_w)
    grad_up = (grad_act * gate_pre * sig_gate).astype(BF16)
    grad_gate = (grad_act * up_pre * sig_gate * (1.0 + gate_pre * (1.0 - sig_gate))).astype(BF16)
    grad_normed_two = from_shared(
        sum_rows(back_product(grad_gate, gate_w) + back_product(grad_up, up_w))
    )
    w_down_grad = scatter_part(rows_product(activated, cot_shared))
    w_gate_grad = scatter_columns(rows_product(normed_two, grad_gate))
    w_up_grad = scatter_columns(rows_product(normed_two, grad_up))
    grad_gain_two = jnp.sum(grad_normed_two * hidden * scale_two, axis=0)
    grad_hidden = cot_rows.astype(F32) + rms_back(grad_normed_two * gain_two, hidden, scale_two)

    branch = share_rows(grad_hidden.astype(BF16))
    grad_gated = back_product(branch, output_w)
    w_output_grad = scatter_part(rows_product(gated, branch))
    grad_outgate = grad_gated * headed * sig_out * (1.0 + outgate * (1.0 - sig_out))
    grad_headed = grad_gated * swish
    grad_gain_head = jnp.sum(grad_headed * attended * scale_head, axis=0)
    grad_attended = rms_back(grad_headed * gain_head, attended, scale_head)
    grad_attended = (grad_attended.reshape(count, length, value_dim) * live).astype(BF16)

    leaving = batched("bik,biv->bkv", start_query, grad_attended)
    ending = chain_before(decay, leaving, True).astype(BF16)
    grad_scores = jnp.where(same, batched("biv,bjv->bij", grad_attended, value), 0.0)
    grad_value = batched("bij,biv->bjv", scores, grad_attended) + batched(
        "bjk,bkv->bjv", end_key, ending
    )
    grad_own = jnp.sum(jnp.where(own, grad_scores, 0.0), axis=-1)[:, :, None]
    level_scores = jnp.where(pairs[None], grad_scores[:, None], 0.0).astype(BF16)
    level_grad_query = batched("bsij,bsjk->bsik", level_scores, level_key)
    level_grad_key = batched("bsij,bsik->bsjk", level_scores, level_query)
    start_grad = batched("biv,bkv->bik", grad_attended, entering)
    end_grad = batched("bjv,bkv->bjk", value, ending)
    grad_query = (
        jnp.sum(level_grad_query * level_decay, axis=1) + grad_own * key + start_grad * from_start
    )
    grad_key = jnp.sum(level_grad_key * level_decay, axis=1) + grad_own * query + end_grad * to_end
    flows = jnp.concatenate(
        [
            level_grad_query * level_query + level_grad_key * level_key,
            (start_grad * start_query)[:, None],
            (end_grad * end_key)[:, None],
        ],
        axis=1,
    ).astype(BF16)
    through = decay * jnp.sum(ending.astype(F32) * entering.astype(F32), axis=-1)
    grad_rates = batched("sim,bsik->bmk", sums, flows) + through[:, None, :]
    grad_logits = grad_rates.reshape(-1, key_dim) / 16.0 * jax.nn.sigmoid(-logits)
    grad_bias = jnp.sum(grad_logits, axis=0)
    grad_gaterank = dot(lowrank, grad_logits, ((0,), (0,)), HIGHEST)
    grad_lowrank = dot(grad_logits, gaterank, ((1,), (1,)), HIGHEST)
    grad_mixed = jnp.concatenate(
        [
            grad_query.reshape(-1, key_dim) * query_scale,
            grad_key.reshape(-1, key_dim),
            grad_value.reshape(-1, value_dim),
            grad_outgate,
            grad_lowrank,
        ],
        axis=1,
    ).astype(BF16)
    grad_normed = from_shared(sum_rows(back_product(grad_mixed, mix_w)))
    grad_mix_w = scatter_columns(rows_product(normed, grad_mixed))
    grad_gain_one = jnp.sum(grad_normed * inputs * scale_one, axis=0)
    tokens_grad = grad_hidden + rms_back(grad_normed * gain_one, inputs, scale_one)
    tokens_grad = tokens_grad.astype(BF16).reshape(tokens.shape)

    query_g, key_g, value_g, outgate_g, lowrank_g = jnp.split(grad_mix_w, edges, axis=2)

    def place(g, axis):
        shape = list(g.shape)
        shape[axis] *= H
        return lax.dynamic_update_slice_in_dim(jnp.zeros(shape, F32), g, here * key_dim, axis)

    small_grads = jnp.concatenate(
        [
            grad_gain_one.reshape(devices, -1),
            grad_gain_two.reshape(devices, -1),
            place(grad_bias, 0).reshape(devices, -1),
            grad_gain_head.reshape(devices, -1),
            place(grad_gaterank, 1)
            .reshape(rank, devices, -1)
            .transpose(1, 0, 2)
            .reshape(devices, -1),
        ],
        axis=1,
    )
    small_grads = lax.all_to_all(small_grads, EVERY, split_axis=0, concat_axis=0, tiled=True)
    small_grads = jnp.sum(small_grads, axis=0)
    norm_g, ffn_g, bias_g, head_g, gaterank_g = jnp.split(
        small_grads, [sum(sizes[:i]) for i in range(1, len(sizes))]
    )
    return (
        output,
        tokens_grad,
        norm_g,
        query_g.reshape(w_query.shape),
        key_g.reshape(w_key.shape),
        value_g.reshape(w_value.shape),
        outgate_g.reshape(w_outgate.shape),
        jnp.sum(lowrank_g, axis=1),
        gaterank_g.reshape(w_gaterank.shape),
        bias_g,
        head_g,
        w_output_grad,
        ffn_g,
        w_gate_grad.reshape(w_gate.shape),
        w_up_grad.reshape(w_up.shape),
        w_down_grad,
    )


def solution(mesh):
    dp, parts = mesh.shape["dp"], mesh.shape["fsdp"]
    fine = Mesh(mesh.devices.reshape(dp // (H * CORES), H, CORES, parts), EVERY)
    seq = ("rep", "head", "core")
    rows, vector = P(EVERY, None), P(EVERY)
    activations = P(seq, "fsdp", None)
    columns = P(None, EVERY)
    return jax.shard_map(
        per_device,
        mesh=fine,
        in_specs=(
            activations,
            P(seq, None),
            vector,
            rows,
            rows,
            rows,
            rows,
            rows,
            columns,
            vector,
            vector,
            rows,
            vector,
            rows,
            rows,
            rows,
            activations,
        ),
        out_specs=(
            activations,
            activations,
            vector,
            rows,
            rows,
            rows,
            rows,
            rows,
            columns,
            vector,
            vector,
            rows,
            vector,
            rows,
            rows,
            rows,
        ),
        check_vma=False,
    )
```

time: 5970 us -> 1160 us (0.19)
  waiting for transfers between devices: 5080 us -> 483 us
  matrix products: 339 us -> 217 us
  other arithmetic: 177 us -> 72.5 us
    reduce_scatter x8 -> x10, waiting for transfers between devices: 4390 us -> 192 us  [the longest x6 126 us: scatter_columns(): g = lax.psum_scatter(g, axis, scatter_dimension=0, tiled=True)]
    all_gather x10 -> x7, waiting for transfers between devices: 603 us -> 51.4 us  [the longest x2 29.8 us: chain_before(): states = lax.all_gather(state.astype(BF16), 'fsdp')]
    all_to_all x0 -> x10, waiting for transfers between devices: none -> 237 us  [the longest x4 161 us: sum_rows(): lax.all_to_all(pieces, 'head', split_axis=0, concat_axis=0, tiled=True)]
    dot_general x58 -> x33, matrix products: 335 us -> 217 us  [the longest x18 163 us: dot(): lax.dot_general(a, b, (dims, ((), ())), precision=precision, preferred_el...]
    all_to_all x0 -> x5, blocking collectives: none -> 107 us  [the longest x1 51.3 us: share_rows(): lax.all_to_all(spread, 'head', split_axis=0, concat_axis=0, tiled=True)]
    unnamed x22 -> x17, waiting for transfers between devices: 91.6 us -> 2.59 us
    all_gather x3 -> x2, blocking collectives: 146 us -> 62.3 us  [the longest x1 49.2 us: per_device(): lengths = lax.all_gather(doc_lengths, 'head', axis=0, tiled=True)]
    reduce_sum x19 -> x12, other arithmetic: 92.8 us -> 26.9 us  [the longest x4 15.8 us: sum_rows(): return jnp.sum(pieces.astype(F32), axis=0)]
  transfers between devices with their start and end apart: 20 -> 27, of which waited for: 15 -> 17; matrix products, arithmetic and copies ran while one was open for 6% -> 23% of each run, Pallas kernels for 0% -> 0%
where the time goes in v1:
time: 1160 us; the launch traced here: 1150 us
  waiting for transfers between devices  483 us (42%)
  matrix products  217 us (19%)
  blocking collectives  214 us (18%)
  local copies, waits for them, and re-layouts  98.2 us (8%)
  other arithmetic  72.5 us (6%)
  starting transfers between devices  48.1 us (4%)
  between operations  15.5 us (1%)
    dot_general x18, matrix products, dot(): lax.dot_general(a, b, (dims, ((), ())), precision=precision, preferred_el...  163 us
    all_to_all x4, waiting for transfers between devices, sum_rows(): lax.all_to_all(pieces, 'head', split_axis=0, concat_axis=0, tiled=True)  161 us
    reduce_scatter x6, waiting for transfers between devices, scatter_columns(): g = lax.psum_scatter(g, axis, scatter_dimension=0, tiled=True)  126 us
    all_to_all x3, waiting for transfers between devices, share_rows(): lax.all_to_all(spread, 'head', split_axis=0, concat_axis=0, tiled=True)  69.2 us
    reduce_scatter x4, waiting for transfers between devices, scatter_part(): g = lax.psum_scatter(g, axis, scatter_dimension=0, tiled=True)  65.9 us
    dot_general x15, matrix products, batched(): return jnp.einsum(form, a, b, preferred_element_type=F32)  54.2 us
    all_to_all x1, blocking collectives, share_rows(): lax.all_to_all(spread, 'head', split_axis=0, concat_axis=0, tiled=True)  51.3 us
    all_gather x1, blocking collectives, per_device(): lengths = lax.all_gather(doc_lengths, 'head', axis=0, tiled=True)  49.2 us
  transfers between devices with their start and end apart: 27, of which 17 were waited for; matrix products, arithmetic and copies ran while one was open for 23% of the time, Pallas kernels for 0%

profile of v1, /device:TPU:0, one launch (start us, length us, event | category | flops | bytes accessed | tf_op | source)
XLA Modules:
  0.0 1148.0 jit_solution(497075202312209120)
XLA Ops:
  12.0 17.3 %all_to_all.79 = bf16[4,64,1552]{2,1,0:T(8,128)(2,1)} all-to-all(bf16[4,64,1552]{2,1,0:T(8,128)(2,1)S(1)} %bitcast.323), channel_id=1, replica_groups=mesh['rep'=1,'head'=4,'core'=2,'fsdp'=4] {'head'}, dimensions={0} | all-to-all | bytes 1589248 | tf_op jit(solution)/shard_map/all_to_all | solution.py:131
  29.7 43.7 %all-reduce = bf16[22016]{0:T(1024)(128)(2,1)S(1)} all-reduce(bf16[22016]{0:T(1024)(128)(2,1)S(1)} %dynamic-update-slice), channel_id=2, replica_groups=mesh['rep'=1,'head'=4,'core'=2,'fsdp'=4] {'rep','head','core','fsdp'}, use_global_device_ids=true, to_apply=%add | all-reduce | flops 22016 | bytes 88064
  85.8 49.2 %all-gather.3 = s32[4,1,8]{2,1,0:T(1,128)S(1)} all-gather(s32[1,1,8]{2,1,0:T(1,128)S(1)} %bitcast.346), channel_id=1, replica_groups=mesh['rep'=1,'head'=4,'core'=2,'fsdp'=4] {'head'}, dimensions={0}, use_global_device_ids=true | all-gather | bytes 160 | tf_op jit(solution)/shard_map/all_gather | solution.py:180
  138.5 12.0 %fusion.149 = f32[1024,1552]{0,1:T(8,128)S(1)} fusion(bf16[1024,2048]{1,0:T(8,128)(2,1)} %bitcast.7, bf16[2048,1552]{1,0:T(8,128)(2,1)} %all-gather.12.cloned.1.call-done), kind=kOutput, calls=%fused_computation.313 | convolution fusion | flops 6509559808 | bytes 16908288 | tf_op jit(solution)/shard_map/dot_general | solution.py:24
  180.7 13.2 %all_to_all.80 = bf16[4,64,1408]{2,1,0:T(8,128)(2,1)} all-to-all(bf16[4,64,1408]{2,1,0:T(8,128)(2,1)S(1)} %copy.361), channel_id=1, replica_groups=mesh['rep'=1,'head'=4,'core'=2,'fsdp'=4] {'head'}, dimensions={0} | all-to-all | bytes 1441792 | tf_op jit(solution)/shard_map/all_to_all | solution.py:131
  223.1 13.2 %all_gather.42 = bf16[4,4,256]{2,1,0:T(4,128)(2,1)S(1)} all-gather(bf16[1,4,256]{2,1,0:T(4,128)(2,1)S(1)} %copy.353), channel_id=1, replica_groups=mesh['rep'=1,'head'=4,'core'=2,'fsdp'=4] {'fsdp'}, dimensions={0}, use_global_device_ids=true | all-gather | bytes 10240 | tf_op jit(solution)/shard_map/all_gather | solution.py:82
  239.9 20.6 %all-gather.22.cloned.1.call-done = bf16[16,256,512]{2,1,0:T(8,128)(2,1)} async-done(((bf16[4,256,512]{2,1,0:T(8,128)(2,1)}), bf16[16,256,512]{2,1,0:T(8,128)(2,1)}) %all-gather.22.cloned.1.call-update) | async-done | bytes 4194320 | tf_op jit(solution)/shard_map/all_gather | solution.py:83
  271.4 18.5 %all-gather.14.cloned.1.call-done = bf16[512,2048]{1,0:T(8,128)(2,1)} async-done(((bf16[64,2048]{1,0:T(8,128)(2,1)}), bf16[512,2048]{1,0:T(8,128)(2,1)}) %all-gather.14.cloned.1.call-update) | async-done | bytes 2097168 | tf_op jit(solution)/shard_map/all_gather | solution.py:143
  301.7 47.5 %all-to-all-done.2 = bf16[4,256,2048]{2,1,0:T(8,128)(2,1)} async-done(((bf16[4,256,2048]{2,1,0:T(8,128)(2,1)}), bf16[4,256,2048]{2,1,0:T(8,128)(2,1)}, u32[]{:S(2)}, u32[]{:S(2)}) %all-to-all-start.2) | async-done | bytes 4194336 | tf_op jit(solution)/shard_map/all_to_all | solution.py:59
  364.4 51.3 %all_to_all.82 = bf16[4,256,2048]{2,1,0:T(8,128)(2,1)} all-to-all(bf16[4,256,2048]{2,1,0:T(8,128)(2,1)S(1)} %broadcast_in_dim.173), channel_id=1, replica_groups=mesh['rep'=1,'head'=4,'core'=2,'fsdp'=4] {'head'}, dimensions={0} | all-to-all | bytes 8388608 | tf_op jit(solution)/shard_map/all_to_all | solution.py:53
  447.0 22.4 %all-to-all-done.7 = bf16[4,256,2048]{2,1,0:T(8,128)(2,1)} async-done(((bf16[4,256,2048]{2,1,0:T(8,128)(2,1)}), bf16[4,256,2048]{2,1,0:T(8,128)(2,1)}, u32[]{:S(2)}, u32[]{:S(2)}) %all-to-all-start.7) | async-done | bytes 4194336 | tf_op jit(solution)/shard_map/all_to_all | solution.py:53
  472.5 15.7 %multiply_convert_fusion.2 = (bf16[1024,1408]{1,0:T(8,128)(2,1)S(1)}, bf16[1024,1408]{1,0:T(8,128)(2,1)S(1)}, bf16[1024,1408]{1,0:T(8,128)(2,1)}) fusion(f32[1024,1408]{1,0:T(8,128)} %fusion.150, f32[1024,1408]{1,0:T(8,128)} %fusion.151, bf16[1024,2048]{1,0:T(8,128)(2,1)} %bitcast.39, bf16[1408,2048]{1,0:T(8,128)(2,1)} %all-gather.20.cloned.1.call-done), kind=kOutput, calls=%fused_computation.19 | convolution fusion | flops 5928648704 | bytes 30146560 | tf_op jit(solution)/shard_map/dot_general | solution.py:24
  523.4 37.1 %all-to-all-done.8 = bf16[4,256,2048]{2,1,0:T(8,128)(2,1)} async-done(((bf16[4,256,2048]{2,1,0:T(8,128)(2,1)}), bf16[4,256,2048]{2,1,0:T(8,128)(2,1)}, u32[]{:S(2)}, u32[]{:S(2)}) %all-to-all-start.8) | async-done | bytes 4194336 | tf_op jit(solution)/shard_map/all_to_all | solution.py:59
  581.8 30.8 %all-to-all-done.6 = bf16[4,256,2048]{2,1,0:T(8,128)(2,1)} async-done(((bf16[4,256,2048]{2,1,0:T(8,128)(2,1)}), bf16[4,256,2048]{2,1,0:T(8,128)(2,1)}, u32[]{:S(2)}, u32[]{:S(2)}) %all-to-all-start.6) | async-done | bytes 4194336 | tf_op jit(solution)/shard_map/all_to_all | solution.py:59
  626.2 46.8 %all-to-all-done.9 = bf16[4,256,2048]{2,1,0:T(8,128)(2,1)} async-done(((bf16[4,256,2048]{2,1,0:T(8,128)(2,1)}), bf16[4,256,2048]{2,1,0:T(8,128)(2,1)}, u32[]{:S(2)}, u32[]{:S(2)}) %all-to-all-start.9) | async-done | bytes 4194336 | tf_op jit(solution)/shard_map/all_to_all | solution.py:53
  747.9 13.4 %multiply_reduce_fusion = (f32[4,256,256]{2,1,0:T(8,128)}, f32[4,256,256]{2,1,0:T(8,128)}, bf16[4,8,256,256]{3,2,1,0:T(8,128)(2,1)}) fusion(f32[4,10,256,256]{3,2,1,0:T(8,128)} %exponential_bitcast_fusion, f32[4,8,256,256]{3,2,1,0:T(8,128)} %fusion.1, bf16[4,8,256,256]{3,2,1,0:T(8,128)(2,1)S(1)} %copy-done.1, bf16[4,8,256,256]{3,2,1,0:T(8,128)(2,1)} %copy-done.19, ...), kind=kOutput, calls=%fused_computation.3 | convolution fusion | flops 1096286208 | bytes 36700160 | tf_op jit(solution)/shard_map/bsij,bsik->bsjk/dot_general | solution.py:40
  815.5 17.4 %reduce-scatter.27.cloned.1.call-done = bf16[704,2048]{1,0:T(8,128)(2,1)} async-done(((bf16[1408,2048]{1,0:T(8,128)(2,1)}), bf16[704,2048]{1,0:T(8,128)(2,1)}) %reduce-scatter.27.cloned.1.call-update) | async-done | bytes 2883600 | tf_op jit(solution)/shard_map/reduce_scatter | solution.py:152
  833.0 17.9 %reduce-scatter.11.cloned.1.call-done = bf16[1024,1552]{0,1:T(8,128)(2,1)} async-done(((bf16[2048,1552]{0,1:T(8,128)(2,1)}), bf16[1024,1552]{0,1:T(8,128)(2,1)}) %reduce-scatter.11.cloned.1.call-update) | async-done | bytes 3178512 | tf_op jit(solution)/shard_map/reduce_scatter | solution.py:137
  851.0 12.6 %convolution_convert_fusion.4 = bf16[1024,2048]{1,0:T(8,128)(2,1)} fusion(bf16[1024,1552]{0,1:T(8,128)(2,1)} %copy-done.53, bf16[2048,1552]{1,0:T(8,128)(2,1)} %all-gather.12.cloned.1.call-done), kind=kOutput, calls=%fused_computation.35 | convolution fusion | flops 6511656960 | bytes 13729792 | tf_op jit(solution)/shard_map/dot_general | solution.py:24
  871.2 45.6 %all-to-all-done.10 = bf16[4,256,2048]{2,1,0:T(8,128)(2,1)} async-done(((bf16[4,256,2048]{2,1,0:T(8,128)(2,1)}), bf16[4,256,2048]{2,1,0:T(8,128)(2,1)}, u32[]{:S(2)}, u32[]{:S(2)}) %all-to-all-start.10) | async-done | bytes 4194336 | tf_op jit(solution)/shard_map/all_to_all | solution.py:59
  927.0 14.2 %all_to_all.83 = f32[32,1,688]{2,1,0:T(1,128)S(1)} all-to-all(f32[32,1,688]{2,1,0:T(1,128)S(1)} %copy.388), channel_id=1, replica_groups=mesh['rep'=1,'head'=4,'core'=2,'fsdp'=4] {'rep','head','core','fsdp'}, dimensions={0} | all-to-all | bytes 176128 | tf_op jit(solution)/shard_map/all_to_all | solution.py:354
  951.8 46.7 %reduce-scatter.25.cloned.1.call-done = bf16[256,1408]{1,0:T(8,128)(2,1)} async-done(((bf16[1024,1408]{1,0:T(8,128)(2,1)}), bf16[256,1408]{1,0:T(8,128)(2,1)}) %reduce-scatter.25.cloned.1.call-update) | async-done | bytes 720912 | tf_op jit(solution)/shard_map/reduce_scatter | solution.py:137
  1008.4 48.4 %reduce-scatter.29.cloned.1.call-done = bf16[176,2048]{1,0:T(8,128)(2,1)} async-done(((bf16[704,2048]{1,0:T(8,128)(2,1)}), bf16[176,2048]{1,0:T(8,128)(2,1)}) %reduce-scatter.29.cloned.1.call-update) | async-done | bytes 720912 | tf_op jit(solution)/shard_map/reduce_scatter | solution.py:152
  1059.2 60.6 %reduce-scatter.13.cloned.1.call-done = bf16[256,1552]{0,1:T(8,128)(2,1)} async-done(((bf16[1024,1552]{0,1:T(8,128)(2,1)}), bf16[256,1552]{0,1:T(8,128)(2,1)}) %reduce-scatter.13.cloned.1.call-update) | async-done | bytes 794640 | tf_op jit(solution)/shard_map/reduce_scatter | solution.py:137
  (419 shorter events, 416.2 us)
Async XLA Ops:
  7.2 131.3 %all-gather.12.cloned.1.call-start = ((), (), s32[]{:S(2)}) async-start(), calls=%async_computation.25 | async-start | bytes 7667712 | tf_op jit(solution)/shard_map/all_gather | solution.py:132
  80.7 57.8 %all-to-all-start = ((bf16[4,256,2048]{2,1,0:T(8,128)(2,1)}), bf16[4,256,2048]{2,1,0:T(8,128)(2,1)}, u32[]{:S(2)}, u32[]{:S(2)}) async-start(bf16[4,256,2048]{2,1,0:T(8,128)(2,1)} %broadcast_in_dim.165), calls=%async_computation | async-start | bytes 8388608 | tf_op jit(solution)/shard_map/all_to_all | solution.py:53
  85.7 174.8 %all-gather.22.cloned.1.call-start = ((), (), s32[]{:S(2)}) async-start(), calls=%async_computation.40 | async-start | bytes 5242880 | tf_op jit(solution)/shard_map/all_gather | solution.py:83
  178.0 111.8 %all-gather.14.cloned.1.call-start = ((), (), s32[]{:S(2)}) async-start(), calls=%async_computation.26 | async-start | bytes 2359296 | tf_op jit(solution)/shard_map/all_gather | solution.py:143
  178.8 244.8 %all-gather.16.cloned.1.call-start = ((), (), s32[]{:S(2)}) async-start(), calls=%async_computation.27 | async-start | bytes 6488064 | tf_op jit(solution)/shard_map/all_gather | solution.py:132
  194.0 241.3 %all-gather.18.cloned.1.call-start = ((), (), s32[]{:S(2)}) async-start(), calls=%async_computation.28 | async-start | bytes 6488064 | tf_op jit(solution)/shard_map/all_gather | solution.py:132
  296.1 53.1 %all-to-all-start.2 = ((bf16[4,256,2048]{2,1,0:T(8,128)(2,1)}), bf16[4,256,2048]{2,1,0:T(8,128)(2,1)}, u32[]{:S(2)}, u32[]{:S(2)}) async-start(bf16[4,256,2048]{2,1,0:T(8,128)(2,1)} %bitcast.308), calls=%async_computation.2 | async-start | bytes 8388608 | tf_op jit(solution)/shard_map/all_to_all | solution.py:59
  301.1 171.4 %all-gather.20.cloned.1.call-start = ((), (), s32[]{:S(2)}) async-start(), calls=%async_computation.29 | async-start | bytes 6488064 | tf_op jit(solution)/shard_map/all_gather | solution.py:143
  507.3 53.1 %all-to-all-start.8 = ((bf16[4,256,2048]{2,1,0:T(8,128)(2,1)}), bf16[4,256,2048]{2,1,0:T(8,128)(2,1)}, u32[]{:S(2)}, u32[]{:S(2)}) async-start(bf16[4,256,2048]{2,1,0:T(8,128)(2,1)} %bitcast.309), calls=%async_computation.8 | async-start | bytes 8388608 | tf_op jit(solution)/shard_map/all_to_all | solution.py:59
  560.5 52.1 %all-to-all-start.6 = ((bf16[4,256,2048]{2,1,0:T(8,128)(2,1)}), bf16[4,256,2048]{2,1,0:T(8,128)(2,1)}, u32[]{:S(2)}, u32[]{:S(2)}) async-start(bf16[4,256,2048]{2,1,0:T(8,128)(2,1)} %bitcast.306), calls=%async_computation.6 | async-start | bytes 8388608 | tf_op jit(solution)/shard_map/all_to_all | solution.py:59
  626.2 144.3 %all-gather.24.cloned.1.call-start = ((), (), s32[]{:S(2)}) async-start(), calls=%async_computation.41 | async-start | bytes 5242880 | tf_op jit(solution)/shard_map/all_gather | solution.py:83
  691.7 121.2 %reduce-scatter.19.cloned.1.call-start = ((), (), s32[]{:S(2)}) async-start(), calls=%async_computation.34 | async-start | bytes 8650752 | tf_op jit(solution)/shard_map/reduce_scatter | solution.py:137
  703.2 110.4 %reduce-scatter.15.cloned.1.call-start = ((), (), s32[]{:S(2)}) async-start(), calls=%async_computation.32 | async-start | bytes 3145728 | tf_op jit(solution)/shard_map/reduce_scatter | solution.py:152
  709.5 106.0 %reduce-scatter.23.cloned.1.call-start = ((), (), s32[]{:S(2)}) async-start(), calls=%async_computation.36 | async-start | bytes 8650752 | tf_op jit(solution)/shard_map/reduce_scatter | solution.py:137
  720.6 112.4 %reduce-scatter.27.cloned.1.call-start = ((), (), s32[]{:S(2)}) async-start(), calls=%async_computation.38 | async-start | bytes 8650752 | tf_op jit(solution)/shard_map/reduce_scatter | solution.py:152
  731.2 119.8 %reduce-scatter.11.cloned.1.call-start = ((), (), s32[]{:S(2)}) async-start(), calls=%async_computation.30 | async-start | bytes 9535488 | tf_op jit(solution)/shard_map/reduce_scatter | solution.py:137
  812.9 128.3 %reduce-scatter.21.cloned.1.call-start = ((), (), s32[]{:S(2)}) async-start(), calls=%async_computation.35 | async-start | bytes 3604480 | tf_op jit(solution)/shard_map/reduce_scatter | solution.py:137
  813.6 131.8 %reduce-scatter.17.cloned.1.call-start = ((), (), s32[]{:S(2)}) async-start(), calls=%async_computation.33 | async-start | bytes 1310720 | tf_op jit(solution)/shard_map/reduce_scatter | solution.py:152
  814.2 184.3 %reduce-scatter.25.cloned.1.call-start = ((), (), s32[]{:S(2)}) async-start(), calls=%async_computation.37 | async-start | bytes 3604480 | tf_op jit(solution)/shard_map/reduce_scatter | solution.py:137
  815.5 241.3 %reduce-scatter.29.cloned.1.call-start = ((), (), s32[]{:S(2)}) async-start(), calls=%async_computation.39 | async-start | bytes 3604480 | tf_op jit(solution)/shard_map/reduce_scatter | solution.py:152
  833.0 286.8 %reduce-scatter.13.cloned.1.call-start = ((), (), s32[]{:S(2)}) async-start(), calls=%async_computation.31 | async-start | bytes 3973120 | tf_op jit(solution)/shard_map/reduce_scatter | solution.py:137
  863.6 53.2 %all-to-all-start.10 = ((bf16[4,256,2048]{2,1,0:T(8,128)(2,1)}), bf16[4,256,2048]{2,1,0:T(8,128)(2,1)}, u32[]{:S(2)}, u32[]{:S(2)}) async-start(bf16[4,256,2048]{2,1,0:T(8,128)(2,1)} %bitcast.307), calls=%async_computation.10 | async-start | bytes 8388608 | tf_op jit(solution)/shard_map/all_to_all | solution.py:59
  941.2 57.3 %all-to-all-start.13 = ((bf16[4,64,1408]{2,1,0:T(8,128)(2,1)}), bf16[4,64,1408]{2,1,0:T(8,128)(2,1)}, u32[]{:S(2)}, u32[]{:S(2)}) async-start(bf16[4,64,1408]{2,1,0:T(8,128)(2,1)} %bitcast.326), calls=%async_computation.19 | async-start | bytes 1441792 | tf_op jit(solution)/shard_map/all_to_all | solution.py:138
  998.5 123.5 %all-to-all-start.14 = ((bf16[4,64,1408]{2,1,0:T(8,128)(2,1)}), bf16[4,64,1408]{2,1,0:T(8,128)(2,1)}, u32[]{:S(2)}, u32[]{:S(2)}) async-start(bf16[4,64,1408]{2,1,0:T(8,128)(2,1)} %bitcast.325), calls=%async_computation.22 | async-start | bytes 1441792 | tf_op jit(solution)/shard_map/all_to_all | solution.py:138
  (85 other events, 1313.9 us)
Sparse Core Ops, SparseCore 0:
  29.4 69.6 all-gather.11
  178.2 82.3 all-gather.21
  262.2 27.6 all-gather.13
  291.3 59.9 all-gather.15
  352.7 59.0 all-gather.17
  413.3 59.1 all-gather.19
  691.9 78.5 all-gather.23
  772.7 12.3 reduce-scatter.18
  787.4 10.8 reduce-scatter.14
  800.4 14.9 reduce-scatter.22
  817.9 15.0 reduce-scatter.26
  835.1 15.7 reduce-scatter.10
  853.3 57.3 reduce-scatter.20
  912.8 28.5 reduce-scatter.16
  943.7 54.7 reduce-scatter.24
  1000.8 56.0 reduce-scatter.28
  1059.1 60.6 reduce-scatter.12

commit v2 on v1

v2 whole, which is shorter than its diff:
```python
import functools

import jax
import jax.experimental.pallas as pl
import jax.experimental.pallas.tpu as pltpu
import jax.numpy as jnp
from jax import lax
from jax.sharding import Mesh
from jax.sharding import PartitionSpec as P

H = 4
DK = 256
DV = 512
CORES = 2
DOCS = 8
PIECES = 2
LANES = 128

EPS = 1e-05
HEAD_EPS = 1.0
HIGHEST = lax.Precision.HIGHEST
F32 = jnp.float32
BF16 = jnp.bfloat16

SHARE = ("rep", "core", "fsdp")
EVERY = ("rep", "head", "core", "fsdp")


def dot(a, b, dims, precision=None):
    return lax.dot_general(a, b, (dims, ((), ())), precision=precision, preferred_element_type=F32)


def after(value, *others):
    return lax.optimization_barrier((value,) + others)


def matmul(a, b):
    return dot(a, b, ((1,), (0,)))


def rows_product(a, b):
    return dot(a, b, ((0,), (0,)))


def back_product(a, b):
    return dot(a, b, ((1,), (1,)))


def batched(form, a, b):
    return jnp.einsum(form, a, b, preferred_element_type=F32)


def rms_scale(values, epsilon):
    return lax.rsqrt(jnp.mean(values * values, axis=-1, keepdims=True) + epsilon)


def rms_back(upstream, values, scale):
    return scale * upstream - values * scale**3 * jnp.mean(upstream * values, axis=-1, keepdims=True)


def share_rows(part):
    spread = jnp.broadcast_to(part[None], (H,) + part.shape)
    whole = lax.all_to_all(spread, "head", split_axis=0, concat_axis=0, tiled=True)
    return whole.reshape(-1, part.shape[-1])


def move_rows(partial):
    pieces = partial.astype(BF16).reshape(H, -1, partial.shape[-1])
    return lax.all_to_all(pieces, "head", split_axis=0, concat_axis=0, tiled=True)


def sum_rows(partial):
    return jnp.sum(move_rows(partial).astype(F32), axis=0)


def level_sums(length):
    rows = jnp.arange(length)[:, None]
    cols = jnp.arange(length)[None, :]
    sums, pairs = [], []
    step = 1
    while step < length:
        bound = rows // (2 * step) * (2 * step) + step - 1
        upper = rows > bound
        sums.append(jnp.where(upper, (cols > bound) & (cols <= rows), (cols > rows) & (cols <= bound)))
        pairs.append(upper & (cols // (2 * step) == rows // (2 * step)) & (cols <= bound))
        step *= 2
    sums.append(cols <= rows)
    sums.append(cols > rows)
    return jnp.stack(sums), jnp.stack(pairs)


def log_sigmoid(x):
    return jnp.minimum(x, 0.0) - jnp.log1p(jnp.exp(-jnp.abs(x)))


def state_copy(send, recv, send_sem, recv_sem, seq, piece, target):
    size = send.shape[1] // PIECES
    part = pl.ds(piece * size, size)
    return pltpu.make_async_remote_copy(
        src_ref=send.at[seq, part],
        dst_ref=recv.at[seq, part],
        send_sem=send_sem.at[seq, piece],
        recv_sem=recv_sem.at[seq, piece],
        device_id={"fsdp": target},
        device_id_type=pl.DeviceIdType.MESH,
    )


def greet_neighbours(place, parts):
    barrier = pltpu.get_barrier_semaphore()
    for near, there in ((place - 1, place > 0), (place + 1, place < parts - 1)):

        @pl.when(there)
        def _(near=near):
            pl.semaphore_signal(
                barrier,
                inc=1,
                device_id={"fsdp": lax.rem(near + parts, parts)},
                device_id_type=pl.DeviceIdType.MESH,
            )

    peers = (place > 0).astype(jnp.int32) + (place < parts - 1).astype(jnp.int32)
    pl.semaphore_wait(barrier, peers)


def pass_state(s, first, last, target, decay, local, send, recv, send_sem, recv_sem):
    size = send.shape[1] // PIECES
    for piece in range(PIECES):
        part = pl.ds(piece * size, size)
        copy = state_copy(send, recv, send_sem, recv_sem, s, piece, target)

        @pl.when(jnp.logical_not(first))
        def _(copy=copy):
            copy.wait_recv()

        @pl.when(jnp.logical_not(last))
        def _(copy=copy, part=part):
            joined = decay * recv[s, part].astype(F32) + local[s, part]
            send[s, part] = joined.astype(BF16)
            copy.start()


def finish_states(count, last, target, send, recv, send_sem, recv_sem):
    @pl.when(jnp.logical_not(last))
    def _():
        def one(s, carry):
            for piece in range(PIECES):
                state_copy(send, recv, send_sem, recv_sem, s, piece, target).wait_send()
            return carry

        lax.fori_loop(0, count, one, 0)


def split_rates(logits):
    rates = log_sigmoid(logits) / 16.0
    high = rates.astype(BF16)
    return high, (rates - high.astype(F32)).astype(BF16)


def decayed(sums, high, low):
    return jnp.exp(matmul(sums, high) + matmul(sums, low))


def forward_kernel(
    key_dim,
    value_dim,
    mixed_ref,
    bias_ref,
    gaterank_ref,
    gain_ref,
    marks_ref,
    segment_ref,
    sums_ref,
    pairs_ref,
    gated_ref,
    attended_ref,
    logits_ref,
    scores_ref,
    start_ref,
    end_ref,
    decay_ref,
    enter_ref,
    local_ref,
    send_ref,
    recv_ref,
    send_sem,
    recv_sem,
):
    count, _, length = segment_ref.shape
    levels = pairs_ref.shape[0]
    parts, place = lax.axis_size("fsdp"), lax.axis_index("fsdp")
    first, last, target = place == 0, place == parts - 1, lax.rem(place + 1, parts)
    rank = gaterank_ref.shape[0]
    scale = key_dim ** (-0.5)
    value_at = 2 * key_dim
    gate_at = value_at + value_dim
    rank_at = gate_at + value_dim

    greet_neighbours(place, parts)

    @pl.when(first)
    def _():
        recv_ref[...] = jnp.zeros_like(recv_ref)

    def rows_of(s):
        return pl.ds(pl.multiple_of(s * length, length), length)

    def ends(s, carry):
        rows = rows_of(s)
        lowrank = mixed_ref[rows, pl.ds(rank_at, rank)]
        logits = dot(lowrank, gaterank_ref[...], ((1,), (0,)), HIGHEST) + bias_ref[...]
        logits_ref[rows, :] = logits
        high, low = split_rates(logits)
        from_start = decayed(sums_ref[levels], high, low)
        to_end = decayed(sums_ref[levels + 1], high, low)
        marks = marks_ref[rows, :]
        decay_ref[s] = from_start[length - 1 :, :] * marks[:1, 4:5]
        query = mixed_ref[rows, pl.ds(0, key_dim)] * scale
        key = mixed_ref[rows, pl.ds(key_dim, key_dim)]
        start_ref[rows, :] = (query * (from_start * marks[:, 1:2])).astype(BF16)
        end_key = (key * (to_end * marks[:, 2:3])).astype(BF16)
        end_ref[rows, :] = end_key
        value = mixed_ref[rows, pl.ds(value_at, value_dim)].astype(BF16)
        local_ref[s] = rows_product(value, end_key)
        return carry

    lax.fori_loop(0, count, ends, 0)

    def mix(s, carry):
        rows = rows_of(s)
        pass_state(
            s, first, last, target, decay_ref[s], local_ref, send_ref, recv_ref, send_sem, recv_sem
        )
        query = mixed_ref[rows, pl.ds(0, key_dim)] * scale
        key = mixed_ref[rows, pl.ds(key_dim, key_dim)]
        high, low = split_rates(logits_ref[rows, :])
        scores = jnp.zeros((length, length), F32)
        for level in range(levels):
            decay = decayed(sums_ref[level], high, low)
            pair = back_product((query * decay).astype(BF16), (key * decay).astype(BF16))
            scores += pair * pairs_ref[level].astype(F32)
        row = lax.broadcasted_iota(jnp.int32, (length, length), 0)
        col = lax.broadcasted_iota(jnp.int32, (length, length), 1)
        own = jnp.sum(query * key, axis=1, keepdims=True)
        scores += jnp.where(row == col, own, 0.0)
        marks = marks_ref[rows, :]
        scores = jnp.where(marks[:, 0:1] == segment_ref[s], scores, 0.0).astype(BF16)
        scores_ref[s] = scores
        value = mixed_ref[rows, pl.ds(value_at, value_dim)].astype(BF16)
        attended = matmul(scores, value) + back_product(start_ref[rows, :], recv_ref[s])
        attended = attended * marks[:, 3:4]
        attended_ref[rows, :] = attended
        headed = attended * rms_scale(attended, HEAD_EPS) * gain_ref[...]
        outgate = mixed_ref[rows, pl.ds(gate_at, value_dim)]
        gated_ref[rows, :] = (headed * (outgate * jax.nn.sigmoid(outgate))).astype(BF16)
        enter_ref[s] = recv_ref[s]
        return carry

    lax.fori_loop(0, count, mix, 0)
    finish_states(count, last, target, send_ref, recv_ref, send_sem, recv_sem)


def backward_kernel(
    key_dim,
    value_dim,
    mixed_ref,
    logits_ref,
    scores_ref,
    start_ref,
    end_ref,
    decay_ref,
    enter_ref,
    attended_ref,
    upstream_ref,
    gaterank_ref,
    gain_ref,
    marks_ref,
    segment_ref,
    sums_ref,
    pairs_ref,
    grad_ref,
    gain_grad_ref,
    bias_grad_ref,
    gaterank_grad_ref,
    out_ref,
    local_ref,
    send_ref,
    recv_ref,
    send_sem,
    recv_sem,
):
    count, _, length = segment_ref.shape
    levels = pairs_ref.shape[0]
    parts, place = lax.axis_size("fsdp"), lax.axis_index("fsdp")
    first, last, target = place == parts - 1, place == 0, lax.rem(place + parts - 1, parts)
    rank = gaterank_ref.shape[0]
    scale = key_dim ** (-0.5)
    value_at = 2 * key_dim
    gate_at = value_at + value_dim
    rank_at = gate_at + value_dim

    greet_neighbours(place, parts)

    @pl.when(first)
    def _():
        recv_ref[...] = jnp.zeros_like(recv_ref)

    gain_grad_ref[...] = jnp.zeros_like(gain_grad_ref)
    bias_grad_ref[...] = jnp.zeros_like(bias_grad_ref)
    gaterank_grad_ref[...] = jnp.zeros_like(gaterank_grad_ref)

    def rows_of(s):
        return pl.ds(pl.multiple_of(s * length, length), length)

    def heads(s, carry):
        rows = rows_of(s)
        upstream = upstream_ref[rows, :]
        attended = attended_ref[rows, :]
        outgate = mixed_ref[rows, pl.ds(gate_at, value_dim)]
        gain = gain_ref[...]
        norm = rms_scale(attended, HEAD_EPS)
        normed = attended * norm
        sig = jax.nn.sigmoid(outgate)
        grad_gate = upstream * (normed * gain) * sig * (1.0 + outgate * (1.0 - sig))
        grad_ref[rows, pl.ds(gate_at, value_dim)] = grad_gate.astype(BF16)
        grad_headed = upstream * (outgate * sig)
        gain_grad_ref[...] += jnp.sum(grad_headed * normed, axis=0, keepdims=True)
        grad_out = rms_back(grad_headed * gain, attended, norm) * marks_ref[rows, pl.ds(3, 1)]
        grad_out = grad_out.astype(BF16)
        out_ref[rows, :] = grad_out
        local_ref[s] = rows_product(grad_out, start_ref[rows, :])
        return carry

    lax.fori_loop(0, count, heads, 0)

    def mix(s, carry):
        rows = rows_of(s)
        decay_row = decay_ref[s]
        pass_state(
            s, first, last, target, decay_row, local_ref, send_ref, recv_ref, send_sem, recv_sem
        )
        query = mixed_ref[rows, pl.ds(0, key_dim)] * scale
        key = mixed_ref[rows, pl.ds(key_dim, key_dim)]
        value = mixed_ref[rows, pl.ds(value_at, value_dim)].astype(BF16)
        marks = marks_ref[rows, :]
        logits = logits_ref[rows, :]
        high, low = split_rates(logits)
        grad_out = out_ref[rows, :]
        row = lax.broadcasted_iota(jnp.int32, (length, length), 0)
        col = lax.broadcasted_iota(jnp.int32, (length, length), 1)
        pair_grads = back_product(grad_out, value)
        pair_grads = jnp.where(marks[:, 0:1] == segment_ref[s], pair_grads, 0.0)
        own = jnp.sum(jnp.where(row == col, pair_grads, 0.0), axis=1, keepdims=True)
        grad_query = own * key
        grad_key = own * query
        grad_rates = jnp.zeros((length, key_dim), F32)
        for level in range(levels):
            decay = decayed(sums_ref[level], high, low)
            level_query = (query * decay).astype(BF16)
            level_key = (key * decay).astype(BF16)
            level_pairs = (pair_grads * pairs_ref[level].astype(F32)).astype(BF16)
            level_grad_query = matmul(level_pairs, level_key)
            level_grad_key = rows_product(level_pairs, level_query)
            grad_query += level_grad_query * decay
            grad_key += level_grad_key * decay
            flow = level_grad_query * level_query.astype(F32)
            flow += level_grad_key * level_key.astype(F32)
            grad_rates += rows_product(sums_ref[level], flow.astype(BF16))
        ending = recv_ref[s]
        entering = enter_ref[s]
        start_query = start_ref[rows, :]
        end_key = end_ref[rows, :]
        start_grad = matmul(grad_out, entering)
        end_grad = matmul(value, ending)
        grad_query += start_grad * (decayed(sums_ref[levels], high, low) * marks[:, 1:2])
        grad_key += end_grad * (decayed(sums_ref[levels + 1], high, low) * marks[:, 2:3])
        grad_rates += rows_product(
            sums_ref[levels], (start_grad * start_query.astype(F32)).astype(BF16)
        )
        grad_rates += rows_product(
            sums_ref[levels + 1], (end_grad * end_key.astype(F32)).astype(BF16)
        )
        grad_rates += decay_row * jnp.sum(
            ending.astype(F32) * entering.astype(F32), axis=0, keepdims=True
        )
        grad_value = rows_product(scores_ref[s], grad_out) + back_product(end_key, ending)
        grad_ref[rows, pl.ds(0, key_dim)] = (grad_query * scale).astype(BF16)
        grad_ref[rows, pl.ds(key_dim, key_dim)] = grad_key.astype(BF16)
        grad_ref[rows, pl.ds(value_at, value_dim)] = grad_value.astype(BF16)
        grad_logits = grad_rates / 16.0 * jax.nn.sigmoid(-logits)
        bias_grad_ref[...] += jnp.sum(grad_logits, axis=0, keepdims=True)
        lowrank = mixed_ref[rows, pl.ds(rank_at, rank)]
        gaterank_grad_ref[...] += dot(lowrank, grad_logits, ((0,), (0,)), HIGHEST)
        grad_lowrank = dot(grad_logits, gaterank_ref[...], ((1,), (1,)), HIGHEST)
        rest = grad_ref.shape[1] - rank_at - rank
        grad_ref[rows, pl.ds(rank_at, rank + rest)] = jnp.concatenate(
            [grad_lowrank, jnp.zeros((length, rest), F32)], axis=1
        ).astype(BF16)
        return carry

    lax.fori_loop(0, count, mix, 0)
    finish_states(count, last, target, send_ref, recv_ref, send_sem, recv_sem)


def state_scratch(count, value_dim, key_dim):
    return [
        pltpu.VMEM((count, value_dim, key_dim), F32),
        pltpu.VMEM((count, value_dim, key_dim), BF16),
        pltpu.VMEM((count, value_dim, key_dim), BF16),
        pltpu.SemaphoreType.DMA((count, PIECES)),
        pltpu.SemaphoreType.DMA((count, PIECES)),
    ]


def kernel_params(number):
    return pltpu.CompilerParams(
        collective_id=number, has_side_effects=True, vmem_limit_bytes=52 * 2**20
    )


def mix_forward(mixed, bias, gaterank, gain, marks, segment, sums, pairs, key_dim, value_dim):
    rows = mixed.shape[0]
    count, _, length = segment.shape
    shapes = (
        ((rows, value_dim), BF16),
        ((rows, value_dim), F32),
        ((rows, key_dim), F32),
        ((count, length, length), BF16),
        ((rows, key_dim), BF16),
        ((rows, key_dim), BF16),
        ((count, 1, key_dim), F32),
        ((count, value_dim, key_dim), BF16),
    )
    whole = pl.BlockSpec(memory_space=pltpu.VMEM)
    return pl.pallas_call(
        functools.partial(forward_kernel, key_dim, value_dim),
        out_shape=[jax.ShapeDtypeStruct(*s) for s in shapes],
        in_specs=[whole] * 8,
        out_specs=[whole] * len(shapes),
        scratch_shapes=state_scratch(count, value_dim, key_dim),
        compiler_params=kernel_params(1),
        cost_estimate=pl.CostEstimate(flops=5 * 10**10, bytes_accessed=10**7, transcendentals=0),
        name="mix_forward",
    )(mixed, bias, gaterank, gain, marks, segment, sums, pairs)


def mix_backward(
    mixed, kept, upstream, gaterank, gain, marks, segment, sums, pairs, key_dim, value_dim
):
    rows = mixed.shape[0]
    count = segment.shape[0]
    shapes = (
        (mixed.shape, BF16),
        ((1, value_dim), F32),
        ((1, key_dim), F32),
        (gaterank.shape, F32),
    )
    attended, logits, scores, start, end, decay, enter = kept
    whole = pl.BlockSpec(memory_space=pltpu.VMEM)
    return pl.pallas_call(
        functools.partial(backward_kernel, key_dim, value_dim),
        out_shape=[jax.ShapeDtypeStruct(*s) for s in shapes],
        in_specs=[whole] * 15,
        out_specs=[whole] * len(shapes),
        scratch_shapes=[pltpu.VMEM((rows, value_dim), BF16)]
        + state_scratch(count, value_dim, key_dim),
        compiler_params=kernel_params(2),
        cost_estimate=pl.CostEstimate(flops=8 * 10**10, bytes_accessed=10**7, transcendentals=0),
        name="mix_backward",
    )(
        mixed,
        logits,
        scores,
        start,
        end,
        decay,
        enter,
        attended,
        upstream,
        gaterank,
        gain,
        marks,
        segment,
        sums,
        pairs,
    )


def per_device(
    tokens,
    doc_lengths,
    norm_gain,
    w_query,
    w_key,
    w_value,
    w_outgate,
    w_lowrank,
    w_gaterank,
    gate_bias,
    head_gain,
    w_output,
    ffn_gain,
    w_gate,
    w_up,
    w_down,
    cotangent,
):
    seqs_here, length, width = tokens.shape
    reps = lax.axis_size("rep")
    parts = lax.axis_size("fsdp")
    devices = reps * H * CORES * parts
    here = lax.axis_index("head")
    key_dim, value_dim = DK, DV
    rank = w_lowrank.shape[1]
    rows = width // devices
    count = H * seqs_here

    rank_at = 2 * key_dim + 2 * value_dim

    def to_shared(a):
        shaped = a.reshape(a.shape[0], reps, H, CORES * parts, rows)
        return shaped.transpose(0, 1, 3, 2, 4).reshape(a.shape)

    def from_shared(a):
        shaped = a.reshape(a.shape[0], reps, CORES * parts, H, rows)
        return shaped.transpose(0, 1, 3, 2, 4).reshape(a.shape)

    def core_sum(g):
        halves = g.reshape(CORES, -1, g.shape[-1])
        core = lax.axis_index("core")
        other = lax.ppermute(halves[1 - core], "core", ((0, 1), (1, 0)))
        return (halves[core].astype(F32) + other.astype(F32)).astype(BF16)

    def pair_rows(g):
        if reps > 1:
            g = lax.psum_scatter(g, "rep", scatter_dimension=0, tiled=True)
        return core_sum(g)

    def scatter_rows(g):
        return lax.psum_scatter(g, "fsdp", scatter_dimension=0, tiled=True)

    def gather_columns(w):
        moved = lax.all_to_all(w.transpose(1, 0, 2), "head", split_axis=0, concat_axis=0, tiled=True)
        return lax.all_gather(moved.reshape(-1, w.shape[2]), SHARE, axis=0, tiled=True)

    def to_columns(g):
        moved = lax.all_to_all(g.reshape(H, rows, -1), "head", split_axis=0, concat_axis=0, tiled=True)
        return moved.transpose(1, 0, 2).astype(F32)

    def gather_part(w):
        if reps == 1:
            return lax.all_gather(w, SHARE, axis=0, tiled=True)
        whole = lax.all_gather(w, EVERY, axis=0, tiled=True)
        size = whole.shape[0] // H
        return lax.dynamic_slice_in_dim(whole, here * size, size, 0)

    def pair_part(g):
        return core_sum(g) if reps == 1 else g

    def scatter_part(g):
        if reps == 1:
            return lax.psum_scatter(g, "fsdp", scatter_dimension=0, tiled=True)
        whole = jnp.zeros((H * g.shape[0], g.shape[1]), BF16)
        whole = lax.dynamic_update_slice_in_dim(whole, g, here * g.shape[0], 0)
        return lax.psum_scatter(whole, EVERY, scatter_dimension=0, tiled=True)

    def with_gain(w, gain):
        return (w.astype(F32) * gain.astype(F32)[:, None]).astype(BF16)

    small = (
        gate_bias,
        head_gain,
        w_gaterank.reshape(-1),
        (doc_lengths // 16).astype(BF16).reshape(-1),
        (doc_lengths % 16).astype(BF16).reshape(-1),
    )
    sizes = [a.shape[0] for a in small]
    small = jnp.concatenate(small)
    small = jnp.pad(small, (0, rows * rank - small.shape[0])).reshape(rows, rank)

    mix_w = gather_columns(
        jnp.concatenate(
            [
                with_gain(w_query, norm_gain).reshape(rows, H, key_dim),
                with_gain(w_key, norm_gain).reshape(rows, H, key_dim),
                with_gain(w_value, norm_gain).reshape(rows, H, value_dim),
                with_gain(w_outgate, norm_gain).reshape(rows, H, value_dim),
                jnp.broadcast_to(with_gain(w_lowrank, norm_gain)[:, None, :], (rows, H, rank)),
                jnp.broadcast_to(small[:, None, :], (rows, H, rank)),
                jnp.zeros((rows, H, -(rank_at + 2 * rank) % LANES), BF16),
            ],
            axis=2,
        )
    )
    output_w = gather_part(w_output)

    small = mix_w[:, rank_at + rank : rank_at + 2 * rank].astype(F32)
    small = small.reshape(reps, CORES * parts, H, rows * rank).transpose(0, 2, 1, 3)
    bias, gain_head, gaterank, long, short = jnp.split(
        small[..., : sum(sizes)], [sum(sizes[:i]) for i in range(1, len(sizes))], axis=3
    )
    gaterank = gaterank.reshape(devices, rank, -1).transpose(1, 0, 2).reshape(rank, -1)
    bias = lax.dynamic_slice_in_dim(bias.reshape(1, -1), here * key_dim, key_dim, 1)
    gaterank = lax.dynamic_slice_in_dim(gaterank, here * key_dim, key_dim, 1)
    gain_head = gain_head.reshape(1, -1)
    lengths = (long * 16.0 + short).reshape(reps, H, CORES, parts, seqs_here, DOCS)
    lengths = lengths[lax.axis_index("rep"), :, lax.axis_index("core"), 0]
    lengths = lengths.reshape(count, DOCS).astype(jnp.int32)

    offset = lax.axis_index("fsdp") * length
    doc_ends = jnp.cumsum(lengths, axis=-1)
    places = offset + jnp.arange(length, dtype=jnp.int32)
    segment = jnp.sum((places[None, :, None] >= doc_ends[:, None, :]).astype(jnp.int32), axis=-1)
    before = jnp.sum((offset - 1 >= doc_ends).astype(jnp.int32), axis=-1)[:, None]
    last = segment[:, -1:]
    marks = jnp.stack(
        [
            segment,
            segment == before,
            segment == last,
            segment != DOCS - 1,
            jnp.broadcast_to(last == before, segment.shape),
        ],
        axis=2,
    )
    marks = jnp.pad(marks.astype(F32).reshape(count * length, 5), ((0, 0), (0, 3)))
    segment = segment.astype(F32).reshape(count, 1, length)

    inputs = tokens.reshape(-1, width).astype(F32)
    scale_one = rms_scale(inputs, EPS)
    normed = share_rows(to_shared((inputs * scale_one).astype(BF16)))
    normed, w_gate_late, w_up_late, w_down_late = after(normed, w_gate, w_up, w_down)
    gate_w = gather_columns(with_gain(w_gate_late, ffn_gain).reshape(rows, H, -1))
    up_w = gather_columns(with_gain(w_up_late, ffn_gain).reshape(rows, H, -1))
    down_w = gather_part(w_down_late)
    mixed = matmul(normed, mix_w)
    sums, pairs = level_sums(length)
    sums, pairs = sums.astype(BF16), pairs.astype(BF16)
    gated, *kept = mix_forward(
        mixed, bias, gaterank, gain_head, marks, segment, sums, pairs, key_dim, value_dim
    )
    cot_rows = cotangent.reshape(-1, width)
    gated, cot_shared = after(gated, share_rows(cot_rows))
    hidden = inputs + sum_rows(matmul(gated, output_w))

    scale_two = rms_scale(hidden, EPS)
    normed_two = share_rows(to_shared((hidden * scale_two).astype(BF16)))
    gate_pre = matmul(normed_two, gate_w)
    up_pre = matmul(normed_two, up_w)
    sig_gate = jax.nn.sigmoid(gate_pre)
    activated = (gate_pre * sig_gate * up_pre).astype(BF16)

    grad_down_w = rows_product(activated, cot_shared).astype(BF16)
    down_w, grad_down_w = after(down_w, grad_down_w)
    grad_act = back_product(cot_shared, down_w)
    grad_up = (grad_act * gate_pre * sig_gate).astype(BF16)
    grad_gate = (grad_act * up_pre * sig_gate * (1.0 + gate_pre * (1.0 - sig_gate))).astype(BF16)
    grad_gate, grad_up, grad_down_w = after(grad_gate, grad_up, pair_part(grad_down_w))
    partial = (back_product(grad_gate, gate_w) + back_product(grad_up, up_w)).astype(BF16)
    grad_gate, grad_up, partial = after(grad_gate, grad_up, partial)
    grad_gate_w = pair_rows(rows_product(normed_two, grad_gate).astype(BF16))
    grad_up_w = pair_rows(rows_product(normed_two, grad_up).astype(BF16))
    down_partial = matmul(activated, down_w).astype(BF16)
    pieces = move_rows(partial)
    pieces, grad_gate_w, down_partial = after(pieces, grad_gate_w, down_partial)
    grad_normed_two = from_shared(jnp.sum(pieces.astype(F32), axis=0))
    grad_down_w = scatter_part(grad_down_w)
    grad_gate_w = scatter_rows(grad_gate_w)
    grad_up_w = scatter_rows(grad_up_w)
    grad_gain_two = jnp.sum(grad_normed_two * hidden * scale_two, axis=0)
    grad_hidden = cot_rows.astype(F32) + rms_back(grad_normed_two, hidden, scale_two)

    branch = share_rows(grad_hidden.astype(BF16))
    branch, down_partial = after(branch, down_partial)
    grad_output_w = pair_part(rows_product(gated, branch).astype(BF16))
    grad_gated = back_product(branch, output_w)
    grad_gated, grad_output_w = after(grad_gated, grad_output_w)
    grad_output_w = scatter_part(grad_output_w)
    pieces = move_rows(down_partial)
    grad_mixed, grad_gain_head, grad_bias, grad_gaterank = mix_backward(
        mixed,
        kept,
        grad_gated,
        gaterank,
        gain_head,
        marks,
        segment,
        sums,
        pairs,
        key_dim,
        value_dim,
    )
    grad_mixed, pieces, grad_down_w, grad_gate_w, grad_output_w = after(
        grad_mixed, pieces, grad_down_w, grad_gate_w, grad_output_w
    )
    output = (hidden + jnp.sum(pieces.astype(F32), axis=0)).astype(BF16).reshape(tokens.shape)
    grad_mix_w = pair_rows(rows_product(normed, grad_mixed).astype(BF16))
    grad_mixed, grad_mix_w = after(grad_mixed, grad_mix_w)
    partial = back_product(grad_mixed, mix_w).astype(BF16)
    grad_mix_w = scatter_rows(grad_mix_w)
    w_gate_grad = to_columns(grad_gate_w)
    w_up_grad = to_columns(grad_up_w)
    pieces = move_rows(partial)
    pieces, w_gate_grad, w_up_grad = after(pieces, w_gate_grad, w_up_grad)
    grad_normed = from_shared(jnp.sum(pieces.astype(F32), axis=0))
    grad_mix_w = to_columns(grad_mix_w)
    grad_gain_one = jnp.sum(grad_normed * inputs * scale_one, axis=0)
    tokens_grad = grad_hidden + rms_back(grad_normed, inputs, scale_one)
    tokens_grad = tokens_grad.astype(BF16).reshape(tokens.shape)

    edges = [key_dim, 2 * key_dim, 2 * key_dim + value_dim, rank_at, rank_at + rank]
    query_g, key_g, value_g, outgate_g, lowrank_g, _ = jnp.split(grad_mix_w, edges, axis=2)
    gain_one = norm_gain.astype(F32)
    gain_two = ffn_gain.astype(F32)

    def scaled(g, gain, w):
        return g.reshape(w.shape) * gain[:, None]

    def place(g, axis):
        shape = list(g.shape)
        shape[axis] *= H
        return lax.dynamic_update_slice_in_dim(jnp.zeros(shape, F32), g, here * key_dim, axis)

    small_grads = jnp.concatenate(
        [
            grad_gain_one.reshape(devices, -1),
            grad_gain_two.reshape(devices, -1),
            place(grad_bias.reshape(-1), 0).reshape(devices, -1),
            grad_gain_head.reshape(devices, -1),
            place(grad_gaterank, 1)
            .reshape(rank, devices, -1)
            .transpose(1, 0, 2)
            .reshape(devices, -1),
        ],
        axis=1,
    )
    small_grads = lax.all_to_all(small_grads, EVERY, split_axis=0, concat_axis=0, tiled=True)
    small_grads = jnp.sum(small_grads, axis=0)
    sizes = [norm_gain.shape[0], ffn_gain.shape[0], gate_bias.shape[0], head_gain.shape[0]]
    norm_g, ffn_g, bias_g, head_g, gaterank_g = jnp.split(
        small_grads, [sum(sizes[: i + 1]) for i in range(len(sizes))]
    )
    return (
        output,
        tokens_grad,
        norm_g / gain_one,
        scaled(query_g, gain_one, w_query),
        scaled(key_g, gain_one, w_key),
        scaled(value_g, gain_one, w_value),
        scaled(outgate_g, gain_one, w_outgate),
        scaled(jnp.sum(lowrank_g, axis=1), gain_one, w_lowrank),
        gaterank_g.reshape(w_gaterank.shape),
        bias_g,
        head_g,
        grad_output_w.astype(F32),
        ffn_g / gain_two,
        scaled(w_gate_grad, gain_two, w_gate),
        scaled(w_up_grad, gain_two, w_up),
        grad_down_w.astype(F32),
    )


def solution(mesh):
    dp, parts = mesh.shape["dp"], mesh.shape["fsdp"]
    fine = Mesh(mesh.devices.reshape(dp // (H * CORES), H, CORES, parts), EVERY)
    seq = ("rep", "head", "core")
    rows, vector = P(EVERY, None), P(EVERY)
    activations = P(seq, "fsdp", None)
    columns = P(None, EVERY)
    return jax.shard_map(
        per_device,
        mesh=fine,
        in_specs=(
            activations,
            P(seq, None),
            vector,
            rows,
            rows,
            rows,
            rows,
            rows,
            columns,
            vector,
            vector,
            rows,
            vector,
            rows,
            rows,
            rows,
            activations,
        ),
        out_specs=(
            activations,
            activations,
            vector,
            rows,
            rows,
            rows,
            rows,
            rows,
            columns,
            vector,
            vector,
            rows,
            vector,
            rows,
            rows,
            rows,
        ),
        check_vma=False,
    )
```

time: 1160 us -> 851 us (0.73)
  waiting for transfers between devices: 483 us -> 207 us
  Pallas kernels: 0 us -> 171 us
  blocking collectives: 214 us -> 78.7 us
  matrix products: 217 us -> 155 us
  local copies, waits for them, and re-layouts: 98.2 us -> 73.5 us
    reduce_scatter x10 -> x5, waiting for transfers between devices: 192 us -> 0.06 us  [the longest x2 0.04 us: scatter_part(): return lax.psum_scatter(g, 'fsdp', scatter_dimension=0, tiled=True)]
    pallas_call x0 -> x2, Pallas kernels: none -> 171 us  [the longest x1 113 us: mix_backward(): pl.pallas_call(functools.partial(backward_kernel, key_dim, value_dim), ou...]
    all_to_all x7 -> x8, waiting for transfers between devices: 168 us -> 80.5 us  [the longest x3 66.4 us: move_rows(): lax.all_to_all(pieces, 'head', split_axis=0, concat_axis=0, tiled=True)]
    all_gather x2 -> x0, blocking collectives: 62.3 us -> none  [the longest x1 49.2 us: per_device(): lengths = lax.all_gather(doc_lengths, 'head', axis=0, tiled=True)]
    dot_general x15 -> x0, matrix products: 54.2 us -> none  [batched(): return jnp.einsum(form, a, b, preferred_element_type=F32)]
    all_to_all x3 -> x4, waiting for transfers between devices: 69.2 us -> 122 us  [share_rows(): lax.all_to_all(spread, 'head', split_axis=0, concat_axis=0, tiled=True)]
    unnamed x1 -> x0, blocking collectives: 43.7 us -> none
    all_gather x2 -> x0, waiting for transfers between devices: 29.8 us -> none  [chain_before(): states = lax.all_gather(state.astype(BF16), 'fsdp')]
  transfers between devices with their start and end apart: 27 -> 27, of which waited for: 17 -> 10; matrix products, arithmetic and copies ran while one was open for 23% -> 31% of each run, Pallas kernels for 0% -> 20%
where the time goes in v2:
time: 851 us; the launch traced here: 840 us
  waiting for transfers between devices  207 us (24%)
  Pallas kernels  171 us (20%)
  matrix products  155 us (18%)
  other arithmetic  84.1 us (10%)
  blocking collectives  78.7 us (9%)
  local copies, waits for them, and re-layouts  73.5 us (9%)
  starting transfers between devices  55.3 us (6%)
  between operations  15.5 us (2%)
    dot_general x15, matrix products, dot(): lax.dot_general(a, b, (dims, ((), ())), precision=precision, preferred_el...  155 us
    all_to_all x4, waiting for transfers between devices, share_rows(): lax.all_to_all(spread, 'head', split_axis=0, concat_axis=0, tiled=True)  122 us
    pallas_call x1, Pallas kernels, mix_backward(): pl.pallas_call(functools.partial(backward_kernel, key_dim, value_dim), ou...  113 us
    all_to_all x3, waiting for transfers between devices, move_rows(): lax.all_to_all(pieces, 'head', split_axis=0, concat_axis=0, tiled=True)  66.4 us
    pallas_call x1, Pallas kernels, mix_forward(): pl.pallas_call(functools.partial(forward_kernel, key_dim, value_dim), out...  57.9 us
    all_to_all x1, blocking collectives, move_rows(): lax.all_to_all(pieces, 'head', split_axis=0, concat_axis=0, tiled=True)  48.1 us
    all_to_all x2, blocking collectives, gather_columns(): lax.all_to_all(w.transpose(1, 0, 2), 'head', split_axis=0, concat_axis=0,...  30.7 us
    all_to_all x4, starting transfers between devices, share_rows(): lax.all_to_all(spread, 'head', split_axis=0, concat_axis=0, tiled=True)  19.7 us
  transfers between devices with their start and end apart: 27, of which 10 were waited for; matrix products, arithmetic and copies ran while one was open for 31% of the time, Pallas kernels for 20%

profile of v2, /device:TPU:0, one launch (start us, length us, event | category | flops | bytes accessed | tf_op | source)
XLA Modules:
  0.0 839.9 jit_solution(13086793518867533716)
XLA Ops:
  15.7 17.3 %all_to_all.79 = bf16[4,64,1664]{2,1,0:T(8,128)(2,1)} all-to-all(bf16[4,64,1664]{2,1,0:T(8,128)(2,1)S(1)} %copy.199), channel_id=1, replica_groups=mesh['rep'=1,'head'=4,'core'=2,'fsdp'=4] {'head'}, dimensions={0} | all-to-all | bytes 1703936 | tf_op jit(solution)/shard_map/all_to_all | solution.py:543
  47.9 45.4 %all-to-all-done = bf16[4,256,2048]{2,1,0:T(8,128)(2,1)} async-done(((bf16[4,256,2048]{2,1,0:T(8,128)(2,1)}), bf16[4,256,2048]{2,1,0:T(8,128)(2,1)}, u32[]{:S(2)}, u32[]{:S(2)}) %all-to-all-start) | async-done | bytes 4194336 | tf_op jit(solution)/shard_map/all_to_all | solution.py:63
  95.0 13.4 %all_to_all.80 = bf16[4,64,1408]{2,1,0:T(8,128)(2,1)} all-to-all(bf16[4,64,1408]{2,1,0:T(8,128)(2,1)S(1)} %copy.210), channel_id=1, replica_groups=mesh['rep'=1,'head'=4,'core'=2,'fsdp'=4] {'head'}, dimensions={0} | all-to-all | bytes 1441792 | tf_op jit(solution)/shard_map/all_to_all | solution.py:543
  135.7 13.4 %fusion.68.mixed_ref = f32[1024,1664]{1,0:T(8,128)} fusion(bf16[1024,2048]{1,0:T(8,128)(2,1)} %bitcast.4, bf16[2048,1664]{1,0:T(8,128)(2,1)} %all-gather.6.cloned.1.call-done), kind=kOutput, calls=%fused_computation.222 | convolution fusion | flops 6979321856 | bytes 17825792 | tf_op jit(solution)/shard_map/dot_general | solution.py:30
  151.1 57.9 %mix_forward.1 = (bf16[1024,512]{1,0:T(8,128)(2,1)}, f32[1024,512]{1,0:T(8,128)}, f32[1024,256]{1,0:T(8,128)}, bf16[4,256,256]{2,1,0:T(8,128)(2,1)S(1)}, bf16[10...) custom-call(f32[1024,1664]{1,0:T(8,128)} %fusion.68.mixed_ref, ...), custom_call_target="tpu_custom_call" | custom-call | flops 49999998976 | bytes 10000000 | tf_op jit(solution)/shard_map/mix_forward/pallas_call | solution.py:435
  214.0 48.1 %all_to_all.81 = bf16[4,256,2048]{2,1,0:T(8,128)(2,1)S(1)} all-to-all(bf16[4,256,2048]{2,1,0:T(8,128)(2,1)S(1)} %bitcast.219), channel_id=1, replica_groups=mesh['rep'=1,'head'=4,'core'=2,'fsdp'=4] {'head'}, dimensions={0} | all-to-all | bytes 8388608 | tf_op jit(solution)/shard_map/all_to_all | solution.py:69
  285.9 41.4 %all-to-all-done.4 = bf16[4,256,2048]{2,1,0:T(8,128)(2,1)} async-done(((bf16[4,256,2048]{2,1,0:T(8,128)(2,1)}), bf16[4,256,2048]{2,1,0:T(8,128)(2,1)}, u32[]{:S(2)}, u32[]{:S(2)}) %all-to-all-start.4) | async-done | bytes 4194336 | tf_op jit(solution)/shard_map/all_to_all | solution.py:63
  327.2 11.8 %fusion.69 = f32[1024,1408]{1,0:T(8,128)} fusion(bf16[1024,2048]{1,0:T(8,128)(2,1)} %bitcast.22, bf16[2048,1408]{1,0:T(8,128)(2,1)} %all-gather.12.cloned.1.call-done), kind=kOutput, calls=%fused_computation.223 | convolution fusion | flops 5905580032 | bytes 15728640 | tf_op jit(solution)/shard_map/dot_general | solution.py:30
  339.0 12.7 %multiply_convert_fusion.2 = (bf16[1024,1408]{1,0:T(8,128)(2,1)S(1)}, f32[1024,1408]{1,0:T(8,128)}) fusion(f32[1024,1408]{1,0:T(8,128)} %fusion.69, bf16[1024,2048]{1,0:T(8,128)(2,1)} %bitcast.22, bf16[2048,1408]{1,0:T(8,128)(2,1)} %all-gather.14.cloned.1.call-done), kind=kOutput, calls=%fused_computation.19 | convolution fusion | flops 5914230784 | bytes 24379392 | tf_op jit(solution)/shard_map/dot_general | solution.py:30
  353.3 10.7 %convolution_convert_fusion.3 = bf16[1408,2048]{1,0:T(8,128)(2,1)} fusion(bf16[1024,1408]{1,0:T(8,128)(2,1)S(1)} %get-tuple-element.239, bf16[1024,2048]{1,0:T(8,128)(2,1)} %bitcast.16), kind=kOutput, calls=%fused_computation.8 | convolution fusion | flops 5908463616 | bytes 12845056 | tf_op jit(solution)/shard_map/dot_general | solution.py:30
  367.9 15.9 %multiply_convert_fusion = (bf16[1024,1408]{1,0:T(8,128)(2,1)}, bf16[1024,1408]{1,0:T(8,128)(2,1)}) fusion(f32[1024,1408]{1,0:T(8,128)} %fusion.69, f32[1024,1408]{1,0:T(8,128)} %get-tuple-element.240, bf16[1024,2048]{1,0:T(8,128)(2,1)} %bitcast.16, bf16[1408,2048]{1,0:T(8,128)(2,1)} %all-gather.10.cloned.1.call-done), kind=kOutput, calls=%fused_computation.17 | convolution fusion | flops 5924323328 | bytes 27262976 | tf_op jit(solution)/shard_map/dot_general | solution.py:30
  386.7 9.7 %fusion.70 = f32[1024,2048]{1,0:T(8,128)S(1)} fusion(bf16[1024,1408]{1,0:T(8,128)(2,1)} %get-tuple-element.92, bf16[2048,1408]{1,0:T(8,128)(2,1)} %all-gather.14.cloned.1.call-done), kind=kOutput, calls=%fused_computation.224 | convolution fusion | flops 5905580032 | bytes 17039360 | tf_op jit(solution)/shard_map/dot_general | solution.py:30
  396.5 11.0 %add_convert_fusion = bf16[1024,2048]{1,0:T(8,128)(2,1)} fusion(f32[1024,2048]{1,0:T(8,128)S(1)} %fusion.70, bf16[1024,1408]{1,0:T(8,128)(2,1)S(1)} %copy-done.39, bf16[2048,1408]{1,0:T(8,128)(2,1)} %all-gather.12.cloned.1.call-done), kind=kOutput, calls=%fused_computation.3 | convolution fusion | flops 5909774336 | bytes 21233664 | tf_op jit(solution)/shard_map/dot_general | solution.py:30
  407.5 9.4 %convolution_convert_fusion.2 = bf16[2048,1408]{1,0:T(8,128)(2,1)S(1)} fusion(bf16[1024,2048]{1,0:T(8,128)(2,1)} %bitcast.22, bf16[1024,1408]{1,0:T(8,128)(2,1)} %get-tuple-element.78), kind=kOutput, calls=%fused_computation.7 | convolution fusion | flops 5908463616 | bytes 12845056 | tf_op jit(solution)/shard_map/dot_general | solution.py:30
  421.6 5.1 all-to-all-start.7
  426.7 11.1 %convolution_convert_fusion.5 = bf16[1024,2048]{1,0:T(8,128)(2,1)} fusion(bf16[1024,1408]{1,0:T(8,128)(2,1)} %copy-done.38, bf16[1408,2048]{1,0:T(8,128)(2,1)} %all-gather.10.cloned.1.call-done), kind=kOutput, calls=%fused_computation.22 | convolution fusion | flops 5907677184 | bytes 12845056 | tf_op jit(solution)/shard_map/dot_general | solution.py:30
  441.9 32.7 %all-to-all-done.7 = bf16[4,256,2048]{2,1,0:T(8,128)(2,1)} async-done(((bf16[4,256,2048]{2,1,0:T(8,128)(2,1)}), bf16[4,256,2048]{2,1,0:T(8,128)(2,1)}, u32[]{:S(2)}, u32[]{:S(2)}) %all-to-all-start.7) | async-done | bytes 4194336 | tf_op jit(solution)/shard_map/all_to_all | solution.py:69
  503.1 11.2 %convolution_convert_fusion = bf16[2048,1408]{1,0:T(8,128)(2,1)} fusion(bf16[1024,2048]{1,0:T(8,128)(2,1)} %bitcast.22, bf16[1024,1408]{1,0:T(8,128)(2,1)} %get-tuple-element.92), kind=kOutput, calls=%fused_computation.5 | convolution fusion | flops 5908463616 | bytes 12845056 | tf_op jit(solution)/shard_map/dot_general | solution.py:30
  514.4 34.9 %all-to-all-done.8 = bf16[4,256,2048]{2,1,0:T(8,128)(2,1)} async-done(((bf16[4,256,2048]{2,1,0:T(8,128)(2,1)}), bf16[4,256,2048]{2,1,0:T(8,128)(2,1)}, u32[]{:S(2)}, u32[]{:S(2)}) %all-to-all-start.8) | async-done | bytes 4194336 | tf_op jit(solution)/shard_map/all_to_all | solution.py:63
  556.5 5.9 fusion.71.upstream_ref
  573.9 113.2 %mix_backward.1 = (bf16[1024,1664]{1,0:T(8,128)(2,1)}, f32[1,512]{1,0:T(1,128)S(1)}, f32[1,256]{1,0:T(1,128)S(1)}, f32[16,256]{1,0:T(8,128)S(1)}) custom-call(f32[1024,1664]{1,0:T(8,128)} %fusion.68.mixed_ref, f32[1024,256]{1,0:T(8,128)} %get-tuple-element.62.logits_ref, bf16[4,256,256]{2,1,0:T(8,128)(2,1)S(1)} %get-tuple-element.63.scores_ref, ...), custom_call_target="tpu_custom_call" | custom-call | flops 80000000000 | bytes 10000000 | tf_op jit(solution)/shard_map/mix_backward/pallas_call | solution.py:460
  687.2 10.7 %convolution_convert_fusion.1 = bf16[2048,1664]{1,0:T(8,128)(2,1)S(1)} fusion(bf16[1024,2048]{1,0:T(8,128)(2,1)} %bitcast.4, bf16[1024,1664]{1,0:T(8,128)(2,1)} %get-tuple-element.90), kind=kOutput, calls=%fused_computation.6 | convolution fusion | flops 6982729728 | bytes 14417920 | tf_op jit(solution)/shard_map/dot_general | solution.py:30
  720.8 12.4 %convolution_convert_fusion.4 = bf16[1024,2048]{1,0:T(8,128)(2,1)} fusion(bf16[1024,1664]{1,0:T(8,128)(2,1)} %get-tuple-element.90, bf16[2048,1664]{1,0:T(8,128)(2,1)} %all-gather.6.cloned.1.call-done), kind=kOutput, calls=%fused_computation.21 | convolution fusion | flops 6981419008 | bytes 14417920 | tf_op jit(solution)/shard_map/dot_general | solution.py:30
  751.9 33.7 %all-to-all-done.10 = bf16[4,256,2048]{2,1,0:T(8,128)(2,1)} async-done(((bf16[4,256,2048]{2,1,0:T(8,128)(2,1)}), bf16[4,256,2048]{2,1,0:T(8,128)(2,1)}, u32[]{:S(2)}, u32[]{:S(2)}) %all-to-all-start.10) | async-done | bytes 4194336 | tf_op jit(solution)/shard_map/all_to_all | solution.py:69
  (310 shorter events, 235.5 us)
Async XLA Ops:
  7.2 125.8 %all-gather.6.cloned.1.call-start = ((), (), s32[]{:S(2)}) async-start(), calls=%async_computation.20 | async-start | bytes 7667712 | tf_op jit(solution)/shard_map/all_gather | solution.py:544
  42.1 51.2 %all-to-all-start = ((bf16[4,256,2048]{2,1,0:T(8,128)(2,1)}), bf16[4,256,2048]{2,1,0:T(8,128)(2,1)}, u32[]{:S(2)}, u32[]{:S(2)}) async-start(bf16[4,256,2048]{2,1,0:T(8,128)(2,1)} %broadcast_in_dim.139), calls=%async_computation | async-start | bytes 8388608 | tf_op jit(solution)/shard_map/all_to_all | solution.py:63
  47.1 162.6 %all-gather.8.cloned.1.call-start = ((), (), s32[]{:S(2)}) async-start(), calls=%async_computation.21 | async-start | bytes 2359296 | tf_op jit(solution)/shard_map/all_gather | solution.py:552
  47.8 238.0 %all-gather.12.cloned.1.call-start = ((), (), s32[]{:S(2)}) async-start(), calls=%async_computation.23 | async-start | bytes 6488064 | tf_op jit(solution)/shard_map/all_gather | solution.py:544
  113.0 12.0 %all-to-all-start.6 = ((bf16[4,64,1408]{2,1,0:T(8,128)(2,1)}), bf16[4,64,1408]{2,1,0:T(8,128)(2,1)S(1)}, u32[]{:S(2)}, u32[]{:S(2)}) async-start(bf16[4,64,1408]{2,1,0:T(8,128)(2,1)} %copy.211), calls=%async_computation.6 | async-start | bytes 1441792 | tf_op jit(solution)/shard_map/all_to_all | solution.py:543
  127.5 82.2 %all-to-all-start.2 = ((bf16[4,256,2048]{2,1,0:T(8,128)(2,1)}), bf16[4,256,2048]{2,1,0:T(8,128)(2,1)}, u32[]{:S(2)}, u32[]{:S(2)}) async-start(bf16[4,256,2048]{2,1,0:T(8,128)(2,1)} %broadcast_in_dim.154), calls=%async_computation.2 | async-start | bytes 8388608 | tf_op jit(solution)/shard_map/all_to_all | solution.py:63
  132.4 206.7 %all-gather.14.cloned.1.call-start = ((), (), s32[]{:S(2)}) async-start(), calls=%async_computation.24 | async-start | bytes 6488064 | tf_op jit(solution)/shard_map/all_gather | solution.py:544
  279.9 47.4 %all-to-all-start.4 = ((bf16[4,256,2048]{2,1,0:T(8,128)(2,1)}), bf16[4,256,2048]{2,1,0:T(8,128)(2,1)}, u32[]{:S(2)}, u32[]{:S(2)}) async-start(bf16[4,256,2048]{2,1,0:T(8,128)(2,1)} %broadcast_in_dim.156), calls=%async_computation.4 | async-start | bytes 8388608 | tf_op jit(solution)/shard_map/all_to_all | solution.py:63
  284.8 79.2 %all-gather.10.cloned.1.call-start = ((), (), s32[]{:S(2)}) async-start(), calls=%async_computation.22 | async-start | bytes 6488064 | tf_op jit(solution)/shard_map/all_gather | solution.py:552
  285.4 401.7 %reduce-scatter.6.cloned.1.call-start = ((), (), s32[]{:S(2)}) async-start(), calls=%async_computation.25 | async-start | bytes 3604480 | tf_op jit(solution)/shard_map/reduce_scatter | solution.py:562
  367.9 15.9 %collective-permute-start = (bf16[704,2048]{1,0:T(8,128)(2,1)}, bf16[704,2048]{1,0:T(8,128)(2,1)S(1)}, u32[]{:S(2)}, u32[]{:S(2)}) collective-permute-start(bf16[704,2048]{1,0:T(8,128)(2,1)} %dynamic-slice_bitcast_fusion.3), channel_id=1, source_target_pairs={{0,4},{4,0},{1,5},{5,1},{2,6},{6,2},{3,7},{7,3},{8,12},{12,8},{9,1... | collective-permute-start | bytes 8650760 | tf_op jit(solution)/shard_map/ppermute | solution.py:531
  421.1 16.7 %collective-permute-start.1 = (bf16[1024,1408]{1,0:T(8,128)(2,1)}, bf16[1024,1408]{1,0:T(8,128)(2,1)}, u32[]{:S(2)}, u32[]{:S(2)}) collective-permute-start(bf16[1024,1408]{1,0:T(8,128)(2,1)} %dynamic-slice_bitcast_fusion.2), channel_id=1, source_target_pairs={{0,4},{4,0},{1,5},{5,1},{2,6},{6,2},{3,7},{7,3},{8,12},{12,8},{9,1... | collective-permute-start | bytes 8650760 | tf_op jit(solution)/shard_map/ppermute | solution.py:531
  421.6 52.9 %all-to-all-start.7 = ((bf16[4,256,2048]{2,1,0:T(8,128)(2,1)}), bf16[4,256,2048]{2,1,0:T(8,128)(2,1)}, u32[]{:S(2)}, u32[]{:S(2)}) async-start(bf16[4,256,2048]{2,1,0:T(8,128)(2,1)} %bitcast.218), calls=%async_computation.7 | async-start | bytes 8388608 | tf_op jit(solution)/shard_map/all_to_all | solution.py:69
  497.4 51.8 %all-to-all-start.8 = ((bf16[4,256,2048]{2,1,0:T(8,128)(2,1)}), bf16[4,256,2048]{2,1,0:T(8,128)(2,1)}, u32[]{:S(2)}, u32[]{:S(2)}) async-start(bf16[4,256,2048]{2,1,0:T(8,128)(2,1)} %broadcast_in_dim.158), calls=%async_computation.8 | async-start | bytes 8388608 | tf_op jit(solution)/shard_map/all_to_all | solution.py:63
  502.3 184.8 %reduce-scatter.8.cloned.1.call-start = ((), (), s32[]{:S(2)}) async-start(), calls=%async_computation.26 | async-start | bytes 3604480 | tf_op jit(solution)/shard_map/reduce_scatter | solution.py:540
  503.1 184.1 %reduce-scatter.10.cloned.1.call-start = ((), (), s32[]{:S(2)}) async-start(), calls=%async_computation.27 | async-start | bytes 1310720 | tf_op jit(solution)/shard_map/reduce_scatter | solution.py:562
  563.8 138.0 %reduce-scatter.12.cloned.1.call-start = ((), (), s32[]{:S(2)}) async-start(), calls=%async_computation.28 | async-start | bytes 3604480 | tf_op jit(solution)/shard_map/reduce_scatter | solution.py:540
  568.9 118.3 %all-to-all-start.9 = ((bf16[4,256,2048]{2,1,0:T(8,128)(2,1)}), bf16[4,256,2048]{2,1,0:T(8,128)(2,1)}, u32[]{:S(2)}, u32[]{:S(2)}) async-start(bf16[4,256,2048]{2,1,0:T(8,128)(2,1)} %bitcast.216), calls=%async_computation.9 | async-start | bytes 8388608 | tf_op jit(solution)/shard_map/all_to_all | solution.py:69
  701.8 15.3 %all-to-all-start.12 = ((bf16[4,64,1408]{2,1,0:T(8,128)(2,1)}), bf16[4,64,1408]{2,1,0:T(8,128)(2,1)}, u32[]{:S(2)}, u32[]{:S(2)}) async-start(bf16[4,64,1408]{2,1,0:T(8,128)(2,1)} %bitcast.238), calls=%async_computation.16 | async-start | bytes 1441792 | tf_op jit(solution)/shard_map/all_to_all | solution.py:547
  705.9 106.7 %reduce-scatter.14.cloned.1.call-start = ((), (), s32[]{:S(2)}) async-start(), calls=%async_computation.29 | async-start | bytes 4259840 | tf_op jit(solution)/shard_map/reduce_scatter | solution.py:540
  717.1 16.1 %all-to-all-start.11 = ((bf16[4,64,1408]{2,1,0:T(8,128)(2,1)}), bf16[4,64,1408]{2,1,0:T(8,128)(2,1)S(1)}, u32[]{:S(2)}, u32[]{:S(2)}) async-start(bf16[4,64,1408]{2,1,0:T(8,128)(2,1)} %bitcast.48), calls=%async_computation.14 | async-start | bytes 1441792 | tf_op jit(solution)/shard_map/all_to_all | solution.py:547
  733.1 52.4 %all-to-all-start.10 = ((bf16[4,256,2048]{2,1,0:T(8,128)(2,1)}), bf16[4,256,2048]{2,1,0:T(8,128)(2,1)}, u32[]{:S(2)}, u32[]{:S(2)}) async-start(bf16[4,256,2048]{2,1,0:T(8,128)(2,1)} %bitcast.217), calls=%async_computation.13 | async-start | bytes 8388608 | tf_op jit(solution)/shard_map/all_to_all | solution.py:69
  801.4 11.2 %all-to-all-start.13 = ((f32[32,1,688]{2,1,0:T(1,128)}), f32[32,1,688]{2,1,0:T(1,128)}, u32[]{:S(2)}, u32[]{:S(2)}) async-start(f32[32,1,688]{2,1,0:T(1,128)} %copy.219), calls=%async_computation.17 | async-start | bytes 196608 | tf_op jit(solution)/shard_map/all_to_all | solution.py:737
  812.6 15.7 %all-to-all-start.14 = ((bf16[4,64,1664]{2,1,0:T(8,128)(2,1)}), bf16[4,64,1664]{2,1,0:T(8,128)(2,1)}, u32[]{:S(2)}, u32[]{:S(2)}) async-start(bf16[4,64,1664]{2,1,0:T(8,128)(2,1)} %bitcast.237), calls=%async_computation.19 | async-start | bytes 1703936 | tf_op jit(solution)/shard_map/all_to_all | solution.py:547
  (45 other events, 485.5 us)
Sparse Core Ops, SparseCore 0:
  33.1 68.6 all-gather.5
  103.4 27.5 all-gather.7
  132.6 77.1 all-gather.11
  211.8 62.1 all-gather.13
  286.9 76.0 all-gather.9
  407.6 72.2 reduce-scatter.5
  505.4 73.4 reduce-scatter.7
  581.8 30.9 reduce-scatter.9
  615.1 71.3 reduce-scatter.11
  712.8 62.4 reduce-scatter.13

commit v3 on v2

--- a/solution.py
+++ b/solution.py
@@ -15,6 +15,7 @@
 DOCS = 8
 PIECES = 2
 LANES = 128
+CHUNKS = 8
 
 EPS = 1e-05
 HEAD_EPS = 1.0
@@ -133,11 +134,19 @@
         def _(copy=copy):
             copy.wait_recv()
 
-        @pl.when(jnp.logical_not(last))
+        @pl.when(jnp.logical_not(jnp.logical_or(first, last)))
         def _(copy=copy, part=part):
             joined = decay * recv[s, part].astype(F32) + local[s, part]
             send[s, part] = joined.astype(BF16)
             copy.start()
+
+
+def start_state(s, first, last, target, local, send, recv, send_sem, recv_sem):
+    @pl.when(jnp.logical_and(first, jnp.logical_not(last)))
+    def _():
+        send[s] = local[s].astype(BF16)
+        for piece in range(PIECES):
+            state_copy(send, recv, send_sem, recv_sem, s, piece, target).start()
 
 
 def finish_states(count, last, target, send, recv, send_sem, recv_sem):
@@ -222,6 +231,7 @@
         end_ref[rows, :] = end_key
         value = mixed_ref[rows, pl.ds(value_at, value_dim)].astype(BF16)
         local_ref[s] = rows_product(value, end_key)
+        start_state(s, first, last, target, local_ref, send_ref, recv_ref, send_sem, recv_sem)
         return carry
 
     lax.fori_loop(0, count, ends, 0)
@@ -329,6 +339,7 @@
         grad_out = grad_out.astype(BF16)
         out_ref[rows, :] = grad_out
         local_ref[s] = rows_product(grad_out, start_ref[rows, :])
+        start_state(s, first, last, target, local_ref, send_ref, recv_ref, send_sem, recv_sem)
         return carry
 
     lax.fori_loop(0, count, heads, 0)
@@ -412,10 +423,486 @@
     ]
 
 
-def kernel_params(number):
+def kernel_params(number, mebibytes=44):
     return pltpu.CompilerParams(
-        collective_id=number, has_side_effects=True, vmem_limit_bytes=52 * 2**20
-    )
+        collective_id=number, has_side_effects=True, vmem_limit_bytes=mebibytes * 2**20
+    )
+
+
+def head_copy(src, dst, send_sem, recv_sem, target):
+    return pltpu.make_async_remote_copy(
+        src_ref=src,
+        dst_ref=dst,
+        send_sem=send_sem,
+        recv_sem=recv_sem,
+        device_id={"head": target},
+        device_id_type=pl.DeviceIdType.MESH,
+    )
+
+
+def greet_heads(targets):
+    barrier = pltpu.get_barrier_semaphore()
+    for target in targets:
+        pl.semaphore_signal(
+            barrier, inc=1, device_id={"head": target}, device_id_type=pl.DeviceIdType.MESH
+        )
+    pl.semaphore_wait(barrier, len(targets))
+
+
+def square(me):
+    return me + 1 - 2 * lax.rem(me, 2), me + 2 - 4 * (me // 2), H - 1 - me
+
+
+def move_columns(weights, gain, out_ref, send_ref, send_sem, recv_sem, own_sem):
+    me = lax.axis_index("head")
+    place = 0
+    for w in weights:
+        n = w.shape[1] // H
+        for h in range(H):
+            part = w[:, pl.ds(h * n, n)].astype(F32) * gain
+            send_ref[h, :, pl.ds(place, n)] = part.astype(BF16)
+        place += n
+    copies = []
+    for ahead in range(1, H):
+        peer = lax.rem(me + ahead, H)
+        copy = head_copy(
+            send_ref.at[peer],
+            out_ref.at[me],
+            send_sem.at[ahead],
+            recv_sem.at[ahead],
+            peer,
+        )
+        copy.start()
+        copies.append(copy)
+    own = pltpu.make_async_copy(send_ref.at[me], out_ref.at[me], own_sem)
+    own.start()
+    return copies + [own]
+
+
+def mix_weights_kernel(*refs):
+    *weights, extra_ref, gain_ref, out_ref, send_ref, send_sem, recv_sem, own_sem = refs
+    me = lax.axis_index("head")
+    greet_heads([lax.rem(me + ahead, H) for ahead in range(1, H)])
+    spare = extra_ref.shape[1]
+    for h in range(H):
+        send_ref[h, :, pl.ds(send_ref.shape[2] - spare, spare)] = extra_ref[...]
+    gain = gain_ref[...].astype(F32)
+    for copy in move_columns(weights, gain, out_ref, send_ref, send_sem, recv_sem, own_sem):
+        copy.wait()
+
+
+def mix_weights(weights, extra, gain):
+    rows = extra.shape[0]
+    n = sum(w.shape[1] for w in weights) // H + extra.shape[1]
+    return pl.pallas_call(
+        mix_weights_kernel,
+        out_shape=jax.ShapeDtypeStruct((H, rows, n), BF16),
+        in_specs=[pl.BlockSpec(memory_space=pltpu.VMEM)] * (len(weights) + 2),
+        out_specs=pl.BlockSpec(memory_space=pl.ANY),
+        scratch_shapes=[
+            pltpu.VMEM((H, rows, n), BF16),
+            pltpu.SemaphoreType.DMA((H,)),
+            pltpu.SemaphoreType.DMA((H,)),
+            pltpu.SemaphoreType.DMA,
+        ],
+        compiler_params=kernel_params(3, 16),
+        cost_estimate=pl.CostEstimate(flops=10**10, bytes_accessed=10**6, transcendentals=0),
+        name="mix_weights",
+    )(*weights, extra, gain)
+
+
+class Share:
+    def __init__(self, mine_ref, out_ref, send_sem, recv_sem, own_sem):
+        self.refs = mine_ref, out_ref, send_sem, recv_sem, own_sem
+        self.me = lax.axis_index("head")
+        self.size = mine_ref.shape[0] // CHUNKS
+
+    def copy(self, c, kind):
+        mine, out, send_sem, recv_sem, _ = self.refs
+        sides = square(self.me)[:2]
+        rows = pl.ds(c * self.size, self.size)
+        if kind < 2:
+            src, dst, target = mine.at[rows], out.at[self.me, rows], sides[kind]
+        else:
+            origin, target = (sides[0], sides[1]) if c % 2 == 0 else (sides[1], sides[0])
+            src = dst = out.at[origin, rows]
+        return head_copy(src, dst, send_sem.at[c, kind], recv_sem.at[c, kind], target)
+
+    def own(self, c):
+        mine, out, _, _, own_sem = self.refs
+        rows = pl.ds(c * self.size, self.size)
+        return pltpu.make_async_copy(mine.at[rows], out.at[self.me, rows], own_sem.at[c])
+
+    def start(self, c):
+        self.copy(c, 0).start()
+        self.copy(c, 1).start()
+        self.own(c).start()
+
+    def forward(self, c):
+        self.copy(c, c % 2).wait_recv()
+        self.copy(c, 2).start()
+
+    def finish(self):
+        for c in range(CHUNKS):
+            self.copy(c, 1 - c % 2).wait_recv()
+            self.copy(c, 2).wait_recv()
+            self.own(c).wait()
+            for kind in range(3):
+                self.copy(c, kind).wait_send()
+
+
+def share_scratch(rows, width):
+    return [
+        pltpu.VMEM((rows, width), BF16),
+        pltpu.SemaphoreType.DMA((CHUNKS, 3)),
+        pltpu.SemaphoreType.DMA((CHUNKS, 3)),
+        pltpu.SemaphoreType.DMA((CHUNKS,)),
+    ]
+
+
+def share_kernel(
+    tokens_ref,
+    gate_ref,
+    up_ref,
+    gain_ref,
+    out_ref,
+    moved_ref,
+    mine_ref,
+    share_send,
+    share_recv,
+    share_own,
+    send_ref,
+    send_sem,
+    recv_sem,
+    own_sem,
+):
+    me = lax.axis_index("head")
+    greet_heads([lax.rem(me + ahead, H) for ahead in range(1, H)])
+    share = Share(mine_ref, out_ref, share_send, share_recv, share_own)
+    for c in range(CHUNKS):
+        rows = pl.ds(c * share.size, share.size)
+        x = tokens_ref[rows, :].astype(F32)
+        mine_ref[rows, :] = (x * rms_scale(x, EPS)).astype(BF16)
+        share.start(c)
+    gain = gain_ref[...].astype(F32)
+    copies = move_columns(
+        [gate_ref, up_ref], gain, moved_ref, send_ref, send_sem, recv_sem, own_sem
+    )
+    for c in range(CHUNKS):
+        share.forward(c)
+    share.finish()
+    for copy in copies:
+        copy.wait()
+
+
+def share_tokens(tokens, w_gate, w_up, gain):
+    rows, n = w_gate.shape[0], 2 * w_gate.shape[1] // H
+    return pl.pallas_call(
+        share_kernel,
+        out_shape=[
+            jax.ShapeDtypeStruct((H,) + tokens.shape, BF16),
+            jax.ShapeDtypeStruct((H, rows, n), BF16),
+        ],
+        in_specs=[pl.BlockSpec(memory_space=pltpu.VMEM)] * 4,
+        out_specs=[pl.BlockSpec(memory_space=pl.ANY)] * 2,
+        scratch_shapes=share_scratch(*tokens.shape)
+        + [
+            pltpu.VMEM((H, rows, n), BF16),
+            pltpu.SemaphoreType.DMA((H,)),
+            pltpu.SemaphoreType.DMA((H,)),
+            pltpu.SemaphoreType.DMA,
+        ],
+        compiler_params=kernel_params(4, 16),
+        cost_estimate=pl.CostEstimate(flops=5 * 10**10, bytes_accessed=10**6, transcendentals=0),
+        name="share_tokens",
+    )(tokens, w_gate, w_up, gain)
+
+
+def turn_rows(
+    partial_ref,
+    first_ref,
+    relay_ref,
+    second_ref,
+    pass_ref,
+    send_sem,
+    recv_sem,
+    done,
+    share=None,
+    fillers=(),
+):
+    me = lax.axis_index("head")
+    side = square(me)
+    far = side[2]
+    size = first_ref.shape[0] // CHUNKS
+    steps = CHUNKS + 3
+    fillers = list(fillers)
+
+    def copies(c):
+        one, two = (side[0], side[1]) if c % 2 == 0 else (side[1], side[0])
+        rows = pl.ds(c * size, size)
+        sems = [(send_sem.at[c, kind], recv_sem.at[c, kind]) for kind in range(3)]
+        return (
+            head_copy(partial_ref.at[far, rows], relay_ref.at[rows], *sems[0], one),
+            head_copy(partial_ref.at[one, rows], first_ref.at[rows], *sems[1], one),
+            head_copy(pass_ref.at[rows], second_ref.at[rows], *sems[2], two),
+            two,
+            rows,
+        )
+
+    for c in range(CHUNKS):
+        relay, first, *_ = copies(c)
+        relay.start()
+        first.start()
+    for step in range(steps):
+        for filler in fillers[step * len(fillers) // steps : (step + 1) * len(fillers) // steps]:
+            filler()
+        if step < CHUNKS:
+            relay, _, second, two, rows = copies(step)
+            relay.wait_recv()
+            both = partial_ref[two, rows, :].astype(F32) + relay_ref[rows, :].astype(F32)
+            pass_ref[rows, :] = both.astype(BF16)
+            second.start()
+        if 1 <= step <= CHUNKS:
+            _, first, second, _, rows = copies(step - 1)
+            first.wait_recv()
+            second.wait_recv()
+            total = partial_ref[me, rows, :].astype(F32) + first_ref[rows, :].astype(F32)
+            made = done(rows, total + second_ref[rows, :].astype(F32))
+            if share is not None:
+                share.refs[0][rows, :] = made
+                share.start(step - 1)
+        if step >= 3 and share is not None:
+            share.forward(step - 3)
+    if share is not None:
+        share.finish()
+    for c in range(CHUNKS):
+        for copy in copies(c)[:3]:
+            copy.wait_send()
+
+
+def turn_scratch(rows, width):
+    return [pltpu.VMEM((rows, width), BF16) for _ in range(4)] + [
+        pltpu.SemaphoreType.DMA((CHUNKS, 3)),
+        pltpu.SemaphoreType.DMA((CHUNKS, 3)),
+    ]
+
+
+def hidden_kernel(partial_ref, tokens_ref, hidden_ref, out_ref, *scratch):
+    greet_heads(square(lax.axis_index("head"))[:2])
+    mine_ref, *sems = scratch[6:]
+
+    def done(rows, total):
+        hidden = tokens_ref[rows, :].astype(F32) + total
+        hidden_ref[rows, :] = hidden
+        return (hidden * rms_scale(hidden, EPS)).astype(BF16)
+
+    turn_rows(partial_ref, *scratch[:6], done, Share(mine_ref, out_ref, *sems))
+
+
+def share_hidden(partial, tokens):
+    whole = pl.BlockSpec(memory_space=pltpu.VMEM)
+    return pl.pallas_call(
+        hidden_kernel,
+        out_shape=[
+            jax.ShapeDtypeStruct(tokens.shape, F32),
+            jax.ShapeDtypeStruct((H,) + tokens.shape, BF16),
+        ],
+        in_specs=[whole] * 2,
+        out_specs=[whole, pl.BlockSpec(memory_space=pl.ANY)],
+        scratch_shapes=turn_scratch(*tokens.shape) + share_scratch(*tokens.shape),
+        compiler_params=kernel_params(5, 24),
+        cost_estimate=pl.CostEstimate(flops=8 * 10**10, bytes_accessed=10**7, transcendentals=0),
+        name="share_hidden",
+    )(partial, tokens)
+
+
+class PairProduct:
+    def __init__(self, left_ref, right_ref, out_ref, give_ref, take_ref, send_sem, recv_sem):
+        self.refs = left_ref, right_ref, out_ref, give_ref, take_ref, send_sem, recv_sem
+        self.core = lax.axis_index("core")
+        self.groups, self.rows, width = out_ref.shape
+        self.cut = width // 2 if width % (2 * LANES) == 0 else width
+
+    def product(self, group, core, at):
+        left, right, *_ = self.refs
+        start = pl.multiple_of((group * CORES + core) * self.rows, LANES)
+        return rows_product(left[:, pl.ds(start, self.rows)], right[:, pl.ds(at, self.cut)])
+
+    def copy(self, group):
+        _, _, _, give, take, send_sem, recv_sem = self.refs
+        return pltpu.make_async_remote_copy(
+            src_ref=give.at[group],
+            dst_ref=take.at[group],
+            send_sem=send_sem.at[group],
+            recv_sem=recv_sem.at[group],
+            device_id={"core": 1 - self.core},
+            device_id_type=pl.DeviceIdType.MESH,
+        )
+
+    def give(self, group, at):
+        out, give = self.refs[2:4]
+        give[group, :, pl.ds(at, self.cut)] = self.product(group, 1 - self.core, at).astype(BF16)
+        if at + self.cut == out.shape[2]:
+            self.copy(group).start()
+
+    def keep(self, group, at):
+        out, _, take = self.refs[2:5]
+        if at == 0:
+            self.copy(group).wait_recv()
+        both = self.product(group, self.core, at)
+        both += take[group, :, pl.ds(at, self.cut)].astype(F32)
+        out[group, :, pl.ds(at, self.cut)] = both.astype(BF16)
+
+    def steps(self):
+        places = [
+            (group, at)
+            for group in range(self.groups)
+            for at in range(0, self.refs[2].shape[2], self.cut)
+        ]
+        return [functools.partial(self.give, *place) for place in places] + [
+            functools.partial(self.keep, *place) for place in places
+        ]
+
+    def finish(self):
+        for group in range(self.groups):
+            self.copy(group).wait_send()
+
+
+def pair_shape(left, right, groups):
+    return (groups, left.shape[1] // (CORES * groups), right.shape[1])
+
+
+def pair_scratch(shape):
+    return [
+        pltpu.VMEM(shape, BF16),
+        pltpu.VMEM(shape, BF16),
+        pltpu.SemaphoreType.DMA((shape[0],)),
+        pltpu.SemaphoreType.DMA((shape[0],)),
+    ]
+
+
+def greet_square_and_core():
+    barrier = pltpu.get_barrier_semaphore()
+    for side in square(lax.axis_index("head"))[:2]:
+        pl.semaphore_signal(
+            barrier, inc=1, device_id={"head": side}, device_id_type=pl.DeviceIdType.MESH
+        )
+    other = 1 - lax.axis_index("core")
+    pl.semaphore_signal(
+        barrier, inc=1, device_id={"core": other}, device_id_type=pl.DeviceIdType.MESH
+    )
+    pl.semaphore_wait(barrier, 3)
+
+
+def pair_kernel(left_ref, right_ref, out_ref, *scratch):
+    barrier = pltpu.get_barrier_semaphore()
+    other = 1 - lax.axis_index("core")
+    pl.semaphore_signal(
+        barrier, inc=1, device_id={"core": other}, device_id_type=pl.DeviceIdType.MESH
+    )
+    pl.semaphore_wait(barrier, 1)
+    pair = PairProduct(left_ref, right_ref, out_ref, *scratch)
+    for step in pair.steps():
+        step()
+    pair.finish()
+
+
+def pair_product(left, right, groups):
+    shape = pair_shape(left, right, groups)
+    whole = pl.BlockSpec(memory_space=pltpu.VMEM)
+    return pl.pallas_call(
+        pair_kernel,
+        out_shape=jax.ShapeDtypeStruct(shape, BF16),
+        in_specs=[whole] * 2,
+        out_specs=whole,
+        scratch_shapes=pair_scratch(shape),
+        compiler_params=kernel_params(7, 32),
+        cost_estimate=pl.CostEstimate(flops=10**10, bytes_accessed=10**7, transcendentals=0),
+        name="pair_product",
+    )(left, right)
+
+
+def branch_kernel(
+    partial_ref,
+    hidden_ref,
+    upstream_ref,
+    left_ref,
+    right_ref,
+    grad_ref,
+    gain_grad_ref,
+    pair_ref,
+    out_ref,
+    *scratch,
+):
+    greet_square_and_core()
+    mine_ref, *sems = scratch[6:10]
+    gain_grad_ref[...] = jnp.zeros_like(gain_grad_ref)
+    pair = PairProduct(left_ref, right_ref, pair_ref, *scratch[10:])
+
+    def done(rows, total):
+        hidden = hidden_ref[rows, :]
+        scale = rms_scale(hidden, EPS)
+        gain_grad_ref[...] += jnp.sum(total * hidden * scale, axis=0, keepdims=True)
+        grad = upstream_ref[rows, :].astype(F32) + rms_back(total, hidden, scale)
+        grad_ref[rows, :] = grad
+        return grad.astype(BF16)
+
+    share = Share(mine_ref, out_ref, *sems)
+    turn_rows(partial_ref, *scratch[:6], done, share, pair.steps())
+    pair.finish()
+
+
+def share_branch(partial, hidden, upstream, left, right, groups):
+    whole = pl.BlockSpec(memory_space=pltpu.VMEM)
+    shape = pair_shape(left, right, groups)
+    return pl.pallas_call(
+        branch_kernel,
+        out_shape=[
+            jax.ShapeDtypeStruct(hidden.shape, F32),
+            jax.ShapeDtypeStruct((1, hidden.shape[1]), F32),
+            jax.ShapeDtypeStruct(shape, BF16),
+            jax.ShapeDtypeStruct((H,) + hidden.shape, BF16),
+        ],
+        in_specs=[whole] * 5,
+        out_specs=[whole] * 3 + [pl.BlockSpec(memory_space=pl.ANY)],
+        scratch_shapes=turn_scratch(*hidden.shape)
+        + share_scratch(*hidden.shape)
+        + pair_scratch(shape),
+        compiler_params=kernel_params(6, 54),
+        cost_estimate=pl.CostEstimate(flops=8 * 10**10, bytes_accessed=10**7, transcendentals=0),
+        name="share_branch",
+    )(partial, hidden, upstream, left, right)
+
+
+def tokens_kernel(partial_ref, tokens_ref, upstream_ref, grad_ref, gain_grad_ref, *scratch):
+    greet_heads(square(lax.axis_index("head"))[:2])
+    gain_grad_ref[...] = jnp.zeros_like(gain_grad_ref)
+
+    def done(rows, total):
+        tokens = tokens_ref[rows, :].astype(F32)
+        scale = rms_scale(tokens, EPS)
+        gain_grad_ref[...] += jnp.sum(total * tokens * scale, axis=0, keepdims=True)
+        grad = upstream_ref[rows, :] + rms_back(total, tokens, scale)
+        grad_ref[rows, :] = grad.astype(BF16)
+
+    turn_rows(partial_ref, *scratch, done)
+
+
+def tokens_back(partial, tokens, upstream):
+    whole = pl.BlockSpec(memory_space=pltpu.VMEM)
+    return pl.pallas_call(
+        tokens_kernel,
+        out_shape=[
+            jax.ShapeDtypeStruct(tokens.shape, BF16),
+            jax.ShapeDtypeStruct((1, tokens.shape[1]), F32),
+        ],
+        in_specs=[whole] * 3,
+        out_specs=[whole] * 2,
+        scratch_shapes=turn_scratch(*tokens.shape),
+        compiler_params=kernel_params(8, 24),
+        cost_estimate=pl.CostEstimate(flops=4 * 10**10, bytes_accessed=10**7, transcendentals=0),
+        name="tokens_back",
+    )(partial, tokens, upstream)
 
 
 def mix_forward(mixed, bias, gaterank, gain, marks, segment, sums, pairs, key_dim, value_dim):
@@ -517,34 +1004,25 @@
 
     rank_at = 2 * key_dim + 2 * value_dim
 
-    def to_shared(a):
-        shaped = a.reshape(a.shape[0], reps, H, CORES * parts, rows)
-        return shaped.transpose(0, 1, 3, 2, 4).reshape(a.shape)
-
-    def from_shared(a):
-        shaped = a.reshape(a.shape[0], reps, CORES * parts, H, rows)
-        return shaped.transpose(0, 1, 3, 2, 4).reshape(a.shape)
-
     def core_sum(g):
-        halves = g.reshape(CORES, -1, g.shape[-1])
+        halves = g.reshape(g.shape[0], CORES, -1, g.shape[-1])
         core = lax.axis_index("core")
-        other = lax.ppermute(halves[1 - core], "core", ((0, 1), (1, 0)))
-        return (halves[core].astype(F32) + other.astype(F32)).astype(BF16)
-
-    def pair_rows(g):
+        other = lax.ppermute(halves[:, 1 - core], "core", ((0, 1), (1, 0)))
+        return (halves[:, core].astype(F32) + other.astype(F32)).astype(BF16)
+
+    def scatter_rows(g):
         if reps > 1:
             g = lax.psum_scatter(g, "rep", scatter_dimension=0, tiled=True)
-        return core_sum(g)
-
-    def scatter_rows(g):
-        return lax.psum_scatter(g, "fsdp", scatter_dimension=0, tiled=True)
-
-    def gather_columns(w):
-        moved = lax.all_to_all(w.transpose(1, 0, 2), "head", split_axis=0, concat_axis=0, tiled=True)
-        return lax.all_gather(moved.reshape(-1, w.shape[2]), SHARE, axis=0, tiled=True)
+        return lax.psum_scatter(g, "fsdp", scatter_dimension=1, tiled=True)
+
+    def gather_columns(moved):
+        whole = lax.all_gather(moved, ("core", "fsdp"), axis=1, tiled=True)
+        if reps > 1:
+            whole = lax.all_gather(whole, "rep", axis=0, tiled=False)
+        return whole.reshape(width, -1)
 
     def to_columns(g):
-        moved = lax.all_to_all(g.reshape(H, rows, -1), "head", split_axis=0, concat_axis=0, tiled=True)
+        moved = lax.all_to_all(g, "head", split_axis=0, concat_axis=0, tiled=True)
         return moved.transpose(1, 0, 2).astype(F32)
 
     def gather_part(w):
@@ -555,7 +1033,7 @@
         return lax.dynamic_slice_in_dim(whole, here * size, size, 0)
 
     def pair_part(g):
-        return core_sum(g) if reps == 1 else g
+        return core_sum(g[None])[0] if reps == 1 else g
 
     def scatter_part(g):
         if reps == 1:
@@ -564,42 +1042,42 @@
         whole = lax.dynamic_update_slice_in_dim(whole, g, here * g.shape[0], 0)
         return lax.psum_scatter(whole, EVERY, scatter_dimension=0, tiled=True)
 
+    rank_at = 2 * key_dim + 2 * value_dim
+
     def with_gain(w, gain):
         return (w.astype(F32) * gain.astype(F32)[:, None]).astype(BF16)
 
     small = (
-        gate_bias,
-        head_gain,
-        w_gaterank.reshape(-1),
-        (doc_lengths // 16).astype(BF16).reshape(-1),
-        (doc_lengths % 16).astype(BF16).reshape(-1),
-    )
-    sizes = [a.shape[0] for a in small]
-    small = jnp.concatenate(small)
-    small = jnp.pad(small, (0, rows * rank - small.shape[0])).reshape(rows, rank)
-
-    mix_w = gather_columns(
-        jnp.concatenate(
-            [
-                with_gain(w_query, norm_gain).reshape(rows, H, key_dim),
-                with_gain(w_key, norm_gain).reshape(rows, H, key_dim),
-                with_gain(w_value, norm_gain).reshape(rows, H, value_dim),
-                with_gain(w_outgate, norm_gain).reshape(rows, H, value_dim),
-                jnp.broadcast_to(with_gain(w_lowrank, norm_gain)[:, None, :], (rows, H, rank)),
-                jnp.broadcast_to(small[:, None, :], (rows, H, rank)),
-                jnp.zeros((rows, H, -(rank_at + 2 * rank) % LANES), BF16),
-            ],
-            axis=2,
-        )
-    )
+        w_gaterank,
+        gate_bias.reshape(1, -1),
+        head_gain.reshape(1, -1),
+        (doc_lengths // 16).astype(BF16).reshape(1, -1),
+        (doc_lengths % 16).astype(BF16).reshape(1, -1),
+    )
+    edges = [rank]
+    extra = jnp.pad(with_gain(w_lowrank, norm_gain), ((0, 0), (0, LANES - rank)))
+    for piece in small:
+        high, wide = piece.shape
+        extra += jnp.pad(piece, ((0, rows - high), (edges[-1], LANES - edges[-1] - wide)))
+        edges.append(edges[-1] + wide)
+
+    mix_moved = mix_weights((w_query, w_key, w_value, w_outgate), extra, norm_gain[:, None])
+    inputs = tokens.reshape(-1, width)
+    inputs, _ = after(inputs, mix_moved)
     output_w = gather_part(w_output)
-
-    small = mix_w[:, rank_at + rank : rank_at + 2 * rank].astype(F32)
-    small = small.reshape(reps, CORES * parts, H, rows * rank).transpose(0, 2, 1, 3)
-    bias, gain_head, gaterank, long, short = jnp.split(
-        small[..., : sum(sizes)], [sum(sizes[:i]) for i in range(1, len(sizes))], axis=3
-    )
-    gaterank = gaterank.reshape(devices, rank, -1).transpose(1, 0, 2).reshape(rank, -1)
+    mix_moved, output_w = after(mix_moved, output_w)
+    mix_w = gather_columns(mix_moved)
+    normed, ffn_moved = share_tokens(inputs, w_gate, w_up, ffn_gain[:, None])
+    normed = normed.reshape(-1, width)
+    ffn_w = gather_columns(ffn_moved)
+    normed, w_down = after(normed, w_down)
+    down_w = gather_part(w_down)
+
+    small = mix_w[:, rank_at:].astype(F32).reshape(devices, rows, LANES)
+    gaterank, bias, gain_head, long, short = (
+        small[:, : rank if i == 0 else 1, edges[i] : edges[i + 1]] for i in range(len(edges) - 1)
+    )
+    gaterank = gaterank.transpose(1, 0, 2).reshape(rank, -1)
     bias = lax.dynamic_slice_in_dim(bias.reshape(1, -1), here * key_dim, key_dim, 1)
     gaterank = lax.dynamic_slice_in_dim(gaterank, here * key_dim, key_dim, 1)
     gain_head = gain_head.reshape(1, -1)
@@ -626,13 +1104,6 @@
     marks = jnp.pad(marks.astype(F32).reshape(count * length, 5), ((0, 0), (0, 3)))
     segment = segment.astype(F32).reshape(count, 1, length)
 
-    inputs = tokens.reshape(-1, width).astype(F32)
-    scale_one = rms_scale(inputs, EPS)
-    normed = share_rows(to_shared((inputs * scale_one).astype(BF16)))
-    normed, w_gate_late, w_up_late, w_down_late = after(normed, w_gate, w_up, w_down)
-    gate_w = gather_columns(with_gain(w_gate_late, ffn_gain).reshape(rows, H, -1))
-    up_w = gather_columns(with_gain(w_up_late, ffn_gain).reshape(rows, H, -1))
-    down_w = gather_part(w_down_late)
     mixed = matmul(normed, mix_w)
     sums, pairs = level_sums(length)
     sums, pairs = sums.astype(BF16), pairs.astype(BF16)
@@ -641,40 +1112,33 @@
     )
     cot_rows = cotangent.reshape(-1, width)
     gated, cot_shared = after(gated, share_rows(cot_rows))
-    hidden = inputs + sum_rows(matmul(gated, output_w))
-
-    scale_two = rms_scale(hidden, EPS)
-    normed_two = share_rows(to_shared((hidden * scale_two).astype(BF16)))
-    gate_pre = matmul(normed_two, gate_w)
-    up_pre = matmul(normed_two, up_w)
+    partial = matmul(gated, output_w).astype(BF16).reshape(H, -1, width)
+    hidden, normed_two = share_hidden(partial, inputs)
+    normed_two = normed_two.reshape(-1, width)
+
+    gate_pre, up_pre = jnp.split(matmul(normed_two, ffn_w), 2, axis=1)
     sig_gate = jax.nn.sigmoid(gate_pre)
     activated = (gate_pre * sig_gate * up_pre).astype(BF16)
 
     grad_down_w = rows_product(activated, cot_shared).astype(BF16)
     down_w, grad_down_w = after(down_w, grad_down_w)
     grad_act = back_product(cot_shared, down_w)
-    grad_up = (grad_act * gate_pre * sig_gate).astype(BF16)
-    grad_gate = (grad_act * up_pre * sig_gate * (1.0 + gate_pre * (1.0 - sig_gate))).astype(BF16)
-    grad_gate, grad_up, grad_down_w = after(grad_gate, grad_up, pair_part(grad_down_w))
-    partial = (back_product(grad_gate, gate_w) + back_product(grad_up, up_w)).astype(BF16)
-    grad_gate, grad_up, partial = after(grad_gate, grad_up, partial)
-    grad_gate_w = pair_rows(rows_product(normed_two, grad_gate).astype(BF16))
-    grad_up_w = pair_rows(rows_product(normed_two, grad_up).astype(BF16))
+    grad_up = grad_act * gate_pre * sig_gate
+    grad_gate = grad_act * up_pre * sig_gate * (1.0 + gate_pre * (1.0 - sig_gate))
+    grad_pre = jnp.concatenate([grad_gate, grad_up], axis=1).astype(BF16)
+    grad_pre, grad_down_w = after(grad_pre, pair_part(grad_down_w))
+    grad_down_w = scatter_part(grad_down_w)
+    partial = back_product(grad_pre, ffn_w).astype(BF16)
     down_partial = matmul(activated, down_w).astype(BF16)
-    pieces = move_rows(partial)
-    pieces, grad_gate_w, down_partial = after(pieces, grad_gate_w, down_partial)
-    grad_normed_two = from_shared(jnp.sum(pieces.astype(F32), axis=0))
-    grad_down_w = scatter_part(grad_down_w)
-    grad_gate_w = scatter_rows(grad_gate_w)
-    grad_up_w = scatter_rows(grad_up_w)
-    grad_gain_two = jnp.sum(grad_normed_two * hidden * scale_two, axis=0)
-    grad_hidden = cot_rows.astype(F32) + rms_back(grad_normed_two, hidden, scale_two)
-
-    branch = share_rows(grad_hidden.astype(BF16))
-    branch, down_partial = after(branch, down_partial)
+
+    grad_hidden, grad_gain_two, grad_ffn_w, branch = share_branch(
+        partial.reshape(H, -1, width), hidden, cot_rows, normed_two, grad_pre, reps * H
+    )
+    grad_ffn_w = scatter_rows(grad_ffn_w)
+    branch = branch.reshape(-1, width)
     grad_output_w = pair_part(rows_product(gated, branch).astype(BF16))
     grad_gated = back_product(branch, output_w)
-    grad_gated, grad_output_w = after(grad_gated, grad_output_w)
+    grad_gated, grad_output_w, grad_down_w = after(grad_gated, grad_output_w, grad_down_w)
     grad_output_w = scatter_part(grad_output_w)
     pieces = move_rows(down_partial)
     grad_mixed, grad_gain_head, grad_bias, grad_gaterank = mix_backward(
@@ -690,23 +1154,18 @@
         key_dim,
         value_dim,
     )
-    grad_mixed, pieces, grad_down_w, grad_gate_w, grad_output_w = after(
-        grad_mixed, pieces, grad_down_w, grad_gate_w, grad_output_w
+    grad_mixed, pieces, grad_down_w, grad_output_w = after(
+        grad_mixed, pieces, grad_down_w, grad_output_w
     )
     output = (hidden + jnp.sum(pieces.astype(F32), axis=0)).astype(BF16).reshape(tokens.shape)
-    grad_mix_w = pair_rows(rows_product(normed, grad_mixed).astype(BF16))
+    grad_mix_w = pair_product(normed, grad_mixed, reps * H)
     grad_mixed, grad_mix_w = after(grad_mixed, grad_mix_w)
     partial = back_product(grad_mixed, mix_w).astype(BF16)
     grad_mix_w = scatter_rows(grad_mix_w)
-    w_gate_grad = to_columns(grad_gate_w)
-    w_up_grad = to_columns(grad_up_w)
-    pieces = move_rows(partial)
-    pieces, w_gate_grad, w_up_grad = after(pieces, w_gate_grad, w_up_grad)
-    grad_normed = from_shared(jnp.sum(pieces.astype(F32), axis=0))
+    tokens_grad, grad_gain_one = tokens_back(partial.reshape(H, -1, width), inputs, grad_hidden)
+    tokens_grad = tokens_grad.reshape(tokens.shape)
+    w_gate_grad, w_up_grad = jnp.split(to_columns(grad_ffn_w), 2, axis=2)
     grad_mix_w = to_columns(grad_mix_w)
-    grad_gain_one = jnp.sum(grad_normed * inputs * scale_one, axis=0)
-    tokens_grad = grad_hidden + rms_back(grad_normed, inputs, scale_one)
-    tokens_grad = tokens_grad.astype(BF16).reshape(tokens.shape)
 
     edges = [key_dim, 2 * key_dim, 2 * key_dim + value_dim, rank_at, rank_at + rank]
     query_g, key_g, value_g, outgate_g, lowrank_g, _ = jnp.split(grad_mix_w, edges, axis=2)

time: 851 us -> 777 us (0.913)
  Pallas kernels: 171 us -> 479 us
  waiting for transfers between devices: 207 us -> 56.3 us
  blocking collectives: 78.7 us -> 0 us
  other arithmetic: 84.1 us -> 34.6 us
  matrix products: 155 us -> 109 us
  starting transfers between devices: 55.3 us -> 20.9 us
  local copies, waits for them, and re-layouts: 73.5 us -> 52.4 us
    pallas_call x0 -> x6, Pallas kernels: none -> 283 us  [the longest x1 85 us: share_branch(): pl.pallas_call(branch_kernel, out_shape=[jax.ShapeDtypeStruct(hidden.shap...]
    all_to_all x4 -> x1, waiting for transfers between devices: 122 us -> 0.01 us  [share_rows(): lax.all_to_all(spread, 'head', split_axis=0, concat_axis=0, tiled=True)]
    all_to_all x3 -> x0, blocking collectives: 78.7 us -> none  [the longest x1 48.1 us: move_rows(): lax.all_to_all(pieces, 'head', split_axis=0, concat_axis=0, tiled=True)]
    all_to_all x3 -> x1, waiting for transfers between devices: 66.4 us -> 0.01 us  [move_rows(): lax.all_to_all(pieces, 'head', split_axis=0, concat_axis=0, tiled=True)]
    dot_general x15 -> x10, matrix products: 155 us -> 109 us  [dot(): lax.dot_general(a, b, (dims, ((), ())), precision=precision, preferred_el...]
    pallas_call x1, Pallas kernels: 113 us -> 146 us  [mix_backward(): pl.pallas_call(functools.partial(backward_kernel, key_dim, value_dim), ou...]
    unnamed x92 -> x117, local copies, waits for them, and re-layouts: 8.65 us -> 34 us
    convert_element_type x6 -> x3, other arithmetic: 22.7 us -> 2.51 us  [the longest x1 1.84 us: per_device(): activated = (gate_pre * sig_gate * up_pre).astype(BF16)]
  transfers between devices with their start and end apart: 27 -> 15, of which waited for: 10 -> 6; matrix products, arithmetic and copies ran while one was open for 31% -> 18% of each run, Pallas kernels for 20% -> 62%
where the time goes in v3:
time: 777 us; the launch traced here: 768 us
  Pallas kernels  479 us (62%)
  matrix products  109 us (14%)
  waiting for transfers between devices  56.3 us (7%)
  local copies, waits for them, and re-layouts  52.4 us (7%)
  other arithmetic  34.6 us (4%)
  starting transfers between devices  20.9 us (3%)
  between operations  15.3 us (2%)
    pallas_call x1, Pallas kernels, mix_backward(): pl.pallas_call(functools.partial(backward_kernel, key_dim, value_dim), ou...  146 us
    dot_general x10, matrix products, dot(): lax.dot_general(a, b, (dims, ((), ())), precision=precision, preferred_el...  109 us
    pallas_call x1, Pallas kernels, share_branch(): pl.pallas_call(branch_kernel, out_shape=[jax.ShapeDtypeStruct(hidden.shap...  85 us
    pallas_call x1, Pallas kernels, share_hidden(): pl.pallas_call(hidden_kernel, out_shape=[jax.ShapeDtypeStruct(tokens.shap...  75.1 us
    pallas_call x1, Pallas kernels, share_tokens(): pl.pallas_call(share_kernel, out_shape=[jax.ShapeDtypeStruct((H,) + token...  53.8 us
    pallas_call x1, Pallas kernels, mix_forward(): pl.pallas_call(functools.partial(forward_kernel, key_dim, value_dim), out...  50.7 us
    pallas_call x1, Pallas kernels, tokens_back(): pl.pallas_call(tokens_kernel, out_shape=[jax.ShapeDtypeStruct(tokens.shap...  43.1 us
    unnamed x117, local copies, waits for them, and re-layouts  34 us
  transfers between devices with their start and end apart: 15, of which 6 were waited for; matrix products, arithmetic and copies ran while one was open for 18% of the time, Pallas kernels for 62%

profile of v3, /device:TPU:0, one launch (start us, length us, event | category | flops | bytes accessed | tf_op | source)
XLA Modules:
  0.0 768.1 jit_solution(11931966073516708091)
XLA Ops:
  15.4 14.5 %mix_weights.1 = bf16[4,64,1664]{2,1,0:T(8,128)(2,1)} custom-call(bf16[64,1024]{1,0:T(8,128)(2,1)S(1)} %copy-done.16, bf16[64,1024]{1,0:T(8,128)(2,1)S(1)} %copy-done.17, bf16[64,2048]{1,0:T(8,128)(2,1)S(1)} %copy-done.14, bf16[64,2048]{1,0:T(8,128)(2,1)S(1)} %copy-done.15, bf16[64,128]{1,0:T(8,128)(2,1)S(1)} %pad_add_fusion.refs_4_, ...), custom_call_target="tpu_custom_call" | custom-call | flops 10000000000 | bytes 1000000 | tf_op jit(solution)/shard_map/mix_weights/pallas_call | solution.py:497
  29.9 11.5 %all-gather.5.cloned.1.call-done = bf16[512,2048]{1,0:T(8,128)(2,1)} async-done(((bf16[64,2048]{1,0:T(8,128)(2,1)}), bf16[512,2048]{1,0:T(8,128)(2,1)}) %all-gather.5.cloned.1.call-update) | async-done | bytes 2097168 | tf_op jit(solution)/shard_map/all_gather | solution.py:1030
  41.7 53.8 %share_tokens.1 = (bf16[4,256,2048]{2,1,0:T(8,128)(2,1)S(1)}, bf16[4,64,2816]{2,1,0:T(8,128)(2,1)}) custom-call(bf16[256,2048]{1,0:T(8,128)(2,1)S(1)} %bitcast.109, bf16[64,5632]{1,0:T(8,128)(2,1)S(1)} %copy-done.12, bf16[64,5632]{1,0:T(8,128)(2,1)S(1)} %copy-done.13, bf16[64,1]{1,0:T(8,128)(2,1)S(1)} %copy.113.gain_ref), custom_call_target="tpu_custom_call" | custom-call | flops 49999998976 | bytes 1000000 | tf_op jit(solution)/shard_map/share_tokens/pallas_call | solution.py:600
  99.9 4.9 all-to-all-start
  114.0 13.3 %fusion.58.mixed_ref = f32[1024,1664]{1,0:T(8,128)} fusion(bf16[1024,2048]{1,0:T(8,128)(2,1)} %bitcast.112, bf16[2048,1664]{1,0:T(8,128)(2,1)} %bitcast.137), kind=kOutput, calls=%fused_computation.180 | convolution fusion | flops 6979321856 | bytes 17825792 | tf_op jit(solution)/shard_map/dot_general | solution.py:31
  133.5 50.7 %mix_forward.1 = (bf16[1024,512]{1,0:T(8,128)(2,1)S(1)}, f32[1024,512]{1,0:T(8,128)S(1)}, f32[1024,256]{1,0:T(8,128)S(1)}, bf16[4,256,256]{2,1,0:T(8,128)(2,1)S(...) custom-call(f32[1024,1664]{1,0:T(8,128)} %fusion.58.mixed_ref, ...), custom_call_target="tpu_custom_call" | custom-call | flops 49999998976 | bytes 10000000 | tf_op jit(solution)/shard_map/mix_forward/pallas_call | solution.py:922
  195.9 75.1 %share_hidden.1 = (f32[256,2048]{1,0:T(8,128)S(1)}, bf16[4,256,2048]{2,1,0:T(8,128)(2,1)S(1)}) custom-call(bf16[4,256,2048]{2,1,0:T(8,128)(2,1)S(1)} %bitcast.117, bf16[256,2048]{1,0:T(8,128)(2,1)S(1)} %bitcast.110), custom_call_target="tpu_custom_call" | custom-call | flops 80000000000 | bytes 10000000 | tf_op jit(solution)/shard_map/share_hidden/pallas_call | solution.py:704
  274.3 17.3 %fusion.59 = f32[1024,2816]{1,0:T(8,128)S(1)} fusion(bf16[1024,2048]{1,0:T(8,128)(2,1)} %bitcast.114, bf16[2048,2816]{1,0:T(8,128)(2,1)} %bitcast.151), kind=kOutput, calls=%fused_computation.181 | convolution fusion | flops 11811160064 | bytes 27262976 | tf_op jit(solution)/shard_map/dot_general | solution.py:31
  297.4 10.7 %convolution_convert_fusion = bf16[1408,2048]{1,0:T(8,128)(2,1)} fusion(bf16[1024,1408]{1,0:T(8,128)(2,1)S(1)} %multiply_convert_fusion.2, bf16[1024,2048]{1,0:T(8,128)(2,1)} %bitcast.14), kind=kOutput, calls=%fused_computation.1 | convolution fusion | flops 5908463616 | bytes 12845056 | tf_op jit(solution)/shard_map/dot_general | solution.py:31
  310.4 16.2 %multiply_convert_fusion.1 = (bf16[1024,1408]{1,0:T(8,128)(2,1)}, bf16[1024,1408]{1,0:T(8,128)(2,1)}) fusion(f32[1024,2816]{1,0:T(8,128)} %copy-done.38, bf16[1024,2048]{1,0:T(8,128)(2,1)} %bitcast.14, bf16[1408,2048]{1,0:T(8,128)(2,1)} %all-gather.9.cloned.1.call-done), kind=kOutput, calls=%fused_computation.6 | convolution fusion | flops 5924323328 | bytes 27262976 | tf_op jit(solution)/shard_map/dot_general | solution.py:31
  326.6 5.5 pad_maximum_fusion.right_ref
  334.9 18.0 %convolution_convert_fusion.1 = bf16[1024,2048]{1,0:T(8,128)(2,1)} fusion(bf16[1024,2816]{1,0:T(8,128)(2,1)} %pad_maximum_fusion.right_ref, bf16[2048,2816]{1,0:T(8,128)(2,1)} %bitcast.152), kind=kOutput, calls=%fused_computation.9 | convolution fusion | flops 11813257216 | bytes 21495808 | tf_op jit(solution)/shard_map/dot_general | solution.py:31
  353.2 85.0 %share_branch.1 = (f32[256,2048]{1,0:T(8,128)}, f32[1,2048]{1,0:T(1,128)}, bf16[4,256,2816]{2,1,0:T(8,128)(2,1)}, bf16[4,256,2048]{2,1,0:T(8,128)(2,1)}) custom-call(bf16[4,256,2048]{2,1,0:T(8,128)(2,1)} %bitcast.153, f32[256,2048]{1,0:T(8,128)} %copy-done, bf16[256,2048]{1,0:T(8,128)(2,1)} %bitcast.129, bf16[1024,2048]{1,0:T(8,128)(2,1)} %bitcast.115, ...), custom_call_target="tpu_custom_call" | custom-call | flops 80000000000 | bytes 10000000 | tf_op jit(solution)/shard_map/share_branch/pallas_call | solution.py:858
  438.2 4.7 convolution_convert_fusion.5
  448.2 11.9 %reduce-scatter.5.cloned.1.call-done = bf16[176,2048]{1,0:T(8,128)(2,1)} async-done(((bf16[704,2048]{1,0:T(8,128)(2,1)}), bf16[176,2048]{1,0:T(8,128)(2,1)}) %reduce-scatter.5.cloned.1.call-update) | async-done | bytes 720912 | tf_op jit(solution)/shard_map/reduce_scatter | solution.py:1040
  460.9 10.9 %convolution_convert_fusion.3 = bf16[1024,2048]{1,0:T(8,128)(2,1)} fusion(bf16[1024,1408]{1,0:T(8,128)(2,1)} %copy-done.39, bf16[1408,2048]{1,0:T(8,128)(2,1)} %all-gather.9.cloned.1.call-done), kind=kOutput, calls=%fused_computation.11 | convolution fusion | flops 5907677184 | bytes 12845056 | tf_op jit(solution)/shard_map/dot_general | solution.py:31
  471.9 5.0 all-to-all-start.1
  485.4 146.0 %mix_backward.1 = (bf16[1024,1664]{1,0:T(8,128)(2,1)}, f32[1,512]{1,0:T(1,128)S(1)}, f32[1,256]{1,0:T(1,128)S(1)}, f32[16,256]{1,0:T(8,128)S(1)}) custom-call(f32[1024,1664]{1,0:T(8,128)} %fusion.58.mixed_ref, f32[1024,256]{1,0:T(8,128)S(1)} %copy-done.29, bf16[4,256,256]{2,1,0:T(8,128)(2,1)S(1)} %copy-done.33, bf16[1024,256]{1,0:T(8,128)(2,1)S(1)} %copy-done.35, ...), custom_call_target="tpu_custom_call" | custom-call | flops 80000000000 | bytes 10000000 | tf_op jit(solution)/shard_map/mix_backward/pallas_call | solution.py:947
  637.1 11.2 %pair_product.1 = bf16[4,256,1664]{2,1,0:T(8,128)(2,1)} custom-call(bf16[1024,2048]{1,0:T(8,128)(2,1)S(1)} %bitcast.113, bf16[1024,1664]{1,0:T(8,128)(2,1)S(1)} %copy-done.23), custom_call_target="tpu_custom_call" | custom-call | flops 10000000000 | bytes 10000000 | tf_op jit(solution)/shard_map/pair_product/pallas_call | solution.py:813
  648.4 10.3 %convolution_convert_fusion.2 = bf16[1024,2048]{1,0:T(8,128)(2,1)S(1)} fusion(bf16[1024,1664]{1,0:T(8,128)(2,1)S(1)} %copy-done.24, bf16[2048,1664]{1,0:T(8,128)(2,1)} %bitcast.138), kind=kOutput, calls=%fused_computation.10 | convolution fusion | flops 6981419008 | bytes 14417920 | tf_op jit(solution)/shard_map/dot_general | solution.py:31
  658.7 43.1 %tokens_back.1 = (bf16[256,2048]{1,0:T(8,128)(2,1)S(1)}, f32[1,2048]{1,0:T(1,128)S(1)}) custom-call(bf16[4,256,2048]{2,1,0:T(8,128)(2,1)S(1)} %bitcast.116, bf16[256,2048]{1,0:T(8,128)(2,1)S(1)} %bitcast.111, f32[256,2048]{1,0:T(8,128)S(1)} %copy-done.25), custom_call_target="tpu_custom_call" | custom-call | flops 40000000000 | bytes 10000000 | tf_op jit(solution)/shard_map/tokens_back/pallas_call | solution.py:893
  708.2 7.9 %all-to-all-done.2 = f32[32,1,688]{2,1,0:T(1,128)S(1)} async-done(((f32[32,1,688]{2,1,0:T(1,128)}), f32[32,1,688]{2,1,0:T(1,128)S(1)}, u32[]{:S(2)}, u32[]{:S(2)}) %all-to-all-start.2) | async-done | bytes 88096 | tf_op jit(solution)/shard_map/all_to_all | solution.py:1196
  727.5 11.4 %all-to-all-done.4 = bf16[4,64,2816]{2,1,0:T(8,128)(2,1)} async-done(((bf16[4,64,2816]{2,1,0:T(8,128)(2,1)}), bf16[4,64,2816]{2,1,0:T(8,128)(2,1)}, u32[]{:S(2)}, u32[]{:S(2)}) %all-to-all-start.4) | async-done | bytes 1441824 | tf_op jit(solution)/shard_map/all_to_all | solution.py:1025
  748.9 7.9 %all-to-all-done.3 = bf16[4,64,1664]{2,1,0:T(8,128)(2,1)S(1)} async-done(((bf16[4,64,1664]{2,1,0:T(8,128)(2,1)}), bf16[4,64,1664]{2,1,0:T(8,128)(2,1)S(1)}, u32[]{:S(2)}, u32[]{:S(2)}) %all-to-all-start.3) | async-done | bytes 852000 | tf_op jit(solution)/shard_map/all_to_all | solution.py:1025
  (254 shorter events, 106.0 us)
Async XLA Ops:
  7.2 34.3 %all-gather.5.cloned.1.call-start = ((), (), s32[]{:S(2)}) async-start(), calls=%async_computation.9 | async-start | bytes 2359296 | tf_op jit(solution)/shard_map/all_gather | solution.py:1030
  7.9 103.7 %all-gather.7.cloned.1.call-start = ((), (), s32[]{:S(2)}) async-start(), calls=%async_computation.10 | async-start | bytes 7667712 | tf_op jit(solution)/shard_map/all_gather | solution.py:1019
  15.4 26.2 %copy-start.12 = (bf16[64,5632]{1,0:T(8,128)(2,1)S(1)}, bf16[64,5632]{1,0:T(8,128)(2,1)}, u32[]{:S(2)}) copy-start(bf16[64,5632]{1,0:T(8,128)(2,1)} %gate_ref.1) | copy-start | bytes 2162692
  15.4 26.2 %copy-start.13 = (bf16[64,5632]{1,0:T(8,128)(2,1)S(1)}, bf16[64,5632]{1,0:T(8,128)(2,1)}, u32[]{:S(2)}) copy-start(bf16[64,5632]{1,0:T(8,128)(2,1)} %up_ref.1) | copy-start | bytes 2162692
  41.5 232.8 %all-gather.11.cloned.1.call-start = ((), (), s32[]{:S(2)}) async-start(), calls=%async_computation.12 | async-start | bytes 12976128 | tf_op jit(solution)/shard_map/all_gather | solution.py:1019
  41.7 55.7 %copy-start.40 = (bf16[1,256,2048]{2,1,0:T(8,128)(2,1)S(1)}, bf16[1,256,2048]{2,1,0:T(8,128)(2,1)}, u32[]{:S(2)}) copy-start(bf16[1,256,2048]{2,1,0:T(8,128)(2,1)} %param.33) | copy-start | bytes 3145732
  99.9 91.7 %all-to-all-start = ((bf16[4,256,2048]{2,1,0:T(8,128)(2,1)}), bf16[4,256,2048]{2,1,0:T(8,128)(2,1)}, u32[]{:S(2)}, u32[]{:S(2)}) async-start(bf16[4,256,2048]{2,1,0:T(8,128)(2,1)} %broadcast_in_dim.108), calls=%async_computation | async-start | bytes 8388608 | tf_op jit(solution)/shard_map/all_to_all | solution.py:64
  104.8 203.4 %all-gather.9.cloned.1.call-start = ((), (), s32[]{:S(2)}) async-start(), calls=%async_computation.11 | async-start | bytes 6488064 | tf_op jit(solution)/shard_map/all_gather | solution.py:1030
  105.4 354.8 %reduce-scatter.5.cloned.1.call-start = ((), (), s32[]{:S(2)}) async-start(), calls=%async_computation.13 | async-start | bytes 3604480 | tf_op jit(solution)/shard_map/reduce_scatter | solution.py:1040
  130.3 53.9 %copy-start.4 = (f32[16,256]{1,0:T(8,128)}, f32[16,256]{1,0:T(8,128)S(1)}, u32[]{:S(2)}) copy-start(f32[16,256]{1,0:T(8,128)S(1)} %constant_dynamic-slice_fusion.gaterank_ref) | copy-start | bytes 49156
  130.4 53.8 %copy-start.8 = (f32[1,512]{1,0:T(1,128)}, f32[1,512]{1,0:T(1,128)S(1)}, u32[]{:S(2)}) copy-start(f32[1,512]{1,0:T(1,128)S(1)} %reshape.2447.gain_ref) | copy-start | bytes 6148
  310.3 21.8 %collective-permute-start = (bf16[1,704,2048]{2,1,0:T(8,128)(2,1)S(1)}, bf16[1,704,2048]{2,1,0:T(8,128)(2,1)S(1)}, u32[]{:S(2)}, u32[]{:S(2)}) collective-permute-start(bf16[1,704,2048]{2,1,0:T(8,128)(2,1)S(1)} %dynamic-slice_bitcast_fusion), channel_id=1, source_target_pairs={{0,4},{4,0},{1,5},{5,1},{2,6},{6,2},{3,7},{7,3},{8,12},{12,8},{9,1... | collective-permute-start | bytes 8650760 | tf_op jit(solution)/shard_map/ppermute | solution.py:1010
  353.0 280.0 %reduce-scatter.7.cloned.1.call-start = ((), (), s32[]{:S(2)}) async-start(), calls=%async_computation.14 | async-start | bytes 1310720 | tf_op jit(solution)/shard_map/reduce_scatter | solution.py:1040
  353.2 85.0 %copy-start.22 = (bf16[1024,512]{1,0:T(8,128)(2,1)S(1)}, bf16[1024,512]{1,0:T(8,128)(2,1)}, u32[]{:S(2)}) copy-start(bf16[1024,512]{1,0:T(8,128)(2,1)} %copy-done.21) | copy-start | bytes 3145732
  443.1 3.8 collective-permute-start.1
  460.2 256.0 %reduce-scatter.11.cloned.1.call-start = ((), (), s32[]{:S(2)}) async-start(), calls=%async_computation.16 | async-start | bytes 7208960 | tf_op jit(solution)/shard_map/reduce_scatter | solution.py:1016
  471.9 161.1 %all-to-all-start.1 = ((bf16[4,256,2048]{2,1,0:T(8,128)(2,1)}), bf16[4,256,2048]{2,1,0:T(8,128)(2,1)}, u32[]{:S(2)}, u32[]{:S(2)}) async-start(bf16[4,256,2048]{2,1,0:T(8,128)(2,1)} %bitcast.124), calls=%async_computation.2 | async-start | bytes 8388608 | tf_op jit(solution)/shard_map/all_to_all | solution.py:70
  476.9 265.2 %reduce-scatter.9.cloned.1.call-start = ((), (), s32[]{:S(2)}) async-start(), calls=%async_computation.15 | async-start | bytes 4259840 | tf_op jit(solution)/shard_map/reduce_scatter | solution.py:1016
  658.7 47.4 %copy-start.47 = (bf16[64]{0:T(256)(128)(2,1)S(1)}, bf16[64]{0:T(256)(128)(2,1)}, u32[]{:S(2)}) copy-start(bf16[64]{0:T(256)(128)(2,1)} %param.29) | copy-start | bytes 388
  658.7 47.4 %copy-start.42 = (bf16[64,2048]{1,0:T(8,128)(2,1)S(1)}, bf16[64,2048]{1,0:T(8,128)(2,1)}, u32[]{:S(2)}) copy-start(bf16[64,2048]{1,0:T(8,128)(2,1)} %reduce-scatter.7.cloned.1.call-done) | copy-start | bytes 786436
  658.7 48.2 %copy-start.41 = (bf16[176,2048]{1,0:T(8,128)(2,1)S(1)}, bf16[176,2048]{1,0:T(8,128)(2,1)}, u32[]{:S(2)}) copy-start(bf16[176,2048]{1,0:T(8,128)(2,1)} %reduce-scatter.5.cloned.1.call-done) | copy-start | bytes 2162692
  703.5 12.6 %all-to-all-start.2 = ((f32[32,1,688]{2,1,0:T(1,128)}), f32[32,1,688]{2,1,0:T(1,128)S(1)}, u32[]{:S(2)}, u32[]{:S(2)}) async-start(f32[32,1,688]{2,1,0:T(1,128)} %copy.118), calls=%async_computation.4 | async-start | bytes 196608 | tf_op jit(solution)/shard_map/all_to_all | solution.py:1196
  716.1 22.8 %all-to-all-start.4 = ((bf16[4,64,2816]{2,1,0:T(8,128)(2,1)}), bf16[4,64,2816]{2,1,0:T(8,128)(2,1)}, u32[]{:S(2)}, u32[]{:S(2)}) async-start(bf16[4,64,2816]{2,1,0:T(8,128)(2,1)} %reduce-scatter.11.cloned.1.call-done), calls=%async_computation.8 | async-start | bytes 2883584 | tf_op jit(solution)/shard_map/all_to_all | solution.py:1025
  742.1 14.7 %all-to-all-start.3 = ((bf16[4,64,1664]{2,1,0:T(8,128)(2,1)}), bf16[4,64,1664]{2,1,0:T(8,128)(2,1)S(1)}, u32[]{:S(2)}, u32[]{:S(2)}) async-start(bf16[4,64,1664]{2,1,0:T(8,128)(2,1)} %reduce-scatter.9.cloned.1.call-done), calls=%async_computation.6 | async-start | bytes 1703936 | tf_op jit(solution)/shard_map/all_to_all | solution.py:1025
  (44 other events, 234.1 us)
Sparse Core Ops, SparseCore 0:
  9.6 31.7 all-gather.4
  43.0 68.5 all-gather.6
  113.2 123.5 all-gather.10
  238.3 63.8 all-gather.8
  353.1 106.9 reduce-scatter.4
  462.8 63.5 reduce-scatter.6
  528.8 123.3 reduce-scatter.10
  654.7 64.9 reduce-scatter.8

commit v4 on v3

--- a/solution.py
+++ b/solution.py
@@ -182,23 +182,30 @@
     sums_ref,
     pairs_ref,
     gated_ref,
-    attended_ref,
-    logits_ref,
-    scores_ref,
-    start_ref,
-    end_ref,
-    decay_ref,
-    enter_ref,
-    local_ref,
-    send_ref,
-    recv_ref,
-    send_sem,
-    recv_sem,
+    *refs,
 ):
+    kept, (attended_ref, logits_ref, scores_ref, start_ref, end_ref, decay_ref) = refs[:7], refs[7:13]
+    local_ref, send_ref, recv_ref, send_sem, recv_sem, keep_sem = refs[13:]
     count, _, length = segment_ref.shape
     levels = pairs_ref.shape[0]
     parts, place = lax.axis_size("fsdp"), lax.axis_index("fsdp")
     first, last, target = place == 0, place == parts - 1, lax.rem(place + 1, parts)
+
+    def rows_of(s):
+        return pl.ds(pl.multiple_of(s * length, length), length)
+
+    def keeps(s, kinds):
+        held = (attended_ref, logits_ref, scores_ref, start_ref, end_ref, decay_ref, recv_ref)
+        rows = rows_of(s)
+        for kind in kinds:
+            at = rows if len(held[kind].shape) == 2 else s
+            yield pltpu.make_async_copy(held[kind].at[at], kept[kind].at[at], keep_sem.at[s, kind])
+
+    def finish_keeps(s, carry):
+        for copy in keeps(s, range(7)):
+            copy.wait()
+        return carry
+
     rank = gaterank_ref.shape[0]
     scale = key_dim ** (-0.5)
     value_at = 2 * key_dim
@@ -210,9 +217,6 @@
     @pl.when(first)
     def _():
         recv_ref[...] = jnp.zeros_like(recv_ref)
-
-    def rows_of(s):
-        return pl.ds(pl.multiple_of(s * length, length), length)
 
     def ends(s, carry):
         rows = rows_of(s)
@@ -232,6 +236,8 @@
         value = mixed_ref[rows, pl.ds(value_at, value_dim)].astype(BF16)
         local_ref[s] = rows_product(value, end_key)
         start_state(s, first, last, target, local_ref, send_ref, recv_ref, send_sem, recv_sem)
+        for copy in keeps(s, (1, 3, 4, 5)):
+            copy.start()
         return carry
 
     lax.fori_loop(0, count, ends, 0)
@@ -263,43 +269,44 @@
         headed = attended * rms_scale(attended, HEAD_EPS) * gain_ref[...]
         outgate = mixed_ref[rows, pl.ds(gate_at, value_dim)]
         gated_ref[rows, :] = (headed * (outgate * jax.nn.sigmoid(outgate))).astype(BF16)
-        enter_ref[s] = recv_ref[s]
+        for copy in keeps(s, (0, 2, 6)):
+            copy.start()
         return carry
 
     lax.fori_loop(0, count, mix, 0)
     finish_states(count, last, target, send_ref, recv_ref, send_sem, recv_sem)
+    lax.fori_loop(0, count, finish_keeps, 0)
 
 
 def backward_kernel(
     key_dim,
     value_dim,
-    mixed_ref,
-    logits_ref,
-    scores_ref,
-    start_ref,
-    end_ref,
-    decay_ref,
-    enter_ref,
-    attended_ref,
-    upstream_ref,
-    gaterank_ref,
-    gain_ref,
-    marks_ref,
-    segment_ref,
-    sums_ref,
-    pairs_ref,
-    grad_ref,
-    gain_grad_ref,
-    bias_grad_ref,
-    gaterank_grad_ref,
-    out_ref,
-    local_ref,
-    send_ref,
-    recv_ref,
-    send_sem,
-    recv_sem,
+    *refs,
 ):
+    given, refs = refs[:9], refs[9:]
+    gaterank_ref, gain_ref, marks_ref, segment_ref, sums_ref, pairs_ref, *refs = refs
+    grad_ref, gain_grad_ref, bias_grad_ref, gaterank_grad_ref, *refs = refs
+    held, refs = refs[:9], refs[9:]
+    mixed_ref, upstream_ref, attended_ref, start_ref, *rest_refs = held
+    logits_ref, scores_ref, end_ref, decay_ref, enter_ref = rest_refs
+    out_ref, local_ref, send_ref, recv_ref, send_sem, recv_sem, take_sem = refs
     count, _, length = segment_ref.shape
+
+    def rows_of(s):
+        return pl.ds(pl.multiple_of(s * length, length), length)
+
+    def takes(s, kinds):
+        rows = rows_of(s)
+        for kind in kinds:
+            at = rows if len(held[kind].shape) == 2 else s
+            yield pltpu.make_async_copy(given[kind].at[at], held[kind].at[at], take_sem.at[s, kind])
+
+    def start_takes(s, carry):
+        for copy in takes(s, range(9)):
+            copy.start()
+        return carry
+
+    lax.fori_loop(0, count, start_takes, 0)
     levels = pairs_ref.shape[0]
     parts, place = lax.axis_size("fsdp"), lax.axis_index("fsdp")
     first, last, target = place == parts - 1, place == 0, lax.rem(place + parts - 1, parts)
@@ -319,11 +326,10 @@
     bias_grad_ref[...] = jnp.zeros_like(bias_grad_ref)
     gaterank_grad_ref[...] = jnp.zeros_like(gaterank_grad_ref)
 
-    def rows_of(s):
-        return pl.ds(pl.multiple_of(s * length, length), length)
-
     def heads(s, carry):
         rows = rows_of(s)
+        for copy in takes(s, range(4)):
+            copy.wait()
         upstream = upstream_ref[rows, :]
         attended = attended_ref[rows, :]
         outgate = mixed_ref[rows, pl.ds(gate_at, value_dim)]
@@ -346,6 +352,8 @@
 
     def mix(s, carry):
         rows = rows_of(s)
+        for copy in takes(s, range(4, 9)):
+            copy.wait()
         decay_row = decay_ref[s]
         pass_state(
             s, first, last, target, decay_row, local_ref, send_ref, recv_ref, send_sem, recv_sem
@@ -717,11 +725,12 @@
 
 
 class PairProduct:
-    def __init__(self, left_ref, right_ref, out_ref, give_ref, take_ref, send_sem, recv_sem):
-        self.refs = left_ref, right_ref, out_ref, give_ref, take_ref, send_sem, recv_sem
+    def __init__(self, left_ref, right_ref, out_ref, give_ref, take_ref, send_sem, recv_sem, own_sem):
+        self.refs = left_ref, right_ref, out_ref, give_ref, take_ref
+        self.sems = send_sem, recv_sem, own_sem
         self.core = lax.axis_index("core")
-        self.groups, self.rows, width = out_ref.shape
-        self.cut = width // 2 if width % (2 * LANES) == 0 else width
+        self.groups, self.rows, self.width = out_ref.shape
+        self.cut = self.width // 2 if self.width % (2 * LANES) == 0 else self.width
 
     def product(self, group, core, at):
         left, right, *_ = self.refs
@@ -729,35 +738,40 @@
         return rows_product(left[:, pl.ds(start, self.rows)], right[:, pl.ds(at, self.cut)])
 
     def copy(self, group):
-        _, _, _, give, take, send_sem, recv_sem = self.refs
+        give, take = self.refs[3:]
         return pltpu.make_async_remote_copy(
             src_ref=give.at[group],
             dst_ref=take.at[group],
-            send_sem=send_sem.at[group],
-            recv_sem=recv_sem.at[group],
+            send_sem=self.sems[0].at[group],
+            recv_sem=self.sems[1].at[group],
             device_id={"core": 1 - self.core},
             device_id_type=pl.DeviceIdType.MESH,
         )
 
+    def store(self, group):
+        return pltpu.make_async_copy(
+            self.refs[3].at[group], self.refs[2].at[group], self.sems[2].at[group]
+        )
+
     def give(self, group, at):
-        out, give = self.refs[2:4]
-        give[group, :, pl.ds(at, self.cut)] = self.product(group, 1 - self.core, at).astype(BF16)
-        if at + self.cut == out.shape[2]:
+        product = self.product(group, 1 - self.core, at)
+        self.refs[3][group, :, pl.ds(at, self.cut)] = product.astype(BF16)
+        if at + self.cut == self.width:
             self.copy(group).start()
 
     def keep(self, group, at):
-        out, _, take = self.refs[2:5]
+        give, take = self.refs[3:]
         if at == 0:
-            self.copy(group).wait_recv()
+            self.copy(group).wait()
         both = self.product(group, self.core, at)
         both += take[group, :, pl.ds(at, self.cut)].astype(F32)
-        out[group, :, pl.ds(at, self.cut)] = both.astype(BF16)
+        give[group, :, pl.ds(at, self.cut)] = both.astype(BF16)
+        if at + self.cut == self.width:
+            self.store(group).start()
 
     def steps(self):
         places = [
-            (group, at)
-            for group in range(self.groups)
-            for at in range(0, self.refs[2].shape[2], self.cut)
+            (group, at) for group in range(self.groups) for at in range(0, self.width, self.cut)
         ]
         return [functools.partial(self.give, *place) for place in places] + [
             functools.partial(self.keep, *place) for place in places
@@ -765,7 +779,7 @@
 
     def finish(self):
         for group in range(self.groups):
-            self.copy(group).wait_send()
+            self.store(group).wait()
 
 
 def pair_shape(left, right, groups):
@@ -776,6 +790,7 @@
     return [
         pltpu.VMEM(shape, BF16),
         pltpu.VMEM(shape, BF16),
+        pltpu.SemaphoreType.DMA((shape[0],)),
         pltpu.SemaphoreType.DMA((shape[0],)),
         pltpu.SemaphoreType.DMA((shape[0],)),
     ]
@@ -814,7 +829,7 @@
         pair_kernel,
         out_shape=jax.ShapeDtypeStruct(shape, BF16),
         in_specs=[whole] * 2,
-        out_specs=whole,
+        out_specs=pl.BlockSpec(memory_space=pl.ANY),
         scratch_shapes=pair_scratch(shape),
         compiler_params=kernel_params(7, 32),
         cost_estimate=pl.CostEstimate(flops=10**10, bytes_accessed=10**7, transcendentals=0),
@@ -828,8 +843,11 @@
     upstream_ref,
     left_ref,
     right_ref,
+    active_ref,
+    down_ref,
     grad_ref,
     gain_grad_ref,
+    down_out_ref,
     pair_ref,
     out_ref,
     *scratch,
@@ -847,12 +865,18 @@
         grad_ref[rows, :] = grad
         return grad.astype(BF16)
 
+    def down(at):
+        rows = pl.ds(at, LANES)
+        down_out_ref[rows, :] = matmul(active_ref[rows, :], down_ref[...]).astype(BF16)
+
     share = Share(mine_ref, out_ref, *sems)
-    turn_rows(partial_ref, *scratch[:6], done, share, pair.steps())
+    fillers = pair.steps()
+    fillers += [functools.partial(down, at) for at in range(0, active_ref.shape[0], LANES)]
+    turn_rows(partial_ref, *scratch[:6], done, share, fillers)
     pair.finish()
 
 
-def share_branch(partial, hidden, upstream, left, right, groups):
+def share_branch(partial, hidden, upstream, left, right, active, down, groups):
     whole = pl.BlockSpec(memory_space=pltpu.VMEM)
     shape = pair_shape(left, right, groups)
     return pl.pallas_call(
@@ -860,18 +884,19 @@
         out_shape=[
             jax.ShapeDtypeStruct(hidden.shape, F32),
             jax.ShapeDtypeStruct((1, hidden.shape[1]), F32),
+            jax.ShapeDtypeStruct((active.shape[0], down.shape[1]), BF16),
             jax.ShapeDtypeStruct(shape, BF16),
             jax.ShapeDtypeStruct((H,) + hidden.shape, BF16),
         ],
-        in_specs=[whole] * 5,
-        out_specs=[whole] * 3 + [pl.BlockSpec(memory_space=pl.ANY)],
+        in_specs=[whole] * 7,
+        out_specs=[whole] * 3 + [pl.BlockSpec(memory_space=pl.ANY)] * 2,
         scratch_shapes=turn_scratch(*hidden.shape)
         + share_scratch(*hidden.shape)
         + pair_scratch(shape),
         compiler_params=kernel_params(6, 54),
         cost_estimate=pl.CostEstimate(flops=8 * 10**10, bytes_accessed=10**7, transcendentals=0),
         name="share_branch",
-    )(partial, hidden, upstream, left, right)
+    )(partial, hidden, upstream, left, right, active, down)
 
 
 def tokens_kernel(partial_ref, tokens_ref, upstream_ref, grad_ref, gain_grad_ref, *scratch):
@@ -905,6 +930,71 @@
     )(partial, tokens, upstream)
 
 
+def hidden_units_kernel(cot_ref, down_ref, pre_ref, out_ref):
+    units = down_ref.shape[0]
+    grad = back_product(cot_ref[...], down_ref[...])
+    gate, up = pre_ref[:, pl.ds(0, units)], pre_ref[:, pl.ds(units, units)]
+    sig = jax.nn.sigmoid(gate)
+    grad_sig = grad * sig
+    out_ref[:, pl.ds(0, units)] = (grad_sig * up * (1.0 + gate * (1.0 - sig))).astype(BF16)
+    out_ref[:, pl.ds(units, units)] = (grad_sig * gate).astype(BF16)
+
+
+def hidden_units_back(cot, down, pre):
+    rows, width = cot.shape
+    size = 2 * LANES
+
+    def rows_block(n):
+        return pl.BlockSpec((size, n), lambda i: (i, 0))
+
+    return pl.pallas_call(
+        hidden_units_kernel,
+        grid=(rows // size,),
+        out_shape=jax.ShapeDtypeStruct(pre.shape, BF16),
+        in_specs=[
+            rows_block(width),
+            pl.BlockSpec(down.shape, lambda i: (0, 0)),
+            rows_block(pre.shape[1]),
+        ],
+        out_specs=rows_block(pre.shape[1]),
+        compiler_params=pltpu.CompilerParams(vmem_limit_bytes=40 * 2**20),
+        cost_estimate=pl.CostEstimate(flops=10**10, bytes_accessed=10**7, transcendentals=0),
+        name="hidden_units_back",
+    )(cot, down, pre)
+
+
+def columns_kernel(g_ref, out_ref, send_sem, recv_sem, own_sem):
+    me = lax.axis_index("head")
+    peers = [lax.rem(me + ahead, H) for ahead in range(1, H)]
+    greet_heads(peers)
+    copies = [
+        head_copy(g_ref.at[peer], out_ref.at[me], send_sem.at[ahead], recv_sem.at[ahead], peer)
+        for ahead, peer in enumerate(peers)
+    ]
+    copies.append(pltpu.make_async_copy(g_ref.at[me], out_ref.at[me], own_sem))
+    for copy in copies:
+        copy.start()
+    for copy in copies:
+        copy.wait()
+
+
+def columns_back(g, number):
+    return pl.pallas_call(
+        columns_kernel,
+        out_shape=jax.ShapeDtypeStruct(g.shape, BF16),
+        in_specs=[pl.BlockSpec(memory_space=pl.ANY)],
+        out_specs=pl.BlockSpec(memory_space=pl.ANY),
+        scratch_shapes=[
+            pltpu.SemaphoreType.DMA((H,)),
+            pltpu.SemaphoreType.DMA((H,)),
+            pltpu.SemaphoreType.DMA,
+        ],
+        compiler_params=kernel_params(number, 16),
+        cost_estimate=pl.CostEstimate(flops=10**10, bytes_accessed=10**6, transcendentals=0),
+        name="columns_back",
+    )(g)
+
+
 def mix_forward(mixed, bias, gaterank, gain, marks, segment, sums, pairs, key_dim, value_dim):
     rows = mixed.shape[0]
     count, _, length = segment.shape
@@ -923,9 +1013,11 @@
         functools.partial(forward_kernel, key_dim, value_dim),
         out_shape=[jax.ShapeDtypeStruct(*s) for s in shapes],
         in_specs=[whole] * 8,
-        out_specs=[whole] * len(shapes),
-        scratch_shapes=state_scratch(count, value_dim, key_dim),
-        compiler_params=kernel_params(1),
+        out_specs=[whole] + [pl.BlockSpec(memory_space=pl.ANY)] * (len(shapes) - 1),
+        scratch_shapes=[pltpu.VMEM(*s) for s in shapes[1:-1]]
+        + state_scratch(count, value_dim, key_dim)
+        + [pltpu.SemaphoreType.DMA((count, 7))],
+        compiler_params=kernel_params(1, 30),
         cost_estimate=pl.CostEstimate(flops=5 * 10**10, bytes_accessed=10**7, transcendentals=0),
         name="mix_forward",
     )(mixed, bias, gaterank, gain, marks, segment, sums, pairs)
@@ -943,27 +1035,22 @@
         (gaterank.shape, F32),
     )
     attended, logits, scores, start, end, decay, enter = kept
+    given = (mixed, upstream, attended, start, logits, scores, end, decay, enter)
     whole = pl.BlockSpec(memory_space=pltpu.VMEM)
     return pl.pallas_call(
         functools.partial(backward_kernel, key_dim, value_dim),
         out_shape=[jax.ShapeDtypeStruct(*s) for s in shapes],
-        in_specs=[whole] * 15,
+        in_specs=[pl.BlockSpec(memory_space=pl.ANY)] * 9 + [whole] * 6,
         out_specs=[whole] * len(shapes),
-        scratch_shapes=[pltpu.VMEM((rows, value_dim), BF16)]
-        + state_scratch(count, value_dim, key_dim),
-        compiler_params=kernel_params(2),
+        scratch_shapes=[pltpu.VMEM(a.shape, a.dtype) for a in given]
+        + [pltpu.VMEM((rows, value_dim), BF16)]
+        + state_scratch(count, value_dim, key_dim)
+        + [pltpu.SemaphoreType.DMA((count, 9))],
+        compiler_params=kernel_params(2, 36),
         cost_estimate=pl.CostEstimate(flops=8 * 10**10, bytes_accessed=10**7, transcendentals=0),
         name="mix_backward",
     )(
-        mixed,
-        logits,
-        scores,
-        start,
-        end,
-        decay,
-        enter,
-        attended,
-        upstream,
+        *given,
         gaterank,
         gain,
         marks,
@@ -1021,10 +1108,6 @@
             whole = lax.all_gather(whole, "rep", axis=0, tiled=False)
         return whole.reshape(width, -1)
 
-    def to_columns(g):
-        moved = lax.all_to_all(g, "head", split_axis=0, concat_axis=0, tiled=True)
-        return moved.transpose(1, 0, 2).astype(F32)
-
     def gather_part(w):
         if reps == 1:
             return lax.all_gather(w, SHARE, axis=0, tiled=True)
@@ -1067,11 +1150,10 @@
     output_w = gather_part(w_output)
     mix_moved, output_w = after(mix_moved, output_w)
     mix_w = gather_columns(mix_moved)
+    w_down, _ = after(w_down, mix_moved)
+    down_w = gather_part(w_down)
     normed, ffn_moved = share_tokens(inputs, w_gate, w_up, ffn_gain[:, None])
     normed = normed.reshape(-1, width)
-    ffn_w = gather_columns(ffn_moved)
-    normed, w_down = after(normed, w_down)
-    down_w = gather_part(w_down)
 
     small = mix_w[:, rank_at:].astype(F32).reshape(devices, rows, LANES)
     gaterank, bias, gain_head, long, short = (
@@ -1110,34 +1192,41 @@
     gated, *kept = mix_forward(
         mixed, bias, gaterank, gain_head, marks, segment, sums, pairs, key_dim, value_dim
     )
-    cot_rows = cotangent.reshape(-1, width)
-    gated, cot_shared = after(gated, share_rows(cot_rows))
+    cot_rows, _ = after(cotangent.reshape(-1, width), normed)
+    gated, cot_shared, down_w = after(gated, share_rows(cot_rows), down_w)
+    ffn_moved, _ = after(ffn_moved, gated)
+    ffn_w = gather_columns(ffn_moved)
     partial = matmul(gated, output_w).astype(BF16).reshape(H, -1, width)
     hidden, normed_two = share_hidden(partial, inputs)
     normed_two = normed_two.reshape(-1, width)
 
-    gate_pre, up_pre = jnp.split(matmul(normed_two, ffn_w), 2, axis=1)
+    pre = matmul(normed_two, ffn_w)
+    gate_pre, up_pre = jnp.split(pre, 2, axis=1)
     sig_gate = jax.nn.sigmoid(gate_pre)
     activated = (gate_pre * sig_gate * up_pre).astype(BF16)
 
     grad_down_w = rows_product(activated, cot_shared).astype(BF16)
     down_w, grad_down_w = after(down_w, grad_down_w)
-    grad_act = back_product(cot_shared, down_w)
-    grad_up = grad_act * gate_pre * sig_gate
-    grad_gate = grad_act * up_pre * sig_gate * (1.0 + gate_pre * (1.0 - sig_gate))
-    grad_pre = jnp.concatenate([grad_gate, grad_up], axis=1).astype(BF16)
+    grad_pre = hidden_units_back(cot_shared, down_w, pre)
     grad_pre, grad_down_w = after(grad_pre, pair_part(grad_down_w))
     grad_down_w = scatter_part(grad_down_w)
     partial = back_product(grad_pre, ffn_w).astype(BF16)
-    down_partial = matmul(activated, down_w).astype(BF16)
-
-    grad_hidden, grad_gain_two, grad_ffn_w, branch = share_branch(
-        partial.reshape(H, -1, width), hidden, cot_rows, normed_two, grad_pre, reps * H
+
+    grad_hidden, grad_gain_two, down_partial, grad_ffn_w, branch = share_branch(
+        partial.reshape(H, -1, width),
+        hidden,
+        cot_rows,
+        normed_two,
+        grad_pre,
+        activated,
+        down_w,
+        reps * H,
     )
     grad_ffn_w = scatter_rows(grad_ffn_w)
     branch = branch.reshape(-1, width)
+    grad_gated = back_product(branch, output_w)
+    gated, grad_gated = after(gated, grad_gated)
     grad_output_w = pair_part(rows_product(gated, branch).astype(BF16))
-    grad_gated = back_product(branch, output_w)
     grad_gated, grad_output_w, grad_down_w = after(grad_gated, grad_output_w, grad_down_w)
     grad_output_w = scatter_part(grad_output_w)
     pieces = move_rows(down_partial)
@@ -1154,26 +1243,31 @@
         key_dim,
         value_dim,
     )
-    grad_mixed, pieces, grad_down_w, grad_output_w = after(
-        grad_mixed, pieces, grad_down_w, grad_output_w
-    )
+    grad_mixed, pieces, grad_down_w = after(grad_mixed, pieces, grad_down_w)
     output = (hidden + jnp.sum(pieces.astype(F32), axis=0)).astype(BF16).reshape(tokens.shape)
     grad_mix_w = pair_product(normed, grad_mixed, reps * H)
     grad_mixed, grad_mix_w = after(grad_mixed, grad_mix_w)
     partial = back_product(grad_mixed, mix_w).astype(BF16)
     grad_mix_w = scatter_rows(grad_mix_w)
+    grad_ffn_w = columns_back(grad_ffn_w, 9)
+    partial, grad_ffn_w, grad_output_w = after(partial, grad_ffn_w, grad_output_w)
     tokens_grad, grad_gain_one = tokens_back(partial.reshape(H, -1, width), inputs, grad_hidden)
     tokens_grad = tokens_grad.reshape(tokens.shape)
-    w_gate_grad, w_up_grad = jnp.split(to_columns(grad_ffn_w), 2, axis=2)
-    grad_mix_w = to_columns(grad_mix_w)
-
-    edges = [key_dim, 2 * key_dim, 2 * key_dim + value_dim, rank_at, rank_at + rank]
-    query_g, key_g, value_g, outgate_g, lowrank_g, _ = jnp.split(grad_mix_w, edges, axis=2)
-    gain_one = norm_gain.astype(F32)
-    gain_two = ffn_gain.astype(F32)
-
-    def scaled(g, gain, w):
-        return g.reshape(w.shape) * gain[:, None]
+
+    def weight_grad(moved, gain, start, w):
+        n = w.shape[1] // H
+        whole = moved[:, :, start : start + n].transpose(1, 0, 2).reshape(rows, -1)
+        return whole.astype(F32) * gain.astype(F32)[:, None]
+
+    w_gate_grad = weight_grad(grad_ffn_w, ffn_gain, 0, w_gate)
+    w_up_grad = weight_grad(grad_ffn_w, ffn_gain, w_gate.shape[1] // H, w_up)
+    grad_mix_w = columns_back(grad_mix_w, 10)
+    query_g = weight_grad(grad_mix_w, norm_gain, 0, w_query)
+    key_g = weight_grad(grad_mix_w, norm_gain, key_dim, w_key)
+    value_g = weight_grad(grad_mix_w, norm_gain, 2 * key_dim, w_value)
+    outgate_g = weight_grad(grad_mix_w, norm_gain, 2 * key_dim + value_dim, w_outgate)
+    lowrank_g = grad_mix_w[:, :, rank_at : rank_at + rank].astype(F32)
+    lowrank_g = jnp.sum(lowrank_g, axis=0) * norm_gain.astype(F32)[:, None]
 
     def place(g, axis):
         shape = list(g.shape)
@@ -1202,19 +1296,19 @@
     return (
         output,
         tokens_grad,
-        norm_g / gain_one,
-        scaled(query_g, gain_one, w_query),
-        scaled(key_g, gain_one, w_key),
-        scaled(value_g, gain_one, w_value),
-        scaled(outgate_g, gain_one, w_outgate),
-        scaled(jnp.sum(lowrank_g, axis=1), gain_one, w_lowrank),
+        norm_g / norm_gain.astype(F32),
+        query_g,
+        key_g,
+        value_g,
+        outgate_g,
+        lowrank_g,
         gaterank_g.reshape(w_gaterank.shape),
         bias_g,
         head_g,
         grad_output_w.astype(F32),
-        ffn_g / gain_two,
-        scaled(w_gate_grad, gain_two, w_gate),
-        scaled(w_up_grad, gain_two, w_up),
+        ffn_g / ffn_gain.astype(F32),
+        w_gate_grad,
+        w_up_grad,
         grad_down_w.astype(F32),
     )
 

time: 777 us -> 767 us (0.987)
  matrix products: 109 us -> 83.4 us
  local copies, waits for them, and re-layouts: 52.4 us -> 71.7 us
    pallas_call x0 -> x3, Pallas kernels: none -> 55.4 us  [the longest x2 31.5 us: columns_back(): pl.pallas_call(columns_kernel, out_shape=jax.ShapeDtypeStruct(g.shape, BF...]
    pallas_call x1, Pallas kernels: 146 us -> 98.8 us  [mix_backward(): pl.pallas_call(functools.partial(backward_kernel, key_dim, value_dim), ou...]
    all_gather x2, waiting for transfers between devices: 3.55 us -> 45.4 us  [gather_columns(): whole = lax.all_gather(moved, ('core', 'fsdp'), axis=1, tiled=True)]
    dot_general x10 -> x8, matrix products: 109 us -> 83.4 us  [dot(): lax.dot_general(a, b, (dims, ((), ())), precision=precision, preferred_el...]
    all_to_all x2 -> x0, waiting for transfers between devices: 19.3 us -> none  [to_columns(): moved = lax.all_to_all(g, 'head', split_axis=0, concat_axis=0, tiled=True)]
    unnamed x117 -> x134, local copies, waits for them, and re-layouts: 34 us -> 51.8 us
    reduce_scatter x2, waiting for transfers between devices: 11.9 us -> 0.02 us  [scatter_part(): return lax.psum_scatter(g, 'fsdp', scatter_dimension=0, tiled=True)]
    all_to_all x2 -> x0, starting transfers between devices: 7.83 us -> none  [to_columns(): moved = lax.all_to_all(g, 'head', split_axis=0, concat_axis=0, tiled=True)]
  transfers between devices with their start and end apart: 15 -> 13, of which waited for: 6 -> 4; matrix products, arithmetic and copies ran while one was open for 18% -> 11% of each run, Pallas kernels for 62% -> 62%
where the time goes in v4:
time: 767 us; the launch traced here: 764 us
  Pallas kernels  486 us (63%)
  matrix products  83.4 us (11%)
  local copies, waits for them, and re-layouts  71.7 us (9%)
  waiting for transfers between devices  63.8 us (8%)
  other arithmetic  30.6 us (4%)
  between operations  15.3 us (2%)
  starting transfers between devices  13.3 us (2%)
    pallas_call x1, Pallas kernels, mix_backward(): pl.pallas_call(functools.partial(backward_kernel, key_dim, value_dim), ou...  98.8 us
    pallas_call x1, Pallas kernels, share_branch(): pl.pallas_call(branch_kernel, out_shape=[jax.ShapeDtypeStruct(hidden.shap...  88.3 us
    dot_general x8, matrix products, dot(): lax.dot_general(a, b, (dims, ((), ())), precision=precision, preferred_el...  83.4 us
    pallas_call x1, Pallas kernels, share_hidden(): pl.pallas_call(hidden_kernel, out_shape=[jax.ShapeDtypeStruct(tokens.shap...  75.2 us
    pallas_call x1, Pallas kernels, share_tokens(): pl.pallas_call(share_kernel, out_shape=[jax.ShapeDtypeStruct((H,) + token...  53.8 us
    unnamed x134, local copies, waits for them, and re-layouts  51.8 us
    pallas_call x1, Pallas kernels, mix_forward(): pl.pallas_call(functools.partial(forward_kernel, key_dim, value_dim), out...  47.9 us
    all_gather x2, waiting for transfers between devices, gather_columns(): whole = lax.all_gather(moved, ('core', 'fsdp'), axis=1, tiled=True)  45.4 us
  transfers between devices with their start and end apart: 13, of which 4 were waited for; matrix products, arithmetic and copies ran while one was open for 11% of the time, Pallas kernels for 62%

profile of v4, /device:TPU:0, one launch (start us, length us, event | category | flops | bytes accessed | tf_op | source)
XLA Modules:
  0.0 764.1 jit_solution(16066865396620342261)
XLA Ops:
  15.4 14.5 %mix_weights.1 = bf16[4,64,1664]{2,1,0:T(8,128)(2,1)} custom-call(bf16[64,1024]{1,0:T(8,128)(2,1)S(1)} %copy-done.18, bf16[64,1024]{1,0:T(8,128)(2,1)S(1)} %copy-done.19, bf16[64,2048]{1,0:T(8,128)(2,1)S(1)} %copy-done.16, bf16[64,2048]{1,0:T(8,128)(2,1)S(1)} %copy-done.17, bf16[64,128]{1,0:T(8,128)(2,1)S(1)} %pad_add_fusion.refs_4_, ...), custom_call_target="tpu_custom_call" | custom-call | flops 10000000000 | bytes 1000000 | tf_op jit(solution)/shard_map/mix_weights/pallas_call | solution.py:505
  29.9 11.5 %all-gather.5.cloned.1.call-done = bf16[512,2048]{1,0:T(8,128)(2,1)} async-done(((bf16[64,2048]{1,0:T(8,128)(2,1)}), bf16[512,2048]{1,0:T(8,128)(2,1)}) %all-gather.5.cloned.1.call-update) | async-done | bytes 2097168 | tf_op jit(solution)/shard_map/all_gather | solution.py:1113
  41.6 53.8 %share_tokens.1 = (bf16[4,256,2048]{2,1,0:T(8,128)(2,1)S(1)}, bf16[4,64,2816]{2,1,0:T(8,128)(2,1)}) custom-call(bf16[256,2048]{1,0:T(8,128)(2,1)S(1)} %bitcast.107, bf16[64,5632]{1,0:T(8,128)(2,1)S(1)} %copy-done.14, bf16[64,5632]{1,0:T(8,128)(2,1)S(1)} %copy-done.15, bf16[64,1]{1,0:T(8,128)(2,1)S(1)} %copy.113.gain_ref), custom_call_target="tpu_custom_call" | custom-call | flops 49999998976 | bytes 1000000 | tf_op jit(solution)/shard_map/share_tokens/pallas_call | solution.py:608
  99.8 4.9 all-to-all-start
  122.4 11.6 %fusion.59.mixed_ref.refs_0_ = f32[1024,1664]{1,0:T(8,128)S(1)} fusion(bf16[1024,2048]{1,0:T(8,128)(2,1)} %bitcast.110, bf16[2048,1664]{1,0:T(8,128)(2,1)} %bitcast.133), kind=kOutput, calls=%fused_computation.174 | convolution fusion | flops 6979321856 | bytes 17825792 | tf_op jit(solution)/shard_map/dot_general | solution.py:31
  134.0 47.9 %mix_forward.1 = (bf16[1024,512]{1,0:T(8,128)(2,1)S(1)}, f32[1024,512]{1,0:T(8,128)S(1)}, f32[1024,256]{1,0:T(8,128)S(1)}, bf16[4,256,256]{2,1,0:T(8,128)(2,1)S(...) custom-call(f32[1024,1664]{1,0:T(8,128)S(1)} %fusion.59.mixed_ref.re, ...), custom_call_target="tpu_custom_call" | custom-call | flops 49999998976 | bytes 10000000 | tf_op jit(solution)/shard_map/mix_forward/pallas_call | solution.py:1012
  191.6 4.3 convolution_convert_fusion.3
  195.8 75.2 %share_hidden.1 = (f32[256,2048]{1,0:T(8,128)S(1)}, bf16[4,256,2048]{2,1,0:T(8,128)(2,1)S(1)}) custom-call(bf16[4,256,2048]{2,1,0:T(8,128)(2,1)S(1)} %bitcast.115, bf16[256,2048]{1,0:T(8,128)(2,1)S(1)} %bitcast.108), custom_call_target="tpu_custom_call" | custom-call | flops 80000000000 | bytes 10000000 | tf_op jit(solution)/shard_map/share_hidden/pallas_call | solution.py:712
  274.3 43.0 %all-gather.11.cloned.1.call-done = bf16[4,512,2816]{2,1,0:T(8,128)(2,1)} async-done(((bf16[4,64,2816]{2,1,0:T(8,128)(2,1)}), bf16[4,512,2816]{2,1,0:T(8,128)(2,1)}) %all-gather.11.cloned.1.call-update) | async-done | bytes 11534352 | tf_op jit(solution)/shard_map/all_gather | solution.py:1106
  317.3 17.2 %fusion.60.pre_ref = f32[1024,2816]{1,0:T(8,128)S(1)} fusion(bf16[1024,2048]{1,0:T(8,128)(2,1)} %bitcast.112, bf16[2048,2816]{1,0:T(8,128)(2,1)} %bitcast.147), kind=kOutput, calls=%fused_computation.175 | convolution fusion | flops 11811160064 | bytes 27262976 | tf_op jit(solution)/shard_map/dot_general | solution.py:31
  338.7 9.1 %convolution_convert_fusion = bf16[1408,2048]{1,0:T(8,128)(2,1)S(1)} fusion(bf16[1024,1408]{1,0:T(8,128)(2,1)S(1)} %fusion.active_ref, bf16[1024,2048]{1,0:T(8,128)(2,1)} %bitcast.14.cot_ref), kind=kOutput, calls=%fused_computation.1 | convolution fusion | flops 5908463616 | bytes 12845056 | tf_op jit(solution)/shard_map/dot_general | solution.py:31
  350.6 23.8 %hidden_units_back.1.right_ref = bf16[1024,2816]{1,0:T(8,128)(2,1)S(1)} custom-call(bf16[1024,2048]{1,0:T(8,128)(2,1)} %bitcast.14.cot_ref, bf16[1408,2048]{1,0:T(8,128)(2,1)} %all-gather.9.cloned.1.call-done.down_ref, f32[1024,2816]{1,0:T(8,128)} %copy-done.44), custom_call_target="tpu_custom_call" | custom-call | flops 10000000000 | bytes 10000000 | tf_op jit(solution)/shard_map/hidden_units_back/pallas_call | solution.py:950
  379.9 18.0 %convolution_convert_fusion.1 = bf16[1024,2048]{1,0:T(8,128)(2,1)} fusion(bf16[1024,2816]{1,0:T(8,128)(2,1)} %copy-done.26, bf16[2048,2816]{1,0:T(8,128)(2,1)} %bitcast.148), kind=kOutput, calls=%fused_computation.6 | convolution fusion | flops 11813257216 | bytes 21495808 | tf_op jit(solution)/shard_map/dot_general | solution.py:31
  398.0 88.3 %share_branch.1 = (f32[256,2048]{1,0:T(8,128)}, f32[1,2048]{1,0:T(1,128)}, bf16[1024,2048]{1,0:T(8,128)(2,1)}, bf16[4,256,2816]{2,1,0:T(8,128)(2,1)}, bf16[4,256,2048]{2,1,0:T(8,128)(2,1)}) custom-call(bf16[4,256,2048]{2,1,0:T(8,128)(2,1)} %bitcast.151, f32[256,2048]{1,0:T(8,128)} %copy-done, bf16[256,2048]{1,0:T(8,128)(2,1)} %bitcast.125, ...), custom_call_target="tpu_custom_call" | custom-call | flops 80000000000 | bytes 10000000 | tf_op jit(solution)/shard_map/share_branch/pallas_call | solution.py:882
  486.3 5.9 fusion.61.refs_1_
  493.4 4.8 convolution_convert_fusion.4
  500.0 5.0 all-to-all-start.1
  518.7 98.8 %mix_backward.1 = (bf16[1024,1664]{1,0:T(8,128)(2,1)S(1)}, f32[1,512]{1,0:T(1,128)S(1)}, f32[1,256]{1,0:T(1,128)S(1)}, f32[16,256]{1,0:T(8,128)S(1)}) custom-call(f32[1024,1664]{1,0:T(8,128)} %copy-done.28, f32[1024,512]{1,0:T(8,128)S(1)} %copy-done.27, f32[1024,512]{1,0:T(8,128)S(1)} %copy-done.33, bf16[1024,256]{1,0:T(8,128)(2,1)S(1)} %copy-done.41, ...), custom_call_target="tpu_custom_call" | custom-call | flops 80000000000 | bytes 10000000 | tf_op jit(solution)/shard_map/mix_backward/pallas_call | solution.py:1040
  623.5 10.4 %pair_product.1 = bf16[4,256,1664]{2,1,0:T(8,128)(2,1)} custom-call(bf16[1024,2048]{1,0:T(8,128)(2,1)S(1)} %bitcast.111, bf16[1024,1664]{1,0:T(8,128)(2,1)S(1)} %copy-done.30), custom_call_target="tpu_custom_call" | custom-call | flops 10000000000 | bytes 10000000 | tf_op jit(solution)/shard_map/pair_product/pallas_call | solution.py:828
  643.2 12.4 %convolution_convert_fusion.2 = bf16[1024,2048]{1,0:T(8,128)(2,1)} fusion(bf16[1024,1664]{1,0:T(8,128)(2,1)} %copy-done.29, bf16[2048,1664]{1,0:T(8,128)(2,1)} %bitcast.134), kind=kOutput, calls=%fused_computation.7 | convolution fusion | flops 6981419008 | bytes 14417920 | tf_op jit(solution)/shard_map/dot_general | solution.py:31
  657.1 19.6 %columns_back.2 = bf16[4,64,2816]{2,1,0:T(8,128)(2,1)S(1)} custom-call(bf16[4,64,2816]{2,1,0:T(8,128)(2,1)S(1)} %copy-done.10), custom_call_target="tpu_custom_call" | custom-call | flops 10000000000 | bytes 1000000 | tf_op jit(solution)/shard_map/columns_back/pallas_call | solution.py:982
  680.5 41.9 %tokens_back.1 = (bf16[256,2048]{1,0:T(8,128)(2,1)S(1)}, f32[1,2048]{1,0:T(1,128)S(1)}) custom-call(bf16[4,256,2048]{2,1,0:T(8,128)(2,1)S(1)} %bitcast.114, bf16[256,2048]{1,0:T(8,128)(2,1)S(1)} %bitcast.109, f32[256,2048]{1,0:T(8,128)S(1)} %copy-done.31), custom_call_target="tpu_custom_call" | custom-call | flops 40000000000 | bytes 10000000 | tf_op jit(solution)/shard_map/tokens_back/pallas_call | solution.py:918
  731.0 6.0 all-to-all-done.2
  740.7 11.9 %columns_back.3 = bf16[4,64,1664]{2,1,0:T(8,128)(2,1)S(1)} custom-call(bf16[4,64,1664]{2,1,0:T(8,128)(2,1)S(1)} %copy-done.13), custom_call_target="tpu_custom_call" | custom-call | flops 10000000000 | bytes 1000000 | tf_op jit(solution)/shard_map/columns_back/pallas_call | solution.py:982
  (267 shorter events, 108.8 us)
Async XLA Ops:
  7.2 34.3 %all-gather.5.cloned.1.call-start = ((), (), s32[]{:S(2)}) async-start(), calls=%async_computation.7 | async-start | bytes 2359296 | tf_op jit(solution)/shard_map/all_gather | solution.py:1113
  7.9 103.7 %all-gather.7.cloned.1.call-start = ((), (), s32[]{:S(2)}) async-start(), calls=%async_computation.8 | async-start | bytes 7667712 | tf_op jit(solution)/shard_map/all_gather | solution.py:1106
  15.4 26.1 %copy-start.57 = (bf16[64]{0:T(256)(128)(2,1)S(1)}, bf16[64]{0:T(256)(128)(2,1)}, u32[]{:S(2)}) copy-start(bf16[64]{0:T(256)(128)(2,1)} %param.29) | copy-start | bytes 388
  15.4 26.2 %copy-start.11 = (bf16[1,256,2048]{2,1,0:T(8,128)(2,1)S(1)}, bf16[1,256,2048]{2,1,0:T(8,128)(2,1)}, u32[]{:S(2)}) copy-start(bf16[1,256,2048]{2,1,0:T(8,128)(2,1)} %param.17) | copy-start | bytes 3145732
  15.4 26.2 %copy-start.14 = (bf16[64,5632]{1,0:T(8,128)(2,1)S(1)}, bf16[64,5632]{1,0:T(8,128)(2,1)}, u32[]{:S(2)}) copy-start(bf16[64,5632]{1,0:T(8,128)(2,1)} %gate_ref.1) | copy-start | bytes 2162692
  15.4 26.2 %copy-start.15 = (bf16[64,5632]{1,0:T(8,128)(2,1)S(1)}, bf16[64,5632]{1,0:T(8,128)(2,1)}, u32[]{:S(2)}) copy-start(bf16[64,5632]{1,0:T(8,128)(2,1)} %up_ref.1) | copy-start | bytes 2162692
  41.6 55.7 %copy-start.50 = (bf16[1,256,2048]{2,1,0:T(8,128)(2,1)S(1)}, bf16[1,256,2048]{2,1,0:T(8,128)(2,1)}, u32[]{:S(2)}) copy-start(bf16[1,256,2048]{2,1,0:T(8,128)(2,1)} %param.33) | copy-start | bytes 3145732
  99.8 91.6 %all-to-all-start = ((bf16[4,256,2048]{2,1,0:T(8,128)(2,1)}), bf16[4,256,2048]{2,1,0:T(8,128)(2,1)}, u32[]{:S(2)}, u32[]{:S(2)}) async-start(bf16[4,256,2048]{2,1,0:T(8,128)(2,1)} %broadcast_in_dim.106), calls=%async_computation | async-start | bytes 8388608 | tf_op jit(solution)/shard_map/all_to_all | solution.py:64
  104.7 86.7 %all-gather.9.cloned.1.call-start = ((), (), s32[]{:S(2)}) async-start(), calls=%async_computation.9 | async-start | bytes 6488064 | tf_op jit(solution)/shard_map/all_gather | solution.py:1113
  106.4 210.9 %all-gather.11.cloned.1.call-start = ((), (), s32[]{:S(2)}) async-start(), calls=%async_computation.10 | async-start | bytes 12976128 | tf_op jit(solution)/shard_map/all_gather | solution.py:1106
  118.0 16.0 %copy-start.8 = (f32[1,512]{1,0:T(1,128)}, f32[1,512]{1,0:T(1,128)S(1)}, u32[]{:S(2)}) copy-start(f32[1,512]{1,0:T(1,128)S(1)} %reshape.2450.gain_ref.refs_10_) | copy-start | bytes 6148
  121.2 12.8 %copy-start.6 = (f32[4,1,256]{2,1,0:T(1,128)}, f32[4,1,256]{2,1,0:T(1,128)S(1)}, u32[]{:S(2)}) copy-start(f32[4,1,256]{2,1,0:T(1,128)S(1)} %convert_element_type.259.segment_ref.refs_12_) | copy-start | bytes 12292
  191.5 318.3 %reduce-scatter.5.cloned.1.call-start = ((), (), s32[]{:S(2)}) async-start(), calls=%async_computation.11 | async-start | bytes 3604480 | tf_op jit(solution)/shard_map/reduce_scatter | solution.py:1123
  350.4 26.6 %collective-permute-start = (bf16[1,704,2048]{2,1,0:T(8,128)(2,1)S(1)}, bf16[1,704,2048]{2,1,0:T(8,128)(2,1)S(1)}, u32[]{:S(2)}, u32[]{:S(2)}) collective-permute-start(bf16[1,704,2048]{2,1,0:T(8,128)(2,1)S(1)} %dynamic-slice_bitcast_fusion), channel_id=1, source_target_pairs={{0,4},{4,0},{1,5},{5,1},{2,6},{6,2},{3,7},{7,3},{8,12},{12,8},{9,1... | collective-permute-start | bytes 8650760 | tf_op jit(solution)/shard_map/ppermute | solution.py:1097
  350.6 26.3 %copy-start.46 = (bf16[1408,2048]{1,0:T(8,128)(2,1)S(1)}, bf16[1408,2048]{1,0:T(8,128)(2,1)}, u32[]{:S(2)}) copy-start(bf16[1408,2048]{1,0:T(8,128)(2,1)} %copy-done.45) | copy-start | bytes 17301508
  398.0 257.8 %reduce-scatter.7.cloned.1.call-start = ((), (), s32[]{:S(2)}) async-start(), calls=%async_computation.12 | async-start | bytes 7208960 | tf_op jit(solution)/shard_map/reduce_scatter | solution.py:1103
  398.0 88.3 %copy-start.62 = (bf16[512,2048]{1,0:T(8,128)(2,1)S(1)}, bf16[512,2048]{1,0:T(8,128)(2,1)}, u32[]{:S(2)}) copy-start(bf16[512,2048]{1,0:T(8,128)(2,1)} %all-gather.5.cloned.1.call-done) | copy-start | bytes 6291460
  499.4 7.5 collective-permute-start.1
  500.0 119.3 %all-to-all-start.1 = ((bf16[4,256,2048]{2,1,0:T(8,128)(2,1)}), bf16[4,256,2048]{2,1,0:T(8,128)(2,1)}, u32[]{:S(2)}, u32[]{:S(2)}) async-start(bf16[4,256,2048]{2,1,0:T(8,128)(2,1)} %bitcast.120), calls=%async_computation.2 | async-start | bytes 8388608 | tf_op jit(solution)/shard_map/all_to_all | solution.py:70
  505.0 171.8 %reduce-scatter.9.cloned.1.call-start = ((), (), s32[]{:S(2)}) async-start(), calls=%async_computation.13 | async-start | bytes 1310720 | tf_op jit(solution)/shard_map/reduce_scatter | solution.py:1123
  623.5 13.7 %copy-start.51 = (bf16[176,2048]{1,0:T(8,128)(2,1)S(1)}, bf16[176,2048]{1,0:T(8,128)(2,1)}, u32[]{:S(2)}) copy-start(bf16[176,2048]{1,0:T(8,128)(2,1)} %reduce-scatter.5.cloned.1.call-done) | copy-start | bytes 2162692
  643.0 96.5 %reduce-scatter.11.cloned.1.call-start = ((), (), s32[]{:S(2)}) async-start(), calls=%async_computation.14 | async-start | bytes 4259840 | tf_op jit(solution)/shard_map/reduce_scatter | solution.py:1103
  657.1 19.6 %copy-start.12 = (bf16[1,256,2048]{2,1,0:T(8,128)(2,1)S(1)}, bf16[1,256,2048]{2,1,0:T(8,128)(2,1)}, u32[]{:S(2)}) copy-start(bf16[1,256,2048]{2,1,0:T(8,128)(2,1)} %param.17) | copy-start | bytes 3145732
  725.0 12.0 %all-to-all-start.2 = ((f32[32,1,688]{2,1,0:T(1,128)}), f32[32,1,688]{2,1,0:T(1,128)S(1)}, u32[]{:S(2)}, u32[]{:S(2)}) async-start(f32[32,1,688]{2,1,0:T(1,128)} %copy.118), calls=%async_computation.5 | async-start | bytes 196608 | tf_op jit(solution)/shard_map/all_to_all | solution.py:1290
  (52 other events, 168.7 us)
Sparse Core Ops, SparseCore 0:
  9.6 31.7 all-gather.4
  43.0 68.5 all-gather.6
  113.3 76.3 all-gather.8
  191.6 125.6 all-gather.10
  398.1 54.4 reduce-scatter.4
  492.4 120.7 reduce-scatter.6
  643.1 25.4 reduce-scatter.8
  671.0 63.1 reduce-scatter.10

commit v5 on v4

--- a/solution.py
+++ b/solution.py
@@ -506,7 +506,7 @@
         mix_weights_kernel,
         out_shape=jax.ShapeDtypeStruct((H, rows, n), BF16),
         in_specs=[pl.BlockSpec(memory_space=pltpu.VMEM)] * (len(weights) + 2),
-        out_specs=pl.BlockSpec(memory_space=pl.ANY),
+        out_specs=pl.BlockSpec(memory_space=pltpu.HBM),
         scratch_shapes=[
             pltpu.VMEM((H, rows, n), BF16),
             pltpu.SemaphoreType.DMA((H,)),
@@ -514,7 +514,7 @@
             pltpu.SemaphoreType.DMA,
         ],
         compiler_params=kernel_params(3, 16),
-        cost_estimate=pl.CostEstimate(flops=10**10, bytes_accessed=10**6, transcendentals=0),
+        cost_estimate=pl.CostEstimate(flops=10**6, bytes_accessed=10**4, transcendentals=0),
         name="mix_weights",
     )(*weights, extra, gain)
 
@@ -612,7 +612,7 @@
             jax.ShapeDtypeStruct((H, rows, n), BF16),
         ],
         in_specs=[pl.BlockSpec(memory_space=pltpu.VMEM)] * 4,
-        out_specs=[pl.BlockSpec(memory_space=pl.ANY)] * 2,
+        out_specs=[pl.BlockSpec(memory_space=pltpu.HBM)] * 2,
         scratch_shapes=share_scratch(*tokens.shape)
         + [
             pltpu.VMEM((H, rows, n), BF16),
@@ -621,7 +621,7 @@
             pltpu.SemaphoreType.DMA,
         ],
         compiler_params=kernel_params(4, 16),
-        cost_estimate=pl.CostEstimate(flops=5 * 10**10, bytes_accessed=10**6, transcendentals=0),
+        cost_estimate=pl.CostEstimate(flops=10**6, bytes_accessed=10**4, transcendentals=0),
         name="share_tokens",
     )(tokens, w_gate, w_up, gain)
 
@@ -716,10 +716,10 @@
             jax.ShapeDtypeStruct((H,) + tokens.shape, BF16),
         ],
         in_specs=[whole] * 2,
-        out_specs=[whole, pl.BlockSpec(memory_space=pl.ANY)],
+        out_specs=[whole, pl.BlockSpec(memory_space=pltpu.HBM)],
         scratch_shapes=turn_scratch(*tokens.shape) + share_scratch(*tokens.shape),
-        compiler_params=kernel_params(5, 24),
-        cost_estimate=pl.CostEstimate(flops=8 * 10**10, bytes_accessed=10**7, transcendentals=0),
+        compiler_params=kernel_params(5, 18),
+        cost_estimate=pl.CostEstimate(flops=10**6, bytes_accessed=10**4, transcendentals=0),
         name="share_hidden",
     )(partial, tokens)
 
@@ -796,66 +796,61 @@
     ]
 
 
-def greet_square_and_core():
+def pair_kernel(moving, left_ref, right_ref, *refs):
+    g_ref, out_ref, moved_ref, *scratch = refs if moving else (None, refs[0], None, *refs[1:])
+    core = 1 - lax.axis_index("core")
+    me = lax.axis_index("head")
+    peers = [lax.rem(me + ahead, H) for ahead in range(1, H)] if moving else []
     barrier = pltpu.get_barrier_semaphore()
-    for side in square(lax.axis_index("head"))[:2]:
+    for target in [{"core": core}] + [{"head": peer} for peer in peers]:
         pl.semaphore_signal(
-            barrier, inc=1, device_id={"head": side}, device_id_type=pl.DeviceIdType.MESH
+            barrier, inc=1, device_id=target, device_id_type=pl.DeviceIdType.MESH
         )
-    other = 1 - lax.axis_index("core")
-    pl.semaphore_signal(
-        barrier, inc=1, device_id={"core": other}, device_id_type=pl.DeviceIdType.MESH
-    )
-    pl.semaphore_wait(barrier, 3)
-
-
-def pair_kernel(left_ref, right_ref, out_ref, *scratch):
-    barrier = pltpu.get_barrier_semaphore()
-    other = 1 - lax.axis_index("core")
-    pl.semaphore_signal(
-        barrier, inc=1, device_id={"core": other}, device_id_type=pl.DeviceIdType.MESH
-    )
-    pl.semaphore_wait(barrier, 1)
-    pair = PairProduct(left_ref, right_ref, out_ref, *scratch)
+    pl.semaphore_wait(barrier, 1 + len(peers))
+    copies = back_copies(g_ref, moved_ref, peers, *scratch[5:]) if moving else []
+    for copy in copies:
+        copy.start()
+    pair = PairProduct(left_ref, right_ref, out_ref, *scratch[:5])
     for step in pair.steps():
         step()
     pair.finish()
-
-
-def pair_product(left, right, groups):
+    for copy in copies:
+        copy.wait()
+
+
+def pair_product(left, right, groups, number, moving=None):
     shape = pair_shape(left, right, groups)
     whole = pl.BlockSpec(memory_space=pltpu.VMEM)
+    hbm = pl.BlockSpec(memory_space=pltpu.HBM)
+    moves = [] if moving is None else [moving]
     return pl.pallas_call(
-        pair_kernel,
-        out_shape=jax.ShapeDtypeStruct(shape, BF16),
-        in_specs=[whole] * 2,
-        out_specs=pl.BlockSpec(memory_space=pl.ANY),
-        scratch_shapes=pair_scratch(shape),
-        compiler_params=kernel_params(7, 32),
-        cost_estimate=pl.CostEstimate(flops=10**10, bytes_accessed=10**7, transcendentals=0),
+        functools.partial(pair_kernel, len(moves) > 0),
+        out_shape=[jax.ShapeDtypeStruct(shape, BF16)]
+        + [jax.ShapeDtypeStruct(m.shape, BF16) for m in moves],
+        in_specs=[whole] * 2 + [hbm] * len(moves),
+        out_specs=[hbm] * (1 + len(moves)),
+        scratch_shapes=pair_scratch(shape) + back_scratch() * len(moves),
+        compiler_params=kernel_params(number, 28),
+        cost_estimate=pl.CostEstimate(flops=10**6, bytes_accessed=10**4, transcendentals=0),
         name="pair_product",
-    )(left, right)
+    )(left, right, *moves)
 
 
 def branch_kernel(
     partial_ref,
     hidden_ref,
     upstream_ref,
-    left_ref,
-    right_ref,
     active_ref,
     down_ref,
     grad_ref,
     gain_grad_ref,
     down_out_ref,
-    pair_ref,
     out_ref,
     *scratch,
 ):
-    greet_square_and_core()
+    greet_heads(square(lax.axis_index("head"))[:2])
     mine_ref, *sems = scratch[6:10]
     gain_grad_ref[...] = jnp.zeros_like(gain_grad_ref)
-    pair = PairProduct(left_ref, right_ref, pair_ref, *scratch[10:])
 
     def done(rows, total):
         hidden = hidden_ref[rows, :]
@@ -870,33 +865,27 @@
         down_out_ref[rows, :] = matmul(active_ref[rows, :], down_ref[...]).astype(BF16)
 
     share = Share(mine_ref, out_ref, *sems)
-    fillers = pair.steps()
-    fillers += [functools.partial(down, at) for at in range(0, active_ref.shape[0], LANES)]
+    fillers = [functools.partial(down, at) for at in range(0, active_ref.shape[0], LANES)]
     turn_rows(partial_ref, *scratch[:6], done, share, fillers)
-    pair.finish()
-
-
-def share_branch(partial, hidden, upstream, left, right, active, down, groups):
+
+
+def share_branch(partial, hidden, upstream, active, down):
     whole = pl.BlockSpec(memory_space=pltpu.VMEM)
-    shape = pair_shape(left, right, groups)
     return pl.pallas_call(
         branch_kernel,
         out_shape=[
             jax.ShapeDtypeStruct(hidden.shape, F32),
             jax.ShapeDtypeStruct((1, hidden.shape[1]), F32),
             jax.ShapeDtypeStruct((active.shape[0], down.shape[1]), BF16),
-            jax.ShapeDtypeStruct(shape, BF16),
             jax.ShapeDtypeStruct((H,) + hidden.shape, BF16),
         ],
-        in_specs=[whole] * 7,
-        out_specs=[whole] * 3 + [pl.BlockSpec(memory_space=pl.ANY)] * 2,
-        scratch_shapes=turn_scratch(*hidden.shape)
-        + share_scratch(*hidden.shape)
-        + pair_scratch(shape),
-        compiler_params=kernel_params(6, 54),
-        cost_estimate=pl.CostEstimate(flops=8 * 10**10, bytes_accessed=10**7, transcendentals=0),
+        in_specs=[whole] * 5,
+        out_specs=[whole] * 3 + [pl.BlockSpec(memory_space=pltpu.HBM)],
+        scratch_shapes=turn_scratch(*hidden.shape) + share_scratch(*hidden.shape),
+        compiler_params=kernel_params(6, 34),
+        cost_estimate=pl.CostEstimate(flops=10**6, bytes_accessed=10**4, transcendentals=0),
         name="share_branch",
-    )(partial, hidden, upstream, left, right, active, down)
+    )(partial, hidden, upstream, active, down)
 
 
 def tokens_kernel(partial_ref, tokens_ref, upstream_ref, grad_ref, gain_grad_ref, *scratch):
@@ -924,8 +913,8 @@
         in_specs=[whole] * 3,
         out_specs=[whole] * 2,
         scratch_shapes=turn_scratch(*tokens.shape),
-        compiler_params=kernel_params(8, 24),
-        cost_estimate=pl.CostEstimate(flops=4 * 10**10, bytes_accessed=10**7, transcendentals=0),
+        compiler_params=kernel_params(8, 18),
+        cost_estimate=pl.CostEstimate(flops=10**6, bytes_accessed=10**4, transcendentals=0),
         name="tokens_back",
     )(partial, tokens, upstream)
 
@@ -957,40 +946,45 @@
             rows_block(pre.shape[1]),
         ],
         out_specs=rows_block(pre.shape[1]),
-        compiler_params=pltpu.CompilerParams(vmem_limit_bytes=40 * 2**20),
-        cost_estimate=pl.CostEstimate(flops=10**10, bytes_accessed=10**7, transcendentals=0),
+        compiler_params=pltpu.CompilerParams(vmem_limit_bytes=32 * 2**20),
+        cost_estimate=pl.CostEstimate(flops=10**6, bytes_accessed=10**4, transcendentals=0),
         name="hidden_units_back",
     )(cot, down, pre)
 
 
-def columns_kernel(g_ref, out_ref, send_sem, recv_sem, own_sem):
+def back_copies(g_ref, out_ref, peers, send_sem, recv_sem, own_sem):
     me = lax.axis_index("head")
-    peers = [lax.rem(me + ahead, H) for ahead in range(1, H)]
-    greet_heads(peers)
     copies = [
         head_copy(g_ref.at[peer], out_ref.at[me], send_sem.at[ahead], recv_sem.at[ahead], peer)
         for ahead, peer in enumerate(peers)
     ]
-    copies.append(pltpu.make_async_copy(g_ref.at[me], out_ref.at[me], own_sem))
+    return copies + [pltpu.make_async_copy(g_ref.at[me], out_ref.at[me], own_sem)]
+
+
+def back_scratch():
+    return [pltpu.SemaphoreType.DMA((H,)), pltpu.SemaphoreType.DMA((H,)), pltpu.SemaphoreType.DMA]
+
+
+def columns_kernel(g_ref, out_ref, *sems):
+    me = lax.axis_index("head")
+    peers = [lax.rem(me + ahead, H) for ahead in range(1, H)]
+    greet_heads(peers)
+    copies = back_copies(g_ref, out_ref, peers, *sems)
     for copy in copies:
         copy.start()
     for copy in copies:
         copy.wait()
 
 
-def columns_back(g, number):
+def columns_back(g):
     return pl.pallas_call(
         columns_kernel,
         out_shape=jax.ShapeDtypeStruct(g.shape, BF16),
-        in_specs=[pl.BlockSpec(memory_space=pl.ANY)],
-        out_specs=pl.BlockSpec(memory_space=pl.ANY),
-        scratch_shapes=[
-            pltpu.SemaphoreType.DMA((H,)),
-            pltpu.SemaphoreType.DMA((H,)),
-            pltpu.SemaphoreType.DMA,
-        ],
-        compiler_params=kernel_params(number, 16),
-        cost_estimate=pl.CostEstimate(flops=10**10, bytes_accessed=10**6, transcendentals=0),
+        in_specs=[pl.BlockSpec(memory_space=pltpu.HBM)],
+        out_specs=pl.BlockSpec(memory_space=pltpu.HBM),
+        scratch_shapes=back_scratch(),
+        compiler_params=kernel_params(10, 16),
+        cost_estimate=pl.CostEstimate(flops=10**6, bytes_accessed=10**4, transcendentals=0),
         name="columns_back",
     )(g)
 
@@ -1013,12 +1007,12 @@
         functools.partial(forward_kernel, key_dim, value_dim),
         out_shape=[jax.ShapeDtypeStruct(*s) for s in shapes],
         in_specs=[whole] * 8,
-        out_specs=[whole] + [pl.BlockSpec(memory_space=pl.ANY)] * (len(shapes) - 1),
+        out_specs=[whole] + [pl.BlockSpec(memory_space=pltpu.HBM)] * (len(shapes) - 1),
         scratch_shapes=[pltpu.VMEM(*s) for s in shapes[1:-1]]
         + state_scratch(count, value_dim, key_dim)
         + [pltpu.SemaphoreType.DMA((count, 7))],
-        compiler_params=kernel_params(1, 30),
-        cost_estimate=pl.CostEstimate(flops=5 * 10**10, bytes_accessed=10**7, transcendentals=0),
+        compiler_params=kernel_params(1, 26),
+        cost_estimate=pl.CostEstimate(flops=10**6, bytes_accessed=10**4, transcendentals=0),
         name="mix_forward",
     )(mixed, bias, gaterank, gain, marks, segment, sums, pairs)
 
@@ -1040,14 +1034,14 @@
     return pl.pallas_call(
         functools.partial(backward_kernel, key_dim, value_dim),
         out_shape=[jax.ShapeDtypeStruct(*s) for s in shapes],
-        in_specs=[pl.BlockSpec(memory_space=pl.ANY)] * 9 + [whole] * 6,
+        in_specs=[pl.BlockSpec(memory_space=pltpu.HBM)] * 9 + [whole] * 6,
         out_specs=[whole] * len(shapes),
         scratch_shapes=[pltpu.VMEM(a.shape, a.dtype) for a in given]
         + [pltpu.VMEM((rows, value_dim), BF16)]
         + state_scratch(count, value_dim, key_dim)
         + [pltpu.SemaphoreType.DMA((count, 9))],
-        compiler_params=kernel_params(2, 36),
-        cost_estimate=pl.CostEstimate(flops=8 * 10**10, bytes_accessed=10**7, transcendentals=0),
+        compiler_params=kernel_params(2, 34),
+        cost_estimate=pl.CostEstimate(flops=10**6, bytes_accessed=10**4, transcendentals=0),
         name="mix_backward",
     )(
         *given,
@@ -1146,11 +1140,9 @@
 
     mix_moved = mix_weights((w_query, w_key, w_value, w_outgate), extra, norm_gain[:, None])
     inputs = tokens.reshape(-1, width)
-    inputs, _ = after(inputs, mix_moved)
+    inputs, w_output, w_down, _ = after(inputs, w_output, w_down, mix_moved)
+    mix_w = gather_columns(mix_moved)
     output_w = gather_part(w_output)
-    mix_moved, output_w = after(mix_moved, output_w)
-    mix_w = gather_columns(mix_moved)
-    w_down, _ = after(w_down, mix_moved)
     down_w = gather_part(w_down)
     normed, ffn_moved = share_tokens(inputs, w_gate, w_up, ffn_gain[:, None])
     normed = normed.reshape(-1, width)
@@ -1193,7 +1185,7 @@
         mixed, bias, gaterank, gain_head, marks, segment, sums, pairs, key_dim, value_dim
     )
     cot_rows, _ = after(cotangent.reshape(-1, width), normed)
-    gated, cot_shared, down_w = after(gated, share_rows(cot_rows), down_w)
+    gated, cot_shared, output_w, down_w = after(gated, share_rows(cot_rows), output_w, down_w)
     ffn_moved, _ = after(ffn_moved, gated)
     ffn_w = gather_columns(ffn_moved)
     partial = matmul(gated, output_w).astype(BF16).reshape(H, -1, width)
@@ -1210,17 +1202,12 @@
     grad_pre = hidden_units_back(cot_shared, down_w, pre)
     grad_pre, grad_down_w = after(grad_pre, pair_part(grad_down_w))
     grad_down_w = scatter_part(grad_down_w)
+    (grad_ffn_w,) = pair_product(normed_two, grad_pre, reps * H, 7)
+    grad_pre, grad_ffn_w = after(grad_pre, grad_ffn_w)
     partial = back_product(grad_pre, ffn_w).astype(BF16)
 
-    grad_hidden, grad_gain_two, down_partial, grad_ffn_w, branch = share_branch(
-        partial.reshape(H, -1, width),
-        hidden,
-        cot_rows,
-        normed_two,
-        grad_pre,
-        activated,
-        down_w,
-        reps * H,
+    grad_hidden, grad_gain_two, down_partial, branch = share_branch(
+        partial.reshape(H, -1, width), hidden, cot_rows, activated, down_w
     )
     grad_ffn_w = scatter_rows(grad_ffn_w)
     branch = branch.reshape(-1, width)
@@ -1243,14 +1230,15 @@
         key_dim,
         value_dim,
     )
-    grad_mixed, pieces, grad_down_w = after(grad_mixed, pieces, grad_down_w)
+    grad_mixed, pieces, grad_down_w, grad_ffn_w = after(
+        grad_mixed, pieces, grad_down_w, grad_ffn_w
+    )
     output = (hidden + jnp.sum(pieces.astype(F32), axis=0)).astype(BF16).reshape(tokens.shape)
-    grad_mix_w = pair_product(normed, grad_mixed, reps * H)
+    grad_mix_w, grad_ffn_w = pair_product(normed, grad_mixed, reps * H, 11, grad_ffn_w)
     grad_mixed, grad_mix_w = after(grad_mixed, grad_mix_w)
     partial = back_product(grad_mixed, mix_w).astype(BF16)
     grad_mix_w = scatter_rows(grad_mix_w)
-    grad_ffn_w = columns_back(grad_ffn_w, 9)
-    partial, grad_ffn_w, grad_output_w = after(partial, grad_ffn_w, grad_output_w)
+    partial, grad_output_w = after(partial, grad_output_w)
     tokens_grad, grad_gain_one = tokens_back(partial.reshape(H, -1, width), inputs, grad_hidden)
     tokens_grad = tokens_grad.reshape(tokens.shape)
 
@@ -1261,7 +1249,7 @@
 
     w_gate_grad = weight_grad(grad_ffn_w, ffn_gain, 0, w_gate)
     w_up_grad = weight_grad(grad_ffn_w, ffn_gain, w_gate.shape[1] // H, w_up)
-    grad_mix_w = columns_back(grad_mix_w, 10)
+    grad_mix_w = columns_back(grad_mix_w)
     query_g = weight_grad(grad_mix_w, norm_gain, 0, w_query)
     key_g = weight_grad(grad_mix_w, norm_gain, key_dim, w_key)
     value_g = weight_grad(grad_mix_w, norm_gain, 2 * key_dim, w_value)

time: 767 us -> 738 us (0.962)
  Pallas kernels: 486 us -> 432 us
  local copies, waits for them, and re-layouts: 71.7 us -> 88.8 us
  waiting for transfers between devices: 63.8 us -> 73.3 us
    pallas_call x1, Pallas kernels: 98.8 us -> 66.3 us  [mix_backward(): pl.pallas_call(functools.partial(backward_kernel, key_dim, value_dim), ou...]
    pallas_call x1 -> x2, Pallas kernels: 10.4 us -> 34.8 us  [pair_product(): pl.pallas_call(functools.partial(pair_kernel, len(moves) > 0), out_shape=...]
    pallas_call x2 -> x1, Pallas kernels: 31.5 us -> 13.1 us  [columns_back(): pl.pallas_call(columns_kernel, out_shape=jax.ShapeDtypeStruct(g.shape, BF...]
    unnamed x134 -> x140, local copies, waits for them, and re-layouts: 51.8 us -> 67.5 us
    pallas_call x1, Pallas kernels: 23.8 us -> 11 us  [hidden_units_back(): pl.pallas_call(hidden_units_kernel, grid=(rows // size,), out_shape=jax.S...]
    all_gather x2, waiting for transfers between devices: 11.5 us -> 23.1 us  [gather_part(): return lax.all_gather(w, SHARE, axis=0, tiled=True)]
    pallas_call x1, Pallas kernels: 88.3 us -> 78.7 us  [share_branch(): pl.pallas_call(branch_kernel, out_shape=[jax.ShapeDtypeStruct(hidden.shap...]
    pallas_call x1, Pallas kernels: 47.9 us -> 39.2 us  [mix_forward(): pl.pallas_call(functools.partial(forward_kernel, key_dim, value_dim), out...]
  transfers between devices with their start and end apart: 13 -> 13, of which waited for: 4 -> 2; matrix products, arithmetic and copies ran while one was open for 11% -> 13% of each run, Pallas kernels for 62% -> 55%
where the time goes in v5:
time: 738 us; the launch traced here: 730 us
  Pallas kernels  432 us (59%)
  local copies, waits for them, and re-layouts  88.8 us (12%)
  matrix products  78.5 us (11%)
  waiting for transfers between devices  73.3 us (10%)
  other arithmetic  29.5 us (4%)
  between operations  15.3 us (2%)
  starting transfers between devices  12.9 us (2%)
    pallas_call x1, Pallas kernels, share_branch(): pl.pallas_call(branch_kernel, out_shape=[jax.ShapeDtypeStruct(hidden.shap...  78.7 us
    dot_general x8, matrix products, dot(): lax.dot_general(a, b, (dims, ((), ())), precision=precision, preferred_el...  78.5 us
    pallas_call x1, Pallas kernels, share_hidden(): pl.pallas_call(hidden_kernel, out_shape=[jax.ShapeDtypeStruct(tokens.shap...  76 us
    unnamed x140, local copies, waits for them, and re-layouts  67.5 us
    pallas_call x1, Pallas kernels, mix_backward(): pl.pallas_call(functools.partial(backward_kernel, key_dim, value_dim), ou...  66.3 us
    pallas_call x1, Pallas kernels, share_tokens(): pl.pallas_call(share_kernel, out_shape=[jax.ShapeDtypeStruct((H,) + token...  53.4 us
    all_gather x2, waiting for transfers between devices, gather_columns(): whole = lax.all_gather(moved, ('core', 'fsdp'), axis=1, tiled=True)  48.7 us
    pallas_call x1, Pallas kernels, tokens_back(): pl.pallas_call(tokens_kernel, out_shape=[jax.ShapeDtypeStruct(tokens.shap...  45.1 us
  transfers between devices with their start and end apart: 13, of which 2 were waited for; matrix products, arithmetic and copies ran while one was open for 13% of the time, Pallas kernels for 55%

profile of v5, /device:TPU:0, one launch (start us, length us, event | category | flops | bytes accessed | tf_op | source)
XLA Modules:
  0.0 730.2 jit_solution(16335257437569725417)
XLA Ops:
  14.8 14.4 %mix_weights.1 = bf16[4,64,1664]{2,1,0:T(8,128)(2,1)} custom-call(bf16[64,1024]{1,0:T(8,128)(2,1)S(1)} %copy-done.48, bf16[64,1024]{1,0:T(8,128)(2,1)S(1)} %copy-done.49, bf16[64,2048]{1,0:T(8,128)(2,1)S(1)} %copy-done.46, bf16[64,2048]{1,0:T(8,128)(2,1)S(1)} %copy-done.47, bf16[64,128]{1,0:T(8,128)(2,1)S(1)} %pad_add_fusion.refs_4_, ...), custom_call_target="tpu_custom_call" | custom-call | flops 1000000 | bytes 10000 | tf_op jit(solution)/shard_map/mix_weights/pallas_call | solution.py:505
  33.8 53.4 %share_tokens.1 = (bf16[4,256,2048]{2,1,0:T(8,128)(2,1)S(1)}, bf16[4,64,2816]{2,1,0:T(8,128)(2,1)S(1)}) custom-call(bf16[256,2048]{1,0:T(8,128)(2,1)S(1)} %bitcast.107, bf16[64,5632]{1,0:T(8,128)(2,1)S(1)} %copy-done.38, bf16[64,5632]{1,0:T(8,128)(2,1)S(1)} %copy-done.39, bf16[64,1]{1,0:T(8,128)(2,1)S(1)} %copy.113.gain_ref), custom_call_target="tpu_custom_call" | custom-call | flops 1000000 | bytes 10000 | tf_op jit(solution)/shard_map/share_tokens/pallas_call | solution.py:608
  92.8 4.9 all-to-all-start
  114.2 11.6 %fusion.59.mixed_ref.refs_0_ = f32[1024,1664]{1,0:T(8,128)S(1)} fusion(bf16[1024,2048]{1,0:T(8,128)(2,1)} %bitcast.112, bf16[2048,1664]{1,0:T(8,128)(2,1)} %bitcast.138), kind=kOutput, calls=%fused_computation.174 | convolution fusion | flops 6979321856 | bytes 17825792 | tf_op jit(solution)/shard_map/dot_general | solution.py:31
  125.8 39.2 %mix_forward.1 = (bf16[1024,512]{1,0:T(8,128)(2,1)S(1)}, f32[1024,512]{1,0:T(8,128)S(1)}, f32[1024,256]{1,0:T(8,128)S(1)}, bf16[4,256,256]{2,1,0:T(8,128)(2,1)S(...) custom-call(f32[1024,1664]{1,0:T(8,128)S(1)} %fusion.59.mixed_ref.re, ...), custom_call_target="tpu_custom_call" | custom-call | flops 1000000 | bytes 10000 | tf_op jit(solution)/shard_map/mix_forward/pallas_call | solution.py:1006
  174.5 23.1 %all-gather.9.cloned.1.call-done.down_ref = bf16[1408,2048]{1,0:T(8,128)(2,1)} async-done(((bf16[176,2048]{1,0:T(8,128)(2,1)}), bf16[1408,2048]{1,0:T(8,128)(2,1)}) %all-gather.9.cloned.1.call-update) | async-done | bytes 5767184 | tf_op jit(solution)/shard_map/all_gather | solution.py:1107
  197.6 4.3 convolution_convert_fusion.3
  201.9 76.0 %share_hidden.1 = (f32[256,2048]{1,0:T(8,128)S(1)}, bf16[4,256,2048]{2,1,0:T(8,128)(2,1)S(1)}) custom-call(bf16[4,256,2048]{2,1,0:T(8,128)(2,1)S(1)} %bitcast.111, bf16[256,2048]{1,0:T(8,128)(2,1)S(1)} %bitcast.108), custom_call_target="tpu_custom_call" | custom-call | flops 1000000 | bytes 10000 | tf_op jit(solution)/shard_map/share_hidden/pallas_call | solution.py:712
  281.2 48.7 %all-gather.11.cloned.1.call-done = bf16[4,512,2816]{2,1,0:T(8,128)(2,1)} async-done(((bf16[4,64,2816]{2,1,0:T(8,128)(2,1)}), bf16[4,512,2816]{2,1,0:T(8,128)(2,1)}) %all-gather.11.cloned.1.call-update) | async-done | bytes 11534352 | tf_op jit(solution)/shard_map/all_gather | solution.py:1100
  329.8 17.2 %fusion.60.pre_ref = f32[1024,2816]{1,0:T(8,128)S(1)} fusion(bf16[1024,2048]{1,0:T(8,128)(2,1)} %bitcast.115, bf16[2048,2816]{1,0:T(8,128)(2,1)} %bitcast.152), kind=kOutput, calls=%fused_computation.175 | convolution fusion | flops 11811160064 | bytes 27262976 | tf_op jit(solution)/shard_map/dot_general | solution.py:31
  348.8 3.5 copy-done.52
  352.4 9.2 %convolution_convert_fusion = bf16[1408,2048]{1,0:T(8,128)(2,1)S(1)} fusion(bf16[1024,1408]{1,0:T(8,128)(2,1)S(1)} %fusion.active_ref, bf16[1024,2048]{1,0:T(8,128)(2,1)} %bitcast.14.cot_ref), kind=kOutput, calls=%fused_computation.1 | convolution fusion | flops 5908463616 | bytes 12845056 | tf_op jit(solution)/shard_map/dot_general | solution.py:31
  364.3 11.0 %hidden_units_back.1.right_ref = bf16[1024,2816]{1,0:T(8,128)(2,1)S(1)} custom-call(bf16[1024,2048]{1,0:T(8,128)(2,1)} %bitcast.14.cot_ref, bf16[1408,2048]{1,0:T(8,128)(2,1)S(1)} %bitcast.106, f32[1024,2816]{1,0:T(8,128)} %copy-done.52), custom_call_target="tpu_custom_call" | custom-call | flops 1000000 | bytes 10000 | tf_op jit(solution)/shard_map/hidden_units_back/pallas_call | solution.py:939
  386.1 16.4 %pair_product.2 = bf16[4,256,2816]{2,1,0:T(8,128)(2,1)S(1)} custom-call(bf16[1024,2048]{1,0:T(8,128)(2,1)S(1)} %bitcast.116, bf16[1024,2816]{1,0:T(8,128)(2,1)S(1)} %copy-done.3), custom_call_target="tpu_custom_call" | custom-call | flops 1000000 | bytes 10000 | tf_op jit(solution)/shard_map/pair_product/pallas_call | solution.py:826
  405.0 16.8 %convolution_convert_fusion.1 = bf16[1024,2048]{1,0:T(8,128)(2,1)S(1)} fusion(bf16[1024,2816]{1,0:T(8,128)(2,1)} %copy-done.2, bf16[2048,2816]{1,0:T(8,128)(2,1)} %bitcast.153), kind=kOutput, calls=%fused_computation.6 | convolution fusion | flops 11813257216 | bytes 21495808 | tf_op jit(solution)/shard_map/dot_general | solution.py:31
  423.1 78.7 %share_branch.1 = (f32[256,2048]{1,0:T(8,128)S(1)}, f32[1,2048]{1,0:T(1,128)S(1)}, bf16[1024,2048]{1,0:T(8,128)(2,1)S(1)}, bf16[4,256,2048]{2,1,0:T(8,128)(2,1)S(1)}) custom-call(bf16[4,256,2048]{2,1,0:T(8,128)(2,1)S(1)} %bitcast.117, f32[256,2048]{1,0:T(8,128)S(1)} %copy-done.8, bf16[256,2048]{1,0:T(8,128)(2,1)S(1)} %bitcast.119, ...), custom_call_target="tpu_custom_call" | custom-call | flops 1000000 | bytes 10000 | tf_op jit(solution)/shard_map/share_branch/pallas_call | solution.py:874
  501.8 3.7 fusion.61.refs_1_
  510.3 4.8 all-to-all-start.1
  528.1 66.3 %mix_backward.1 = (bf16[1024,1664]{1,0:T(8,128)(2,1)S(1)}, f32[1,512]{1,0:T(1,128)S(1)}, f32[1,256]{1,0:T(1,128)S(1)}, f32[16,256]{1,0:T(8,128)S(1)}) custom-call(f32[1024,1664]{1,0:T(8,128)} %copy-done, f32[1024,512]{1,0:T(8,128)S(1)} %copy-done.27, f32[1024,512]{1,0:T(8,128)S(1)} %copy-done.24, bf16[1024,256]{1,0:T(8,128)(2,1)S(1)} %copy-done.43, ...), custom_call_target="tpu_custom_call" | custom-call | flops 1000000 | bytes 10000 | tf_op jit(solution)/shard_map/mix_backward/pallas_call | solution.py:1034
  601.7 18.4 %pair_product.3 = (bf16[4,256,1664]{2,1,0:T(8,128)(2,1)S(1)}, bf16[4,64,2816]{2,1,0:T(8,128)(2,1)S(1)}) custom-call(bf16[1024,2048]{1,0:T(8,128)(2,1)S(1)} %bitcast.113, bf16[1024,1664]{1,0:T(8,128)(2,1)S(1)} %copy-done.21, bf16[4,64,2816]{2,1,0:T(8,128)(2,1)S(1)} %copy-done.28), custom_call_target="tpu_custom_call" | custom-call | flops 1000000 | bytes 10000 | tf_op jit(solution)/shard_map/pair_product/pallas_call | solution.py:826
  625.7 13.3 %convolution_convert_fusion.2 = bf16[1024,2048]{1,0:T(8,128)(2,1)} fusion(bf16[1024,1664]{1,0:T(8,128)(2,1)} %copy-done.20, bf16[2048,1664]{1,0:T(8,128)(2,1)} %bitcast.139), kind=kOutput, calls=%fused_computation.7 | convolution fusion | flops 6981419008 | bytes 14417920 | tf_op jit(solution)/shard_map/dot_general | solution.py:31
  641.4 45.1 %tokens_back.1 = (bf16[256,2048]{1,0:T(8,128)(2,1)S(1)}, f32[1,2048]{1,0:T(1,128)S(1)}) custom-call(bf16[4,256,2048]{2,1,0:T(8,128)(2,1)S(1)} %bitcast.110, bf16[256,2048]{1,0:T(8,128)(2,1)S(1)} %bitcast.109, f32[256,2048]{1,0:T(8,128)S(1)} %copy-done.26), custom_call_target="tpu_custom_call" | custom-call | flops 1000000 | bytes 10000 | tf_op jit(solution)/shard_map/tokens_back/pallas_call | solution.py:907
  693.4 3.3 convert_reduce_fusion
  705.9 13.1 %columns_back.1 = bf16[4,64,1664]{2,1,0:T(8,128)(2,1)S(1)} custom-call(bf16[4,64,1664]{2,1,0:T(8,128)(2,1)S(1)} %copy-done.37), custom_call_target="tpu_custom_call" | custom-call | flops 1000000 | bytes 10000 | tf_op jit(solution)/shard_map/columns_back/pallas_call | solution.py:980
  (274 shorter events, 118.6 us)
Async XLA Ops:
  7.2 24.4 %copy-start.6 = (bf16[1,256,2048]{2,1,0:T(8,128)(2,1)S(1)}, bf16[1,256,2048]{2,1,0:T(8,128)(2,1)}, u32[]{:S(2)}) copy-start(bf16[1,256,2048]{2,1,0:T(8,128)(2,1)} %param.17) | copy-start | bytes 3145732
  7.2 83.0 %copy-start.18 = (bf16[1,256,2048]{2,1,0:T(8,128)(2,1)S(1)}, bf16[1,256,2048]{2,1,0:T(8,128)(2,1)}, u32[]{:S(2)}) copy-start(bf16[1,256,2048]{2,1,0:T(8,128)(2,1)} %param.33) | copy-start | bytes 3145732
  7.2 93.3 %all-gather.5.cloned.1.call-start = ((), (), s32[]{:S(2)}) async-start(), calls=%async_computation.7 | async-start | bytes 7667712 | tf_op jit(solution)/shard_map/all_gather | solution.py:1100
  9.5 83.3 %copy-start.59 = (f32[64]{0:T(128)}, f32[64]{0:T(128)S(1)}, u32[]{:S(2)}) copy-start(f32[64]{0:T(128)S(1)} %convert_element_type.244) | copy-start | bytes 772
  29.3 145.2 %all-gather.7.cloned.1.call-start = ((), (), s32[]{:S(2)}) async-start(), calls=%async_computation.8 | async-start | bytes 2359296 | tf_op jit(solution)/shard_map/all_gather | solution.py:1107
  30.0 167.5 %all-gather.9.cloned.1.call-start = ((), (), s32[]{:S(2)}) async-start(), calls=%async_computation.9 | async-start | bytes 6488064 | tf_op jit(solution)/shard_map/all_gather | solution.py:1107
  92.8 81.6 %all-to-all-start = ((bf16[4,256,2048]{2,1,0:T(8,128)(2,1)}), bf16[4,256,2048]{2,1,0:T(8,128)(2,1)}, u32[]{:S(2)}, u32[]{:S(2)}) async-start(bf16[4,256,2048]{2,1,0:T(8,128)(2,1)} %broadcast_in_dim.106), calls=%async_computation | async-start | bytes 8388608 | tf_op jit(solution)/shard_map/all_to_all | solution.py:64
  97.7 232.1 %all-gather.11.cloned.1.call-start = ((), (), s32[]{:S(2)}) async-start(), calls=%async_computation.10 | async-start | bytes 12976128 | tf_op jit(solution)/shard_map/all_gather | solution.py:1100
  197.6 320.6 %reduce-scatter.5.cloned.1.call-start = ((), (), s32[]{:S(2)}) async-start(), calls=%async_computation.11 | async-start | bytes 3604480 | tf_op jit(solution)/shard_map/reduce_scatter | solution.py:1117
  347.0 17.3 %slice-start = ((s8[5767168]{0:T(1024)(128)(4,1)}), s8[4194304]{0:T(1024)(128)(4,1)S(1)}, s32[]{:S(2)}) async-start(s8[5767168]{0:T(1024)(128)(4,1)} %bitcast.105), calls=%async_computation.15 | async-start | bytes 8388608
  364.1 13.8 %collective-permute-start = (bf16[1,704,2048]{2,1,0:T(8,128)(2,1)S(1)}, bf16[1,704,2048]{2,1,0:T(8,128)(2,1)S(1)}, u32[]{:S(2)}, u32[]{:S(2)}) collective-permute-start(bf16[1,704,2048]{2,1,0:T(8,128)(2,1)S(1)} %dynamic-slice_bitcast_fusion), channel_id=1, source_target_pairs={{0,4},{4,0},{1,5},{5,1},{2,6},{6,2},{3,7},{7,3},{8,12},{12,8},{9,1... | collective-permute-start | bytes 8650760 | tf_op jit(solution)/shard_map/ppermute | solution.py:1091
  364.3 13.5 %copy-start.54 = (bf16[1408,2048]{1,0:T(8,128)(2,1)S(1)}, bf16[1408,2048]{1,0:T(8,128)(2,1)}, u32[]{:S(2)}) copy-start(bf16[1408,2048]{1,0:T(8,128)(2,1)} %copy-done.53) | copy-start | bytes 17301508
  380.8 215.3 %reduce-scatter.7.cloned.1.call-start = ((), (), s32[]{:S(2)}) async-start(), calls=%async_computation.12 | async-start | bytes 7208960 | tf_op jit(solution)/shard_map/reduce_scatter | solution.py:1097
  405.0 16.8 %copy-start.5 = (bf16[1024,1408]{1,0:T(8,128)(2,1)S(1)}, bf16[1024,1408]{1,0:T(8,128)(2,1)}, u32[]{:S(2)}) copy-start(bf16[1024,1408]{1,0:T(8,128)(2,1)} %copy-done.4) | copy-start | bytes 8650756
  405.0 16.8 %copy-start.8 = (f32[256,2048]{1,0:T(8,128)S(1)}, f32[256,2048]{1,0:T(8,128)}, u32[]{:S(2)}) copy-start(f32[256,2048]{1,0:T(8,128)} %copy-done.7) | copy-start | bytes 6291460
  423.1 78.7 %copy-start.63 = (bf16[512,2048]{1,0:T(8,128)(2,1)S(1)}, bf16[512,2048]{1,0:T(8,128)(2,1)}, u32[]{:S(2)}) copy-start(bf16[512,2048]{1,0:T(8,128)(2,1)} %all-gather.7.cloned.1.call-done) | copy-start | bytes 6291460
  510.3 4.9 collective-permute-start.1
  510.3 85.8 %all-to-all-start.1 = ((bf16[4,256,2048]{2,1,0:T(8,128)(2,1)}), bf16[4,256,2048]{2,1,0:T(8,128)(2,1)}, u32[]{:S(2)}, u32[]{:S(2)}) async-start(bf16[4,256,2048]{2,1,0:T(8,128)(2,1)} %bitcast.114), calls=%async_computation.2 | async-start | bytes 8388608 | tf_op jit(solution)/shard_map/all_to_all | solution.py:70
  515.2 124.0 %reduce-scatter.9.cloned.1.call-start = ((), (), s32[]{:S(2)}) async-start(), calls=%async_computation.13 | async-start | bytes 1310720 | tf_op jit(solution)/shard_map/reduce_scatter | solution.py:1117
  518.2 186.6 %reduce-scatter.11.cloned.1.call-start = ((), (), s32[]{:S(2)}) async-start(), calls=%async_computation.14 | async-start | bytes 4259840 | tf_op jit(solution)/shard_map/reduce_scatter | solution.py:1097
  601.7 21.3 %copy-start.61 = (bf16[64]{0:T(256)(128)(2,1)S(1)}, bf16[64]{0:T(256)(128)(2,1)}, u32[]{:S(2)}) copy-start(bf16[64]{0:T(256)(128)(2,1)} %param.29) | copy-start | bytes 388
  625.7 13.4 %copy-start.26 = (f32[256,2048]{1,0:T(8,128)S(1)}, f32[256,2048]{1,0:T(8,128)}, u32[]{:S(2)}) copy-start(f32[256,2048]{1,0:T(8,128)} %copy-done.25) | copy-start | bytes 6291460
  689.0 13.2 %all-to-all-start.2 = ((f32[32,1,688]{2,1,0:T(1,128)}), f32[32,1,688]{2,1,0:T(1,128)S(1)}, u32[]{:S(2)}, u32[]{:S(2)}) async-start(f32[32,1,688]{2,1,0:T(1,128)} %copy.118), calls=%async_computation.5 | async-start | bytes 196608 | tf_op jit(solution)/shard_map/all_to_all | solution.py:1278
  702.3 17.1 %copy-start.60 = (f32[64]{0:T(128)S(1)}, f32[64]{0:T(128)}, u32[]{:S(2)}) copy-start(f32[64]{0:T(128)} %copy-done.59) | copy-start | bytes 772
  (55 other events, 128.7 us)
Sparse Core Ops, SparseCore 0:
  29.4 70.1 all-gather.4
  101.2 27.7 all-gather.6
  130.6 66.8 all-gather.8
  199.6 130.2 all-gather.10
  380.9 54.4 reduce-scatter.4
  437.6 102.6 reduce-scatter.6
  543.1 39.1 reduce-scatter.8
  623.1 62.4 reduce-scatter.10

commit v6 on v5

--- a/solution.py
+++ b/solution.py
@@ -173,7 +173,7 @@
 def forward_kernel(
     key_dim,
     value_dim,
-    mixed_ref,
+    given_ref,
     bias_ref,
     gaterank_ref,
     gain_ref,
@@ -185,7 +185,7 @@
     *refs,
 ):
     kept, (attended_ref, logits_ref, scores_ref, start_ref, end_ref, decay_ref) = refs[:7], refs[7:13]
-    local_ref, send_ref, recv_ref, send_sem, recv_sem, keep_sem = refs[13:]
+    local_ref, send_ref, recv_ref, send_sem, recv_sem, keep_sem, mixed_ref, take_sem = refs[13:]
     count, _, length = segment_ref.shape
     levels = pairs_ref.shape[0]
     parts, place = lax.axis_size("fsdp"), lax.axis_index("fsdp")
@@ -201,6 +201,16 @@
             at = rows if len(held[kind].shape) == 2 else s
             yield pltpu.make_async_copy(held[kind].at[at], kept[kind].at[at], keep_sem.at[s, kind])
 
+    def take(s):
+        rows = rows_of(s)
+        return pltpu.make_async_copy(given_ref.at[rows], mixed_ref.at[rows], take_sem.at[s])
+
+    def start_take(s, carry):
+        take(s).start()
+        return carry
+
+    lax.fori_loop(0, count, start_take, 0)
+
     def finish_keeps(s, carry):
         for copy in keeps(s, range(7)):
             copy.wait()
@@ -220,6 +230,7 @@
 
     def ends(s, carry):
         rows = rows_of(s)
+        take(s).wait()
         lowrank = mixed_ref[rows, pl.ds(rank_at, rank)]
         logits = dot(lowrank, gaterank_ref[...], ((1,), (0,)), HIGHEST) + bias_ref[...]
         logits_ref[rows, :] = logits
@@ -506,7 +517,7 @@
         mix_weights_kernel,
         out_shape=jax.ShapeDtypeStruct((H, rows, n), BF16),
         in_specs=[pl.BlockSpec(memory_space=pltpu.VMEM)] * (len(weights) + 2),
-        out_specs=pl.BlockSpec(memory_space=pltpu.HBM),
+        out_specs=pl.BlockSpec(memory_space=pl.ANY),
         scratch_shapes=[
             pltpu.VMEM((H, rows, n), BF16),
             pltpu.SemaphoreType.DMA((H,)),
@@ -612,7 +623,7 @@
             jax.ShapeDtypeStruct((H, rows, n), BF16),
         ],
         in_specs=[pl.BlockSpec(memory_space=pltpu.VMEM)] * 4,
-        out_specs=[pl.BlockSpec(memory_space=pltpu.HBM)] * 2,
+        out_specs=[pl.BlockSpec(memory_space=pl.ANY)] * 2,
         scratch_shapes=share_scratch(*tokens.shape)
         + [
             pltpu.VMEM((H, rows, n), BF16),
@@ -716,7 +727,7 @@
             jax.ShapeDtypeStruct((H,) + tokens.shape, BF16),
         ],
         in_specs=[whole] * 2,
-        out_specs=[whole, pl.BlockSpec(memory_space=pltpu.HBM)],
+        out_specs=[whole, pl.BlockSpec(memory_space=pl.ANY)],
         scratch_shapes=turn_scratch(*tokens.shape) + share_scratch(*tokens.shape),
         compiler_params=kernel_params(5, 18),
         cost_estimate=pl.CostEstimate(flops=10**6, bytes_accessed=10**4, transcendentals=0),
@@ -821,7 +832,7 @@
 def pair_product(left, right, groups, number, moving=None):
     shape = pair_shape(left, right, groups)
     whole = pl.BlockSpec(memory_space=pltpu.VMEM)
-    hbm = pl.BlockSpec(memory_space=pltpu.HBM)
+    hbm = pl.BlockSpec(memory_space=pl.ANY)
     moves = [] if moving is None else [moving]
     return pl.pallas_call(
         functools.partial(pair_kernel, len(moves) > 0),
@@ -830,7 +841,7 @@
         in_specs=[whole] * 2 + [hbm] * len(moves),
         out_specs=[hbm] * (1 + len(moves)),
         scratch_shapes=pair_scratch(shape) + back_scratch() * len(moves),
-        compiler_params=kernel_params(number, 28),
+        compiler_params=kernel_params(number, 58),
         cost_estimate=pl.CostEstimate(flops=10**6, bytes_accessed=10**4, transcendentals=0),
         name="pair_product",
     )(left, right, *moves)
@@ -842,6 +853,7 @@
     upstream_ref,
     active_ref,
     down_ref,
+    rest_ref,
     grad_ref,
     gain_grad_ref,
     down_out_ref,
@@ -862,30 +874,33 @@
 
     def down(at):
         rows = pl.ds(at, LANES)
-        down_out_ref[rows, :] = matmul(active_ref[rows, :], down_ref[...]).astype(BF16)
+        half = down_ref.shape[1]
+        for place, ref in ((0, down_ref), (half, rest_ref)):
+            product = matmul(active_ref[rows, :], ref[...])
+            down_out_ref[rows, pl.ds(place, half)] = product.astype(BF16)
 
     share = Share(mine_ref, out_ref, *sems)
     fillers = [functools.partial(down, at) for at in range(0, active_ref.shape[0], LANES)]
     turn_rows(partial_ref, *scratch[:6], done, share, fillers)
 
 
-def share_branch(partial, hidden, upstream, active, down):
+def share_branch(partial, hidden, upstream, active, down, rest):
     whole = pl.BlockSpec(memory_space=pltpu.VMEM)
     return pl.pallas_call(
         branch_kernel,
         out_shape=[
             jax.ShapeDtypeStruct(hidden.shape, F32),
             jax.ShapeDtypeStruct((1, hidden.shape[1]), F32),
-            jax.ShapeDtypeStruct((active.shape[0], down.shape[1]), BF16),
+            jax.ShapeDtypeStruct((active.shape[0], hidden.shape[1]), BF16),
             jax.ShapeDtypeStruct((H,) + hidden.shape, BF16),
         ],
-        in_specs=[whole] * 5,
-        out_specs=[whole] * 3 + [pl.BlockSpec(memory_space=pltpu.HBM)],
+        in_specs=[whole] * 6,
+        out_specs=[whole] * 3 + [pl.BlockSpec(memory_space=pl.ANY)],
         scratch_shapes=turn_scratch(*hidden.shape) + share_scratch(*hidden.shape),
         compiler_params=kernel_params(6, 34),
         cost_estimate=pl.CostEstimate(flops=10**6, bytes_accessed=10**4, transcendentals=0),
         name="share_branch",
-    )(partial, hidden, upstream, active, down)
+    )(partial, hidden, upstream, active, down, rest)
 
 
 def tokens_kernel(partial_ref, tokens_ref, upstream_ref, grad_ref, gain_grad_ref, *scratch):
@@ -919,9 +934,10 @@
     )(partial, tokens, upstream)
 
 
-def hidden_units_kernel(cot_ref, down_ref, pre_ref, out_ref):
-    units = down_ref.shape[0]
-    grad = back_product(cot_ref[...], down_ref[...])
+def hidden_units_kernel(cot_ref, down_ref, rest_ref, pre_ref, out_ref):
+    units, half = down_ref.shape
+    grad = back_product(cot_ref[:, pl.ds(0, half)], down_ref[...])
+    grad += back_product(cot_ref[:, pl.ds(half, half)], rest_ref[...])
     gate, up = pre_ref[:, pl.ds(0, units)], pre_ref[:, pl.ds(units, units)]
     sig = jax.nn.sigmoid(gate)
     grad_sig = grad * sig
@@ -929,7 +945,7 @@
     out_ref[:, pl.ds(units, units)] = (grad_sig * gate).astype(BF16)
 
 
-def hidden_units_back(cot, down, pre):
+def hidden_units_back(cot, down, rest, pre):
     rows, width = cot.shape
     size = 2 * LANES
 
@@ -943,13 +959,14 @@
         in_specs=[
             rows_block(width),
             pl.BlockSpec(down.shape, lambda i: (0, 0)),
+            pl.BlockSpec(rest.shape, lambda i: (0, 0)),
             rows_block(pre.shape[1]),
         ],
         out_specs=rows_block(pre.shape[1]),
-        compiler_params=pltpu.CompilerParams(vmem_limit_bytes=32 * 2**20),
+        compiler_params=pltpu.CompilerParams(vmem_limit_bytes=58 * 2**20),
         cost_estimate=pl.CostEstimate(flops=10**6, bytes_accessed=10**4, transcendentals=0),
         name="hidden_units_back",
-    )(cot, down, pre)
+    )(cot, down, rest, pre)
 
 
 def back_copies(g_ref, out_ref, peers, send_sem, recv_sem, own_sem):
@@ -963,30 +980,6 @@
 
 def back_scratch():
     return [pltpu.SemaphoreType.DMA((H,)), pltpu.SemaphoreType.DMA((H,)), pltpu.SemaphoreType.DMA]
-
-
-def columns_kernel(g_ref, out_ref, *sems):
-    me = lax.axis_index("head")
-    peers = [lax.rem(me + ahead, H) for ahead in range(1, H)]
-    greet_heads(peers)
-    copies = back_copies(g_ref, out_ref, peers, *sems)
-    for copy in copies:
-        copy.start()
-    for copy in copies:
-        copy.wait()
-
-
-def columns_back(g):
-    return pl.pallas_call(
-        columns_kernel,
-        out_shape=jax.ShapeDtypeStruct(g.shape, BF16),
-        in_specs=[pl.BlockSpec(memory_space=pltpu.HBM)],
-        out_specs=pl.BlockSpec(memory_space=pltpu.HBM),
-        scratch_shapes=back_scratch(),
-        compiler_params=kernel_params(10, 16),
-        cost_estimate=pl.CostEstimate(flops=10**6, bytes_accessed=10**4, transcendentals=0),
-        name="columns_back",
-    )(g)
 
 
 def mix_forward(mixed, bias, gaterank, gain, marks, segment, sums, pairs, key_dim, value_dim):
@@ -1006,12 +999,16 @@
     return pl.pallas_call(
         functools.partial(forward_kernel, key_dim, value_dim),
         out_shape=[jax.ShapeDtypeStruct(*s) for s in shapes],
-        in_specs=[whole] * 8,
-        out_specs=[whole] + [pl.BlockSpec(memory_space=pltpu.HBM)] * (len(shapes) - 1),
+        in_specs=[pl.BlockSpec(memory_space=pl.ANY)] + [whole] * 7,
+        out_specs=[whole] + [pl.BlockSpec(memory_space=pl.ANY)] * (len(shapes) - 1),
         scratch_shapes=[pltpu.VMEM(*s) for s in shapes[1:-1]]
         + state_scratch(count, value_dim, key_dim)
-        + [pltpu.SemaphoreType.DMA((count, 7))],
-        compiler_params=kernel_params(1, 26),
+        + [
+            pltpu.SemaphoreType.DMA((count, 7)),
+            pltpu.VMEM(mixed.shape, mixed.dtype),
+            pltpu.SemaphoreType.DMA((count,)),
+        ],
+        compiler_params=kernel_params(1, 58),
         cost_estimate=pl.CostEstimate(flops=10**6, bytes_accessed=10**4, transcendentals=0),
         name="mix_forward",
     )(mixed, bias, gaterank, gain, marks, segment, sums, pairs)
@@ -1034,13 +1031,13 @@
     return pl.pallas_call(
         functools.partial(backward_kernel, key_dim, value_dim),
         out_shape=[jax.ShapeDtypeStruct(*s) for s in shapes],
-        in_specs=[pl.BlockSpec(memory_space=pltpu.HBM)] * 9 + [whole] * 6,
+        in_specs=[pl.BlockSpec(memory_space=pl.ANY)] * 9 + [whole] * 6,
         out_specs=[whole] * len(shapes),
         scratch_shapes=[pltpu.VMEM(a.shape, a.dtype) for a in given]
         + [pltpu.VMEM((rows, value_dim), BF16)]
         + state_scratch(count, value_dim, key_dim)
         + [pltpu.SemaphoreType.DMA((count, 9))],
-        compiler_params=kernel_params(2, 34),
+        compiler_params=kernel_params(2, 58),
         cost_estimate=pl.CostEstimate(flops=10**6, bytes_accessed=10**4, transcendentals=0),
         name="mix_backward",
     )(
@@ -1140,10 +1137,12 @@
 
     mix_moved = mix_weights((w_query, w_key, w_value, w_outgate), extra, norm_gain[:, None])
     inputs = tokens.reshape(-1, width)
-    inputs, w_output, w_down, _ = after(inputs, w_output, w_down, mix_moved)
+    inputs, _ = after(inputs, mix_moved)
+    output_w = gather_part(w_output)
+    mix_moved, output_w = after(mix_moved, output_w)
     mix_w = gather_columns(mix_moved)
-    output_w = gather_part(w_output)
-    down_w = gather_part(w_down)
+    w_down, _ = after(w_down, mix_moved)
+    down_w = gather_part(w_down[:, : width // 2])
     normed, ffn_moved = share_tokens(inputs, w_gate, w_up, ffn_gain[:, None])
     normed = normed.reshape(-1, width)
 
@@ -1185,9 +1184,10 @@
         mixed, bias, gaterank, gain_head, marks, segment, sums, pairs, key_dim, value_dim
     )
     cot_rows, _ = after(cotangent.reshape(-1, width), normed)
-    gated, cot_shared, output_w, down_w = after(gated, share_rows(cot_rows), output_w, down_w)
-    ffn_moved, _ = after(ffn_moved, gated)
+    gated, cot_shared, down_w = after(gated, share_rows(cot_rows), down_w)
+    ffn_moved, w_down_rest, _ = after(ffn_moved, w_down[:, width // 2 :], gated)
     ffn_w = gather_columns(ffn_moved)
+    down_rest = gather_part(w_down_rest)
     partial = matmul(gated, output_w).astype(BF16).reshape(H, -1, width)
     hidden, normed_two = share_hidden(partial, inputs)
     normed_two = normed_two.reshape(-1, width)
@@ -1199,7 +1199,7 @@
 
     grad_down_w = rows_product(activated, cot_shared).astype(BF16)
     down_w, grad_down_w = after(down_w, grad_down_w)
-    grad_pre = hidden_units_back(cot_shared, down_w, pre)
+    grad_pre = hidden_units_back(cot_shared, down_w, down_rest, pre)
     grad_pre, grad_down_w = after(grad_pre, pair_part(grad_down_w))
     grad_down_w = scatter_part(grad_down_w)
     (grad_ffn_w,) = pair_product(normed_two, grad_pre, reps * H, 7)
@@ -1207,7 +1207,7 @@
     partial = back_product(grad_pre, ffn_w).astype(BF16)
 
     grad_hidden, grad_gain_two, down_partial, branch = share_branch(
-        partial.reshape(H, -1, width), hidden, cot_rows, activated, down_w
+        partial.reshape(H, -1, width), hidden, cot_rows, activated, down_w, down_rest
     )
     grad_ffn_w = scatter_rows(grad_ffn_w)
     branch = branch.reshape(-1, width)
@@ -1249,7 +1249,7 @@
 
     w_gate_grad = weight_grad(grad_ffn_w, ffn_gain, 0, w_gate)
     w_up_grad = weight_grad(grad_ffn_w, ffn_gain, w_gate.shape[1] // H, w_up)
-    grad_mix_w = columns_back(grad_mix_w)
+    grad_mix_w = lax.all_to_all(grad_mix_w, "head", split_axis=0, concat_axis=0, tiled=True)
     query_g = weight_grad(grad_mix_w, norm_gain, 0, w_query)
     key_g = weight_grad(grad_mix_w, norm_gain, key_dim, w_key)
     value_g = weight_grad(grad_mix_w, norm_gain, 2 * key_dim, w_value)

time: 738 us -> 696 us (0.943)
  local copies, waits for them, and re-layouts: 88.8 us -> 41.6 us
  waiting for transfers between devices: 73.3 us -> 64.7 us
    unnamed x140 -> x94, local copies, waits for them, and re-layouts: 67.5 us -> 22.7 us
    pallas_call x1 -> x0, Pallas kernels: 13.1 us -> none  [columns_back(): pl.pallas_call(columns_kernel, out_shape=jax.ShapeDtypeStruct(g.shape, BF...]
    pallas_call x1, Pallas kernels: 66.3 us -> 76.4 us  [mix_backward(): pl.pallas_call(functools.partial(backward_kernel, key_dim, value_dim), ou...]
    all_gather x2, waiting for transfers between devices: 48.7 us -> 40.5 us  [gather_columns(): whole = lax.all_gather(moved, ('core', 'fsdp'), axis=1, tiled=True)]
    all_gather x2 -> x3, waiting for transfers between devices: 23.1 us -> 16.9 us  [gather_part(): return lax.all_gather(w, SHARE, axis=0, tiled=True)]
  transfers between devices with their start and end apart: 13 -> 15, of which waited for: 2 -> 4; matrix products, arithmetic and copies ran while one was open for 13% -> 19% of each run, Pallas kernels for 55% -> 62%
where the time goes in v6:
time: 696 us; the launch traced here: 688 us
  Pallas kernels  430 us (62%)
  matrix products  83 us (12%)
  waiting for transfers between devices  64.7 us (9%)
  local copies, waits for them, and re-layouts  41.6 us (6%)
  other arithmetic  36.6 us (5%)
  starting transfers between devices  17.7 us (3%)
  between operations  14.9 us (2%)
    dot_general x8, matrix products, dot(): lax.dot_general(a, b, (dims, ((), ())), precision=precision, preferred_el...  83 us
    pallas_call x1, Pallas kernels, share_branch(): pl.pallas_call(branch_kernel, out_shape=[jax.ShapeDtypeStruct(hidden.shap...  78.9 us
    pallas_call x1, Pallas kernels, mix_backward(): pl.pallas_call(functools.partial(backward_kernel, key_dim, value_dim), ou...  76.4 us
    pallas_call x1, Pallas kernels, share_hidden(): pl.pallas_call(hidden_kernel, out_shape=[jax.ShapeDtypeStruct(tokens.shap...  75.2 us
    pallas_call x1, Pallas kernels, share_tokens(): pl.pallas_call(share_kernel, out_shape=[jax.ShapeDtypeStruct((H,) + token...  53.7 us
    pallas_call x2, Pallas kernels, pair_product(): pl.pallas_call(functools.partial(pair_kernel, len(moves) > 0), out_shape=...  42.1 us
    pallas_call x1, Pallas kernels, tokens_back(): pl.pallas_call(tokens_kernel, out_shape=[jax.ShapeDtypeStruct(tokens.shap...  42 us
    all_gather x2, waiting for transfers between devices, gather_columns(): whole = lax.all_gather(moved, ('core', 'fsdp'), axis=1, tiled=True)  40.5 us
  transfers between devices with their start and end apart: 15, of which 4 were waited for; matrix products, arithmetic and copies ran while one was open for 19% of the time, Pallas kernels for 62%

profile of v6, /device:TPU:0, one launch (start us, length us, event | category | flops | bytes accessed | tf_op | source)
XLA Modules:
  0.0 688.4 jit_solution(11989875743497079197)
XLA Ops:
  15.4 14.4 %mix_weights.1 = bf16[4,64,1664]{2,1,0:T(8,128)(2,1)} custom-call(bf16[64,1024]{1,0:T(8,128)(2,1)S(1)} %copy-done.22, bf16[64,1024]{1,0:T(8,128)(2,1)S(1)} %copy-done.23, bf16[64,2048]{1,0:T(8,128)(2,1)S(1)} %copy-done.20, bf16[64,2048]{1,0:T(8,128)(2,1)S(1)} %copy-done.21, bf16[64,128]{1,0:T(8,128)(2,1)S(1)} %pad_add_fusion.refs_4_, ...), custom_call_target="tpu_custom_call" | custom-call | flops 1000000 | bytes 10000 | tf_op jit(solution)/shard_map/mix_weights/pallas_call | solution.py:516
  29.9 11.6 %all-gather.6.cloned.1.call-done = bf16[512,2048]{1,0:T(8,128)(2,1)} async-done(((bf16[64,2048]{1,0:T(8,128)(2,1)}), bf16[512,2048]{1,0:T(8,128)(2,1)}) %all-gather.6.cloned.1.call-update) | async-done | bytes 2097168 | tf_op jit(solution)/shard_map/all_gather | solution.py:1104
  45.7 53.7 %share_tokens.1 = (bf16[4,256,2048]{2,1,0:T(8,128)(2,1)S(1)}, bf16[4,64,2816]{2,1,0:T(8,128)(2,1)}) custom-call(bf16[256,2048]{1,0:T(8,128)(2,1)S(1)} %bitcast.105, bf16[64,5632]{1,0:T(8,128)(2,1)S(1)} %copy-done.18, bf16[64,5632]{1,0:T(8,128)(2,1)S(1)} %copy-done.19, bf16[64,1]{1,0:T(8,128)(2,1)S(1)} %copy.113.gain_ref), custom_call_target="tpu_custom_call" | custom-call | flops 1000000 | bytes 10000 | tf_op jit(solution)/shard_map/share_tokens/pallas_call | solution.py:619
  103.8 5.0 all-to-all-start
  121.0 13.3 %fusion.60.given_ref.refs_0_ = f32[1024,1664]{1,0:T(8,128)} fusion(bf16[1024,2048]{1,0:T(8,128)(2,1)} %bitcast.110, bf16[2048,1664]{1,0:T(8,128)(2,1)} %bitcast.133), kind=kOutput, calls=%fused_computation.175 | convolution fusion | flops 6979321856 | bytes 17825792 | tf_op jit(solution)/shard_map/dot_general | solution.py:31
  134.3 33.4 %mix_forward.1 = (bf16[1024,512]{1,0:T(8,128)(2,1)}, f32[1024,512]{1,0:T(8,128)}, f32[1024,256]{1,0:T(8,128)}, bf16[4,256,256]{2,1,0:T(8,128)(2,1)}, bf16[1024,2...) custom-call(f32[1024,1664]{1,0:T(8,128)} %fusion.60.given_ref.refs_0_, ...), custom_call_target="tpu_custom_call" | custom-call | flops 1000000 | bytes 10000 | tf_op jit(solution)/shard_map/mix_forward/pallas_call | solution.py:999
  171.5 75.2 %share_hidden.1 = (f32[256,2048]{1,0:T(8,128)S(1)}, bf16[4,256,2048]{2,1,0:T(8,128)(2,1)S(1)}) custom-call(bf16[4,256,2048]{2,1,0:T(8,128)(2,1)S(1)} %bitcast.109, bf16[256,2048]{1,0:T(8,128)(2,1)S(1)} %bitcast.106), custom_call_target="tpu_custom_call" | custom-call | flops 1000000 | bytes 10000 | tf_op jit(solution)/shard_map/share_hidden/pallas_call | solution.py:723
  250.5 40.5 %all-gather.12.cloned.1.call-done = bf16[4,512,2816]{2,1,0:T(8,128)(2,1)} async-done(((bf16[4,64,2816]{2,1,0:T(8,128)(2,1)}), bf16[4,512,2816]{2,1,0:T(8,128)(2,1)}) %all-gather.12.cloned.1.call-update) | async-done | bytes 11534352 | tf_op jit(solution)/shard_map/all_gather | solution.py:1097
  291.0 17.2 %fusion.61.pre_ref = f32[1024,2816]{1,0:T(8,128)S(1)} fusion(bf16[1024,2048]{1,0:T(8,128)(2,1)} %bitcast.113, bf16[2048,2816]{1,0:T(8,128)(2,1)} %bitcast.148), kind=kOutput, calls=%fused_computation.176 | convolution fusion | flops 11811160064 | bytes 27262976 | tf_op jit(solution)/shard_map/dot_general | solution.py:31
  312.3 8.1 %convolution_convert_fusion = bf16[1408,2048]{1,0:T(8,128)(2,1)S(1)} fusion(bf16[1024,1408]{1,0:T(8,128)(2,1)S(1)} %fusion.active_ref, bf16[1024,2048]{1,0:T(8,128)(2,1)} %bitcast.14.cot_ref), kind=kOutput, calls=%fused_computation.1 | convolution fusion | flops 5908463616 | bytes 12845056 | tf_op jit(solution)/shard_map/dot_general | solution.py:31
  325.0 5.2 all-gather.14.cloned.1.call-done.rest_ref
  330.2 13.8 %hidden_units_back.1.right_ref = bf16[1024,2816]{1,0:T(8,128)(2,1)} custom-call(bf16[1024,2048]{1,0:T(8,128)(2,1)} %bitcast.14.cot_ref, bf16[1408,1024]{1,0:T(8,128)(2,1)} %all-gather.10.cloned.1.call-done.down_ref, bf16[1408,1024]{1,0:T(8,128)(2,1)} %all-gather.14.cloned.1.call-done.rest_ref, f32[1024,2816]{1,0:T(8,128)} %copy-done.24), custom_call_target="tpu_custom_call" | custom-call | flops 1000000 | bytes 10000 | tf_op jit(solution)/shard_map/hidden_units_back/pallas_call | solution.py:955
  344.1 5.6 fusion.2
  349.9 20.2 %pair_product.2 = bf16[4,256,2816]{2,1,0:T(8,128)(2,1)} custom-call(bf16[1024,2048]{1,0:T(8,128)(2,1)} %bitcast.114, bf16[1024,2816]{1,0:T(8,128)(2,1)} %hidden_units_back.1.right_ref), custom_call_target="tpu_custom_call" | custom-call | flops 1000000 | bytes 10000 | tf_op jit(solution)/shard_map/pair_product/pallas_call | solution.py:837
  370.3 18.3 %convolution_convert_fusion.1 = bf16[1024,2048]{1,0:T(8,128)(2,1)} fusion(bf16[1024,2816]{1,0:T(8,128)(2,1)} %hidden_units_back.1.right_ref, bf16[2048,2816]{1,0:T(8,128)(2,1)} %bitcast.149), kind=kOutput, calls=%fused_computation.6 | convolution fusion | flops 11813257216 | bytes 21495808 | tf_op jit(solution)/shard_map/dot_general | solution.py:31
  388.7 78.9 %share_branch.1 = (f32[256,2048]{1,0:T(8,128)S(1)}, f32[1,2048]{1,0:T(1,128)S(1)}, bf16[1024,2048]{1,0:T(8,128)(2,1)S(1)}, bf16[4,256,2048]{2,1,0:T(8,128)(2,1)}) custom-call(bf16[4,256,2048]{2,1,0:T(8,128)(2,1)} %bitcast.122, f32[256,2048]{1,0:T(8,128)S(1)} %copy-done.6, bf16[256,2048]{1,0:T(8,128)(2,1)S(1)} %bitcast.116, ...), custom_call_target="tpu_custom_call" | custom-call | flops 1000000 | bytes 10000 | tf_op jit(solution)/shard_map/share_branch/pallas_call | solution.py:889
  467.6 8.1 %fusion.62.refs_1_ = f32[1024,512]{1,0:T(8,128)} fusion(bf16[1024,2048]{1,0:T(8,128)(2,1)} %bitcast.150, bf16[512,2048]{1,0:T(8,128)(2,1)S(1)} %copy-done.41), kind=kOutput, calls=%fused_computation.177 | convolution fusion | flops 2147483648 | bytes 8388608 | tf_op jit(solution)/shard_map/dot_general | solution.py:31
  478.8 4.8 all-to-all-start.1
  486.3 76.4 %mix_backward.1 = (bf16[1024,1664]{1,0:T(8,128)(2,1)}, f32[1,512]{1,0:T(1,128)}, f32[1,256]{1,0:T(1,128)}, f32[16,256]{1,0:T(8,128)}) custom-call(f32[1024,1664]{1,0:T(8,128)} %fusion.60.given_ref.refs_0_, f32[1024,512]{1,0:T(8,128)} %fusion.62.refs_1_, f32[1024,512]{1,0:T(8,128)} %get-tuple-element.93.refs_2_, bf16[1024,256]{1,0:T(8,128)(2,1)} %get-tuple-element.94.refs_3_, ...), custom_call_target="tpu_custom_call" | custom-call | flops 1000000 | bytes 10000 | tf_op jit(solution)/shard_map/mix_backward/pallas_call | solution.py:1031
  562.8 21.9 %pair_product.3 = (bf16[4,256,1664]{2,1,0:T(8,128)(2,1)}, bf16[4,64,2816]{2,1,0:T(8,128)(2,1)}) custom-call(bf16[1024,2048]{1,0:T(8,128)(2,1)} %bitcast.111, bf16[1024,1664]{1,0:T(8,128)(2,1)} %get-tuple-element.108.right_ref, bf16[4,64,2816]{2,1,0:T(8,128)(2,1)} %reduce-scatter.7.cloned.1.call-done.refs_0_), custom_call_target="tpu_custom_call" | custom-call | flops 1000000 | bytes 10000 | tf_op jit(solution)/shard_map/pair_product/pallas_call | solution.py:837
  590.9 11.5 %convolution_convert_fusion.2 = bf16[1024,2048]{1,0:T(8,128)(2,1)} fusion(bf16[1024,1664]{1,0:T(8,128)(2,1)S(1)} %copy-done.28, bf16[2048,1664]{1,0:T(8,128)(2,1)} %bitcast.134), kind=kOutput, calls=%fused_computation.7 | convolution fusion | flops 6981419008 | bytes 14417920 | tf_op jit(solution)/shard_map/dot_general | solution.py:31
  604.6 42.0 %tokens_back.1 = (bf16[256,2048]{1,0:T(8,128)(2,1)S(1)}, f32[1,2048]{1,0:T(1,128)S(1)}) custom-call(bf16[4,256,2048]{2,1,0:T(8,128)(2,1)S(1)} %bitcast.108, bf16[256,2048]{1,0:T(8,128)(2,1)S(1)} %bitcast.107, f32[256,2048]{1,0:T(8,128)S(1)} %copy-done.15), custom_call_target="tpu_custom_call" | custom-call | flops 1000000 | bytes 10000 | tf_op jit(solution)/shard_map/tokens_back/pallas_call | solution.py:922
  657.1 4.7 convert_reduce_fusion
  671.1 6.5 all-to-all-done.3
  (232 shorter events, 83.1 us)
Async XLA Ops:
  7.2 94.1 %copy-start.12 = (bf16[1,256,2048]{2,1,0:T(8,128)(2,1)S(1)}, bf16[1,256,2048]{2,1,0:T(8,128)(2,1)}, u32[]{:S(2)}) copy-start(bf16[1,256,2048]{2,1,0:T(8,128)(2,1)} %param.33) | copy-start | bytes 3145732
  7.2 34.3 %all-gather.6.cloned.1.call-start = ((), (), s32[]{:S(2)}) async-start(), calls=%async_computation.8 | async-start | bytes 2359296 | tf_op jit(solution)/shard_map/all_gather | solution.py:1104
  7.9 106.6 %all-gather.8.cloned.1.call-start = ((), (), s32[]{:S(2)}) async-start(), calls=%async_computation.9 | async-start | bytes 7667712 | tf_op jit(solution)/shard_map/all_gather | solution.py:1097
  8.6 92.7 %copy-start.33 = (f32[64]{0:T(128)}, f32[64]{0:T(128)S(1)}, u32[]{:S(2)}) copy-start(f32[64]{0:T(128)S(1)} %convert_element_type.244) | copy-start | bytes 772
  103.8 63.9 %all-to-all-start = ((bf16[4,256,2048]{2,1,0:T(8,128)(2,1)}), bf16[4,256,2048]{2,1,0:T(8,128)(2,1)}, u32[]{:S(2)}, u32[]{:S(2)}) async-start(bf16[4,256,2048]{2,1,0:T(8,128)(2,1)} %broadcast_in_dim.106), calls=%async_computation | async-start | bytes 8388608 | tf_op jit(solution)/shard_map/all_to_all | solution.py:64
  108.8 58.9 %all-gather.10.cloned.1.call-start = ((), (), s32[]{:S(2)}) async-start(), calls=%async_computation.10 | async-start | bytes 3244032 | tf_op jit(solution)/shard_map/all_gather | solution.py:1104
  111.7 179.3 %all-gather.12.cloned.1.call-start = ((), (), s32[]{:S(2)}) async-start(), calls=%async_computation.11 | async-start | bytes 12976128 | tf_op jit(solution)/shard_map/all_gather | solution.py:1097
  134.3 33.5 %copy-start.40 = (bf16[512,2048]{1,0:T(8,128)(2,1)S(1)}, bf16[512,2048]{1,0:T(8,128)(2,1)}, u32[]{:S(2)}) copy-start(bf16[512,2048]{1,0:T(8,128)(2,1)} %all-gather.6.cloned.1.call-done) | copy-start | bytes 6291460
  167.8 162.5 %all-gather.14.cloned.1.call-start = ((), (), s32[]{:S(2)}) async-start(), calls=%async_computation.12 | async-start | bytes 3244032 | tf_op jit(solution)/shard_map/all_gather | solution.py:1104
  250.0 236.2 %reduce-scatter.5.cloned.1.call-start = ((), (), s32[]{:S(2)}) async-start(), calls=%async_computation.13 | async-start | bytes 3604480 | tf_op jit(solution)/shard_map/reduce_scatter | solution.py:1114
  324.8 19.3 %collective-permute-start = (bf16[1,704,2048]{2,1,0:T(8,128)(2,1)}, bf16[1,704,2048]{2,1,0:T(8,128)(2,1)}, u32[]{:S(2)}, u32[]{:S(2)}) collective-permute-start(bf16[1,704,2048]{2,1,0:T(8,128)(2,1)} %dynamic-slice_bitcast_fusion), channel_id=1, source_target_pairs={{0,4},{4,0},{1,5},{5,1},{2,6},{6,2},{3,7},{7,3},{8,12},{12,8},{9,1... | collective-permute-start | bytes 8650760 | tf_op jit(solution)/shard_map/ppermute | solution.py:1088
  349.7 213.1 %reduce-scatter.7.cloned.1.call-start = ((), (), s32[]{:S(2)}) async-start(), calls=%async_computation.14 | async-start | bytes 7208960 | tf_op jit(solution)/shard_map/reduce_scatter | solution.py:1094
  370.2 18.4 %copy-start = (bf16[1408,1024]{1,0:T(8,128)(2,1)S(1)}, bf16[1408,1024]{1,0:T(8,128)(2,1)}, u32[]{:S(2)}) copy-start(bf16[1408,1024]{1,0:T(8,128)(2,1)} %all-gather.10.cloned.1.call-done.down_ref) | copy-start | bytes 8650756
  370.2 18.4 %copy-start.1 = (bf16[1408,1024]{1,0:T(8,128)(2,1)S(1)}, bf16[1408,1024]{1,0:T(8,128)(2,1)}, u32[]{:S(2)}) copy-start(bf16[1408,1024]{1,0:T(8,128)(2,1)} %all-gather.14.cloned.1.call-done.rest_ref) | copy-start | bytes 8650756
  388.7 78.9 %copy-start.41 = (bf16[512,2048]{1,0:T(8,128)(2,1)S(1)}, bf16[512,2048]{1,0:T(8,128)(2,1)}, u32[]{:S(2)}) copy-start(bf16[512,2048]{1,0:T(8,128)(2,1)} %all-gather.6.cloned.1.call-done) | copy-start | bytes 6291460
  478.7 5.0 collective-permute-start.1
  478.8 84.0 %all-to-all-start.1 = ((bf16[4,256,2048]{2,1,0:T(8,128)(2,1)}), bf16[4,256,2048]{2,1,0:T(8,128)(2,1)}, u32[]{:S(2)}, u32[]{:S(2)}) async-start(bf16[4,256,2048]{2,1,0:T(8,128)(2,1)} %bitcast.112), calls=%async_computation.2 | async-start | bytes 8388608 | tf_op jit(solution)/shard_map/all_to_all | solution.py:70
  483.6 118.8 %reduce-scatter.9.cloned.1.call-start = ((), (), s32[]{:S(2)}) async-start(), calls=%async_computation.15 | async-start | bytes 1310720 | tf_op jit(solution)/shard_map/reduce_scatter | solution.py:1114
  486.3 175.5 %reduce-scatter.11.cloned.1.call-start = ((), (), s32[]{:S(2)}) async-start(), calls=%async_computation.16 | async-start | bytes 4259840 | tf_op jit(solution)/shard_map/reduce_scatter | solution.py:1094
  562.8 22.0 %copy-start.36 = (bf16[64]{0:T(256)(128)(2,1)S(1)}, bf16[64]{0:T(256)(128)(2,1)}, u32[]{:S(2)}) copy-start(bf16[64]{0:T(256)(128)(2,1)} %param.29) | copy-start | bytes 388
  562.8 23.2 %copy-start.32 = (f32[16,256]{1,0:T(8,128)S(1)}, f32[16,256]{1,0:T(8,128)}, u32[]{:S(2)}) copy-start(f32[16,256]{1,0:T(8,128)} %get-tuple-element.117) | copy-start | bytes 49156
  604.6 47.3 %copy-start.31 = (bf16[64,2048]{1,0:T(8,128)(2,1)S(1)}, bf16[64,2048]{1,0:T(8,128)(2,1)}, u32[]{:S(2)}) copy-start(bf16[64,2048]{1,0:T(8,128)(2,1)} %reduce-scatter.9.cloned.1.call-done) | copy-start | bytes 786436
  649.3 12.4 %all-to-all-start.2 = ((f32[32,1,688]{2,1,0:T(1,128)}), f32[32,1,688]{2,1,0:T(1,128)S(1)}, u32[]{:S(2)}, u32[]{:S(2)}) async-start(f32[32,1,688]{2,1,0:T(1,128)} %copy.118), calls=%async_computation.5 | async-start | bytes 196608 | tf_op jit(solution)/shard_map/all_to_all | solution.py:1278
  661.8 15.8 %all-to-all-start.3 = ((bf16[4,64,1664]{2,1,0:T(8,128)(2,1)}), bf16[4,64,1664]{2,1,0:T(8,128)(2,1)S(1)}, u32[]{:S(2)}, u32[]{:S(2)}) async-start(bf16[4,64,1664]{2,1,0:T(8,128)(2,1)} %reduce-scatter.11.cloned.1.call-done), calls=%async_computation.7 | async-start | bytes 1703936 | tf_op jit(solution)/shard_map/all_to_all | solution.py:1252
  (34 other events, 189.6 us)
Sparse Core Ops, SparseCore 0:
  9.6 31.7 all-gather.5
  43.1 68.5 all-gather.7
  113.8 34.7 all-gather.9
  167.9 123.0 all-gather.11
  293.0 37.2 all-gather.13
  349.8 54.4 reduce-scatter.4
  406.7 113.5 reduce-scatter.6
  523.1 36.3 reduce-scatter.8
  584.9 61.7 reduce-scatter.10

commit v7 on v6

--- a/solution.py
+++ b/solution.py
@@ -13,7 +13,7 @@
 DV = 512
 CORES = 2
 DOCS = 8
-PIECES = 2
+PIECES = 4
 LANES = 128
 CHUNKS = 8
 
@@ -807,44 +807,32 @@
     ]
 
 
-def pair_kernel(moving, left_ref, right_ref, *refs):
-    g_ref, out_ref, moved_ref, *scratch = refs if moving else (None, refs[0], None, *refs[1:])
-    core = 1 - lax.axis_index("core")
-    me = lax.axis_index("head")
-    peers = [lax.rem(me + ahead, H) for ahead in range(1, H)] if moving else []
+def pair_kernel(left_ref, right_ref, out_ref, *scratch):
     barrier = pltpu.get_barrier_semaphore()
-    for target in [{"core": core}] + [{"head": peer} for peer in peers]:
-        pl.semaphore_signal(
-            barrier, inc=1, device_id=target, device_id_type=pl.DeviceIdType.MESH
-        )
-    pl.semaphore_wait(barrier, 1 + len(peers))
-    copies = back_copies(g_ref, moved_ref, peers, *scratch[5:]) if moving else []
-    for copy in copies:
-        copy.start()
-    pair = PairProduct(left_ref, right_ref, out_ref, *scratch[:5])
+    other = 1 - lax.axis_index("core")
+    pl.semaphore_signal(
+        barrier, inc=1, device_id={"core": other}, device_id_type=pl.DeviceIdType.MESH
+    )
+    pl.semaphore_wait(barrier, 1)
+    pair = PairProduct(left_ref, right_ref, out_ref, *scratch)
     for step in pair.steps():
         step()
     pair.finish()
-    for copy in copies:
-        copy.wait()
-
-
-def pair_product(left, right, groups, number, moving=None):
+
+
+def pair_product(left, right, groups, number):
     shape = pair_shape(left, right, groups)
     whole = pl.BlockSpec(memory_space=pltpu.VMEM)
-    hbm = pl.BlockSpec(memory_space=pl.ANY)
-    moves = [] if moving is None else [moving]
     return pl.pallas_call(
-        functools.partial(pair_kernel, len(moves) > 0),
-        out_shape=[jax.ShapeDtypeStruct(shape, BF16)]
-        + [jax.ShapeDtypeStruct(m.shape, BF16) for m in moves],
-        in_specs=[whole] * 2 + [hbm] * len(moves),
-        out_specs=[hbm] * (1 + len(moves)),
-        scratch_shapes=pair_scratch(shape) + back_scratch() * len(moves),
+        pair_kernel,
+        out_shape=jax.ShapeDtypeStruct(shape, BF16),
+        in_specs=[whole] * 2,
+        out_specs=pl.BlockSpec(memory_space=pl.ANY),
+        scratch_shapes=pair_scratch(shape),
         compiler_params=kernel_params(number, 58),
         cost_estimate=pl.CostEstimate(flops=10**6, bytes_accessed=10**4, transcendentals=0),
         name="pair_product",
-    )(left, right, *moves)
+    )(left, right)
 
 
 def branch_kernel(
@@ -967,19 +955,6 @@
         cost_estimate=pl.CostEstimate(flops=10**6, bytes_accessed=10**4, transcendentals=0),
         name="hidden_units_back",
     )(cot, down, rest, pre)
-
-
-def back_copies(g_ref, out_ref, peers, send_sem, recv_sem, own_sem):
-    me = lax.axis_index("head")
-    copies = [
-        head_copy(g_ref.at[peer], out_ref.at[me], send_sem.at[ahead], recv_sem.at[ahead], peer)
-        for ahead, peer in enumerate(peers)
-    ]
-    return copies + [pltpu.make_async_copy(g_ref.at[me], out_ref.at[me], own_sem)]
-
-
-def back_scratch():
-    return [pltpu.SemaphoreType.DMA((H,)), pltpu.SemaphoreType.DMA((H,)), pltpu.SemaphoreType.DMA]
 
 
 def mix_forward(mixed, bias, gaterank, gain, marks, segment, sums, pairs, key_dim, value_dim):
@@ -1202,7 +1177,7 @@
     grad_pre = hidden_units_back(cot_shared, down_w, down_rest, pre)
     grad_pre, grad_down_w = after(grad_pre, pair_part(grad_down_w))
     grad_down_w = scatter_part(grad_down_w)
-    (grad_ffn_w,) = pair_product(normed_two, grad_pre, reps * H, 7)
+    grad_ffn_w = pair_product(normed_two, grad_pre, reps * H, 7)
     grad_pre, grad_ffn_w = after(grad_pre, grad_ffn_w)
     partial = back_product(grad_pre, ffn_w).astype(BF16)
 
@@ -1234,11 +1209,12 @@
         grad_mixed, pieces, grad_down_w, grad_ffn_w
     )
     output = (hidden + jnp.sum(pieces.astype(F32), axis=0)).astype(BF16).reshape(tokens.shape)
-    grad_mix_w, grad_ffn_w = pair_product(normed, grad_mixed, reps * H, 11, grad_ffn_w)
+    grad_mix_w = pair_product(normed, grad_mixed, reps * H, 11)
     grad_mixed, grad_mix_w = after(grad_mixed, grad_mix_w)
     partial = back_product(grad_mixed, mix_w).astype(BF16)
     grad_mix_w = scatter_rows(grad_mix_w)
-    partial, grad_output_w = after(partial, grad_output_w)
+    grad_ffn_w = lax.all_to_all(grad_ffn_w, "head", split_axis=0, concat_axis=0, tiled=True)
+    partial, grad_output_w, grad_ffn_w = after(partial, grad_output_w, grad_ffn_w)
     tokens_grad, grad_gain_one = tokens_back(partial.reshape(H, -1, width), inputs, grad_hidden)
     tokens_grad = tokens_grad.reshape(tokens.shape)
 

time: 696 us -> 698 us (level)
  Pallas kernels: 430 us -> 420 us
    pallas_call x2, Pallas kernels: 42.1 us -> 33.8 us  [pair_product(): pl.pallas_call(pair_kernel, out_shape=jax.ShapeDtypeStruct(shape, BF16),...]
    unnamed x94 -> x90, local copies, waits for them, and re-layouts: 22.7 us -> 22.3 us
  transfers between devices with their start and end apart: 15 -> 16, of which waited for: 4 -> 6; matrix products, arithmetic and copies ran while one was open for 19% -> 19% of each run, Pallas kernels for 62% -> 61%
where the time goes in v7:
time: 698 us; the launch traced here: 690 us
  Pallas kernels  420 us (60%)
  matrix products  83 us (12%)
  waiting for transfers between devices  71 us (10%)
  local copies, waits for them, and re-layouts  42 us (6%)
  other arithmetic  36.8 us (5%)
  starting transfers between devices  22.4 us (3%)
  between operations  15 us (2%)
    dot_general x8, matrix products, dot(): lax.dot_general(a, b, (dims, ((), ())), precision=precision, preferred_el...  83 us
    pallas_call x1, Pallas kernels, share_branch(): pl.pallas_call(branch_kernel, out_shape=[jax.ShapeDtypeStruct(hidden.shap...  78.9 us
    pallas_call x1, Pallas kernels, share_hidden(): pl.pallas_call(hidden_kernel, out_shape=[jax.ShapeDtypeStruct(tokens.shap...  75.2 us
    pallas_call x1, Pallas kernels, mix_backward(): pl.pallas_call(functools.partial(backward_kernel, key_dim, value_dim), ou...  74.5 us
    pallas_call x1, Pallas kernels, share_tokens(): pl.pallas_call(share_kernel, out_shape=[jax.ShapeDtypeStruct((H,) + token...  53.7 us
    pallas_call x1, Pallas kernels, tokens_back(): pl.pallas_call(tokens_kernel, out_shape=[jax.ShapeDtypeStruct(tokens.shap...  42.2 us
    all_gather x2, waiting for transfers between devices, gather_columns(): whole = lax.all_gather(moved, ('core', 'fsdp'), axis=1, tiled=True)  39.5 us
    pallas_call x2, Pallas kernels, pair_product(): pl.pallas_call(pair_kernel, out_shape=jax.ShapeDtypeStruct(shape, BF16),...  33.8 us
  transfers between devices with their start and end apart: 16, of which 6 were waited for; matrix products, arithmetic and copies ran while one was open for 19% of the time, Pallas kernels for 61%

profile of v7, /device:TPU:0, one launch (start us, length us, event | category | flops | bytes accessed | tf_op | source)
XLA Modules:
  0.0 690.4 jit_solution(201545406318322784)
XLA Ops:
  15.4 14.4 %mix_weights.1 = bf16[4,64,1664]{2,1,0:T(8,128)(2,1)} custom-call(bf16[64,1024]{1,0:T(8,128)(2,1)S(1)} %copy-done.22, bf16[64,1024]{1,0:T(8,128)(2,1)S(1)} %copy-done.23, bf16[64,2048]{1,0:T(8,128)(2,1)S(1)} %copy-done.20, bf16[64,2048]{1,0:T(8,128)(2,1)S(1)} %copy-done.21, bf16[64,128]{1,0:T(8,128)(2,1)S(1)} %pad_add_fusion.refs_4_, ...), custom_call_target="tpu_custom_call" | custom-call | flops 1000000 | bytes 10000 | tf_op jit(solution)/shard_map/mix_weights/pallas_call | solution.py:516
  29.9 11.6 %all-gather.6.cloned.1.call-done = bf16[512,2048]{1,0:T(8,128)(2,1)} async-done(((bf16[64,2048]{1,0:T(8,128)(2,1)}), bf16[512,2048]{1,0:T(8,128)(2,1)}) %all-gather.6.cloned.1.call-update) | async-done | bytes 2097168 | tf_op jit(solution)/shard_map/all_gather | solution.py:1079
  45.7 53.7 %share_tokens.1 = (bf16[4,256,2048]{2,1,0:T(8,128)(2,1)S(1)}, bf16[4,64,2816]{2,1,0:T(8,128)(2,1)}) custom-call(bf16[256,2048]{1,0:T(8,128)(2,1)S(1)} %bitcast.105, bf16[64,5632]{1,0:T(8,128)(2,1)S(1)} %copy-done.18, bf16[64,5632]{1,0:T(8,128)(2,1)S(1)} %copy-done.19, bf16[64,1]{1,0:T(8,128)(2,1)S(1)} %copy.113.gain_ref), custom_call_target="tpu_custom_call" | custom-call | flops 1000000 | bytes 10000 | tf_op jit(solution)/shard_map/share_tokens/pallas_call | solution.py:619
  103.8 5.0 all-to-all-start
  121.0 13.3 %fusion.60.given_ref.refs_0_ = f32[1024,1664]{1,0:T(8,128)} fusion(bf16[1024,2048]{1,0:T(8,128)(2,1)} %bitcast.110, bf16[2048,1664]{1,0:T(8,128)(2,1)} %bitcast.133), kind=kOutput, calls=%fused_computation.175 | convolution fusion | flops 6979321856 | bytes 17825792 | tf_op jit(solution)/shard_map/dot_general | solution.py:31
  134.3 33.6 %mix_forward.1 = (bf16[1024,512]{1,0:T(8,128)(2,1)}, f32[1024,512]{1,0:T(8,128)}, f32[1024,256]{1,0:T(8,128)}, bf16[4,256,256]{2,1,0:T(8,128)(2,1)}, bf16[1024,2...) custom-call(f32[1024,1664]{1,0:T(8,128)} %fusion.60.given_ref.refs_0_, ...), custom_call_target="tpu_custom_call" | custom-call | flops 1000000 | bytes 10000 | tf_op jit(solution)/shard_map/mix_forward/pallas_call | solution.py:974
  171.7 75.2 %share_hidden.1 = (f32[256,2048]{1,0:T(8,128)S(1)}, bf16[4,256,2048]{2,1,0:T(8,128)(2,1)S(1)}) custom-call(bf16[4,256,2048]{2,1,0:T(8,128)(2,1)S(1)} %bitcast.109, bf16[256,2048]{1,0:T(8,128)(2,1)S(1)} %bitcast.106), custom_call_target="tpu_custom_call" | custom-call | flops 1000000 | bytes 10000 | tf_op jit(solution)/shard_map/share_hidden/pallas_call | solution.py:723
  250.6 39.5 %all-gather.12.cloned.1.call-done = bf16[4,512,2816]{2,1,0:T(8,128)(2,1)} async-done(((bf16[4,64,2816]{2,1,0:T(8,128)(2,1)}), bf16[4,512,2816]{2,1,0:T(8,128)(2,1)}) %all-gather.12.cloned.1.call-update) | async-done | bytes 11534352 | tf_op jit(solution)/shard_map/all_gather | solution.py:1072
  290.1 17.2 %fusion.61.pre_ref = f32[1024,2816]{1,0:T(8,128)S(1)} fusion(bf16[1024,2048]{1,0:T(8,128)(2,1)} %bitcast.113, bf16[2048,2816]{1,0:T(8,128)(2,1)} %bitcast.148), kind=kOutput, calls=%fused_computation.176 | convolution fusion | flops 11811160064 | bytes 27262976 | tf_op jit(solution)/shard_map/dot_general | solution.py:31
  311.5 8.1 %convolution_convert_fusion = bf16[1408,2048]{1,0:T(8,128)(2,1)S(1)} fusion(bf16[1024,1408]{1,0:T(8,128)(2,1)S(1)} %fusion.active_ref, bf16[1024,2048]{1,0:T(8,128)(2,1)} %bitcast.14.cot_ref), kind=kOutput, calls=%fused_computation.1 | convolution fusion | flops 5908463616 | bytes 12845056 | tf_op jit(solution)/shard_map/dot_general | solution.py:31
  324.2 5.2 all-gather.14.cloned.1.call-done.rest_ref
  329.4 13.8 %hidden_units_back.1.right_ref = bf16[1024,2816]{1,0:T(8,128)(2,1)} custom-call(bf16[1024,2048]{1,0:T(8,128)(2,1)} %bitcast.14.cot_ref, bf16[1408,1024]{1,0:T(8,128)(2,1)} %all-gather.10.cloned.1.call-done.down_ref, bf16[1408,1024]{1,0:T(8,128)(2,1)} %all-gather.14.cloned.1.call-done.rest_ref, f32[1024,2816]{1,0:T(8,128)} %copy-done.24), custom_call_target="tpu_custom_call" | custom-call | flops 1000000 | bytes 10000 | tf_op jit(solution)/shard_map/hidden_units_back/pallas_call | solution.py:943
  343.2 5.6 fusion.2
  349.1 20.2 %pair_product.2 = bf16[4,256,2816]{2,1,0:T(8,128)(2,1)} custom-call(bf16[1024,2048]{1,0:T(8,128)(2,1)} %bitcast.114, bf16[1024,2816]{1,0:T(8,128)(2,1)} %hidden_units_back.1.right_ref), custom_call_target="tpu_custom_call" | custom-call | flops 1000000 | bytes 10000 | tf_op jit(solution)/shard_map/pair_product/pallas_call | solution.py:826
  369.4 18.4 %convolution_convert_fusion.1 = bf16[1024,2048]{1,0:T(8,128)(2,1)} fusion(bf16[1024,2816]{1,0:T(8,128)(2,1)} %hidden_units_back.1.right_ref, bf16[2048,2816]{1,0:T(8,128)(2,1)} %bitcast.149), kind=kOutput, calls=%fused_computation.6 | convolution fusion | flops 11813257216 | bytes 21495808 | tf_op jit(solution)/shard_map/dot_general | solution.py:31
  387.9 78.9 %share_branch.1 = (f32[256,2048]{1,0:T(8,128)S(1)}, f32[1,2048]{1,0:T(1,128)S(1)}, bf16[1024,2048]{1,0:T(8,128)(2,1)S(1)}, bf16[4,256,2048]{2,1,0:T(8,128)(2,1)}) custom-call(bf16[4,256,2048]{2,1,0:T(8,128)(2,1)} %bitcast.122, f32[256,2048]{1,0:T(8,128)S(1)} %copy-done.6, bf16[256,2048]{1,0:T(8,128)(2,1)S(1)} %bitcast.116, ...), custom_call_target="tpu_custom_call" | custom-call | flops 1000000 | bytes 10000 | tf_op jit(solution)/shard_map/share_branch/pallas_call | solution.py:877
  466.8 8.1 %fusion.62.refs_1_ = f32[1024,512]{1,0:T(8,128)} fusion(bf16[1024,2048]{1,0:T(8,128)(2,1)} %bitcast.150, bf16[512,2048]{1,0:T(8,128)(2,1)S(1)} %copy-done.39), kind=kOutput, calls=%fused_computation.177 | convolution fusion | flops 2147483648 | bytes 8388608 | tf_op jit(solution)/shard_map/dot_general | solution.py:31
  478.0 4.8 all-to-all-start.1
  485.5 74.5 %mix_backward.1 = (bf16[1024,1664]{1,0:T(8,128)(2,1)}, f32[1,512]{1,0:T(1,128)}, f32[1,256]{1,0:T(1,128)}, f32[16,256]{1,0:T(8,128)}) custom-call(f32[1024,1664]{1,0:T(8,128)} %fusion.60.given_ref.refs_0_, f32[1024,512]{1,0:T(8,128)} %fusion.62.refs_1_, f32[1024,512]{1,0:T(8,128)} %get-tuple-element.92.refs_2_, bf16[1024,256]{1,0:T(8,128)(2,1)} %get-tuple-element.93.refs_3_, ...), custom_call_target="tpu_custom_call" | custom-call | flops 1000000 | bytes 10000 | tf_op jit(solution)/shard_map/mix_backward/pallas_call | solution.py:1006
  560.1 13.6 %pair_product.3 = bf16[4,256,1664]{2,1,0:T(8,128)(2,1)} custom-call(bf16[1024,2048]{1,0:T(8,128)(2,1)} %bitcast.111, bf16[1024,1664]{1,0:T(8,128)(2,1)} %get-tuple-element.105.right_ref), custom_call_target="tpu_custom_call" | custom-call | flops 1000000 | bytes 10000 | tf_op jit(solution)/shard_map/pair_product/pallas_call | solution.py:826
  584.7 11.5 %convolution_convert_fusion.2 = bf16[1024,2048]{1,0:T(8,128)(2,1)} fusion(bf16[1024,1664]{1,0:T(8,128)(2,1)S(1)} %copy-done.26, bf16[2048,1664]{1,0:T(8,128)(2,1)} %bitcast.134), kind=kOutput, calls=%fused_computation.7 | convolution fusion | flops 6981419008 | bytes 14417920 | tf_op jit(solution)/shard_map/dot_general | solution.py:31
  605.7 42.2 %tokens_back.1 = (bf16[256,2048]{1,0:T(8,128)(2,1)S(1)}, f32[1,2048]{1,0:T(1,128)S(1)}) custom-call(bf16[4,256,2048]{2,1,0:T(8,128)(2,1)S(1)} %bitcast.108, bf16[256,2048]{1,0:T(8,128)(2,1)S(1)} %bitcast.107, f32[256,2048]{1,0:T(8,128)S(1)} %copy-done.15), custom_call_target="tpu_custom_call" | custom-call | flops 1000000 | bytes 10000 | tf_op jit(solution)/shard_map/tokens_back/pallas_call | solution.py:910
  654.8 6.1 all-to-all-done.3
  670.5 6.2 all-to-all-done.4
  (230 shorter events, 94.7 us)
Async XLA Ops:
  7.2 94.1 %copy-start.12 = (bf16[1,256,2048]{2,1,0:T(8,128)(2,1)S(1)}, bf16[1,256,2048]{2,1,0:T(8,128)(2,1)}, u32[]{:S(2)}) copy-start(bf16[1,256,2048]{2,1,0:T(8,128)(2,1)} %param.33) | copy-start | bytes 3145732
  7.2 34.3 %all-gather.6.cloned.1.call-start = ((), (), s32[]{:S(2)}) async-start(), calls=%async_computation.9 | async-start | bytes 2359296 | tf_op jit(solution)/shard_map/all_gather | solution.py:1079
  7.9 106.6 %all-gather.8.cloned.1.call-start = ((), (), s32[]{:S(2)}) async-start(), calls=%async_computation.10 | async-start | bytes 7667712 | tf_op jit(solution)/shard_map/all_gather | solution.py:1072
  8.6 92.7 %copy-start.31 = (f32[64]{0:T(128)}, f32[64]{0:T(128)S(1)}, u32[]{:S(2)}) copy-start(f32[64]{0:T(128)S(1)} %convert_element_type.244) | copy-start | bytes 772
  103.8 64.1 %all-to-all-start = ((bf16[4,256,2048]{2,1,0:T(8,128)(2,1)}), bf16[4,256,2048]{2,1,0:T(8,128)(2,1)}, u32[]{:S(2)}, u32[]{:S(2)}) async-start(bf16[4,256,2048]{2,1,0:T(8,128)(2,1)} %broadcast_in_dim.106), calls=%async_computation | async-start | bytes 8388608 | tf_op jit(solution)/shard_map/all_to_all | solution.py:64
  108.8 59.1 %all-gather.10.cloned.1.call-start = ((), (), s32[]{:S(2)}) async-start(), calls=%async_computation.11 | async-start | bytes 3244032 | tf_op jit(solution)/shard_map/all_gather | solution.py:1079
  111.7 178.4 %all-gather.12.cloned.1.call-start = ((), (), s32[]{:S(2)}) async-start(), calls=%async_computation.12 | async-start | bytes 12976128 | tf_op jit(solution)/shard_map/all_gather | solution.py:1072
  134.3 33.7 %copy-start.38 = (bf16[512,2048]{1,0:T(8,128)(2,1)S(1)}, bf16[512,2048]{1,0:T(8,128)(2,1)}, u32[]{:S(2)}) copy-start(bf16[512,2048]{1,0:T(8,128)(2,1)} %all-gather.6.cloned.1.call-done) | copy-start | bytes 6291460
  167.9 161.5 %all-gather.14.cloned.1.call-start = ((), (), s32[]{:S(2)}) async-start(), calls=%async_computation.13 | async-start | bytes 3244032 | tf_op jit(solution)/shard_map/all_gather | solution.py:1079
  250.2 235.3 %reduce-scatter.5.cloned.1.call-start = ((), (), s32[]{:S(2)}) async-start(), calls=%async_computation.14 | async-start | bytes 3604480 | tf_op jit(solution)/shard_map/reduce_scatter | solution.py:1089
  323.9 19.3 %collective-permute-start = (bf16[1,704,2048]{2,1,0:T(8,128)(2,1)}, bf16[1,704,2048]{2,1,0:T(8,128)(2,1)}, u32[]{:S(2)}, u32[]{:S(2)}) collective-permute-start(bf16[1,704,2048]{2,1,0:T(8,128)(2,1)} %dynamic-slice_bitcast_fusion), channel_id=1, source_target_pairs={{0,4},{4,0},{1,5},{5,1},{2,6},{6,2},{3,7},{7,3},{8,12},{12,8},{9,1... | collective-permute-start | bytes 8650760 | tf_op jit(solution)/shard_map/ppermute | solution.py:1063
  348.9 211.2 %reduce-scatter.7.cloned.1.call-start = ((), (), s32[]{:S(2)}) async-start(), calls=%async_computation.15 | async-start | bytes 7208960 | tf_op jit(solution)/shard_map/reduce_scatter | solution.py:1069
  369.4 18.5 %copy-start = (bf16[1408,1024]{1,0:T(8,128)(2,1)S(1)}, bf16[1408,1024]{1,0:T(8,128)(2,1)}, u32[]{:S(2)}) copy-start(bf16[1408,1024]{1,0:T(8,128)(2,1)} %all-gather.10.cloned.1.call-done.down_ref) | copy-start | bytes 8650756
  369.4 18.5 %copy-start.1 = (bf16[1408,1024]{1,0:T(8,128)(2,1)S(1)}, bf16[1408,1024]{1,0:T(8,128)(2,1)}, u32[]{:S(2)}) copy-start(bf16[1408,1024]{1,0:T(8,128)(2,1)} %all-gather.14.cloned.1.call-done.rest_ref) | copy-start | bytes 8650756
  369.4 18.5 %copy-start.6 = (f32[256,2048]{1,0:T(8,128)S(1)}, f32[256,2048]{1,0:T(8,128)}, u32[]{:S(2)}) copy-start(f32[256,2048]{1,0:T(8,128)} %copy-done.5) | copy-start | bytes 6291460
  369.4 18.5 %copy-start.13 = (bf16[1,256,2048]{2,1,0:T(8,128)(2,1)S(1)}, bf16[1,256,2048]{2,1,0:T(8,128)(2,1)}, u32[]{:S(2)}) copy-start(bf16[1,256,2048]{2,1,0:T(8,128)(2,1)} %param.33) | copy-start | bytes 3145732
  387.9 78.9 %copy-start.39 = (bf16[512,2048]{1,0:T(8,128)(2,1)S(1)}, bf16[512,2048]{1,0:T(8,128)(2,1)}, u32[]{:S(2)}) copy-start(bf16[512,2048]{1,0:T(8,128)(2,1)} %all-gather.6.cloned.1.call-done) | copy-start | bytes 6291460
  477.9 5.0 collective-permute-start.1
  478.0 82.1 %all-to-all-start.1 = ((bf16[4,256,2048]{2,1,0:T(8,128)(2,1)}), bf16[4,256,2048]{2,1,0:T(8,128)(2,1)}, u32[]{:S(2)}, u32[]{:S(2)}) async-start(bf16[4,256,2048]{2,1,0:T(8,128)(2,1)} %bitcast.112), calls=%async_computation.2 | async-start | bytes 8388608 | tf_op jit(solution)/shard_map/all_to_all | solution.py:70
  482.8 119.1 %reduce-scatter.9.cloned.1.call-start = ((), (), s32[]{:S(2)}) async-start(), calls=%async_computation.16 | async-start | bytes 1310720 | tf_op jit(solution)/shard_map/reduce_scatter | solution.py:1089
  485.5 175.5 %reduce-scatter.11.cloned.1.call-start = ((), (), s32[]{:S(2)}) async-start(), calls=%async_computation.17 | async-start | bytes 4259840 | tf_op jit(solution)/shard_map/reduce_scatter | solution.py:1069
  580.1 23.4 %all-to-all-start.2 = ((bf16[4,64,2816]{2,1,0:T(8,128)(2,1)}), bf16[4,64,2816]{2,1,0:T(8,128)(2,1)}, u32[]{:S(2)}, u32[]{:S(2)}) async-start(bf16[4,64,2816]{2,1,0:T(8,128)(2,1)} %reduce-scatter.7.cloned.1.call-done), calls=%async_computation.5 | async-start | bytes 2883584 | tf_op jit(solution)/shard_map/all_to_all | solution.py:1216
  650.4 10.5 %all-to-all-start.3 = ((f32[32,1,688]{2,1,0:T(1,128)}), f32[32,1,688]{2,1,0:T(1,128)S(1)}, u32[]{:S(2)}, u32[]{:S(2)}) async-start(f32[32,1,688]{2,1,0:T(1,128)} %copy.118), calls=%async_computation.6 | async-start | bytes 196608 | tf_op jit(solution)/shard_map/all_to_all | solution.py:1254
  661.0 15.7 %all-to-all-start.4 = ((bf16[4,64,1664]{2,1,0:T(8,128)(2,1)}), bf16[4,64,1664]{2,1,0:T(8,128)(2,1)}, u32[]{:S(2)}, u32[]{:S(2)}) async-start(bf16[4,64,1664]{2,1,0:T(8,128)(2,1)} %reduce-scatter.11.cloned.1.call-done), calls=%async_computation.8 | async-start | bytes 1703936 | tf_op jit(solution)/shard_map/all_to_all | solution.py:1228
  (33 other events, 190.1 us)
Sparse Core Ops, SparseCore 0:
  9.6 31.7 all-gather.5
  43.1 68.5 all-gather.7
  113.8 34.7 all-gather.9
  168.0 122.0 all-gather.11
  292.1 37.2 all-gather.13
  349.0 54.4 reduce-scatter.4
  405.8 113.5 reduce-scatter.6
  522.2 35.5 reduce-scatter.8
  573.8 62.1 reduce-scatter.10

commit v8 on v7

--- a/solution.py
+++ b/solution.py
@@ -957,6 +957,38 @@
     )(cot, down, rest, pre)
 
 
+def columns_kernel(widths, total_width, moved_ref, gain_ref, *outs):
+    gain = gain_ref[...].astype(F32)
+    place = 0
+    for out, width in zip(outs, widths):
+        for p in range(H):
+            piece = moved_ref[p, :, pl.ds(place, width)].astype(F32)
+            out[:, pl.ds(p * width, width)] = piece * gain
+        place += width
+    if total_width:
+        total = moved_ref[0, :, pl.ds(place, total_width)].astype(F32)
+        for p in range(1, H):
+            total += moved_ref[p, :, pl.ds(place, total_width)].astype(F32)
+        outs[-1][...] = total * gain
+
+
+def lay_columns(moved, gain, widths, total_width=0):
+    rows = moved.shape[1]
+    shapes = [(rows, H * width) for width in widths]
+    if total_width:
+        shapes.append((rows, total_width))
+    whole = pl.BlockSpec(memory_space=pltpu.VMEM)
+    return pl.pallas_call(
+        functools.partial(columns_kernel, tuple(widths), total_width),
+        out_shape=[jax.ShapeDtypeStruct(shape, F32) for shape in shapes],
+        in_specs=[whole] * 2,
+        out_specs=[whole] * len(shapes),
+        compiler_params=pltpu.CompilerParams(vmem_limit_bytes=16 * 2**20),
+        cost_estimate=pl.CostEstimate(flops=10**6, bytes_accessed=10**4, transcendentals=0),
+        name="lay_columns",
+    )(moved, gain)
+
+
 def mix_forward(mixed, bias, gaterank, gain, marks, segment, sums, pairs, key_dim, value_dim):
     rows = mixed.shape[0]
     count, _, length = segment.shape
@@ -1218,20 +1250,13 @@
     tokens_grad, grad_gain_one = tokens_back(partial.reshape(H, -1, width), inputs, grad_hidden)
     tokens_grad = tokens_grad.reshape(tokens.shape)
 
-    def weight_grad(moved, gain, start, w):
-        n = w.shape[1] // H
-        whole = moved[:, :, start : start + n].transpose(1, 0, 2).reshape(rows, -1)
-        return whole.astype(F32) * gain.astype(F32)[:, None]
-
-    w_gate_grad = weight_grad(grad_ffn_w, ffn_gain, 0, w_gate)
-    w_up_grad = weight_grad(grad_ffn_w, ffn_gain, w_gate.shape[1] // H, w_up)
+    units = w_gate.shape[1] // H
+    w_gate_grad, w_up_grad = lay_columns(grad_ffn_w, ffn_gain[:, None], (units, units))
+    grad_mix_w, _ = after(grad_mix_w, grad_gain_one)
     grad_mix_w = lax.all_to_all(grad_mix_w, "head", split_axis=0, concat_axis=0, tiled=True)
-    query_g = weight_grad(grad_mix_w, norm_gain, 0, w_query)
-    key_g = weight_grad(grad_mix_w, norm_gain, key_dim, w_key)
-    value_g = weight_grad(grad_mix_w, norm_gain, 2 * key_dim, w_value)
-    outgate_g = weight_grad(grad_mix_w, norm_gain, 2 * key_dim + value_dim, w_outgate)
-    lowrank_g = grad_mix_w[:, :, rank_at : rank_at + rank].astype(F32)
-    lowrank_g = jnp.sum(lowrank_g, axis=0) * norm_gain.astype(F32)[:, None]
+    query_g, key_g, value_g, outgate_g, lowrank_g = lay_columns(
+        grad_mix_w, norm_gain[:, None], (key_dim, key_dim, value_dim, value_dim), rank
+    )
 
     def place(g, axis):
         shape = list(g.shape)
@@ -1251,6 +1276,7 @@
         ],
         axis=1,
     )
+    small_grads, _ = after(small_grads, grad_mix_w)
     small_grads = lax.all_to_all(small_grads, EVERY, split_axis=0, concat_axis=0, tiled=True)
     small_grads = jnp.sum(small_grads, axis=0)
     sizes = [norm_gain.shape[0], ffn_gain.shape[0], gate_bias.shape[0], head_gain.shape[0]]

time: 698 us -> 709 us (1.016)
  local copies, waits for them, and re-layouts: 42 us -> 56.6 us
  waiting for transfers between devices: 71 us -> 63.3 us
    unnamed x90 -> x86, local copies, waits for them, and re-layouts: 22.3 us -> 24.4 us
  transfers between devices with their start and end apart: 16 -> 16, of which waited for: 6 -> 4; matrix products, arithmetic and copies ran while one was open for 19% -> 20% of each run, Pallas kernels for 61% -> 60%
where the time goes in v8:
time: 709 us; the launch traced here: 701 us
  Pallas kernels  424 us (60%)
  matrix products  84.1 us (12%)
  waiting for transfers between devices  63.3 us (9%)
  local copies, waits for them, and re-layouts  56.6 us (8%)
  other arithmetic  35.7 us (5%)
  starting transfers between devices  22.5 us (3%)
  between operations  14.8 us (2%)
    dot_general x8, matrix products, dot(): lax.dot_general(a, b, (dims, ((), ())), precision=precision, preferred_el...  84.1 us
    pallas_call x1, Pallas kernels, share_branch(): pl.pallas_call(branch_kernel, out_shape=[jax.ShapeDtypeStruct(hidden.shap...  78.9 us
    pallas_call x1, Pallas kernels, share_hidden(): pl.pallas_call(hidden_kernel, out_shape=[jax.ShapeDtypeStruct(tokens.shap...  75.2 us
    pallas_call x1, Pallas kernels, mix_backward(): pl.pallas_call(functools.partial(backward_kernel, key_dim, value_dim), ou...  74.3 us
    pallas_call x1, Pallas kernels, share_tokens(): pl.pallas_call(share_kernel, out_shape=[jax.ShapeDtypeStruct((H,) + token...  53.7 us
    pallas_call x1, Pallas kernels, tokens_back(): pl.pallas_call(tokens_kernel, out_shape=[jax.ShapeDtypeStruct(tokens.shap...  41.9 us
    all_gather x2, waiting for transfers between devices, gather_columns(): whole = lax.all_gather(moved, ('core', 'fsdp'), axis=1, tiled=True)  39.5 us
    pallas_call x2, Pallas kernels, pair_product(): pl.pallas_call(pair_kernel, out_shape=jax.ShapeDtypeStruct(shape, BF16),...  33.8 us
  transfers between devices with their start and end apart: 16, of which 4 were waited for; matrix products, arithmetic and copies ran while one was open for 20% of the time, Pallas kernels for 60%

profile of v8, /device:TPU:0, one launch (start us, length us, event | category | flops | bytes accessed | tf_op | source)
XLA Modules:
  0.0 700.7 jit_solution(13567160420247664267)
XLA Ops:
  15.4 14.4 %mix_weights.1 = bf16[4,64,1664]{2,1,0:T(8,128)(2,1)} custom-call(bf16[64,1024]{1,0:T(8,128)(2,1)S(1)} %copy-done.24, bf16[64,1024]{1,0:T(8,128)(2,1)S(1)} %copy-done.25, bf16[64,2048]{1,0:T(8,128)(2,1)S(1)} %copy-done.20, bf16[64,2048]{1,0:T(8,128)(2,1)S(1)} %copy-done.21, bf16[64,128]{1,0:T(8,128)(2,1)S(1)} %pad_add_fusion.refs_4_, ...), custom_call_target="tpu_custom_call" | custom-call | flops 1000000 | bytes 10000 | tf_op jit(solution)/shard_map/mix_weights/pallas_call | solution.py:516
  29.9 11.6 %all-gather.6.cloned.1.call-done = bf16[512,2048]{1,0:T(8,128)(2,1)} async-done(((bf16[64,2048]{1,0:T(8,128)(2,1)}), bf16[512,2048]{1,0:T(8,128)(2,1)}) %all-gather.6.cloned.1.call-update) | async-done | bytes 2097168 | tf_op jit(solution)/shard_map/all_gather | solution.py:1111
  45.7 53.7 %share_tokens.1 = (bf16[4,256,2048]{2,1,0:T(8,128)(2,1)S(1)}, bf16[4,64,2816]{2,1,0:T(8,128)(2,1)}) custom-call(bf16[256,2048]{1,0:T(8,128)(2,1)S(1)} %bitcast.81, bf16[64,5632]{1,0:T(8,128)(2,1)S(1)} %copy-done.18, bf16[64,5632]{1,0:T(8,128)(2,1)S(1)} %copy-done.19, bf16[64,1]{1,0:T(8,128)(2,1)S(1)} %copy.99.gain_ref), custom_call_target="tpu_custom_call" | custom-call | flops 1000000 | bytes 10000 | tf_op jit(solution)/shard_map/share_tokens/pallas_call | solution.py:619
  103.8 5.0 all-to-all-start
  121.0 13.3 %fusion.60.given_ref.refs_0_ = f32[1024,1664]{1,0:T(8,128)} fusion(bf16[1024,2048]{1,0:T(8,128)(2,1)} %bitcast.86, bf16[2048,1664]{1,0:T(8,128)(2,1)} %bitcast.103), kind=kOutput, calls=%fused_computation.161 | convolution fusion | flops 6979321856 | bytes 17825792 | tf_op jit(solution)/shard_map/dot_general | solution.py:31
  134.3 33.6 %mix_forward.1 = (bf16[1024,512]{1,0:T(8,128)(2,1)}, f32[1024,512]{1,0:T(8,128)}, f32[1024,256]{1,0:T(8,128)}, bf16[4,256,256]{2,1,0:T(8,128)(2,1)}, bf16[1024,2...) custom-call(f32[1024,1664]{1,0:T(8,128)} %fusion.60.given_ref.refs_0_, ...), custom_call_target="tpu_custom_call" | custom-call | flops 1000000 | bytes 10000 | tf_op jit(solution)/shard_map/mix_forward/pallas_call | solution.py:1006
  171.7 75.2 %share_hidden.1 = (f32[256,2048]{1,0:T(8,128)S(1)}, bf16[4,256,2048]{2,1,0:T(8,128)(2,1)S(1)}) custom-call(bf16[4,256,2048]{2,1,0:T(8,128)(2,1)S(1)} %bitcast.85, bf16[256,2048]{1,0:T(8,128)(2,1)S(1)} %bitcast.82), custom_call_target="tpu_custom_call" | custom-call | flops 1000000 | bytes 10000 | tf_op jit(solution)/shard_map/share_hidden/pallas_call | solution.py:723
  250.6 39.5 %all-gather.12.cloned.1.call-done = bf16[4,512,2816]{2,1,0:T(8,128)(2,1)} async-done(((bf16[4,64,2816]{2,1,0:T(8,128)(2,1)}), bf16[4,512,2816]{2,1,0:T(8,128)(2,1)}) %all-gather.12.cloned.1.call-update) | async-done | bytes 11534352 | tf_op jit(solution)/shard_map/all_gather | solution.py:1104
  290.1 17.2 %fusion.61.pre_ref = f32[1024,2816]{1,0:T(8,128)S(1)} fusion(bf16[1024,2048]{1,0:T(8,128)(2,1)} %bitcast.89, bf16[2048,2816]{1,0:T(8,128)(2,1)} %bitcast.118), kind=kOutput, calls=%fused_computation.162 | convolution fusion | flops 11811160064 | bytes 27262976 | tf_op jit(solution)/shard_map/dot_general | solution.py:31
  311.5 8.0 %convolution_convert_fusion = bf16[1408,2048]{1,0:T(8,128)(2,1)S(1)} fusion(bf16[1024,1408]{1,0:T(8,128)(2,1)S(1)} %fusion.active_ref, bf16[1024,2048]{1,0:T(8,128)(2,1)} %bitcast.14.cot_ref), kind=kOutput, calls=%fused_computation.1 | convolution fusion | flops 5908463616 | bytes 12845056 | tf_op jit(solution)/shard_map/dot_general | solution.py:31
  324.1 5.2 all-gather.14.cloned.1.call-done.rest_ref
  329.4 13.8 %hidden_units_back.1.right_ref = bf16[1024,2816]{1,0:T(8,128)(2,1)} custom-call(bf16[1024,2048]{1,0:T(8,128)(2,1)} %bitcast.14.cot_ref, bf16[1408,1024]{1,0:T(8,128)(2,1)} %all-gather.10.cloned.1.call-done.down_ref, bf16[1408,1024]{1,0:T(8,128)(2,1)} %all-gather.14.cloned.1.call-done.rest_ref, f32[1024,2816]{1,0:T(8,128)} %copy-done.28), custom_call_target="tpu_custom_call" | custom-call | flops 1000000 | bytes 10000 | tf_op jit(solution)/shard_map/hidden_units_back/pallas_call | solution.py:943
  343.2 5.6 fusion.2
  349.0 20.2 %pair_product.2 = bf16[4,256,2816]{2,1,0:T(8,128)(2,1)} custom-call(bf16[1024,2048]{1,0:T(8,128)(2,1)} %bitcast.90, bf16[1024,2816]{1,0:T(8,128)(2,1)} %hidden_units_back.1.right_ref), custom_call_target="tpu_custom_call" | custom-call | flops 1000000 | bytes 10000 | tf_op jit(solution)/shard_map/pair_product/pallas_call | solution.py:826
  369.4 18.5 %convolution_convert_fusion.1 = bf16[1024,2048]{1,0:T(8,128)(2,1)} fusion(bf16[1024,2816]{1,0:T(8,128)(2,1)} %hidden_units_back.1.right_ref, bf16[2048,2816]{1,0:T(8,128)(2,1)} %bitcast.119), kind=kOutput, calls=%fused_computation.6 | convolution fusion | flops 11813257216 | bytes 21495808 | tf_op jit(solution)/shard_map/dot_general | solution.py:31
  388.0 78.9 %share_branch.1 = (f32[256,2048]{1,0:T(8,128)S(1)}, f32[1,2048]{1,0:T(1,128)S(1)}, bf16[1024,2048]{1,0:T(8,128)(2,1)S(1)}, bf16[4,256,2048]{2,1,0:T(8,128)(2,1)}) custom-call(bf16[4,256,2048]{2,1,0:T(8,128)(2,1)} %bitcast.96, f32[256,2048]{1,0:T(8,128)S(1)} %copy-done.6, bf16[256,2048]{1,0:T(8,128)(2,1)S(1)} %bitcast.92, ...), custom_call_target="tpu_custom_call" | custom-call | flops 1000000 | bytes 10000 | tf_op jit(solution)/shard_map/share_branch/pallas_call | solution.py:877
  466.9 8.1 %fusion.62.refs_1_ = f32[1024,512]{1,0:T(8,128)} fusion(bf16[1024,2048]{1,0:T(8,128)(2,1)} %bitcast.120, bf16[512,2048]{1,0:T(8,128)(2,1)S(1)} %copy-done.37), kind=kOutput, calls=%fused_computation.163 | convolution fusion | flops 2147483648 | bytes 8388608 | tf_op jit(solution)/shard_map/dot_general | solution.py:31
  477.9 4.9 all-to-all-start.1
  485.5 74.3 %mix_backward.1 = (bf16[1024,1664]{1,0:T(8,128)(2,1)}, f32[1,512]{1,0:T(1,128)}, f32[1,256]{1,0:T(1,128)}, f32[16,256]{1,0:T(8,128)}) custom-call(f32[1024,1664]{1,0:T(8,128)} %fusion.60.given_ref.refs_0_, f32[1024,512]{1,0:T(8,128)} %fusion.62.refs_1_, f32[1024,512]{1,0:T(8,128)} %get-tuple-element.101.refs_2_, ...), custom_call_target="tpu_custom_call" | custom-call | flops 1000000 | bytes 10000 | tf_op jit(solution)/shard_map/mix_backward/pallas_call | solution.py:1038
  559.8 13.6 %pair_product.3 = bf16[4,256,1664]{2,1,0:T(8,128)(2,1)} custom-call(bf16[1024,2048]{1,0:T(8,128)(2,1)} %bitcast.87, bf16[1024,1664]{1,0:T(8,128)(2,1)} %get-tuple-element.114.right_ref), custom_call_target="tpu_custom_call" | custom-call | flops 1000000 | bytes 10000 | tf_op jit(solution)/shard_map/pair_product/pallas_call | solution.py:826
  577.0 12.7 %convolution_convert_fusion.2 = bf16[1024,2048]{1,0:T(8,128)(2,1)} fusion(bf16[1024,1664]{1,0:T(8,128)(2,1)} %get-tuple-element.114.right_ref, bf16[2048,1664]{1,0:T(8,128)(2,1)} %bitcast.104), kind=kOutput, calls=%fused_computation.7 | convolution fusion | flops 6981419008 | bytes 14417920 | tf_op jit(solution)/shard_map/dot_general | solution.py:31
  589.8 6.0 all-to-all-done.2.moved_ref
  599.6 41.9 %tokens_back.1 = (bf16[256,2048]{1,0:T(8,128)(2,1)S(1)}, f32[1,2048]{1,0:T(1,128)S(1)}) custom-call(bf16[4,256,2048]{2,1,0:T(8,128)(2,1)S(1)} %bitcast.84, bf16[256,2048]{1,0:T(8,128)(2,1)S(1)} %bitcast.83, f32[256,2048]{1,0:T(8,128)S(1)} %copy-done.15), custom_call_target="tpu_custom_call" | custom-call | flops 1000000 | bytes 10000 | tf_op jit(solution)/shard_map/tokens_back/pallas_call | solution.py:910
  665.2 4.5 convert_reduce_fusion
  (213 shorter events, 106.1 us)
Async XLA Ops:
  7.2 94.1 %copy-start.12 = (bf16[1,256,2048]{2,1,0:T(8,128)(2,1)S(1)}, bf16[1,256,2048]{2,1,0:T(8,128)(2,1)}, u32[]{:S(2)}) copy-start(bf16[1,256,2048]{2,1,0:T(8,128)(2,1)} %param.33) | copy-start | bytes 3145732
  7.2 34.3 %all-gather.6.cloned.1.call-start = ((), (), s32[]{:S(2)}) async-start(), calls=%async_computation.9 | async-start | bytes 2359296 | tf_op jit(solution)/shard_map/all_gather | solution.py:1111
  7.9 106.6 %all-gather.8.cloned.1.call-start = ((), (), s32[]{:S(2)}) async-start(), calls=%async_computation.10 | async-start | bytes 7667712 | tf_op jit(solution)/shard_map/all_gather | solution.py:1104
  10.2 93.6 %copy-start.22 = (bf16[64,1]{1,0:T(8,128)(2,1)}, bf16[64,1]{1,0:T(8,128)(2,1)S(1)}, u32[]{:S(2)}) copy-start(bf16[64,1]{1,0:T(8,128)(2,1)S(1)} %copy.98.refs_5_.gain_ref) | copy-start | bytes 388
  103.8 64.1 %all-to-all-start = ((bf16[4,256,2048]{2,1,0:T(8,128)(2,1)}), bf16[4,256,2048]{2,1,0:T(8,128)(2,1)}, u32[]{:S(2)}, u32[]{:S(2)}) async-start(bf16[4,256,2048]{2,1,0:T(8,128)(2,1)} %broadcast_in_dim.101), calls=%async_computation | async-start | bytes 8388608 | tf_op jit(solution)/shard_map/all_to_all | solution.py:64
  108.8 59.1 %all-gather.10.cloned.1.call-start = ((), (), s32[]{:S(2)}) async-start(), calls=%async_computation.11 | async-start | bytes 3244032 | tf_op jit(solution)/shard_map/all_gather | solution.py:1111
  111.7 178.5 %all-gather.12.cloned.1.call-start = ((), (), s32[]{:S(2)}) async-start(), calls=%async_computation.12 | async-start | bytes 12976128 | tf_op jit(solution)/shard_map/all_gather | solution.py:1104
  134.3 33.7 %copy-start.36 = (bf16[512,2048]{1,0:T(8,128)(2,1)S(1)}, bf16[512,2048]{1,0:T(8,128)(2,1)}, u32[]{:S(2)}) copy-start(bf16[512,2048]{1,0:T(8,128)(2,1)} %all-gather.6.cloned.1.call-done) | copy-start | bytes 6291460
  167.9 161.5 %all-gather.14.cloned.1.call-start = ((), (), s32[]{:S(2)}) async-start(), calls=%async_computation.13 | async-start | bytes 3244032 | tf_op jit(solution)/shard_map/all_gather | solution.py:1111
  250.1 235.2 %reduce-scatter.5.cloned.1.call-start = ((), (), s32[]{:S(2)}) async-start(), calls=%async_computation.14 | async-start | bytes 3604480 | tf_op jit(solution)/shard_map/reduce_scatter | solution.py:1121
  323.9 19.3 %collective-permute-start = (bf16[1,704,2048]{2,1,0:T(8,128)(2,1)}, bf16[1,704,2048]{2,1,0:T(8,128)(2,1)}, u32[]{:S(2)}, u32[]{:S(2)}) collective-permute-start(bf16[1,704,2048]{2,1,0:T(8,128)(2,1)} %dynamic-slice_bitcast_fusion), channel_id=1, source_target_pairs={{0,4},{4,0},{1,5},{5,1},{2,6},{6,2},{3,7},{7,3},{8,12},{12,8},{9,1... | collective-permute-start | bytes 8650760 | tf_op jit(solution)/shard_map/ppermute | solution.py:1095
  348.8 211.0 %reduce-scatter.7.cloned.1.call-start = ((), (), s32[]{:S(2)}) async-start(), calls=%async_computation.15 | async-start | bytes 7208960 | tf_op jit(solution)/shard_map/reduce_scatter | solution.py:1101
  369.3 18.6 %copy-start = (bf16[1408,1024]{1,0:T(8,128)(2,1)S(1)}, bf16[1408,1024]{1,0:T(8,128)(2,1)}, u32[]{:S(2)}) copy-start(bf16[1408,1024]{1,0:T(8,128)(2,1)} %all-gather.10.cloned.1.call-done.down_ref) | copy-start | bytes 8650756
  369.3 18.6 %copy-start.1 = (bf16[1408,1024]{1,0:T(8,128)(2,1)S(1)}, bf16[1408,1024]{1,0:T(8,128)(2,1)}, u32[]{:S(2)}) copy-start(bf16[1408,1024]{1,0:T(8,128)(2,1)} %all-gather.14.cloned.1.call-done.rest_ref) | copy-start | bytes 8650756
  388.0 78.9 %copy-start.37 = (bf16[512,2048]{1,0:T(8,128)(2,1)S(1)}, bf16[512,2048]{1,0:T(8,128)(2,1)}, u32[]{:S(2)}) copy-start(bf16[512,2048]{1,0:T(8,128)(2,1)} %all-gather.6.cloned.1.call-done) | copy-start | bytes 6291460
  477.8 5.0 collective-permute-start.1
  477.9 81.9 %all-to-all-start.1 = ((bf16[4,256,2048]{2,1,0:T(8,128)(2,1)}), bf16[4,256,2048]{2,1,0:T(8,128)(2,1)}, u32[]{:S(2)}, u32[]{:S(2)}) async-start(bf16[4,256,2048]{2,1,0:T(8,128)(2,1)} %bitcast.88), calls=%async_computation.2 | async-start | bytes 8388608 | tf_op jit(solution)/shard_map/all_to_all | solution.py:70
  482.7 107.0 %reduce-scatter.9.cloned.1.call-start = ((), (), s32[]{:S(2)}) async-start(), calls=%async_computation.16 | async-start | bytes 1310720 | tf_op jit(solution)/shard_map/reduce_scatter | solution.py:1121
  485.4 157.6 %reduce-scatter.11.cloned.1.call-start = ((), (), s32[]{:S(2)}) async-start(), calls=%async_computation.17 | async-start | bytes 4259840 | tf_op jit(solution)/shard_map/reduce_scatter | solution.py:1101
  573.5 22.3 %all-to-all-start.2 = ((bf16[4,64,2816]{2,1,0:T(8,128)(2,1)}), bf16[4,64,2816]{2,1,0:T(8,128)(2,1)S(1)}, u32[]{:S(2)}, u32[]{:S(2)}) async-start(bf16[4,64,2816]{2,1,0:T(8,128)(2,1)} %reduce-scatter.7.cloned.1.call-done), calls=%async_computation.5 | async-start | bytes 2883584 | tf_op jit(solution)/shard_map/all_to_all | solution.py:1248
  577.0 18.8 %copy-start.4 = (bf16[1,256,2048]{2,1,0:T(8,128)(2,1)S(1)}, bf16[1,256,2048]{2,1,0:T(8,128)(2,1)}, u32[]{:S(2)}) copy-start(bf16[1,256,2048]{2,1,0:T(8,128)(2,1)} %param.17) | copy-start | bytes 3145732
  643.0 31.6 %all-to-all-start.3 = ((bf16[4,64,1664]{2,1,0:T(8,128)(2,1)}), bf16[4,64,1664]{2,1,0:T(8,128)(2,1)}, u32[]{:S(2)}, u32[]{:S(2)}) async-start(bf16[4,64,1664]{2,1,0:T(8,128)(2,1)} %reduce-scatter.11.cloned.1.call-done), calls=%async_computation.7 | async-start | bytes 1703936 | tf_op jit(solution)/shard_map/all_to_all | solution.py:1256
  647.5 32.2 %copy-start.7 = (f32[256,2048]{1,0:T(8,128)S(1)}, f32[256,2048]{1,0:T(8,128)}, u32[]{:S(2)}) copy-start(f32[256,2048]{1,0:T(8,128)} %copy-done.5) | copy-start | bytes 6291460
  676.3 13.3 %all-to-all-start.4 = ((f32[32,1,688]{2,1,0:T(1,128)}), f32[32,1,688]{2,1,0:T(1,128)}, u32[]{:S(2)}, u32[]{:S(2)}) async-start(f32[32,1,688]{2,1,0:T(1,128)} %copy.104), calls=%async_computation.8 | async-start | bytes 196608 | tf_op jit(solution)/shard_map/all_to_all | solution.py:1280
  (31 other events, 153.3 us)
Sparse Core Ops, SparseCore 0:
  9.6 31.7 all-gather.5
  43.1 68.5 all-gather.7
  113.8 34.7 all-gather.9
  168.0 122.0 all-gather.11
  292.1 37.1 all-gather.13
  348.9 54.4 reduce-scatter.4
  405.8 113.5 reduce-scatter.6
  522.2 35.5 reduce-scatter.8
  573.6 62.0 reduce-scatter.10

commit v9 on v8

--- a/solution.py
+++ b/solution.py
@@ -1246,18 +1246,6 @@
     partial = back_product(grad_mixed, mix_w).astype(BF16)
     grad_mix_w = scatter_rows(grad_mix_w)
     grad_ffn_w = lax.all_to_all(grad_ffn_w, "head", split_axis=0, concat_axis=0, tiled=True)
-    partial, grad_output_w, grad_ffn_w = after(partial, grad_output_w, grad_ffn_w)
-    tokens_grad, grad_gain_one = tokens_back(partial.reshape(H, -1, width), inputs, grad_hidden)
-    tokens_grad = tokens_grad.reshape(tokens.shape)
-
-    units = w_gate.shape[1] // H
-    w_gate_grad, w_up_grad = lay_columns(grad_ffn_w, ffn_gain[:, None], (units, units))
-    grad_mix_w, _ = after(grad_mix_w, grad_gain_one)
-    grad_mix_w = lax.all_to_all(grad_mix_w, "head", split_axis=0, concat_axis=0, tiled=True)
-    query_g, key_g, value_g, outgate_g, lowrank_g = lay_columns(
-        grad_mix_w, norm_gain[:, None], (key_dim, key_dim, value_dim, value_dim), rank
-    )
-
     def place(g, axis):
         shape = list(g.shape)
         shape[axis] *= H
@@ -1265,7 +1253,6 @@
 
     small_grads = jnp.concatenate(
         [
-            grad_gain_one.reshape(devices, -1),
             grad_gain_two.reshape(devices, -1),
             place(grad_bias.reshape(-1), 0).reshape(devices, -1),
             grad_gain_head.reshape(devices, -1),
@@ -1276,6 +1263,21 @@
         ],
         axis=1,
     )
+    partial, grad_output_w, grad_ffn_w, small_grads = after(
+        partial, grad_output_w, grad_ffn_w, small_grads
+    )
+    tokens_grad, grad_gain_one = tokens_back(partial.reshape(H, -1, width), inputs, grad_hidden)
+    tokens_grad = tokens_grad.reshape(tokens.shape)
+
+    units = w_gate.shape[1] // H
+    w_gate_grad, w_up_grad = lay_columns(grad_ffn_w, ffn_gain[:, None], (units, units))
+    grad_mix_w, _ = after(grad_mix_w, grad_gain_one)
+    grad_mix_w = lax.all_to_all(grad_mix_w, "head", split_axis=0, concat_axis=0, tiled=True)
+    query_g, key_g, value_g, outgate_g, lowrank_g = lay_columns(
+        grad_mix_w, norm_gain[:, None], (key_dim, key_dim, value_dim, value_dim), rank
+    )
+
+    small_grads = jnp.concatenate([grad_gain_one.reshape(devices, -1), small_grads], axis=1)
     small_grads, _ = after(small_grads, grad_mix_w)
     small_grads = lax.all_to_all(small_grads, EVERY, split_axis=0, concat_axis=0, tiled=True)
     small_grads = jnp.sum(small_grads, axis=0)

time: 709 us -> 695 us (0.980)
  local copies, waits for them, and re-layouts: 56.6 us -> 42.7 us
    unnamed x86 -> x90, local copies, waits for them, and re-layouts: 24.4 us -> 24.5 us
  transfers between devices with their start and end apart: 16 -> 16, of which waited for: 4 -> 4; matrix products, arithmetic and copies ran while one was open for 20% -> 19% of each run, Pallas kernels for 60% -> 62%
where the time goes in v9:
time: 695 us; the launch traced here: 687 us
  Pallas kernels  424 us (61%)
  matrix products  83.9 us (12%)
  waiting for transfers between devices  63.5 us (9%)
  local copies, waits for them, and re-layouts  42.7 us (6%)
  other arithmetic  35.4 us (5%)
  starting transfers between devices  22.6 us (3%)
  between operations  14.8 us (2%)
    dot_general x8, matrix products, dot(): lax.dot_general(a, b, (dims, ((), ())), precision=precision, preferred_el...  83.9 us
    pallas_call x1, Pallas kernels, share_branch(): pl.pallas_call(branch_kernel, out_shape=[jax.ShapeDtypeStruct(hidden.shap...  78.9 us
    pallas_call x1, Pallas kernels, share_hidden(): pl.pallas_call(hidden_kernel, out_shape=[jax.ShapeDtypeStruct(tokens.shap...  75.2 us
    pallas_call x1, Pallas kernels, mix_backward(): pl.pallas_call(functools.partial(backward_kernel, key_dim, value_dim), ou...  74.4 us
    pallas_call x1, Pallas kernels, share_tokens(): pl.pallas_call(share_kernel, out_shape=[jax.ShapeDtypeStruct((H,) + token...  53.7 us
    pallas_call x1, Pallas kernels, tokens_back(): pl.pallas_call(tokens_kernel, out_shape=[jax.ShapeDtypeStruct(tokens.shap...  42.3 us
    all_gather x2, waiting for transfers between devices, gather_columns(): whole = lax.all_gather(moved, ('core', 'fsdp'), axis=1, tiled=True)  39.5 us
    pallas_call x2, Pallas kernels, pair_product(): pl.pallas_call(pair_kernel, out_shape=jax.ShapeDtypeStruct(shape, BF16),...  33.8 us
  transfers between devices with their start and end apart: 16, of which 4 were waited for; matrix products, arithmetic and copies ran while one was open for 19% of the time, Pallas kernels for 62%

profile of v9, /device:TPU:0, one launch (start us, length us, event | category | flops | bytes accessed | tf_op | source)
XLA Modules:
  0.0 687.2 jit_solution(13526416751823127180)
XLA Ops:
  15.4 14.4 %mix_weights.1 = bf16[4,64,1664]{2,1,0:T(8,128)(2,1)} custom-call(bf16[64,1024]{1,0:T(8,128)(2,1)S(1)} %copy-done.24, bf16[64,1024]{1,0:T(8,128)(2,1)S(1)} %copy-done.25, bf16[64,2048]{1,0:T(8,128)(2,1)S(1)} %copy-done.20, bf16[64,2048]{1,0:T(8,128)(2,1)S(1)} %copy-done.21, bf16[64,128]{1,0:T(8,128)(2,1)S(1)} %pad_add_fusion.refs_4_, ...), custom_call_target="tpu_custom_call" | custom-call | flops 1000000 | bytes 10000 | tf_op jit(solution)/shard_map/mix_weights/pallas_call | solution.py:516
  29.9 11.6 %all-gather.6.cloned.1.call-done = bf16[512,2048]{1,0:T(8,128)(2,1)} async-done(((bf16[64,2048]{1,0:T(8,128)(2,1)}), bf16[512,2048]{1,0:T(8,128)(2,1)}) %all-gather.6.cloned.1.call-update) | async-done | bytes 2097168 | tf_op jit(solution)/shard_map/all_gather | solution.py:1111
  45.7 53.7 %share_tokens.1 = (bf16[4,256,2048]{2,1,0:T(8,128)(2,1)S(1)}, bf16[4,64,2816]{2,1,0:T(8,128)(2,1)}) custom-call(bf16[256,2048]{1,0:T(8,128)(2,1)S(1)} %bitcast.81, bf16[64,5632]{1,0:T(8,128)(2,1)S(1)} %copy-done.18, bf16[64,5632]{1,0:T(8,128)(2,1)S(1)} %copy-done.19, bf16[64,1]{1,0:T(8,128)(2,1)S(1)} %copy.99.gain_ref), custom_call_target="tpu_custom_call" | custom-call | flops 1000000 | bytes 10000 | tf_op jit(solution)/shard_map/share_tokens/pallas_call | solution.py:619
  103.8 5.0 all-to-all-start
  121.0 13.3 %fusion.60.given_ref.refs_0_ = f32[1024,1664]{1,0:T(8,128)} fusion(bf16[1024,2048]{1,0:T(8,128)(2,1)} %bitcast.86, bf16[2048,1664]{1,0:T(8,128)(2,1)} %bitcast.103), kind=kOutput, calls=%fused_computation.163 | convolution fusion | flops 6979321856 | bytes 17825792 | tf_op jit(solution)/shard_map/dot_general | solution.py:31
  134.3 33.6 %mix_forward.1 = (bf16[1024,512]{1,0:T(8,128)(2,1)}, f32[1024,512]{1,0:T(8,128)}, f32[1024,256]{1,0:T(8,128)}, bf16[4,256,256]{2,1,0:T(8,128)(2,1)}, bf16[1024,2...) custom-call(f32[1024,1664]{1,0:T(8,128)} %fusion.60.given_ref.refs_0_, ...), custom_call_target="tpu_custom_call" | custom-call | flops 1000000 | bytes 10000 | tf_op jit(solution)/shard_map/mix_forward/pallas_call | solution.py:1006
  171.7 75.2 %share_hidden.1 = (f32[256,2048]{1,0:T(8,128)S(1)}, bf16[4,256,2048]{2,1,0:T(8,128)(2,1)S(1)}) custom-call(bf16[4,256,2048]{2,1,0:T(8,128)(2,1)S(1)} %bitcast.85, bf16[256,2048]{1,0:T(8,128)(2,1)S(1)} %bitcast.82), custom_call_target="tpu_custom_call" | custom-call | flops 1000000 | bytes 10000 | tf_op jit(solution)/shard_map/share_hidden/pallas_call | solution.py:723
  250.6 39.5 %all-gather.12.cloned.1.call-done = bf16[4,512,2816]{2,1,0:T(8,128)(2,1)} async-done(((bf16[4,64,2816]{2,1,0:T(8,128)(2,1)}), bf16[4,512,2816]{2,1,0:T(8,128)(2,1)}) %all-gather.12.cloned.1.call-update) | async-done | bytes 11534352 | tf_op jit(solution)/shard_map/all_gather | solution.py:1104
  290.1 17.2 %fusion.61.pre_ref = f32[1024,2816]{1,0:T(8,128)S(1)} fusion(bf16[1024,2048]{1,0:T(8,128)(2,1)} %bitcast.89, bf16[2048,2816]{1,0:T(8,128)(2,1)} %bitcast.118), kind=kOutput, calls=%fused_computation.164 | convolution fusion | flops 11811160064 | bytes 27262976 | tf_op jit(solution)/shard_map/dot_general | solution.py:31
  311.5 8.1 %convolution_convert_fusion = bf16[1408,2048]{1,0:T(8,128)(2,1)S(1)} fusion(bf16[1024,1408]{1,0:T(8,128)(2,1)S(1)} %fusion.active_ref, bf16[1024,2048]{1,0:T(8,128)(2,1)} %bitcast.14.cot_ref), kind=kOutput, calls=%fused_computation.1 | convolution fusion | flops 5908463616 | bytes 12845056 | tf_op jit(solution)/shard_map/dot_general | solution.py:31
  324.2 5.2 all-gather.14.cloned.1.call-done.rest_ref
  329.4 13.8 %hidden_units_back.1.right_ref = bf16[1024,2816]{1,0:T(8,128)(2,1)} custom-call(bf16[1024,2048]{1,0:T(8,128)(2,1)} %bitcast.14.cot_ref, bf16[1408,1024]{1,0:T(8,128)(2,1)} %all-gather.10.cloned.1.call-done.down_ref, bf16[1408,1024]{1,0:T(8,128)(2,1)} %all-gather.14.cloned.1.call-done.rest_ref, f32[1024,2816]{1,0:T(8,128)} %copy-done.27), custom_call_target="tpu_custom_call" | custom-call | flops 1000000 | bytes 10000 | tf_op jit(solution)/shard_map/hidden_units_back/pallas_call | solution.py:943
  343.2 5.6 fusion.2
  349.1 20.2 %pair_product.2 = bf16[4,256,2816]{2,1,0:T(8,128)(2,1)} custom-call(bf16[1024,2048]{1,0:T(8,128)(2,1)} %bitcast.90, bf16[1024,2816]{1,0:T(8,128)(2,1)} %hidden_units_back.1.right_ref), custom_call_target="tpu_custom_call" | custom-call | flops 1000000 | bytes 10000 | tf_op jit(solution)/shard_map/pair_product/pallas_call | solution.py:826
  369.4 18.3 %convolution_convert_fusion.1 = bf16[1024,2048]{1,0:T(8,128)(2,1)} fusion(bf16[1024,2816]{1,0:T(8,128)(2,1)} %hidden_units_back.1.right_ref, bf16[2048,2816]{1,0:T(8,128)(2,1)} %bitcast.119), kind=kOutput, calls=%fused_computation.6 | convolution fusion | flops 11813257216 | bytes 21495808 | tf_op jit(solution)/shard_map/dot_general | solution.py:31
  387.8 78.9 %share_branch.1 = (f32[256,2048]{1,0:T(8,128)S(1)}, f32[1,2048]{1,0:T(1,128)S(1)}, bf16[1024,2048]{1,0:T(8,128)(2,1)S(1)}, bf16[4,256,2048]{2,1,0:T(8,128)(2,1)}) custom-call(bf16[4,256,2048]{2,1,0:T(8,128)(2,1)} %bitcast.96, f32[256,2048]{1,0:T(8,128)S(1)} %copy-done.6, bf16[256,2048]{1,0:T(8,128)(2,1)S(1)} %bitcast.92, ...), custom_call_target="tpu_custom_call" | custom-call | flops 1000000 | bytes 10000 | tf_op jit(solution)/shard_map/share_branch/pallas_call | solution.py:877
  466.7 8.1 %fusion.62.refs_1_ = f32[1024,512]{1,0:T(8,128)} fusion(bf16[1024,2048]{1,0:T(8,128)(2,1)} %bitcast.120, bf16[512,2048]{1,0:T(8,128)(2,1)S(1)} %copy-done.39), kind=kOutput, calls=%fused_computation.165 | convolution fusion | flops 2147483648 | bytes 8388608 | tf_op jit(solution)/shard_map/dot_general | solution.py:31
  477.9 4.8 all-to-all-start.1
  485.5 74.4 %mix_backward.1 = (bf16[1024,1664]{1,0:T(8,128)(2,1)}, f32[1,512]{1,0:T(1,128)}, f32[1,256]{1,0:T(1,128)}, f32[16,256]{1,0:T(8,128)}) custom-call(f32[1024,1664]{1,0:T(8,128)} %fusion.60.given_ref.refs_0_, f32[1024,512]{1,0:T(8,128)} %fusion.62.refs_1_, f32[1024,512]{1,0:T(8,128)} %get-tuple-element.102.refs_2_, ...), custom_call_target="tpu_custom_call" | custom-call | flops 1000000 | bytes 10000 | tf_op jit(solution)/shard_map/mix_backward/pallas_call | solution.py:1038
  559.9 13.6 %pair_product.3 = bf16[4,256,1664]{2,1,0:T(8,128)(2,1)} custom-call(bf16[1024,2048]{1,0:T(8,128)(2,1)} %bitcast.87, bf16[1024,1664]{1,0:T(8,128)(2,1)} %get-tuple-element.115.right_ref), custom_call_target="tpu_custom_call" | custom-call | flops 1000000 | bytes 10000 | tf_op jit(solution)/shard_map/pair_product/pallas_call | solution.py:826
  580.9 12.4 %convolution_convert_fusion.2 = bf16[1024,2048]{1,0:T(8,128)(2,1)} fusion(bf16[1024,1664]{1,0:T(8,128)(2,1)} %get-tuple-element.115.right_ref, bf16[2048,1664]{1,0:T(8,128)(2,1)} %bitcast.104), kind=kOutput, calls=%fused_computation.7 | convolution fusion | flops 6981419008 | bytes 14417920 | tf_op jit(solution)/shard_map/dot_general | solution.py:31
  593.3 6.3 all-to-all-done.2.moved_ref
  603.4 42.3 %tokens_back.1 = (bf16[256,2048]{1,0:T(8,128)(2,1)S(1)}, f32[1,2048]{1,0:T(1,128)S(1)}) custom-call(bf16[4,256,2048]{2,1,0:T(8,128)(2,1)S(1)} %bitcast.84, bf16[256,2048]{1,0:T(8,128)(2,1)S(1)} %bitcast.83, f32[256,2048]{1,0:T(8,128)S(1)} %copy-done.15), custom_call_target="tpu_custom_call" | custom-call | flops 1000000 | bytes 10000 | tf_op jit(solution)/shard_map/tokens_back/pallas_call | solution.py:910
  651.7 4.5 convert_reduce_fusion
  (218 shorter events, 92.3 us)
Async XLA Ops:
  7.2 94.1 %copy-start.12 = (bf16[1,256,2048]{2,1,0:T(8,128)(2,1)S(1)}, bf16[1,256,2048]{2,1,0:T(8,128)(2,1)}, u32[]{:S(2)}) copy-start(bf16[1,256,2048]{2,1,0:T(8,128)(2,1)} %param.33) | copy-start | bytes 3145732
  7.2 34.3 %all-gather.6.cloned.1.call-start = ((), (), s32[]{:S(2)}) async-start(), calls=%async_computation.9 | async-start | bytes 2359296 | tf_op jit(solution)/shard_map/all_gather | solution.py:1111
  7.9 106.6 %all-gather.8.cloned.1.call-start = ((), (), s32[]{:S(2)}) async-start(), calls=%async_computation.10 | async-start | bytes 7667712 | tf_op jit(solution)/shard_map/all_gather | solution.py:1104
  10.2 93.6 %copy-start.22 = (bf16[64,1]{1,0:T(8,128)(2,1)}, bf16[64,1]{1,0:T(8,128)(2,1)S(1)}, u32[]{:S(2)}) copy-start(bf16[64,1]{1,0:T(8,128)(2,1)S(1)} %copy.98.refs_5_.gain_ref) | copy-start | bytes 388
  103.8 64.1 %all-to-all-start = ((bf16[4,256,2048]{2,1,0:T(8,128)(2,1)}), bf16[4,256,2048]{2,1,0:T(8,128)(2,1)}, u32[]{:S(2)}, u32[]{:S(2)}) async-start(bf16[4,256,2048]{2,1,0:T(8,128)(2,1)} %broadcast_in_dim.101), calls=%async_computation | async-start | bytes 8388608 | tf_op jit(solution)/shard_map/all_to_all | solution.py:64
  108.8 59.1 %all-gather.10.cloned.1.call-start = ((), (), s32[]{:S(2)}) async-start(), calls=%async_computation.11 | async-start | bytes 3244032 | tf_op jit(solution)/shard_map/all_gather | solution.py:1111
  111.7 178.4 %all-gather.12.cloned.1.call-start = ((), (), s32[]{:S(2)}) async-start(), calls=%async_computation.12 | async-start | bytes 12976128 | tf_op jit(solution)/shard_map/all_gather | solution.py:1104
  134.3 33.7 %copy-start.38 = (bf16[512,2048]{1,0:T(8,128)(2,1)S(1)}, bf16[512,2048]{1,0:T(8,128)(2,1)}, u32[]{:S(2)}) copy-start(bf16[512,2048]{1,0:T(8,128)(2,1)} %all-gather.6.cloned.1.call-done) | copy-start | bytes 6291460
  167.9 161.5 %all-gather.14.cloned.1.call-start = ((), (), s32[]{:S(2)}) async-start(), calls=%async_computation.13 | async-start | bytes 3244032 | tf_op jit(solution)/shard_map/all_gather | solution.py:1111
  250.1 235.3 %reduce-scatter.5.cloned.1.call-start = ((), (), s32[]{:S(2)}) async-start(), calls=%async_computation.14 | async-start | bytes 3604480 | tf_op jit(solution)/shard_map/reduce_scatter | solution.py:1121
  323.9 19.3 %collective-permute-start = (bf16[1,704,2048]{2,1,0:T(8,128)(2,1)}, bf16[1,704,2048]{2,1,0:T(8,128)(2,1)}, u32[]{:S(2)}, u32[]{:S(2)}) collective-permute-start(bf16[1,704,2048]{2,1,0:T(8,128)(2,1)} %dynamic-slice_bitcast_fusion), channel_id=1, source_target_pairs={{0,4},{4,0},{1,5},{5,1},{2,6},{6,2},{3,7},{7,3},{8,12},{12,8},{9,1... | collective-permute-start | bytes 8650760 | tf_op jit(solution)/shard_map/ppermute | solution.py:1095
  348.9 211.0 %reduce-scatter.7.cloned.1.call-start = ((), (), s32[]{:S(2)}) async-start(), calls=%async_computation.15 | async-start | bytes 7208960 | tf_op jit(solution)/shard_map/reduce_scatter | solution.py:1101
  369.4 18.4 %copy-start = (bf16[1408,1024]{1,0:T(8,128)(2,1)S(1)}, bf16[1408,1024]{1,0:T(8,128)(2,1)}, u32[]{:S(2)}) copy-start(bf16[1408,1024]{1,0:T(8,128)(2,1)} %all-gather.10.cloned.1.call-done.down_ref) | copy-start | bytes 8650756
  369.4 18.4 %copy-start.1 = (bf16[1408,1024]{1,0:T(8,128)(2,1)S(1)}, bf16[1408,1024]{1,0:T(8,128)(2,1)}, u32[]{:S(2)}) copy-start(bf16[1408,1024]{1,0:T(8,128)(2,1)} %all-gather.14.cloned.1.call-done.rest_ref) | copy-start | bytes 8650756
  387.8 78.9 %copy-start.39 = (bf16[512,2048]{1,0:T(8,128)(2,1)S(1)}, bf16[512,2048]{1,0:T(8,128)(2,1)}, u32[]{:S(2)}) copy-start(bf16[512,2048]{1,0:T(8,128)(2,1)} %all-gather.6.cloned.1.call-done) | copy-start | bytes 6291460
  477.8 5.0 collective-permute-start.1
  477.9 81.9 %all-to-all-start.1 = ((bf16[4,256,2048]{2,1,0:T(8,128)(2,1)}), bf16[4,256,2048]{2,1,0:T(8,128)(2,1)}, u32[]{:S(2)}, u32[]{:S(2)}) async-start(bf16[4,256,2048]{2,1,0:T(8,128)(2,1)} %bitcast.88), calls=%async_computation.2 | async-start | bytes 8388608 | tf_op jit(solution)/shard_map/all_to_all | solution.py:70
  482.7 110.6 %reduce-scatter.9.cloned.1.call-start = ((), (), s32[]{:S(2)}) async-start(), calls=%async_computation.16 | async-start | bytes 1310720 | tf_op jit(solution)/shard_map/reduce_scatter | solution.py:1121
  485.4 161.9 %reduce-scatter.11.cloned.1.call-start = ((), (), s32[]{:S(2)}) async-start(), calls=%async_computation.17 | async-start | bytes 4259840 | tf_op jit(solution)/shard_map/reduce_scatter | solution.py:1101
  577.1 22.5 %all-to-all-start.2 = ((bf16[4,64,2816]{2,1,0:T(8,128)(2,1)}), bf16[4,64,2816]{2,1,0:T(8,128)(2,1)S(1)}, u32[]{:S(2)}, u32[]{:S(2)}) async-start(bf16[4,64,2816]{2,1,0:T(8,128)(2,1)} %reduce-scatter.7.cloned.1.call-done), calls=%async_computation.5 | async-start | bytes 2883584 | tf_op jit(solution)/shard_map/all_to_all | solution.py:1248
  580.8 18.7 %copy-start.4 = (bf16[1,256,2048]{2,1,0:T(8,128)(2,1)S(1)}, bf16[1,256,2048]{2,1,0:T(8,128)(2,1)}, u32[]{:S(2)}) copy-start(bf16[1,256,2048]{2,1,0:T(8,128)(2,1)} %param.17) | copy-start | bytes 3145732
  647.3 18.9 %copy-start.7 = (f32[256,2048]{1,0:T(8,128)S(1)}, f32[256,2048]{1,0:T(8,128)}, u32[]{:S(2)}) copy-start(f32[256,2048]{1,0:T(8,128)} %copy-done.5) | copy-start | bytes 6291460
  647.3 13.9 %all-to-all-start.3 = ((bf16[4,64,1664]{2,1,0:T(8,128)(2,1)}), bf16[4,64,1664]{2,1,0:T(8,128)(2,1)}, u32[]{:S(2)}, u32[]{:S(2)}) async-start(bf16[4,64,1664]{2,1,0:T(8,128)(2,1)} %reduce-scatter.11.cloned.1.call-done), calls=%async_computation.7 | async-start | bytes 1703936 | tf_op jit(solution)/shard_map/all_to_all | solution.py:1275
  662.8 13.3 %all-to-all-start.4 = ((f32[32,1,688]{2,1,0:T(1,128)}), f32[32,1,688]{2,1,0:T(1,128)}, u32[]{:S(2)}, u32[]{:S(2)}) async-start(f32[32,1,688]{2,1,0:T(1,128)} %copy.104), calls=%async_computation.8 | async-start | bytes 196608 | tf_op jit(solution)/shard_map/all_to_all | solution.py:1282
  (33 other events, 163.6 us)
Sparse Core Ops, SparseCore 0:
  9.6 31.7 all-gather.5
  43.1 68.5 all-gather.7
  113.8 34.7 all-gather.9
  168.0 122.0 all-gather.11
  292.1 37.2 all-gather.13
  349.0 54.5 reduce-scatter.4
  405.9 113.6 reduce-scatter.6
  522.4 35.5 reduce-scatter.8
  573.7 62.2 reduce-scatter.10

commit v10 on v9

--- a/solution.py
+++ b/solution.py
@@ -885,7 +885,7 @@
         in_specs=[whole] * 6,
         out_specs=[whole] * 3 + [pl.BlockSpec(memory_space=pl.ANY)],
         scratch_shapes=turn_scratch(*hidden.shape) + share_scratch(*hidden.shape),
-        compiler_params=kernel_params(6, 34),
+        compiler_params=kernel_params(6, 30),
         cost_estimate=pl.CostEstimate(flops=10**6, bytes_accessed=10**4, transcendentals=0),
         name="share_branch",
     )(partial, hidden, upstream, active, down, rest)

time: 695 us -> 679 us (0.977)
  Pallas kernels: 424 us -> 411 us
    pallas_call x1, Pallas kernels: 74.4 us -> 62 us  [mix_backward(): pl.pallas_call(functools.partial(backward_kernel, key_dim, value_dim), ou...]
    unnamed x90 -> x88, local copies, waits for them, and re-layouts: 24.5 us -> 25.7 us
  transfers between devices with their start and end apart: 16 -> 16, of which waited for: 4 -> 4; matrix products, arithmetic and copies ran while one was open for 19% -> 18% of each run, Pallas kernels for 62% -> 61%
where the time goes in v10:
time: 679 us; the launch traced here: 671 us
  Pallas kernels  411 us (61%)
  matrix products  79.8 us (12%)
  waiting for transfers between devices  63 us (9%)
  local copies, waits for them, and re-layouts  43.9 us (6%)
  other arithmetic  35.4 us (5%)
  starting transfers between devices  22.8 us (3%)
  between operations  14.7 us (2%)
    dot_general x8, matrix products, dot(): lax.dot_general(a, b, (dims, ((), ())), precision=precision, preferred_el...  79.8 us
    pallas_call x1, Pallas kernels, share_branch(): pl.pallas_call(branch_kernel, out_shape=[jax.ShapeDtypeStruct(hidden.shap...  78.5 us
    pallas_call x1, Pallas kernels, share_hidden(): pl.pallas_call(hidden_kernel, out_shape=[jax.ShapeDtypeStruct(tokens.shap...  75.2 us
    pallas_call x1, Pallas kernels, mix_backward(): pl.pallas_call(functools.partial(backward_kernel, key_dim, value_dim), ou...  62 us
    pallas_call x1, Pallas kernels, share_tokens(): pl.pallas_call(share_kernel, out_shape=[jax.ShapeDtypeStruct((H,) + token...  53.7 us
    pallas_call x1, Pallas kernels, tokens_back(): pl.pallas_call(tokens_kernel, out_shape=[jax.ShapeDtypeStruct(tokens.shap...  41.9 us
    all_gather x2, waiting for transfers between devices, gather_columns(): whole = lax.all_gather(moved, ('core', 'fsdp'), axis=1, tiled=True)  39.7 us
    pallas_call x2, Pallas kernels, pair_product(): pl.pallas_call(pair_kernel, out_shape=jax.ShapeDtypeStruct(shape, BF16),...  33.9 us
  transfers between devices with their start and end apart: 16, of which 4 were waited for; matrix products, arithmetic and copies ran while one was open for 18% of the time, Pallas kernels for 61%

profile of v10, /device:TPU:0, one launch (start us, length us, event | category | flops | bytes accessed | tf_op | source)
XLA Modules:
  0.0 670.7 jit_solution(8964459764500834260)
XLA Ops:
  15.4 14.4 %mix_weights.1 = bf16[4,64,1664]{2,1,0:T(8,128)(2,1)} custom-call(bf16[64,1024]{1,0:T(8,128)(2,1)S(1)} %copy-done.24, bf16[64,1024]{1,0:T(8,128)(2,1)S(1)} %copy-done.25, bf16[64,2048]{1,0:T(8,128)(2,1)S(1)} %copy-done.20, bf16[64,2048]{1,0:T(8,128)(2,1)S(1)} %copy-done.21, bf16[64,128]{1,0:T(8,128)(2,1)S(1)} %pad_add_fusion.refs_4_, ...), custom_call_target="tpu_custom_call" | custom-call | flops 1000000 | bytes 10000 | tf_op jit(solution)/shard_map/mix_weights/pallas_call | solution.py:516
  29.9 11.6 %all-gather.6.cloned.1.call-done = bf16[512,2048]{1,0:T(8,128)(2,1)} async-done(((bf16[64,2048]{1,0:T(8,128)(2,1)}), bf16[512,2048]{1,0:T(8,128)(2,1)}) %all-gather.6.cloned.1.call-update) | async-done | bytes 2097168 | tf_op jit(solution)/shard_map/all_gather | solution.py:1111
  45.7 53.7 %share_tokens.1 = (bf16[4,256,2048]{2,1,0:T(8,128)(2,1)S(1)}, bf16[4,64,2816]{2,1,0:T(8,128)(2,1)}) custom-call(bf16[256,2048]{1,0:T(8,128)(2,1)S(1)} %bitcast.81, bf16[64,5632]{1,0:T(8,128)(2,1)S(1)} %copy-done.18, bf16[64,5632]{1,0:T(8,128)(2,1)S(1)} %copy-done.19, bf16[64,1]{1,0:T(8,128)(2,1)S(1)} %copy.99.gain_ref), custom_call_target="tpu_custom_call" | custom-call | flops 1000000 | bytes 10000 | tf_op jit(solution)/shard_map/share_tokens/pallas_call | solution.py:619
  103.8 5.0 all-to-all-start
  121.0 13.3 %fusion.60.given_ref.refs_0_ = f32[1024,1664]{1,0:T(8,128)} fusion(bf16[1024,2048]{1,0:T(8,128)(2,1)} %bitcast.86, bf16[2048,1664]{1,0:T(8,128)(2,1)} %bitcast.105), kind=kOutput, calls=%fused_computation.163 | convolution fusion | flops 6979321856 | bytes 17825792 | tf_op jit(solution)/shard_map/dot_general | solution.py:31
  134.3 33.6 %mix_forward.1 = (bf16[1024,512]{1,0:T(8,128)(2,1)}, f32[1024,512]{1,0:T(8,128)}, f32[1024,256]{1,0:T(8,128)}, bf16[4,256,256]{2,1,0:T(8,128)(2,1)}, bf16[1024,2...) custom-call(f32[1024,1664]{1,0:T(8,128)} %fusion.60.given_ref.refs_0_, ...), custom_call_target="tpu_custom_call" | custom-call | flops 1000000 | bytes 10000 | tf_op jit(solution)/shard_map/mix_forward/pallas_call | solution.py:1006
  171.7 75.2 %share_hidden.1 = (f32[256,2048]{1,0:T(8,128)S(1)}, bf16[4,256,2048]{2,1,0:T(8,128)(2,1)S(1)}) custom-call(bf16[4,256,2048]{2,1,0:T(8,128)(2,1)S(1)} %bitcast.85, bf16[256,2048]{1,0:T(8,128)(2,1)S(1)} %bitcast.82), custom_call_target="tpu_custom_call" | custom-call | flops 1000000 | bytes 10000 | tf_op jit(solution)/shard_map/share_hidden/pallas_call | solution.py:723
  250.4 39.7 %all-gather.12.cloned.1.call-done = bf16[4,512,2816]{2,1,0:T(8,128)(2,1)} async-done(((bf16[4,64,2816]{2,1,0:T(8,128)(2,1)}), bf16[4,512,2816]{2,1,0:T(8,128)(2,1)}) %all-gather.12.cloned.1.call-update) | async-done | bytes 11534352 | tf_op jit(solution)/shard_map/all_gather | solution.py:1104
  290.1 17.2 %fusion.61.pre_ref = f32[1024,2816]{1,0:T(8,128)S(1)} fusion(bf16[1024,2048]{1,0:T(8,128)(2,1)} %bitcast.89, bf16[2048,2816]{1,0:T(8,128)(2,1)} %bitcast.120), kind=kOutput, calls=%fused_computation.164 | convolution fusion | flops 11811160064 | bytes 27262976 | tf_op jit(solution)/shard_map/dot_general | solution.py:31
  311.5 8.1 %convolution_convert_fusion = bf16[1408,2048]{1,0:T(8,128)(2,1)S(1)} fusion(bf16[1024,1408]{1,0:T(8,128)(2,1)S(1)} %fusion.active_ref, bf16[1024,2048]{1,0:T(8,128)(2,1)} %bitcast.14.cot_ref), kind=kOutput, calls=%fused_computation.1 | convolution fusion | flops 5908463616 | bytes 12845056 | tf_op jit(solution)/shard_map/dot_general | solution.py:31
  324.1 5.2 all-gather.14.cloned.1.call-done.rest_ref
  329.4 13.8 %hidden_units_back.1.right_ref = bf16[1024,2816]{1,0:T(8,128)(2,1)} custom-call(bf16[1024,2048]{1,0:T(8,128)(2,1)} %bitcast.14.cot_ref, bf16[1408,1024]{1,0:T(8,128)(2,1)} %all-gather.10.cloned.1.call-done.down_ref, bf16[1408,1024]{1,0:T(8,128)(2,1)} %all-gather.14.cloned.1.call-done.rest_ref, f32[1024,2816]{1,0:T(8,128)} %copy-done.27), custom_call_target="tpu_custom_call" | custom-call | flops 1000000 | bytes 10000 | tf_op jit(solution)/shard_map/hidden_units_back/pallas_call | solution.py:943
  343.2 5.6 fusion.2
  349.3 20.2 %pair_product.2 = bf16[4,256,2816]{2,1,0:T(8,128)(2,1)} custom-call(bf16[1024,2048]{1,0:T(8,128)(2,1)} %bitcast.90, bf16[1024,2816]{1,0:T(8,128)(2,1)} %hidden_units_back.1.right_ref), custom_call_target="tpu_custom_call" | custom-call | flops 1000000 | bytes 10000 | tf_op jit(solution)/shard_map/pair_product/pallas_call | solution.py:826
  369.6 18.4 %convolution_convert_fusion.1 = bf16[1024,2048]{1,0:T(8,128)(2,1)} fusion(bf16[1024,2816]{1,0:T(8,128)(2,1)} %hidden_units_back.1.right_ref, bf16[2048,2816]{1,0:T(8,128)(2,1)} %bitcast.121), kind=kOutput, calls=%fused_computation.6 | convolution fusion | flops 11813257216 | bytes 21495808 | tf_op jit(solution)/shard_map/dot_general | solution.py:31
  389.3 78.5 %share_branch.1 = (f32[256,2048]{1,0:T(8,128)S(1)}, f32[1,2048]{1,0:T(1,128)S(1)}, bf16[1024,2048]{1,0:T(8,128)(2,1)S(1)}, bf16[4,256,2048]{2,1,0:T(8,128)(2,1)S(1)}) custom-call(bf16[4,256,2048]{2,1,0:T(8,128)(2,1)} %bitcast.98, f32[256,2048]{1,0:T(8,128)S(1)} %copy-done.6, bf16[256,2048]{1,0:T(8,128)(2,1)S(1)} %bitcast.92, ...), custom_call_target="tpu_custom_call" | custom-call | flops 1000000 | bytes 10000 | tf_op jit(solution)/shard_map/share_branch/pallas_call | solution.py:877
  474.2 4.8 all-to-all-start.1
  481.8 62.0 %mix_backward.1 = (bf16[1024,1664]{1,0:T(8,128)(2,1)}, f32[1,512]{1,0:T(1,128)}, f32[1,256]{1,0:T(1,128)}, f32[16,256]{1,0:T(8,128)}) custom-call(f32[1024,1664]{1,0:T(8,128)} %fusion.60.given_ref.refs_0_, f32[1024,512]{1,0:T(8,128)} %fusion.62.refs_1_, f32[1024,512]{1,0:T(8,128)} %get-tuple-element.102.refs_2_, ...), custom_call_target="tpu_custom_call" | custom-call | flops 1000000 | bytes 10000 | tf_op jit(solution)/shard_map/mix_backward/pallas_call | solution.py:1038
  543.9 13.6 %pair_product.3 = bf16[4,256,1664]{2,1,0:T(8,128)(2,1)} custom-call(bf16[1024,2048]{1,0:T(8,128)(2,1)} %bitcast.87, bf16[1024,1664]{1,0:T(8,128)(2,1)} %get-tuple-element.115.right_ref), custom_call_target="tpu_custom_call" | custom-call | flops 1000000 | bytes 10000 | tf_op jit(solution)/shard_map/pair_product/pallas_call | solution.py:826
  565.1 12.9 %convolution_convert_fusion.2 = bf16[1024,2048]{1,0:T(8,128)(2,1)} fusion(bf16[1024,1664]{1,0:T(8,128)(2,1)} %get-tuple-element.115.right_ref, bf16[2048,1664]{1,0:T(8,128)(2,1)} %bitcast.106), kind=kOutput, calls=%fused_computation.7 | convolution fusion | flops 6981419008 | bytes 14417920 | tf_op jit(solution)/shard_map/dot_general | solution.py:31
  578.0 5.6 all-to-all-done.2.moved_ref
  587.4 41.9 %tokens_back.1 = (bf16[256,2048]{1,0:T(8,128)(2,1)S(1)}, f32[1,2048]{1,0:T(1,128)S(1)}) custom-call(bf16[4,256,2048]{2,1,0:T(8,128)(2,1)S(1)} %bitcast.84, bf16[256,2048]{1,0:T(8,128)(2,1)S(1)} %bitcast.83, f32[256,2048]{1,0:T(8,128)S(1)} %copy-done.15), custom_call_target="tpu_custom_call" | custom-call | flops 1000000 | bytes 10000 | tf_op jit(solution)/shard_map/tokens_back/pallas_call | solution.py:910
  630.9 4.4 all-to-all-start.3
  635.3 4.5 convert_reduce_fusion
  (216 shorter events, 92.7 us)
Async XLA Ops:
  7.2 94.1 %copy-start.12 = (bf16[1,256,2048]{2,1,0:T(8,128)(2,1)S(1)}, bf16[1,256,2048]{2,1,0:T(8,128)(2,1)}, u32[]{:S(2)}) copy-start(bf16[1,256,2048]{2,1,0:T(8,128)(2,1)} %param.33) | copy-start | bytes 3145732
  7.2 34.3 %all-gather.6.cloned.1.call-start = ((), (), s32[]{:S(2)}) async-start(), calls=%async_computation.9 | async-start | bytes 2359296 | tf_op jit(solution)/shard_map/all_gather | solution.py:1111
  7.9 106.6 %all-gather.8.cloned.1.call-start = ((), (), s32[]{:S(2)}) async-start(), calls=%async_computation.10 | async-start | bytes 7667712 | tf_op jit(solution)/shard_map/all_gather | solution.py:1104
  10.2 93.6 %copy-start.22 = (bf16[64,1]{1,0:T(8,128)(2,1)}, bf16[64,1]{1,0:T(8,128)(2,1)S(1)}, u32[]{:S(2)}) copy-start(bf16[64,1]{1,0:T(8,128)(2,1)S(1)} %copy.98.refs_5_.gain_ref) | copy-start | bytes 388
  103.8 64.1 %all-to-all-start = ((bf16[4,256,2048]{2,1,0:T(8,128)(2,1)}), bf16[4,256,2048]{2,1,0:T(8,128)(2,1)}, u32[]{:S(2)}, u32[]{:S(2)}) async-start(bf16[4,256,2048]{2,1,0:T(8,128)(2,1)} %broadcast_in_dim.101), calls=%async_computation | async-start | bytes 8388608 | tf_op jit(solution)/shard_map/all_to_all | solution.py:64
  108.8 59.1 %all-gather.10.cloned.1.call-start = ((), (), s32[]{:S(2)}) async-start(), calls=%async_computation.11 | async-start | bytes 3244032 | tf_op jit(solution)/shard_map/all_gather | solution.py:1111
  111.7 178.4 %all-gather.12.cloned.1.call-start = ((), (), s32[]{:S(2)}) async-start(), calls=%async_computation.12 | async-start | bytes 12976128 | tf_op jit(solution)/shard_map/all_gather | solution.py:1104
  134.3 33.7 %copy-start.37 = (bf16[512,2048]{1,0:T(8,128)(2,1)S(1)}, bf16[512,2048]{1,0:T(8,128)(2,1)}, u32[]{:S(2)}) copy-start(bf16[512,2048]{1,0:T(8,128)(2,1)} %all-gather.6.cloned.1.call-done) | copy-start | bytes 6291460
  167.9 161.5 %all-gather.14.cloned.1.call-start = ((), (), s32[]{:S(2)}) async-start(), calls=%async_computation.13 | async-start | bytes 3244032 | tf_op jit(solution)/shard_map/all_gather | solution.py:1111
  250.1 231.6 %reduce-scatter.5.cloned.1.call-start = ((), (), s32[]{:S(2)}) async-start(), calls=%async_computation.14 | async-start | bytes 3604480 | tf_op jit(solution)/shard_map/reduce_scatter | solution.py:1121
  323.9 19.3 %collective-permute-start = (bf16[1,704,2048]{2,1,0:T(8,128)(2,1)}, bf16[1,704,2048]{2,1,0:T(8,128)(2,1)}, u32[]{:S(2)}, u32[]{:S(2)}) collective-permute-start(bf16[1,704,2048]{2,1,0:T(8,128)(2,1)} %dynamic-slice_bitcast_fusion), channel_id=1, source_target_pairs={{0,4},{4,0},{1,5},{5,1},{2,6},{6,2},{3,7},{7,3},{8,12},{12,8},{9,1... | collective-permute-start | bytes 8650760 | tf_op jit(solution)/shard_map/ppermute | solution.py:1095
  348.8 195.0 %reduce-scatter.7.cloned.1.call-start = ((), (), s32[]{:S(2)}) async-start(), calls=%async_computation.15 | async-start | bytes 7208960 | tf_op jit(solution)/shard_map/reduce_scatter | solution.py:1101
  369.6 18.5 %copy-start = (bf16[1408,1024]{1,0:T(8,128)(2,1)S(1)}, bf16[1408,1024]{1,0:T(8,128)(2,1)}, u32[]{:S(2)}) copy-start(bf16[1408,1024]{1,0:T(8,128)(2,1)} %all-gather.10.cloned.1.call-done.down_ref) | copy-start | bytes 8650756
  369.6 18.5 %copy-start.1 = (bf16[1408,1024]{1,0:T(8,128)(2,1)S(1)}, bf16[1408,1024]{1,0:T(8,128)(2,1)}, u32[]{:S(2)}) copy-start(bf16[1408,1024]{1,0:T(8,128)(2,1)} %all-gather.14.cloned.1.call-done.rest_ref) | copy-start | bytes 8650756
  389.3 78.5 %copy-start.38 = (bf16[512,2048]{1,0:T(8,128)(2,1)S(1)}, bf16[512,2048]{1,0:T(8,128)(2,1)}, u32[]{:S(2)}) copy-start(bf16[512,2048]{1,0:T(8,128)(2,1)} %all-gather.6.cloned.1.call-done) | copy-start | bytes 6291460
  474.2 5.0 collective-permute-start.1
  474.2 69.6 %all-to-all-start.1 = ((bf16[4,256,2048]{2,1,0:T(8,128)(2,1)}), bf16[4,256,2048]{2,1,0:T(8,128)(2,1)}, u32[]{:S(2)}, u32[]{:S(2)}) async-start(bf16[4,256,2048]{2,1,0:T(8,128)(2,1)} %bitcast.88), calls=%async_computation.2 | async-start | bytes 8388608 | tf_op jit(solution)/shard_map/all_to_all | solution.py:70
  479.1 98.9 %reduce-scatter.9.cloned.1.call-start = ((), (), s32[]{:S(2)}) async-start(), calls=%async_computation.16 | async-start | bytes 1310720 | tf_op jit(solution)/shard_map/reduce_scatter | solution.py:1121
  481.8 149.1 %reduce-scatter.11.cloned.1.call-start = ((), (), s32[]{:S(2)}) async-start(), calls=%async_computation.17 | async-start | bytes 4259840 | tf_op jit(solution)/shard_map/reduce_scatter | solution.py:1101
  561.1 22.5 %all-to-all-start.2 = ((bf16[4,64,2816]{2,1,0:T(8,128)(2,1)}), bf16[4,64,2816]{2,1,0:T(8,128)(2,1)S(1)}, u32[]{:S(2)}, u32[]{:S(2)}) async-start(bf16[4,64,2816]{2,1,0:T(8,128)(2,1)} %reduce-scatter.7.cloned.1.call-done), calls=%async_computation.5 | async-start | bytes 2883584 | tf_op jit(solution)/shard_map/all_to_all | solution.py:1248
  565.1 18.5 %copy-start.4 = (bf16[1,256,2048]{2,1,0:T(8,128)(2,1)S(1)}, bf16[1,256,2048]{2,1,0:T(8,128)(2,1)}, u32[]{:S(2)}) copy-start(bf16[1,256,2048]{2,1,0:T(8,128)(2,1)} %param.17) | copy-start | bytes 3145732
  630.9 18.8 %copy-start.7 = (f32[256,2048]{1,0:T(8,128)S(1)}, f32[256,2048]{1,0:T(8,128)}, u32[]{:S(2)}) copy-start(f32[256,2048]{1,0:T(8,128)} %copy-done.5) | copy-start | bytes 6291460
  630.9 13.8 %all-to-all-start.3 = ((bf16[4,64,1664]{2,1,0:T(8,128)(2,1)}), bf16[4,64,1664]{2,1,0:T(8,128)(2,1)}, u32[]{:S(2)}, u32[]{:S(2)}) async-start(bf16[4,64,1664]{2,1,0:T(8,128)(2,1)} %reduce-scatter.11.cloned.1.call-done), calls=%async_computation.7 | async-start | bytes 1703936 | tf_op jit(solution)/shard_map/all_to_all | solution.py:1275
  646.4 13.3 %all-to-all-start.4 = ((f32[32,1,688]{2,1,0:T(1,128)}), f32[32,1,688]{2,1,0:T(1,128)}, u32[]{:S(2)}, u32[]{:S(2)}) async-start(f32[32,1,688]{2,1,0:T(1,128)} %copy.104), calls=%async_computation.8 | async-start | bytes 196608 | tf_op jit(solution)/shard_map/all_to_all | solution.py:1282
  (32 other events, 125.3 us)
Sparse Core Ops, SparseCore 0:
  9.6 31.7 all-gather.5
  43.1 68.5 all-gather.7
  113.8 34.7 all-gather.9
  168.0 121.9 all-gather.11
  292.1 37.2 all-gather.13
  349.0 54.5 reduce-scatter.4
  405.9 117.4 reduce-scatter.6
  526.2 32.5 reduce-scatter.8
  561.2 62.9 reduce-scatter.10
